TPU v7x, 32 devices: a whole 2x2x4 slice. The times are simulated.
32 devices in a mesh: chan: 8 (over y, x, core), win: 4 (over z).
Axes of the slice: x: 2, y: 2, z: 4, core: 2. Of those that a mesh axis runs over, the one named last changes fastest.
Arguments:
- traces: bfloat16 [64, 512, 512], P('win', 'chan'), may hold values from -80 to 80
- valid: int32 [64, 512], P('win', 'chan'), may hold values 0 or 1
- reach: int32 [512], P('chan'), may hold values from 1 to 256
Outputs:
- stack: float32 [256, 512, 256], P('win', 'chan')
All inputs are finite; a program needn't handle non-finite values. No bound on the sum of `valid` on one device may be relied on, other than what follows from the above.
Results may differ from a plain program's by a relative error of at most 0.0045.
Values may be sent and summed in bfloat16 or wider, within the bound.
No kernel may reach another device: no remote copies, remote signals or barrier semaphores. Data moves between devices by JAX's collectives and lax.ppermute only.
A program may use at most 128 MiB of HBM per device.

v0:
```python
import math

import jax
import jax.numpy as jnp
from jax import lax
from jax.sharding import PartitionSpec as P

F = 128
FIRST = 16
BAND = 256


def passed_along(array, axis, by):
    peers = lax.axis_size(axis)
    return lax.ppermute(array, axis, [(i, (i + by) % peers) for i in range(peers)])


def make_table(samples):
    t_int = jnp.arange(samples, dtype=jnp.int32)
    j_int = jnp.arange(F, dtype=jnp.int32) + FIRST
    phase = t_int[:, None] * j_int[None, :] % samples
    angle = 2.0 * math.pi / samples * phase.astype(jnp.float32)
    hann = 0.5 - 0.5 * jnp.cos(2.0 * math.pi / samples * t_int.astype(jnp.float32))
    return jnp.concatenate(
        [hann[:, None] * jnp.cos(angle), -hann[:, None] * jnp.sin(angle)], axis=1
    ).astype(jnp.bfloat16)


def whiten(spectra, valid):
    real_part = spectra[..., :F]
    imag_part = spectra[..., F:]
    amplitude = jnp.sqrt(real_part * real_part + imag_part * imag_part)
    level = jnp.sqrt(jnp.mean(amplitude * amplitude, axis=-1, keepdims=True) + 1e-06)
    factor = valid.astype(jnp.float32)[..., None] / (amplitude + 0.1 * level)
    return jnp.concatenate([real_part * factor, imag_part * factor], axis=-1).astype(jnp.bfloat16)


def extend(spectra, first_offset):
    width = spectra.shape[1]
    groups = lax.axis_size("win")
    offsets = BAND // groups
    farthest = (BAND - offsets) // width
    hop_count = first_offset // width
    remainder = first_offset % width
    moved = spectra
    for bit_index in range(farthest.bit_length()):
        arrived = passed_along(moved, "chan", -(1 << bit_index))
        moved = jnp.where(hop_count >> bit_index & 1 == 1, arrived, moved)
    joined = [moved]
    current = moved
    current = passed_along(current, "chan", -1)
    joined.append(current)
    window = lax.dynamic_slice_in_dim(
        jnp.concatenate(joined, axis=1), remainder, offsets + width, 1
    )
    return (jnp.concatenate([spectra, window], axis=1), width)


def accumulate(carry, extended, first_offset):
    width = carry.shape[1]
    offsets = carry.shape[0]
    block = math.gcd(offsets, 16)
    own = extended[:, :width]
    a_re = own[..., :F]
    a_im = own[..., F:]

    def one_block(index, total):
        begin = first_offset + index * block
        terms = []
        for shift_by in range(block):
            partner = lax.dynamic_slice_in_dim(extended, begin + shift_by, width, 1)
            b_re = partner[..., :F]
            b_im = partner[..., F:]
            real_sum = jnp.sum(
                a_re.astype(jnp.float32) * b_re.astype(jnp.float32)
                + a_im.astype(jnp.float32) * b_im.astype(jnp.float32),
                axis=0,
            )
            imag_sum = jnp.sum(
                a_im.astype(jnp.float32) * b_re.astype(jnp.float32)
                - a_re.astype(jnp.float32) * b_im.astype(jnp.float32),
                axis=0,
            )
            terms.append(jnp.concatenate([real_sum, imag_sum], axis=-1))
        term = jnp.stack(terms, axis=0)
        before = lax.dynamic_slice_in_dim(total, index * block, block, 0)
        return lax.dynamic_update_slice_in_dim(total, before + term, index * block, 0)

    return lax.fori_loop(0, offsets // block, one_block, carry)


def on_device(traces, valid, reach):
    samples = traces.shape[2]
    local_windows = traces.shape[0]
    width = traces.shape[1]
    groups = lax.axis_size("win")
    offsets = BAND // groups
    first_offset = lax.axis_index("win") * offsets
    table = make_table(samples)
    spectra = jnp.einsum("wct,tj->wcj", traces, table, preferred_element_type=jnp.float32)
    whitened = whiten(spectra, valid)
    initial = jnp.zeros((offsets, width, 2 * F), jnp.float32)
    every_window = lax.all_gather(whitened, "win", axis=0, tiled=True)
    extended, region_start = extend(every_window, first_offset)
    summed = accumulate(initial, extended, region_start)
    offset_ids = first_offset + jnp.arange(offsets, dtype=jnp.int32)
    inside = (offset_ids[:, None] < reach[None, :]).astype(jnp.float32)
    scale = 1.0 / math.sqrt(local_windows * groups)
    return summed * inside[:, :, None] * scale


def solution(mesh):
    in_specs = (P("win", "chan", None), P("win", "chan"), P("chan"))
    out_specs = P("win", "chan", None)
    return jax.shard_map(
        on_device, mesh=mesh, in_specs=in_specs, out_specs=out_specs, check_vma=False
    )
```

profile of v0, /device:TPU:11, one launch (start us, length us, event | category | flops | bytes accessed | tf_op | source)
XLA Modules:
  0.0 372.7 jit_solution(3143741957029411808)
XLA Ops:
  6.6 1.2 multiply_convert_fusion.3
  8.9 0.9 pad_maximum_fusion.1
  9.8 45.4 %all-gather.2.cloned.1.call-done = bf16[64,64,256]{2,1,0:T(8,128)(2,1)} async-done(((bf16[16,64,256]{2,1,0:T(8,128)(2,1)}), bf16[64,64,256]{2,1,0:T(8,128)(2,1)}) %all-gather.2.cloned.1.call-update) | async-done | bytes 2097168 | tf_op jit(solution)/shard_map/all_gather | solution.py:103
  55.2 0.9 collective-permute-start
  56.1 25.7 %collective-permute-done = bf16[64,64,256]{2,1,0:T(8,128)(2,1)} collective-permute-done((bf16[64,64,256]{2,1,0:T(8,128)(2,1)}, bf16[64,64,256]{2,1,0:T(8,128)(2,1)}, u32[]{:S(2)}, u32[]{:S(2)}) %collective-permute-start) | collective-permute-done | bytes 2097184 | tf_op jit(solution)/shard_map/ppermute | solution.py:15
  81.8 1.8 broadcast_select_fusion
  83.7 46.9 %collective-permute-done.1 = bf16[64,64,256]{2,1,0:T(8,128)(2,1)} collective-permute-done((bf16[64,64,256]{2,1,0:T(8,128)(2,1)S(1)}, bf16[64,64,256]{2,1,0:T(8,128)(2,1)}, u32[]{:S(2)}, u32[]{:S(2)}) %collective-permute-start.1) | collective-permute-done | bytes 2097184 | tf_op jit(solution)/shard_map/ppermute | solution.py:15
  130.6 1.5 broadcast_select_fusion.1
  132.3 1.9 fusion.90
  134.1 24.7 %collective-permute-done.2 = bf16[64,64,256]{2,1,0:T(8,128)(2,1)} collective-permute-done((bf16[64,64,256]{2,1,0:T(8,128)(2,1)}, bf16[64,64,256]{2,1,0:T(8,128)(2,1)}, u32[]{:S(2)}, u32[]{:S(2)}) %collective-permute-start.2) | collective-permute-done | bytes 2097184 | tf_op jit(solution)/shard_map/ppermute | solution.py:15
  158.9 5.5 %pad_maximum_fusion = bf16[64,192,256]{2,1,0:T(8,128)(2,1)} fusion(bf16[64,64,256]{2,1,0:T(8,128)(2,1)} %collective-permute-done.2, bf16[64,64,256]{2,1,0:T(8,128)(2,1)} %broadcast_select_fusion.1, bf16[64,64,256]{2,1,0:T(8,128)(2,1)S(1)} %copy-done.1), kind=kLoop, calls=%fused_computation.161 | loop fusion | flops 18874368 | bytes 12582912 | tf_op jit(solution)/shard_map/concatenate | solution.py:56
  164.3 2.5 broadcast_in_dim.2
  166.9 195.1 %while.17 = (s32[]{:T(128)}, f32[64,64,256]{2,1,0:T(8,128)}, bf16[64,64,128]{2,1,0:T(8,128)(2,1)S(1)}, bf16[64,192,256]{2,1,0:T(8,128)(2,1)}, bf16[64,64,128]{2,...) while((s32[]{:T(128)}, f32[64,64,256]{2,1,0:T(8,128)}, ...), condition=%wide.region_34.35_spmd, body=%wide.region_1.34_spmd.sunk | while | flops 86245440 | bytes 44041396 | solution.py:89
  166.9 32.8 %fusion.110 = (f32[64,128]{1,0:T(8,128)S(1)}, f32[64,128]{1,0:T(8,128)S(1)}, f32[64,128]{1,0:T(8,128)S(1)}, f32[64,128]{1,0:T(8,128)S(1)}, f32[64,128]{1,0:T(8,1...) fusion(bf16[64,64,128]{2,1,0:T(8,128)(2,1)S(1)} %get-tuple-elem, ...), kind=kLoop, calls=%fused_computation.125.clone.1 | loop fusion | flops 79446016 | bytes 34537536 | tf_op jit(solution)/shard_map/while/body/eval_jaxpr/reduce_sum | solution.py:74
  199.7 0.6 fusion.111
  208.4 3.2 fusion.125
  211.6 0.6 fusion.126
  212.9 2.7 add_dynamic-update-slice_fusion.2
  215.6 32.7 %fusion.110 = (f32[64,128]{1,0:T(8,128)S(1)}, f32[64,128]{1,0:T(8,128)S(1)}, f32[64,128]{1,0:T(8,128)S(1)}, f32[64,128]{1,0:T(8,128)S(1)}, f32[64,128]{1,0:T(8,1...) fusion(bf16[64,64,128]{2,1,0:T(8,128)(2,1)S(1)} %get-tuple-elem, ...), kind=kLoop, calls=%fused_computation.125.clone.1 | loop fusion | flops 79446016 | bytes 34537536 | tf_op jit(solution)/shard_map/while/body/eval_jaxpr/reduce_sum | solution.py:74
  256.9 3.2 fusion.125
  260.2 0.6 fusion.126
  260.8 0.6 fusion.127
  261.4 2.7 add_dynamic-update-slice_fusion.2
  264.1 33.1 %fusion.110 = (f32[64,128]{1,0:T(8,128)S(1)}, f32[64,128]{1,0:T(8,128)S(1)}, f32[64,128]{1,0:T(8,128)S(1)}, f32[64,128]{1,0:T(8,128)S(1)}, f32[64,128]{1,0:T(8,1...) fusion(bf16[64,64,128]{2,1,0:T(8,128)(2,1)S(1)} %get-tuple-elem, ...), kind=kLoop, calls=%fused_computation.125.clone.1 | loop fusion | flops 79446016 | bytes 34537536 | tf_op jit(solution)/shard_map/while/body/eval_jaxpr/reduce_sum | solution.py:74
  305.9 3.2 fusion.125
  309.1 0.6 fusion.126
  310.4 2.7 add_dynamic-update-slice_fusion.2
  313.1 33.0 %fusion.110 = (f32[64,128]{1,0:T(8,128)S(1)}, f32[64,128]{1,0:T(8,128)S(1)}, f32[64,128]{1,0:T(8,128)S(1)}, f32[64,128]{1,0:T(8,128)S(1)}, f32[64,128]{1,0:T(8,1...) fusion(bf16[64,64,128]{2,1,0:T(8,128)(2,1)S(1)} %get-tuple-elem, ...), kind=kLoop, calls=%fused_computation.125.clone.1 | loop fusion | flops 79446016 | bytes 34537536 | tf_op jit(solution)/shard_map/while/body/eval_jaxpr/reduce_sum | solution.py:74
  354.8 3.2 fusion.125
  358.0 0.6 fusion.126
  359.3 2.7 add_dynamic-update-slice_fusion.2
  362.0 3.9 %multiply_multiply_fusion = f32[64,64,256]{2,1,0:T(8,128)} fusion(f32[64,64,256]{2,1,0:T(8,128)} %get-tuple-element.204, f32[64,64]{1,0:T(8,128)S(1)} %compare_convert_fusion), kind=kLoop, calls=%fused_computation.162 | loop fusion | flops 2097152 | bytes 8404992 | tf_op jit(solution)/shard_map/mul | solution.py:109
  (79 shorter events, 37.3 us)
Async XLA Ops:
  6.5 1.2 copy-start
  6.5 2.0 copy-start.2
  6.5 48.6 %all-gather.2.cloned.1.call-start = ((), (), s32[]{:S(2)}) async-start(), calls=%async_computation | async-start | bytes 2621440 | tf_op jit(solution)/shard_map/all_gather | solution.py:103
  55.2 26.7 %collective-permute-start = (bf16[64,64,256]{2,1,0:T(8,128)(2,1)}, bf16[64,64,256]{2,1,0:T(8,128)(2,1)}, u32[]{:S(2)}, u32[]{:S(2)}) collective-permute-start(bf16[64,64,256]{2,1,0:T(8,128)(2,1)} %all-gather.2.cloned.1.call-done), channel_id=1, source_target_pairs={{0,28},{4,0},{8,4},{12,8},{16,12},{20,16},{24,20},{28,24},{1,29},{... | collective-permute-start | bytes 6291464 | tf_op jit(solution)/shard_map/ppermute | solution.py:15
  83.6 47.0 %collective-permute-start.1 = (bf16[64,64,256]{2,1,0:T(8,128)(2,1)S(1)}, bf16[64,64,256]{2,1,0:T(8,128)(2,1)}, u32[]{:S(2)}, u32[]{:S(2)}) collective-permute-start(bf16[64,64,256]{2,1,0:T(8,128)(2,1)S(1)} %broadcast_select_fusion), channel_id=1, source_target_pairs={{0,24},{4,28},{8,0},{12,4},{16,8},{20,12},{24,16},{28,20},{1,25},{... | collective-permute-start | bytes 6291464 | tf_op jit(solution)/shard_map/ppermute | solution.py:15
  83.7 48.5 %copy-start.3 = (s32[64]{0:T(128)S(1)}, s32[64]{0:T(128)}, u32[]{:S(2)}) copy-start(s32[64]{0:T(128)} %param.7) | copy-start | bytes 772
  132.2 26.7 %collective-permute-start.2 = (bf16[64,64,256]{2,1,0:T(8,128)(2,1)}, bf16[64,64,256]{2,1,0:T(8,128)(2,1)}, u32[]{:S(2)}, u32[]{:S(2)}) collective-permute-start(bf16[64,64,256]{2,1,0:T(8,128)(2,1)} %broadcast_select_fusion.1), channel_id=1, source_target_pairs={{0,28},{4,0},{8,4},{12,8},{16,12},{20,16},{24,20},{28,24},{1,29},{... | collective-permute-start | bytes 6291464 | tf_op jit(solution)/shard_map/ppermute | solution.py:15
  132.3 26.6 %copy-start.1 = (bf16[64,64,256]{2,1,0:T(8,128)(2,1)S(1)}, bf16[64,64,256]{2,1,0:T(8,128)(2,1)}, u32[]{:S(2)}) copy-start(bf16[64,64,256]{2,1,0:T(8,128)(2,1)} %all-gather.2.cloned.1.call-done) | copy-start | bytes 6291460
Sparse Core Ops, SparseCore 0:
  9.9 45.2 all-gather.1
where the time goes:
time: 375 us; the launch traced here: 373 us
  other arithmetic  211 us (56%)
  waiting for transfers between devices  143 us (38%)
  between operations  13.5 us (4%)
  local copies, waits for them, and re-layouts  4.41 us (1%)
    reduce_sum x8, other arithmetic, one_block(): jnp.sum(a_re.astype(jnp.float32) * b_re.astype(jnp.float32) + a_im.astype...  145 us
    ppermute x3, waiting for transfers between devices, passed_along(): lax.ppermute(array, axis, [(i, (i + by) % peers) for i in range(peers)])  97.4 us
    all_gather x1, waiting for transfers between devices, on_device(): every_window = lax.all_gather(whitened, 'win', axis=0, tiled=True)  45.4 us
    while x60, other arithmetic  37.3 us
    dynamic_update_slice x4, other arithmetic, one_block(): lax.dynamic_update_slice_in_dim(total, before + term, index * block, 0)  10.7 us
  transfers between devices with their start and end apart: 4, of which 4 were waited for; matrix products, arithmetic and copies ran while one was open for 1% of the time, Pallas kernels for 0%

commit v1 on v0

v1 whole, which is shorter than its diff:
```python
import functools
import math

import jax
import jax.numpy as jnp
import numpy as np
from jax import lax
from jax.experimental import pallas as pl
from jax.experimental.pallas import tpu as pltpu
from jax.sharding import PartitionSpec as P

F = 128
FIRST = 16
BAND = 256
AXES = ("chan", "win")
VMEM_LIMIT = 48 * 1024 * 1024
FREQUENCY_STEPS = 4
CHANNEL_BLOCK = 8


def make_table(samples):
    t_int = np.arange(samples, dtype=np.int64)
    j_int = np.arange(F, dtype=np.int64) + FIRST
    angle = 2.0 * np.pi / samples * (j_int[:, None] * t_int[None, :] % samples)
    hann = 0.5 - 0.5 * np.cos(2.0 * np.pi / samples * t_int)
    rows = np.concatenate([hann * np.cos(angle), -hann * np.sin(angle)], axis=0)
    return jnp.asarray(rows.astype(np.float32)).astype(jnp.bfloat16)


def whiten_kernel(table_ref, traces_ref, valid_ref, out_ref, rows):
    windows, width, samples = traces_ref.shape
    for g in range(windows // 2):
        block = traces_ref[2 * g : 2 * g + 2].reshape(2 * width, samples)
        spectra = lax.dot_general(
            table_ref[...], block, (((1,), (1,)), ((), ())), preferred_element_type=jnp.float32
        )
        re, im = spectra[:F], spectra[F:]
        power = re * re + im * im
        level = jnp.sqrt(jnp.mean(power, axis=0, keepdims=True) + 1e-06)
        usable = jnp.concatenate(
            [valid_ref[2 * g : 2 * g + 1, :], valid_ref[2 * g + 1 : 2 * g + 2, :]], axis=1
        ).astype(jnp.float32)
        factor = usable / (jnp.sqrt(power) + 0.1 * level)
        re, im = re * factor, im * factor
        for k in range(2):
            half = slice(k * width, (k + 1) * width)
            rows[pl.ds(2 * g + k, F, stride=windows), :] = jnp.concatenate(
                [re[:, half], im[:, half]], axis=1
            )
    out_ref[...] = rows[...].reshape(out_ref.shape).astype(jnp.bfloat16)


def whitened_chunk(traces, valid):
    windows, width, samples = traces.shape
    return pl.pallas_call(
        whiten_kernel,
        out_shape=jax.ShapeDtypeStruct((F, windows, 2 * width), jnp.bfloat16),
        in_specs=[pl.BlockSpec(memory_space=pltpu.VMEM)] * 3,
        out_specs=pl.BlockSpec(memory_space=pltpu.VMEM),
        scratch_shapes=[pltpu.VMEM((F * windows, 2 * width), jnp.float32)],
        compiler_params=pltpu.CompilerParams(vmem_limit_bytes=VMEM_LIMIT),
        cost_estimate=pl.CostEstimate(
            flops=4 * F * windows * width * samples, bytes_accessed=2 * traces.size, transcendentals=0
        ),
        name="whiten",
    )(make_table(samples), traces, valid)


def stack_kernel(slots, f_steps, scale, place_ref, reach_ref, *refs):
    own_refs, first_refs, second_refs = refs[:slots], refs[slots : 2 * slots], refs[2 * slots : 3 * slots]
    out_ref, products = refs[3 * slots], refs[3 * slots + 1]
    step = pl.program_id(0)
    f_block, _, lanes = own_refs[0].shape
    width = lanes // 2
    offsets, i_block, _ = out_ref.shape

    @pl.when(step < f_steps)
    def _():
        def one_bin(f, carry):
            a = jnp.concatenate([r[f] for r in own_refs], axis=0)
            at = a.T
            left = jnp.concatenate([at[:width], at[width:]], axis=1)
            tops, bottoms = [], []
            for group in (first_refs, second_refs):
                b = jnp.concatenate([r[f] for r in group], axis=0)
                tops.append(b)
                bottoms.append(jnp.concatenate([b[:, width:], -b[:, :width]], axis=1))
            right = jnp.concatenate(
                [jnp.concatenate(tops, axis=1), jnp.concatenate(bottoms, axis=1)], axis=0
            )
            row = (step * f_block + f) * width
            both = jnp.dot(left, right, preferred_element_type=jnp.float32)
            for half in range(2):
                products[half, pl.ds(pl.multiple_of(row, width), width), :] = both[
                    :, half * lanes : (half + 1) * lanes
                ]
            return carry

        lax.fori_loop(0, f_block, one_bin, 0, unroll=4)

    @pl.when(step >= f_steps)
    def _():
        lane = lax.broadcasted_iota(jnp.int32, (offsets, 2 * lanes), 1)
        k = lax.broadcasted_iota(jnp.int32, (offsets, 2 * lanes), 0)
        partner = lane % width + jnp.where(lane >= lanes, width, 0)
        is_real = lane % lanes < width
        far = 4 * lanes
        shift_re = jnp.where(is_real, partner - k, far)
        shift_im = jnp.where(is_real, far, partner - k)
        first_k = place_ref[0]
        base = (step - f_steps) * i_block
        row_k = lax.broadcasted_iota(jnp.int32, (offsets, F), 0) + first_k
        for il in range(i_block):
            i = base + il
            at = i + place_ref[1]
            pick = jnp.concatenate(
                [
                    jnp.where(shift_re == at, 1.0, 0.0),
                    jnp.where(shift_im == at, -1.0, 0.0),
                ],
                axis=0,
            ).astype(jnp.bfloat16)
            x = jnp.concatenate(
                [products[half, pl.ds(i, F, stride=width), :] for half in range(2)], axis=1
            ).astype(jnp.bfloat16)
            y = lax.dot_general(
                pick, x, (((1,), (1,)), ((), ())), preferred_element_type=jnp.float32
            )
            inside = jnp.where(row_k < reach_ref[i], scale, 0.0)
            out_ref[:, il, 0:F] = y[:offsets] * inside
            out_ref[:, il, F : 2 * F] = y[offsets:] * inside


def stacked(own, first, second, place, reach, offsets, windows):
    slots = len(own)
    bins, chunk_windows, lanes = own[0].shape
    width = lanes // 2
    f_steps, i_steps = FREQUENCY_STEPS, width // CHANNEL_BLOCK
    chunk_spec = pl.BlockSpec(
        (bins // f_steps, chunk_windows, lanes), lambda s, *_: (jnp.minimum(s, f_steps - 1), 0, 0)
    )
    return pl.pallas_call(
        functools.partial(stack_kernel, slots, f_steps, 1.0 / math.sqrt(windows)),
        out_shape=jax.ShapeDtypeStruct((offsets, width, 2 * F), jnp.float32),
        grid_spec=pltpu.PrefetchScalarGridSpec(
            num_scalar_prefetch=2,
            grid=(f_steps + i_steps,),
            in_specs=[chunk_spec] * (3 * slots),
            out_specs=pl.BlockSpec(
                (offsets, CHANNEL_BLOCK, 2 * F), lambda s, *_: (0, jnp.maximum(s - f_steps, 0), 0)
            ),
            scratch_shapes=[pltpu.VMEM((2, bins * width, lanes), jnp.float32)],
        ),
        compiler_params=pltpu.CompilerParams(vmem_limit_bytes=VMEM_LIMIT),
        cost_estimate=pl.CostEstimate(
            flops=16 * bins * width * width * windows,
            bytes_accessed=8 * offsets * width * F + 6 * slots * own[0].size,
            transcendentals=0,
        ),
        name="stack",
    )(place, reach, *own, *first, *second)


def send(array, pairs):
    return lax.ppermute(array, AXES, pairs)


def pairs_of(n_win, n_chan, target):
    pairs = []
    for z in range(n_win):
        for c in range(n_chan):
            to = target(z, c)
            if to is not None:
                pairs.append((c * n_win + z, to * n_win + z))
    return pairs


def partners_direct(piece, hops, n_win, n_chan):
    first = send(piece, pairs_of(n_win, n_chan, lambda z, c: (c - hops[z]) % n_chan))
    second = send(piece, pairs_of(n_win, n_chan, lambda z, c: (c - hops[z] - 1) % n_chan))
    return first, second


def partners_square(piece, n_win, n_chan):
    z, c = lax.axis_index("win"), lax.axis_index("chan")
    core, x = c % 2, c // 2 % 2
    along_y = pairs_of(n_win, n_chan, lambda z, c: c ^ 4 if z == 3 or c % 2 == 0 else None)

    def x_target(z, c):
        core, x = c % 2, c // 2 % 2
        if z == 0:
            return c ^ 2 if x == 1 and core == 0 else None
        if z == 3:
            return c ^ 2 if x == 1 and core == 1 else None
        return c ^ 2 if x == 1 or core == 1 else None

    def onward_target(z, c):
        core, x = c % 2, c // 2 % 2
        if z == 0:
            return c ^ 2 if x == 0 and core == 0 else None
        if z == 3:
            return c ^ 2 if x == 0 and core == 1 else None
        if core == 0:
            return c ^ 2 if x == 0 else None
        return c ^ 4 if x == 1 else None

    from_y = send(piece, along_y)
    from_x = send(piece, pairs_of(n_win, n_chan, x_target))
    relay = jnp.where((core == 0) | (z == 3), from_y, from_x)
    onward = send(relay, pairs_of(n_win, n_chan, onward_target))
    next_chip = jnp.where(x == 0, from_x, onward)
    for_core = jnp.where(
        core == 0, jnp.where(z < 2, next_chip, from_y), jnp.where(z < 2, piece, next_chip)
    )
    swapped = send(for_core, pairs_of(n_win, n_chan, lambda z, c: c ^ 1))
    first = jnp.where(z == 0, piece, jnp.where(z == 2, next_chip, swapped))
    second = jnp.where(z == 1, next_chip, jnp.where(z == 3, from_y, swapped))
    return first, second


def on_device(traces, valid, reach):
    width = traces.shape[1]
    n_win, n_chan = lax.axis_size("win"), lax.axis_size("chan")
    windows = traces.shape[0] * n_win
    offsets = BAND // n_win
    hops = [z * offsets // width for z in range(n_win)]
    first_offset = lax.axis_index("win") * offsets
    place = jnp.stack([first_offset, first_offset % width]).astype(jnp.int32)
    piece = whitened_chunk(traces, valid)
    own, first, second = [], [], []
    for slot in range(n_win):
        if slot:
            piece = lax.ppermute(piece, "win", [(z, (z + 1) % n_win) for z in range(n_win)])
        if n_chan == 8 and hops == list(range(4)):
            b1, b2 = partners_square(piece, n_win, n_chan)
        else:
            b1, b2 = partners_direct(piece, hops, n_win, n_chan)
        own.append(piece)
        first.append(b1)
        second.append(b2)
    return stacked(own, first, second, place, reach, offsets, windows)


def solution(mesh):
    in_specs = (P("win", "chan", None), P("win", "chan"), P("chan"))
    out_specs = P("win", "chan", None)
    return jax.shard_map(
        on_device, mesh=mesh, in_specs=in_specs, out_specs=out_specs, check_vma=False
    )
```

time: 375 us -> 98.8 us (0.26)
  other arithmetic: 211 us -> 7.18 us
  waiting for transfers between devices: 143 us -> 25.1 us
  starting transfers between devices: 1 us -> 41.1 us
  Pallas kernels: 0 us -> 21.7 us
  between operations: 13.5 us -> 0.29 us
    reduce_sum x9 -> x0, other arithmetic: 145 us -> none  [the longest x8 145 us: one_block(): jnp.sum(a_re.astype(jnp.float32) * b_re.astype(jnp.float32) + a_im.astype...]
    ppermute x3 -> x19, waiting for transfers between devices: 97.4 us -> 25.1 us  [the longest x3 13.2 us: on_device(): lax.ppermute(piece, 'win', [(z, (z + 1) % n_win) for z in range(n_win)])]
    all_gather x1 -> x0, waiting for transfers between devices: 45.4 us -> none  [on_device(): every_window = lax.all_gather(whitened, 'win', axis=0, tiled=True)]
    ppermute x3 -> x19, starting transfers between devices: 0.99 us -> 41.1 us  [the longest x16 38.2 us: send(): return lax.ppermute(array, AXES, pairs)]
    while x60 -> x0, other arithmetic: 37.3 us -> none
    pallas_call x0 -> x2, Pallas kernels: none -> 21.7 us  [the longest x1 20.5 us: stacked(): pl.pallas_call(functools.partial(stack_kernel, slots, f_steps, 1.0 / math...]
    dynamic_update_slice x4 -> x0, other arithmetic: 10.7 us -> none  [one_block(): lax.dynamic_update_slice_in_dim(total, before + term, index * block, 0)]
    concatenate x2 -> x0, other arithmetic: 6.34 us -> none  [the longest x1 5.48 us: extend(): return (jnp.concatenate([spectra, window], axis=1), width)]
  transfers between devices with their start and end apart: 4 -> 19, of which waited for: 4 -> 6; matrix products, arithmetic and copies ran while one was open for 1% -> 6% of each run, Pallas kernels for 0% -> 0%
where the time goes in v1:
time: 98.8 us; the launch traced here: 98.2 us
  starting transfers between devices  41.1 us (42%)
  waiting for transfers between devices  25.1 us (25%)
  Pallas kernels  21.7 us (22%)
  other arithmetic  7.18 us (7%)
  local copies, waits for them, and re-layouts  2.88 us (3%)
    ppermute x16, starting transfers between devices, send(): return lax.ppermute(array, AXES, pairs)  38.2 us
    pallas_call x1, Pallas kernels, stacked(): pl.pallas_call(functools.partial(stack_kernel, slots, f_steps, 1.0 / math...  20.5 us
    ppermute x3, waiting for transfers between devices, on_device(): lax.ppermute(piece, 'win', [(z, (z + 1) % n_win) for z in range(n_win)])  13.2 us
    ppermute x16, waiting for transfers between devices, send(): return lax.ppermute(array, AXES, pairs)  11.9 us
    select_n x4, other arithmetic, partners_square(): relay = jnp.where((core == 0) | (z == 3), from_y, from_x)  2.96 us
    ppermute x3, starting transfers between devices, on_device(): lax.ppermute(piece, 'win', [(z, (z + 1) % n_win) for z in range(n_win)])  2.94 us
    unnamed x10, local copies, waits for them, and re-layouts  2.88 us
    select_n x4, other arithmetic, partners_square(): jnp.where(core == 0, jnp.where(z < 2, next_chip, from_y), jnp.where(z < 2...  2.65 us
  transfers between devices with their start and end apart: 19, of which 6 were waited for; matrix products, arithmetic and copies ran while one was open for 6% of the time, Pallas kernels for 0%

profile of v1, /device:TPU:11, one launch (start us, length us, event | category | flops | bytes accessed | tf_op | source)
XLA Modules:
  0.0 98.2 jit_solution(14003584467896439532)
XLA Ops:
  0.0 1.2 %copy-done = bf16[16,64,512]{2,1,0:T(8,128)(2,1)S(1)} copy-done((bf16[16,64,512]{2,1,0:T(8,128)(2,1)S(1)}, bf16[16,64,512]{2,1,0:T(8,128)(2,1)}, u32[]{:S(2)}) %copy-start) | copy-done | bytes 1048600
  1.2 0.9 copy-done.1
  2.2 0.7 copy-done.2
  2.9 1.2 %whiten.1.refs_0_ = bf16[128,16,128]{2,1,0:T(8,128)(2,1)S(1)} custom-call(bf16[256,512]{1,0:T(8,128)(2,1)S(1)} %copy-done.1, bf16[16,64,512]{2,1,0:T(8,128)(2,1)S(1)} %copy-done, s32[16,64]{1,0:T(8,128)S(1)} %copy-done.2), custom_call_target="tpu_custom_call" | custom-call | flops 268435456 | bytes 1048576 | tf_op jit(solution)/shard_map/whiten/pallas_call | solution.py:55
  4.1 1.4 %collective-permute-start = (bf16[128,16,128]{2,1,0:T(8,128)(2,1)S(1)}, bf16[128,16,128]{2,1,0:T(8,128)(2,1)S(1)}, u32[]{:S(2)}, u32[]{:S(2)}) collective-permute-start(bf16[128,16,128]{2,1,0:T(8,128)(2,1)S(1)} %whiten.1.refs_0_), channel_id=1, source_target_pairs={{0,1},{1,2},{2,3},{3,0},{4,5},{5,6},{6,7},{7,4},{8,9},{9,10},{10,1... | collective-permute-start | bytes 1572872 | tf_op jit(solution)/shard_map/ppermute | solution.py:233
  6.2 2.2 %collective-permute-start.3 = (bf16[128,16,128]{2,1,0:T(8,128)(2,1)S(1)}, bf16[128,16,128]{2,1,0:T(8,128)(2,1)S(1)}, u32[]{:S(2)}, u32[]{:S(2)}) collective-permute-start(bf16[128,16,128]{2,1,0:T(8,128)(2,1)S(1)} %whiten.1.refs_0_), channel_id=1, source_target_pairs={{8,0},{24,16},{5,13},{9,1},{13,5},{21,29},{25,17},{29,21},{6,14},{... | collective-permute-start | bytes 1572872 | tf_op jit(solution)/shard_map/ppermute | solution.py:165
  8.3 8.6 %collective-permute-done.refs_1_ = bf16[128,16,128]{2,1,0:T(8,128)(2,1)S(1)} collective-permute-done((bf16[128,16,128]{2,1,0:T(8,128)(2,1)S(1)}, bf16[128,16,128]{2,1,0:T(8,128)(2,1)S(1)}, u32[]{:S(2)}, u32[]{:S(2)}) %collective-permute-start) | collective-permute-done | bytes 524320 | tf_op jit(solution)/shard_map/ppermute | solution.py:233
  17.0 1.3 %collective-permute-start.1 = (bf16[128,16,128]{2,1,0:T(8,128)(2,1)S(1)}, bf16[128,16,128]{2,1,0:T(8,128)(2,1)S(1)}, u32[]{:S(2)}, u32[]{:S(2)}) collective-permute-start(bf16[128,16,128]{2,1,0:T(8,128)(2,1)S(1)} %collective-permute-done.refs_1_), channel_id=1, source_target_pairs={{0,1},{1,2},{2,3},{3,0},{4,5},{5,6},{6,7},{7,4},{8,9},{9,10},{10,1... | collective-permute-start | bytes 1572872 | tf_op jit(solution)/shard_map/ppermute | solution.py:233
  19.0 2.2 %collective-permute-start.7 = (bf16[128,16,128]{2,1,0:T(8,128)(2,1)S(1)}, bf16[128,16,128]{2,1,0:T(8,128)(2,1)}, u32[]{:S(2)}, u32[]{:S(2)}) collective-permute-start(bf16[128,16,128]{2,1,0:T(8,128)(2,1)S(1)} %collective-permute-done.refs_1_), channel_id=1, source_target_pairs={{8,0},{24,16},{5,13},{9,1},{13,5},{21,29},{25,17},{29,21},{6,14},{... | collective-permute-start | bytes 1572872 | tf_op jit(solution)/shard_map/ppermute | solution.py:165
  21.2 0.9 broadcast_select_fusion.3
  22.1 3.1 %collective-permute-start.5 = (bf16[128,16,128]{2,1,0:T(8,128)(2,1)}, bf16[128,16,128]{2,1,0:T(8,128)(2,1)}, u32[]{:S(2)}, u32[]{:S(2)}) collective-permute-start(bf16[128,16,128]{2,1,0:T(8,128)(2,1)} %broadcast_select_fusion.3), channel_id=1, source_target_pairs={{0,8},{16,24},{1,9},{13,29},{17,25},{29,13},{2,10},{14,30},{18,26}... | collective-permute-start | bytes 1572872 | tf_op jit(solution)/shard_map/ppermute | solution.py:165
  25.3 4.6 %collective-permute-done.1.refs_2_ = bf16[128,16,128]{2,1,0:T(8,128)(2,1)S(1)} collective-permute-done((bf16[128,16,128]{2,1,0:T(8,128)(2,1)S(1)}, bf16[128,16,128]{2,1,0:T(8,128)(2,1)S(1)}, u32[]{:S(2)}, u32[]{:S(2)}) %collective-permute-start.1) | collective-permute-done | bytes 524320 | tf_op jit(solution)/shard_map/ppermute | solution.py:233
  30.1 1.9 %broadcast_select_fusion.2 = bf16[128,16,128]{2,1,0:T(8,128)(2,1)} fusion(bf16[128,16,128]{2,1,0:T(8,128)(2,1)S(1)} %collective-permute-done.8, bf16[128,16,128]{2,1,0:T(8,128)(2,1)} %collective-permute-done.7, pred[]{:T(512)S(6)} %or.2), kind=kLoop, calls=%fused_computation.14 | loop fusion | flops 262144 | bytes 1572865 | tf_op jit(solution)/shard_map/jit(_where)/select_n | solution.py:209
  32.1 3.1 %collective-permute-start.9 = (bf16[128,16,128]{2,1,0:T(8,128)(2,1)}, bf16[128,16,128]{2,1,0:T(8,128)(2,1)}, u32[]{:S(2)}, u32[]{:S(2)}) collective-permute-start(bf16[128,16,128]{2,1,0:T(8,128)(2,1)} %broadcast_select_fusion.2), channel_id=1, source_target_pairs={{0,8},{16,24},{1,9},{13,29},{17,25},{29,13},{2,10},{14,30},{18,26}... | collective-permute-start | bytes 1572872 | tf_op jit(solution)/shard_map/ppermute | solution.py:165
  35.3 0.7 collective-permute-start.12
  36.0 1.9 %collective-permute-start.11 = (bf16[128,16,128]{2,1,0:T(8,128)(2,1)S(1)}, bf16[128,16,128]{2,1,0:T(8,128)(2,1)S(1)}, u32[]{:S(2)}, u32[]{:S(2)}) collective-permute-start(bf16[128,16,128]{2,1,0:T(8,128)(2,1)S(1)} %collective-permute-done.1.refs_2_), channel_id=1, source_target_pairs={{8,0},{24,16},{5,13},{9,1},{13,5},{21,29},{25,17},{29,21},{6,14},{... | collective-permute-start | bytes 1572872 | tf_op jit(solution)/shard_map/ppermute | solution.py:165
  38.0 1.2 %select_select_fusion.11 = (bf16[128,16,128]{2,1,0:T(8,128)(2,1)S(1)}, bf16[128,16,128]{2,1,0:T(8,128)(2,1)S(1)}) fusion(bf16[128,16,128]{2,1,0:T(8,128)(2,1)S(1)} %whiten.1.refs_0_, bf16[128,16,128]{2,1,0:T(8,128)(2,1)S(1)} %collective-permute-done.4, pred[]{:T(512)S(6)} %lt.39, pred[]{:T(512)S(6)} %eq.25, bf16[128,16,128]{2,1,0:T(8,128)(2,1)} %copy-done.4, ...), kind=kLoop, calls=%fused_computation.11 | loop fusion | flops 1048576 | bytes 3145731 | tf_op jit(solution)/shard_map/jit(_where)/select_n | solution.py:212
  39.1 8.1 %collective-permute-start.6 = (bf16[128,16,128]{2,1,0:T(8,128)(2,1)S(1)}, bf16[128,16,128]{2,1,0:T(8,128)(2,1)S(1)}, u32[]{:S(2)}, u32[]{:S(2)}) collective-permute-start(bf16[128,16,128]{2,1,0:T(8,128)(2,1)S(1)} %get-tuple-element.11), channel_id=1, source_target_pairs={{0,4},{4,0},{8,12},{12,8},{16,20},{20,16},{24,28},{28,24},{1,5},{5... | collective-permute-start | bytes 1572872 | tf_op jit(solution)/shard_map/ppermute | solution.py:165
  47.2 0.7 collective-permute-start.16
  47.9 1.9 %collective-permute-start.15 = (bf16[128,16,128]{2,1,0:T(8,128)(2,1)S(1)}, bf16[128,16,128]{2,1,0:T(8,128)(2,1)S(1)}, u32[]{:S(2)}, u32[]{:S(2)}) collective-permute-start(bf16[128,16,128]{2,1,0:T(8,128)(2,1)S(1)} %collective-permute-done.2.refs_3_), channel_id=1, source_target_pairs={{8,0},{24,16},{5,13},{9,1},{13,5},{21,29},{25,17},{29,21},{6,14},{... | collective-permute-start | bytes 1572872 | tf_op jit(solution)/shard_map/ppermute | solution.py:165
  49.9 1.2 %select_select_fusion.9 = (bf16[128,16,128]{2,1,0:T(8,128)(2,1)S(1)}, bf16[128,16,128]{2,1,0:T(8,128)(2,1)S(1)}) fusion(bf16[128,16,128]{2,1,0:T(8,128)(2,1)S(1)} %collective-permute-done.refs_1_, bf16[128,16,128]{2,1,0:T(8,128)(2,1)S(1)} %collective-permute-done.8, pred[]{:T(512)S(6)} %lt.39, pred[]{:T(512)S(6)} %eq.25, ...), kind=kLoop, calls=%fused_computation.9 | loop fusion | flops 1048576 | bytes 3145731 | tf_op jit(solution)/shard_map/jit(_where)/select_n | solution.py:212
  51.1 4.0 %collective-permute-start.10 = (bf16[128,16,128]{2,1,0:T(8,128)(2,1)S(1)}, bf16[128,16,128]{2,1,0:T(8,128)(2,1)S(1)}, u32[]{:S(2)}, u32[]{:S(2)}) collective-permute-start(bf16[128,16,128]{2,1,0:T(8,128)(2,1)S(1)} %get-tuple-element.9), channel_id=1, source_target_pairs={{0,4},{4,0},{8,12},{12,8},{16,20},{20,16},{24,28},{28,24},{1,5},{5... | collective-permute-start | bytes 1572872 | tf_op jit(solution)/shard_map/ppermute | solution.py:165
  55.1 2.1 %collective-permute-start.13 = (bf16[128,16,128]{2,1,0:T(8,128)(2,1)S(1)}, bf16[128,16,128]{2,1,0:T(8,128)(2,1)S(1)}, u32[]{:S(2)}, u32[]{:S(2)}) collective-permute-start(bf16[128,16,128]{2,1,0:T(8,128)(2,1)S(1)} %broadcast_select_fusion.1), channel_id=1, source_target_pairs={{0,8},{16,24},{1,9},{13,29},{17,25},{29,13},{2,10},{14,30},{18,26}... | collective-permute-start | bytes 1572872 | tf_op jit(solution)/shard_map/ppermute | solution.py:165
  57.3 3.9 %collective-permute-done.15 = bf16[128,16,128]{2,1,0:T(8,128)(2,1)S(1)} collective-permute-done((bf16[128,16,128]{2,1,0:T(8,128)(2,1)S(1)}, bf16[128,16,128]{2,1,0:T(8,128)(2,1)S(1)}, u32[]{:S(2)}, u32[]{:S(2)}) %collective-permute-start.15) | collective-permute-done | bytes 524320 | tf_op jit(solution)/shard_map/ppermute | solution.py:165
  61.2 2.2 %collective-permute-start.17 = (bf16[128,16,128]{2,1,0:T(8,128)(2,1)S(1)}, bf16[128,16,128]{2,1,0:T(8,128)(2,1)S(1)}, u32[]{:S(2)}, u32[]{:S(2)}) collective-permute-start(bf16[128,16,128]{2,1,0:T(8,128)(2,1)S(1)} %broadcast_select_fusion), channel_id=1, source_target_pairs={{0,8},{16,24},{1,9},{13,29},{17,25},{29,13},{2,10},{14,30},{18,26}... | collective-permute-start | bytes 1572872 | tf_op jit(solution)/shard_map/ppermute | solution.py:165
  63.6 1.8 %collective-permute-done.13 = bf16[128,16,128]{2,1,0:T(8,128)(2,1)S(1)} collective-permute-done((bf16[128,16,128]{2,1,0:T(8,128)(2,1)S(1)}, bf16[128,16,128]{2,1,0:T(8,128)(2,1)S(1)}, u32[]{:S(2)}, u32[]{:S(2)}) %collective-permute-start.13) | collective-permute-done | bytes 524320 | tf_op jit(solution)/shard_map/ppermute | solution.py:165
  65.5 0.9 collective-permute-start.14
  66.5 5.0 %collective-permute-done.17 = bf16[128,16,128]{2,1,0:T(8,128)(2,1)S(1)} collective-permute-done((bf16[128,16,128]{2,1,0:T(8,128)(2,1)S(1)}, bf16[128,16,128]{2,1,0:T(8,128)(2,1)S(1)}, u32[]{:S(2)}, u32[]{:S(2)}) %collective-permute-start.17) | collective-permute-done | bytes 524320 | tf_op jit(solution)/shard_map/ppermute | solution.py:165
  71.6 3.6 %collective-permute-start.18 = (bf16[128,16,128]{2,1,0:T(8,128)(2,1)S(1)}, bf16[128,16,128]{2,1,0:T(8,128)(2,1)S(1)}, u32[]{:S(2)}, u32[]{:S(2)}) collective-permute-start(bf16[128,16,128]{2,1,0:T(8,128)(2,1)S(1)} %get-tuple-element.5), channel_id=1, source_target_pairs={{0,4},{4,0},{8,12},{12,8},{16,20},{20,16},{24,28},{28,24},{1,5},{5... | collective-permute-start | bytes 1572872 | tf_op jit(solution)/shard_map/ppermute | solution.py:165
  75.6 1.2 %collective-permute-done.18 = bf16[128,16,128]{2,1,0:T(8,128)(2,1)S(1)} collective-permute-done((bf16[128,16,128]{2,1,0:T(8,128)(2,1)S(1)}, bf16[128,16,128]{2,1,0:T(8,128)(2,1)S(1)}, u32[]{:S(2)}, u32[]{:S(2)}) %collective-permute-start.18) | collective-permute-done | bytes 524320 | tf_op jit(solution)/shard_map/ppermute | solution.py:165
  76.8 1.0 select_select_fusion
  77.8 20.5 %stack.13 = f32[64,64,256]{2,1,0:T(8,128)} custom-call(s32[2]{0:T(128)S(1)} %pad_add_fusion.place_ref, s32[64]{0:T(128)S(1)} %copy-done.3, bf16[128,16,128]{2,1,0:T(8,128)(2,1)S(1)} %whiten.1.refs_0_, bf16[128,16,128]{2,1,0:T(8,128)(2,1)S(1)} %collective-permute-done.refs_1_, bf16[128,16,128]{2,1,0:T(8,128)(2,1)S(1)} %collective-permute-done.1.refs_2_, ...), custom_call_target="tpu_custom_call" | custom-call | flops 536870912 | bytes 10485760 | tf_op jit(solution)/shard_map/stack/pallas_call | solution.py:142
  (31 shorter events, 2.7 us)
Async XLA Ops:
  0.0 1.2 %copy-start = (bf16[16,64,512]{2,1,0:T(8,128)(2,1)S(1)}, bf16[16,64,512]{2,1,0:T(8,128)(2,1)}, u32[]{:S(2)}) copy-start(bf16[16,64,512]{2,1,0:T(8,128)(2,1)} %traces_ref.1) | copy-start | bytes 3145732
  1.2 0.9 copy-start.1
  2.2 0.7 copy-start.2
  4.1 12.8 %collective-permute-start = (bf16[128,16,128]{2,1,0:T(8,128)(2,1)S(1)}, bf16[128,16,128]{2,1,0:T(8,128)(2,1)S(1)}, u32[]{:S(2)}, u32[]{:S(2)}) collective-permute-start(bf16[128,16,128]{2,1,0:T(8,128)(2,1)S(1)} %whiten.1.refs_0_), channel_id=1, source_target_pairs={{0,1},{1,2},{2,3},{3,0},{4,5},{5,6},{6,7},{7,4},{8,9},{9,10},{10,1... | collective-permute-start | bytes 1572872 | tf_op jit(solution)/shard_map/ppermute | solution.py:233
  5.5 15.7 %collective-permute-start.4 = (bf16[128,16,128]{2,1,0:T(8,128)(2,1)S(1)}, bf16[128,16,128]{2,1,0:T(8,128)(2,1)S(1)}, u32[]{:S(2)}, u32[]{:S(2)}) collective-permute-start(bf16[128,16,128]{2,1,0:T(8,128)(2,1)S(1)} %whiten.1.refs_0_), channel_id=1, source_target_pairs={{0,16},{8,24},{16,0},{24,8},{1,17},{9,25},{17,1},{25,9},{2,18},{10... | collective-permute-start | bytes 1572872 | tf_op jit(solution)/shard_map/ppermute | solution.py:165
  6.2 15.0 %collective-permute-start.3 = (bf16[128,16,128]{2,1,0:T(8,128)(2,1)S(1)}, bf16[128,16,128]{2,1,0:T(8,128)(2,1)S(1)}, u32[]{:S(2)}, u32[]{:S(2)}) collective-permute-start(bf16[128,16,128]{2,1,0:T(8,128)(2,1)S(1)} %whiten.1.refs_0_), channel_id=1, source_target_pairs={{8,0},{24,16},{5,13},{9,1},{13,5},{21,29},{25,17},{29,21},{6,14},{... | collective-permute-start | bytes 1572872 | tf_op jit(solution)/shard_map/ppermute | solution.py:165
  17.0 12.9 %collective-permute-start.1 = (bf16[128,16,128]{2,1,0:T(8,128)(2,1)S(1)}, bf16[128,16,128]{2,1,0:T(8,128)(2,1)S(1)}, u32[]{:S(2)}, u32[]{:S(2)}) collective-permute-start(bf16[128,16,128]{2,1,0:T(8,128)(2,1)S(1)} %collective-permute-done.refs_1_), channel_id=1, source_target_pairs={{0,1},{1,2},{2,3},{3,0},{4,5},{5,6},{6,7},{7,4},{8,9},{9,10},{10,1... | collective-permute-start | bytes 1572872 | tf_op jit(solution)/shard_map/ppermute | solution.py:233
  18.3 11.9 %collective-permute-start.8 = (bf16[128,16,128]{2,1,0:T(8,128)(2,1)S(1)}, bf16[128,16,128]{2,1,0:T(8,128)(2,1)S(1)}, u32[]{:S(2)}, u32[]{:S(2)}) collective-permute-start(bf16[128,16,128]{2,1,0:T(8,128)(2,1)S(1)} %collective-permute-done.refs_1_), channel_id=1, source_target_pairs={{0,16},{8,24},{16,0},{24,8},{1,17},{9,25},{17,1},{25,9},{2,18},{10... | collective-permute-start | bytes 1572872 | tf_op jit(solution)/shard_map/ppermute | solution.py:165
  19.0 11.2 %collective-permute-start.7 = (bf16[128,16,128]{2,1,0:T(8,128)(2,1)S(1)}, bf16[128,16,128]{2,1,0:T(8,128)(2,1)}, u32[]{:S(2)}, u32[]{:S(2)}) collective-permute-start(bf16[128,16,128]{2,1,0:T(8,128)(2,1)S(1)} %collective-permute-done.refs_1_), channel_id=1, source_target_pairs={{8,0},{24,16},{5,13},{9,1},{13,5},{21,29},{25,17},{29,21},{6,14},{... | collective-permute-start | bytes 1572872 | tf_op jit(solution)/shard_map/ppermute | solution.py:165
  21.2 4.1 %copy-start.4 = (bf16[128,16,128]{2,1,0:T(8,128)(2,1)}, bf16[128,16,128]{2,1,0:T(8,128)(2,1)S(1)}, u32[]{:S(2)}) copy-start(bf16[128,16,128]{2,1,0:T(8,128)(2,1)S(1)} %collective-permute-done.3) | copy-start | bytes 1572868
  22.1 15.8 %collective-permute-start.5 = (bf16[128,16,128]{2,1,0:T(8,128)(2,1)}, bf16[128,16,128]{2,1,0:T(8,128)(2,1)}, u32[]{:S(2)}, u32[]{:S(2)}) collective-permute-start(bf16[128,16,128]{2,1,0:T(8,128)(2,1)} %broadcast_select_fusion.3), channel_id=1, source_target_pairs={{0,8},{16,24},{1,9},{13,29},{17,25},{29,13},{2,10},{14,30},{18,26}... | collective-permute-start | bytes 1572872 | tf_op jit(solution)/shard_map/ppermute | solution.py:165
  29.8 17.4 %collective-permute-start.2 = (bf16[128,16,128]{2,1,0:T(8,128)(2,1)S(1)}, bf16[128,16,128]{2,1,0:T(8,128)(2,1)S(1)}, u32[]{:S(2)}, u32[]{:S(2)}) collective-permute-start(bf16[128,16,128]{2,1,0:T(8,128)(2,1)S(1)} %collective-permute-done.1.refs_2_), channel_id=1, source_target_pairs={{0,1},{1,2},{2,3},{3,0},{4,5},{5,6},{6,7},{7,4},{8,9},{9,10},{10,1... | collective-permute-start | bytes 1572872 | tf_op jit(solution)/shard_map/ppermute | solution.py:233
  32.1 15.9 %collective-permute-start.9 = (bf16[128,16,128]{2,1,0:T(8,128)(2,1)}, bf16[128,16,128]{2,1,0:T(8,128)(2,1)}, u32[]{:S(2)}, u32[]{:S(2)}) collective-permute-start(bf16[128,16,128]{2,1,0:T(8,128)(2,1)} %broadcast_select_fusion.2), channel_id=1, source_target_pairs={{0,8},{16,24},{1,9},{13,29},{17,25},{29,13},{2,10},{14,30},{18,26}... | collective-permute-start | bytes 1572872 | tf_op jit(solution)/shard_map/ppermute | solution.py:165
  35.3 15.7 %collective-permute-start.12 = (bf16[128,16,128]{2,1,0:T(8,128)(2,1)S(1)}, bf16[128,16,128]{2,1,0:T(8,128)(2,1)S(1)}, u32[]{:S(2)}, u32[]{:S(2)}) collective-permute-start(bf16[128,16,128]{2,1,0:T(8,128)(2,1)S(1)} %collective-permute-done.1.refs_2_), channel_id=1, source_target_pairs={{0,16},{8,24},{16,0},{24,8},{1,17},{9,25},{17,1},{25,9},{2,18},{10... | collective-permute-start | bytes 1572872 | tf_op jit(solution)/shard_map/ppermute | solution.py:165
  36.0 19.1 %collective-permute-start.11 = (bf16[128,16,128]{2,1,0:T(8,128)(2,1)S(1)}, bf16[128,16,128]{2,1,0:T(8,128)(2,1)S(1)}, u32[]{:S(2)}, u32[]{:S(2)}) collective-permute-start(bf16[128,16,128]{2,1,0:T(8,128)(2,1)S(1)} %collective-permute-done.1.refs_2_), channel_id=1, source_target_pairs={{8,0},{24,16},{5,13},{9,1},{13,5},{21,29},{25,17},{29,21},{6,14},{... | collective-permute-start | bytes 1572872 | tf_op jit(solution)/shard_map/ppermute | solution.py:165
  39.1 24.3 %collective-permute-start.6 = (bf16[128,16,128]{2,1,0:T(8,128)(2,1)S(1)}, bf16[128,16,128]{2,1,0:T(8,128)(2,1)S(1)}, u32[]{:S(2)}, u32[]{:S(2)}) collective-permute-start(bf16[128,16,128]{2,1,0:T(8,128)(2,1)S(1)} %get-tuple-element.11), channel_id=1, source_target_pairs={{0,4},{4,0},{8,12},{12,8},{16,20},{20,16},{24,28},{28,24},{1,5},{5... | collective-permute-start | bytes 1572872 | tf_op jit(solution)/shard_map/ppermute | solution.py:165
  47.2 10.1 %collective-permute-start.16 = (bf16[128,16,128]{2,1,0:T(8,128)(2,1)S(1)}, bf16[128,16,128]{2,1,0:T(8,128)(2,1)S(1)}, u32[]{:S(2)}, u32[]{:S(2)}) collective-permute-start(bf16[128,16,128]{2,1,0:T(8,128)(2,1)S(1)} %collective-permute-done.2.refs_3_), channel_id=1, source_target_pairs={{0,16},{8,24},{16,0},{24,8},{1,17},{9,25},{17,1},{25,9},{2,18},{10... | collective-permute-start | bytes 1572872 | tf_op jit(solution)/shard_map/ppermute | solution.py:165
  47.9 13.2 %collective-permute-start.15 = (bf16[128,16,128]{2,1,0:T(8,128)(2,1)S(1)}, bf16[128,16,128]{2,1,0:T(8,128)(2,1)S(1)}, u32[]{:S(2)}, u32[]{:S(2)}) collective-permute-start(bf16[128,16,128]{2,1,0:T(8,128)(2,1)S(1)} %collective-permute-done.2.refs_3_), channel_id=1, source_target_pairs={{8,0},{24,16},{5,13},{9,1},{13,5},{21,29},{25,17},{29,21},{6,14},{... | collective-permute-start | bytes 1572872 | tf_op jit(solution)/shard_map/ppermute | solution.py:165
  51.1 24.2 %collective-permute-start.10 = (bf16[128,16,128]{2,1,0:T(8,128)(2,1)S(1)}, bf16[128,16,128]{2,1,0:T(8,128)(2,1)S(1)}, u32[]{:S(2)}, u32[]{:S(2)}) collective-permute-start(bf16[128,16,128]{2,1,0:T(8,128)(2,1)S(1)} %get-tuple-element.9), channel_id=1, source_target_pairs={{0,4},{4,0},{8,12},{12,8},{16,20},{20,16},{24,28},{28,24},{1,5},{5... | collective-permute-start | bytes 1572872 | tf_op jit(solution)/shard_map/ppermute | solution.py:165
  55.1 10.2 %collective-permute-start.13 = (bf16[128,16,128]{2,1,0:T(8,128)(2,1)S(1)}, bf16[128,16,128]{2,1,0:T(8,128)(2,1)S(1)}, u32[]{:S(2)}, u32[]{:S(2)}) collective-permute-start(bf16[128,16,128]{2,1,0:T(8,128)(2,1)S(1)} %broadcast_select_fusion.1), channel_id=1, source_target_pairs={{0,8},{16,24},{1,9},{13,29},{17,25},{29,13},{2,10},{14,30},{18,26}... | collective-permute-start | bytes 1572872 | tf_op jit(solution)/shard_map/ppermute | solution.py:165
  61.2 10.2 %collective-permute-start.17 = (bf16[128,16,128]{2,1,0:T(8,128)(2,1)S(1)}, bf16[128,16,128]{2,1,0:T(8,128)(2,1)S(1)}, u32[]{:S(2)}, u32[]{:S(2)}) collective-permute-start(bf16[128,16,128]{2,1,0:T(8,128)(2,1)S(1)} %broadcast_select_fusion), channel_id=1, source_target_pairs={{0,8},{16,24},{1,9},{13,29},{17,25},{29,13},{2,10},{14,30},{18,26}... | collective-permute-start | bytes 1572872 | tf_op jit(solution)/shard_map/ppermute | solution.py:165
  65.5 9.9 %collective-permute-start.14 = (bf16[128,16,128]{2,1,0:T(8,128)(2,1)S(1)}, bf16[128,16,128]{2,1,0:T(8,128)(2,1)S(1)}, u32[]{:S(2)}, u32[]{:S(2)}) collective-permute-start(bf16[128,16,128]{2,1,0:T(8,128)(2,1)S(1)} %get-tuple-element.7), channel_id=1, source_target_pairs={{0,4},{4,0},{8,12},{12,8},{16,20},{20,16},{24,28},{28,24},{1,5},{5... | collective-permute-start | bytes 1572872 | tf_op jit(solution)/shard_map/ppermute | solution.py:165
  71.6 5.1 %collective-permute-start.18 = (bf16[128,16,128]{2,1,0:T(8,128)(2,1)S(1)}, bf16[128,16,128]{2,1,0:T(8,128)(2,1)S(1)}, u32[]{:S(2)}, u32[]{:S(2)}) collective-permute-start(bf16[128,16,128]{2,1,0:T(8,128)(2,1)S(1)} %get-tuple-element.5), channel_id=1, source_target_pairs={{0,4},{4,0},{8,12},{12,8},{16,20},{20,16},{24,28},{28,24},{1,5},{5... | collective-permute-start | bytes 1572872 | tf_op jit(solution)/shard_map/ppermute | solution.py:165
  75.2 2.5 %copy-start.3 = (s32[64]{0:T(128)S(1)}, s32[64]{0:T(128)}, u32[]{:S(2)}) copy-start(s32[64]{0:T(128)} %reach_ref.1) | copy-start | bytes 772

commit v2 on v1

v2 whole, which is shorter than its diff:
```python
import functools
import math

import jax
import jax.numpy as jnp
import numpy as np
from jax import lax
from jax.experimental import pallas as pl
from jax.experimental.pallas import tpu as pltpu
from jax.sharding import PartitionSpec as P

F = 128
FIRST = 16
BAND = 256
AXES = ("chan", "win")
VMEM_LIMIT = 48 * 1024 * 1024
FREQUENCY_STEPS = 4
CHANNEL_BLOCK = 8
WHITEN_WINDOWS = 4


def make_table(samples):
    t_int = np.arange(samples, dtype=np.int64)
    j_int = np.arange(F, dtype=np.int64) + FIRST
    angle = 2.0 * np.pi / samples * (j_int[:, None] * t_int[None, :] % samples)
    hann = 0.5 - 0.5 * np.cos(2.0 * np.pi / samples * t_int)
    rows = np.concatenate([hann * np.cos(angle), -hann * np.sin(angle)], axis=0)
    return jnp.asarray(rows.astype(np.float32)).astype(jnp.bfloat16)


def whiten_kernel(table_ref, traces_ref, valid_ref, out_ref, rows):
    step, steps = pl.program_id(0), pl.num_programs(0)
    block_windows, width, samples = traces_ref.shape
    windows = out_ref.shape[1]
    for g in range(block_windows // 2):
        block = traces_ref[2 * g : 2 * g + 2].reshape(2 * width, samples)
        spectra = lax.dot_general(
            table_ref[...], block, (((1,), (1,)), ((), ())), preferred_element_type=jnp.float32
        )
        re, im = spectra[:F], spectra[F:]
        power = re * re + im * im
        level = jnp.sqrt(jnp.mean(power, axis=0, keepdims=True) + 1e-06)
        w = step * block_windows + 2 * g
        usable = jnp.concatenate(
            [valid_ref[pl.ds(w, 1), :], valid_ref[pl.ds(w + 1, 1), :]], axis=1
        ).astype(jnp.float32)
        factor = usable / (jnp.sqrt(power) + 0.1 * level)
        re, im = re * factor, im * factor
        for k in range(2):
            half = slice(k * width, (k + 1) * width)
            rows[pl.ds(w + k, F, stride=windows), :] = jnp.concatenate(
                [re[:, half], im[:, half]], axis=1
            )

    @pl.when(step == steps - 1)
    def _():
        out_ref[...] = rows[...].reshape(out_ref.shape).astype(jnp.bfloat16)


def whitened_chunk(traces, valid):
    windows, width, samples = traces.shape
    block = math.gcd(windows, WHITEN_WINDOWS)
    return pl.pallas_call(
        whiten_kernel,
        out_shape=jax.ShapeDtypeStruct((F, windows, 2 * width), jnp.bfloat16),
        grid=(windows // block,),
        in_specs=[
            pl.BlockSpec((2 * F, samples), lambda s: (0, 0)),
            pl.BlockSpec((block, width, samples), lambda s: (s, 0, 0)),
            pl.BlockSpec((windows, width), lambda s: (0, 0)),
        ],
        out_specs=pl.BlockSpec((F, windows, 2 * width), lambda s: (0, 0, 0)),
        scratch_shapes=[pltpu.VMEM((F * windows, 2 * width), jnp.float32)],
        compiler_params=pltpu.CompilerParams(vmem_limit_bytes=VMEM_LIMIT),
        cost_estimate=pl.CostEstimate(
            flops=4 * F * windows * width * samples, bytes_accessed=2 * traces.size, transcendentals=0
        ),
        name="whiten",
    )(make_table(samples), traces, valid)


def stack_kernel(counts, f_steps, scale, has_partial, place_ref, reach_ref, *refs):
    slots = len(counts)
    refs = list(refs)
    groups = [[refs.pop(0) for _ in range(count)] for count in counts]
    partial_ref = refs.pop(0) if has_partial else None
    out_ref, products, chosen, diagonals = refs
    step = pl.program_id(0)
    f_block, chunk_windows, lanes = groups[0][0].shape
    width = lanes // 2
    pitch = products.shape[1] // (f_block * f_steps)
    offsets, i_block, _ = out_ref.shape

    @pl.when(step < f_steps)
    def _():
        for slot, group in enumerate(groups):
            rows = slice(slot * chunk_windows, (slot + 1) * chunk_windows)
            for which in range(2):
                code = place_ref[2 + 2 * slot + which]
                for index, ref in enumerate(group):

                    @pl.when(code == index)
                    def _(ref=ref, which=which, rows=rows):
                        chosen[which, :, rows, :] = ref[...]

        def one_bin(f, carry):
            at = jnp.concatenate([group[0][f] for group in groups], axis=0).T
            left = jnp.concatenate([at[:width], at[width:]], axis=1)
            tops = [chosen[which, f] for which in range(2)]
            bottoms = [jnp.concatenate([b[:, width:], -b[:, :width]], axis=1) for b in tops]
            right = jnp.concatenate(
                [jnp.concatenate(tops, axis=1), jnp.concatenate(bottoms, axis=1)], axis=0
            )
            row = (step * f_block + f) * pitch
            both = jnp.dot(left, right, preferred_element_type=jnp.float32)
            for half in range(2):
                products[half, pl.ds(pl.multiple_of(row, 8), width), :] = both[
                    :, half * lanes : (half + 1) * lanes
                ]
            return carry

        lax.fori_loop(0, f_block, one_bin, 0, unroll=4)

    @pl.when(step >= f_steps)
    def _():
        lane = lax.broadcasted_iota(jnp.int32, (offsets, 2 * lanes), 1)
        k = lax.broadcasted_iota(jnp.int32, (offsets, 2 * lanes), 0)
        partner = lane % width + jnp.where(lane >= lanes, width, 0)
        is_real = lane % lanes < width
        far = 4 * lanes
        shift_re = jnp.where(is_real, partner - k, far)
        shift_im = jnp.where(is_real, far, partner - k)
        base = (step - f_steps) * i_block
        row_k = lax.broadcasted_iota(jnp.int32, (offsets, F), 0) + place_ref[0]
        for il in range(i_block):
            i = base + il
            at = i + place_ref[1]
            pick = jnp.concatenate(
                [
                    jnp.where(shift_re == at, 1.0, 0.0),
                    jnp.where(shift_im == at, -1.0, 0.0),
                ],
                axis=0,
            ).astype(jnp.bfloat16)
            x = jnp.concatenate(
                [products[half, pl.ds(i, F, stride=pitch), :] for half in range(2)], axis=1
            ).astype(jnp.bfloat16)
            y = lax.dot_general(
                pick, x, (((1,), (1,)), ((), ())), preferred_element_type=jnp.float32
            )
            inside = jnp.where(row_k < reach_ref[i], scale, 0.0)
            for part in range(2):
                diagonals[part, pl.ds(il, offsets, stride=i_block), :] = (
                    y[part * offsets : (part + 1) * offsets] * inside
                )
        for part in range(2):
            columns = slice(part * F, (part + 1) * F)
            value = diagonals[part].reshape(offsets, i_block, F)
            if has_partial:
                value = value + partial_ref[:, :, columns]
            out_ref[:, :, columns] = value


def stacked(slot_buffers, slot_codes, place, reach, offsets, windows, partial):
    slots = len(slot_buffers)
    bins, chunk_windows, lanes = slot_buffers[0][0].shape
    width = lanes // 2
    f_steps, i_steps = FREQUENCY_STEPS, width // CHANNEL_BLOCK
    codes = [code for pair in slot_codes for code in pair]
    place = jnp.stack([jnp.asarray(v, jnp.int32) for v in place + codes])

    def chunk_spec(slot, index):
        def block(s, place_ref, reach_ref):
            f = jnp.minimum(s, f_steps - 1)
            if index == 0:
                return f, 0, 0
            used = (place_ref[2 + 2 * slot] == index) | (place_ref[3 + 2 * slot] == index)
            return jnp.where(used, f, 0), 0, 0

        return pl.BlockSpec((bins // f_steps, chunk_windows, lanes), block)

    out_spec = pl.BlockSpec(
        (offsets, CHANNEL_BLOCK, 2 * F), lambda s, *_: (0, jnp.maximum(s - f_steps, 0), 0)
    )
    in_specs = [chunk_spec(s, n) for s in range(slots) for n in range(len(slot_buffers[s]))]
    operands = [buffer for buffers in slot_buffers for buffer in buffers]
    if partial is not None:
        in_specs.append(out_spec)
        operands.append(partial)
    counts = tuple(len(buffers) for buffers in slot_buffers)
    return pl.pallas_call(
        functools.partial(
            stack_kernel, counts, f_steps, 1.0 / math.sqrt(windows), partial is not None
        ),
        out_shape=jax.ShapeDtypeStruct((offsets, width, 2 * F), jnp.float32),
        grid_spec=pltpu.PrefetchScalarGridSpec(
            num_scalar_prefetch=2,
            grid=(f_steps + i_steps,),
            in_specs=in_specs,
            out_specs=out_spec,
            scratch_shapes=[
                pltpu.VMEM((2, bins * (width + 8), lanes), jnp.float32),
                pltpu.VMEM((2, bins // f_steps, slots * chunk_windows, lanes), jnp.bfloat16),
                pltpu.VMEM((2, offsets * CHANNEL_BLOCK, F), jnp.float32),
            ],
        ),
        compiler_params=pltpu.CompilerParams(vmem_limit_bytes=VMEM_LIMIT),
        cost_estimate=pl.CostEstimate(
            flops=16 * bins * width * width * windows,
            bytes_accessed=30_000_000,
            transcendentals=0,
        ),
        name="stack",
    )(place, reach, *operands)


def send(array, pairs):
    return lax.ppermute(array, AXES, pairs)


def pairs_of(n_win, n_chan, target):
    pairs = []
    for z in range(n_win):
        for c in range(n_chan):
            to = target(z, c)
            if to is not None:
                pairs.append((c * n_win + z, to * n_win + z))
    return pairs


def partners_direct(piece, hops, n_win, n_chan):
    first = send(piece, pairs_of(n_win, n_chan, lambda z, c: (c - hops[z]) % n_chan))
    second = send(piece, pairs_of(n_win, n_chan, lambda z, c: (c - hops[z] - 1) % n_chan))
    return (piece, first, second), (1, 2)


def crosses(z, core):
    return core == 0 if z == 0 else core == 1 if z == 3 else True


def partners_square(piece, n_win, n_chan, last):
    z, c = lax.axis_index("win"), lax.axis_index("chan")
    core, x = c % 2, c // 2 % 2

    def pairs(target):
        return pairs_of(n_win, n_chan, lambda z, c: target(z, c, c % 2, c // 2 % 2))

    def swap(next_chip, from_y):
        outgoing = jnp.where(
            core == 0, jnp.where(z < 2, next_chip, from_y), jnp.where(z < 2, piece, next_chip)
        )
        return send(outgoing, pairs(lambda z, c, core, x: c ^ 1))

    def codes(next_code, y_code, swap_code):
        first = jnp.where(z == 0, 0, jnp.where(z == 2, next_code, swap_code))
        second = jnp.where(z == 1, next_code, jnp.where(z == 3, y_code, swap_code))
        return first, second

    if not last:

        def y_target(z, c, core, x):
            needed = z == 3 or (z == 2 and core == 0) or (x == 0 and crosses(z, core))
            return c ^ 4 if needed else None

        from_y = send(piece, pairs(y_target))
        next_chip = send(
            jnp.where(x == 1, piece, from_y),
            pairs(lambda z, c, core, x: c ^ 2 if crosses(z, core) else None),
        )
        swapped = swap(next_chip, from_y)
        return (piece, next_chip, from_y, swapped), codes(1, 2, 3)

    def early_target(z, c, core, x):
        return c ^ 4 if (core == 1 if z == 3 else x == 0 and core == 0) else None

    def x_target(z, c, core, x):
        needed = crosses(z, core) if x == 1 else z in (1, 2) and core == 1
        return c ^ 2 if needed else None

    def onward_target(z, c, core, x):
        if x == 0:
            return c ^ 2 if crosses(z, core) and (z == 3 or core == 0) else None
        return c ^ 4 if z in (1, 2) and core == 1 else None

    def late_target(z, c, core, x):
        return c ^ 4 if core == 0 and (z == 3 or (z == 2 and x == 1)) else None

    early = send(piece, pairs(early_target))
    from_x = send(piece, pairs(x_target))
    relay = jnp.where((core == 0) | (z == 3), early, from_x)
    onward = send(relay, pairs(onward_target))
    piece_then, _ = lax.optimization_barrier((piece, early))
    late = send(piece_then, pairs(late_target))
    is_early = ((z == 3) & (core == 1)) | ((z == 2) & (x == 0))
    swapped = swap(jnp.where(x == 0, from_x, onward), jnp.where(is_early, early, late))
    return (
        (piece, from_x, onward, early, late, swapped),
        codes(jnp.where(x == 0, 1, 2), jnp.where(is_early, 3, 4), 5),
    )


def on_device(traces, valid, reach):
    width = traces.shape[1]
    n_win, n_chan = lax.axis_size("win"), lax.axis_size("chan")
    windows = traces.shape[0] * n_win
    offsets = BAND // n_win
    hops = [z * offsets // width for z in range(n_win)]
    first_offset = lax.axis_index("win") * offsets
    place = [first_offset, first_offset % width]
    piece = whitened_chunk(traces, valid)
    buffers, codes = [], []
    partial = None
    for slot in range(n_win):
        if slot:
            piece = lax.ppermute(piece, "win", [(z, (z + 1) % n_win) for z in range(n_win)])
        if n_chan == 8 and hops == list(range(4)):
            found, code = partners_square(piece, n_win, n_chan, slot == n_win - 1)
        else:
            found, code = partners_direct(piece, hops, n_win, n_chan)
        buffers.append(found)
        codes.append(code)
        if slot in (n_win // 2 - 1, n_win - 1):
            partial = stacked(buffers, codes, place, reach, offsets, windows, partial)
            buffers, codes = [], []
    return partial


def solution(mesh):
    in_specs = (P("win", "chan", None), P("win", "chan"), P("chan"))
    out_specs = P("win", "chan", None)
    return jax.shard_map(
        on_device, mesh=mesh, in_specs=in_specs, out_specs=out_specs, check_vma=False
    )
```

time: 98.8 us -> 127 us (1.29)
  the two profiles are of different devices: /device:TPU:11 before, /device:TPU:9 now
where the time goes in v2:
time: 127 us
  starting transfers between devices  41.4 us (33%)
  Pallas kernels  38.4 us (30%)
  waiting for transfers between devices  33.4 us (26%)
  other arithmetic  7.16 us (6%)
  local copies, waits for them, and re-layouts  5.84 us (5%)
    ppermute x14, starting transfers between devices, send(): return lax.ppermute(array, AXES, pairs)  38.8 us
    pallas_call x2, Pallas kernels, stacked(): pl.pallas_call(functools.partial(stack_kernel, counts, f_steps, 1.0 / mat...  36.3 us
    ppermute x3, waiting for transfers between devices, on_device(): lax.ppermute(piece, 'win', [(z, (z + 1) % n_win) for z in range(n_win)])  18.9 us
    ppermute x14, waiting for transfers between devices, send(): return lax.ppermute(array, AXES, pairs)  14.4 us
    select_n x4, other arithmetic, swap(): jnp.where(core == 0, jnp.where(z < 2, next_chip, from_y), jnp.where(z < 2...  6.13 us
    unnamed x32, local copies, waits for them, and re-layouts  5.67 us
    ppermute x3, starting transfers between devices, on_device(): lax.ppermute(piece, 'win', [(z, (z + 1) % n_win) for z in range(n_win)])  2.65 us
  transfers between devices with their start and end apart: 17, of which 6 were waited for; matrix products, arithmetic and copies ran while one was open for 6% of the time, Pallas kernels for 13%

profile of v2, /device:TPU:9, one launch (start us, length us, event | category | flops | bytes accessed | tf_op | source)
XLA Modules:
  0.0 126.6 jit_solution(17689930664219513614)
XLA Ops:
  0.0 1.2 copy-done.12
  1.2 0.9 copy-done.13
  2.2 0.7 copy-done.14
  2.9 2.1 %whiten.1.refs_0_ = bf16[128,16,128]{2,1,0:T(8,128)(2,1)S(1)} custom-call(bf16[256,512]{1,0:T(8,128)(2,1)S(1)} %copy-done.13, bf16[16,64,512]{2,1,0:T(8,128)(2,1)S(1)} %copy-done.12, s32[16,64]{1,0:T(8,128)S(1)} %copy-done.14), custom_call_target="tpu_custom_call" | custom-call | flops 268435456 | bytes 1048576 | tf_op jit(solution)/shard_map/whiten/pallas_call | solution.py:63
  5.0 1.4 %collective-permute-start = (bf16[128,16,128]{2,1,0:T(8,128)(2,1)S(1)}, bf16[128,16,128]{2,1,0:T(8,128)(2,1)S(1)}, u32[]{:S(2)}, u32[]{:S(2)}) collective-permute-start(bf16[128,16,128]{2,1,0:T(8,128)(2,1)S(1)} %whiten.1.refs_0_), channel_id=1, source_target_pairs={{0,1},{1,2},{2,3},{3,0},{4,5},{5,6},{6,7},{7,4},{8,9},{9,10},{10,1... | collective-permute-start | bytes 1572872 | tf_op jit(solution)/shard_map/ppermute | solution.py:315
  6.4 3.1 %collective-permute-start.11 = (bf16[128,16,128]{2,1,0:T(8,128)(2,1)S(1)}, bf16[128,16,128]{2,1,0:T(8,128)(2,1)S(1)}, u32[]{:S(2)}, u32[]{:S(2)}) collective-permute-start(bf16[128,16,128]{2,1,0:T(8,128)(2,1)S(1)} %whiten.1.refs_0_), channel_id=1, source_target_pairs={{0,16},{16,0},{1,17},{5,21},{17,1},{21,5},{2,18},{6,22},{10,26},{1... | collective-permute-start | bytes 1572872 | tf_op jit(solution)/shard_map/ppermute | solution.py:218
  9.5 8.3 %collective-permute-done.refs_4_ = bf16[128,16,128]{2,1,0:T(8,128)(2,1)S(1)} collective-permute-done((bf16[128,16,128]{2,1,0:T(8,128)(2,1)S(1)}, bf16[128,16,128]{2,1,0:T(8,128)(2,1)S(1)}, u32[]{:S(2)}, u32[]{:S(2)}) %collective-permute-start) | collective-permute-done | bytes 524320 | tf_op jit(solution)/shard_map/ppermute | solution.py:315
  17.9 1.3 %collective-permute-start.1 = (bf16[128,16,128]{2,1,0:T(8,128)(2,1)S(1)}, bf16[128,16,128]{2,1,0:T(8,128)(2,1)S(1)}, u32[]{:S(2)}, u32[]{:S(2)}) collective-permute-start(bf16[128,16,128]{2,1,0:T(8,128)(2,1)S(1)} %collective-permute-done.refs_4_), channel_id=1, source_target_pairs={{0,1},{1,2},{2,3},{3,0},{4,5},{5,6},{6,7},{7,4},{8,9},{9,10},{10,1... | collective-permute-start | bytes 1572872 | tf_op jit(solution)/shard_map/ppermute | solution.py:315
  19.2 1.6 %collective-permute-done.11.refs_2_ = bf16[128,16,128]{2,1,0:T(8,128)(2,1)S(1)} collective-permute-done((bf16[128,16,128]{2,1,0:T(8,128)(2,1)S(1)}, bf16[128,16,128]{2,1,0:T(8,128)(2,1)S(1)}, u32[]{:S(2)}, u32[]{:S(2)}) %collective-permute-start.11) | collective-permute-done | bytes 524320 | tf_op jit(solution)/shard_map/ppermute | solution.py:218
  20.7 0.8 broadcast_select_fusion.2
  21.6 1.9 %collective-permute-start.12 = (bf16[128,16,128]{2,1,0:T(8,128)(2,1)}, bf16[128,16,128]{2,1,0:T(8,128)(2,1)}, u32[]{:S(2)}, u32[]{:S(2)}) collective-permute-start(bf16[128,16,128]{2,1,0:T(8,128)(2,1)} %broadcast_select_fusion.2), channel_id=1, source_target_pairs={{0,8},{8,0},{16,24},{24,16},{1,9},{5,13},{9,1},{13,5},{17,25},{21,... | collective-permute-start | bytes 1572872 | tf_op jit(solution)/shard_map/ppermute | solution.py:218
  23.5 7.8 %collective-permute-done.1.refs_0_ = bf16[128,16,128]{2,1,0:T(8,128)(2,1)S(1)} collective-permute-done((bf16[128,16,128]{2,1,0:T(8,128)(2,1)S(1)}, bf16[128,16,128]{2,1,0:T(8,128)(2,1)S(1)}, u32[]{:S(2)}, u32[]{:S(2)}) %collective-permute-start.1) | collective-permute-done | bytes 524320 | tf_op jit(solution)/shard_map/ppermute | solution.py:315
  31.3 2.9 %collective-permute-start.14 = (bf16[128,16,128]{2,1,0:T(8,128)(2,1)S(1)}, bf16[128,16,128]{2,1,0:T(8,128)(2,1)S(1)}, u32[]{:S(2)}, u32[]{:S(2)}) collective-permute-start(bf16[128,16,128]{2,1,0:T(8,128)(2,1)S(1)} %collective-permute-done.refs_4_), channel_id=1, source_target_pairs={{0,16},{16,0},{1,17},{5,21},{17,1},{21,5},{2,18},{6,22},{10,26},{1... | collective-permute-start | bytes 1572872 | tf_op jit(solution)/shard_map/ppermute | solution.py:218
  34.3 2.3 %collective-permute-start.2 = (bf16[128,16,128]{2,1,0:T(8,128)(2,1)S(1)}, bf16[128,16,128]{2,1,0:T(8,128)(2,1)S(1)}, u32[]{:S(2)}, u32[]{:S(2)}) collective-permute-start(bf16[128,16,128]{2,1,0:T(8,128)(2,1)S(1)} %collective-permute-done.1.refs_0_), channel_id=1, source_target_pairs={{0,16},{16,0},{1,17},{5,21},{17,1},{21,5},{2,18},{6,22},{10,26},{1... | collective-permute-start | bytes 1572872 | tf_op jit(solution)/shard_map/ppermute | solution.py:218
  36.7 1.9 %select_select_fusion.1 = bf16[128,16,128]{2,1,0:T(8,128)(2,1)} fusion(bf16[128,16,128]{2,1,0:T(8,128)(2,1)S(1)} %whiten.1.refs_0_, bf16[128,16,128]{2,1,0:T(8,128)(2,1)} %collective-permute-done.12.refs_1_, bf16[128,16,128]{2,1,0:T(8,128)(2,1)S(1)} %collective-permute-done.11.refs_2_, pred[]{:T(512)S(6)} %lt.39, pred[]{:T(512)S(6)} %eq.64), kind=kLoop, calls=%fused_computation.1 | loop fusion | flops 786432 | bytes 2097154 | tf_op jit(solution)/shard_map/jit(_where)/select_n | solution.py:249
  38.6 3.0 %collective-permute-start.13 = (bf16[128,16,128]{2,1,0:T(8,128)(2,1)}, bf16[128,16,128]{2,1,0:T(8,128)(2,1)}, u32[]{:S(2)}, u32[]{:S(2)}) collective-permute-start(bf16[128,16,128]{2,1,0:T(8,128)(2,1)} %select_select_fusion.1), channel_id=1, source_target_pairs={{0,4},{4,0},{8,12},{12,8},{16,20},{20,16},{24,28},{28,24},{1,5},{5... | collective-permute-start | bytes 1572872 | tf_op jit(solution)/shard_map/ppermute | solution.py:218
  41.6 2.8 %collective-permute-done.5.refs_4_ = bf16[128,16,128]{2,1,0:T(8,128)(2,1)} collective-permute-done((bf16[128,16,128]{2,1,0:T(8,128)(2,1)S(1)}, bf16[128,16,128]{2,1,0:T(8,128)(2,1)}, u32[]{:S(2)}, u32[]{:S(2)}) %collective-permute-start.5) | collective-permute-done | bytes 524320 | tf_op jit(solution)/shard_map/ppermute | solution.py:315
  45.1 2.4 %collective-permute-start.6 = (bf16[128,16,128]{2,1,0:T(8,128)(2,1)}, bf16[128,16,128]{2,1,0:T(8,128)(2,1)S(1)}, u32[]{:S(2)}, u32[]{:S(2)}) collective-permute-start(bf16[128,16,128]{2,1,0:T(8,128)(2,1)} %collective-permute-done.5.refs_4_), channel_id=1, source_target_pairs={{8,0},{24,16},{5,13},{9,1},{13,5},{21,29},{25,17},{29,21},{6,14},{... | collective-permute-start | bytes 1572872 | tf_op jit(solution)/shard_map/ppermute | solution.py:218
  47.5 2.9 %collective-permute-start.15 = (bf16[128,16,128]{2,1,0:T(8,128)(2,1)S(1)}, bf16[128,16,128]{2,1,0:T(8,128)(2,1)S(1)}, u32[]{:S(2)}, u32[]{:S(2)}) collective-permute-start(bf16[128,16,128]{2,1,0:T(8,128)(2,1)S(1)} %broadcast_select_fusion.1), channel_id=1, source_target_pairs={{0,8},{8,0},{16,24},{24,16},{1,9},{5,13},{9,1},{13,5},{17,25},{21,... | collective-permute-start | bytes 1572872 | tf_op jit(solution)/shard_map/ppermute | solution.py:218
  50.5 5.0 %collective-permute-done.2.refs_2_ = bf16[128,16,128]{2,1,0:T(8,128)(2,1)S(1)} collective-permute-done((bf16[128,16,128]{2,1,0:T(8,128)(2,1)S(1)}, bf16[128,16,128]{2,1,0:T(8,128)(2,1)S(1)}, u32[]{:S(2)}, u32[]{:S(2)}) %collective-permute-start.2) | collective-permute-done | bytes 524320 | tf_op jit(solution)/shard_map/ppermute | solution.py:218
  55.5 1.9 %collective-permute-start.3 = (bf16[128,16,128]{2,1,0:T(8,128)(2,1)S(1)}, bf16[128,16,128]{2,1,0:T(8,128)(2,1)S(1)}, u32[]{:S(2)}, u32[]{:S(2)}) collective-permute-start(bf16[128,16,128]{2,1,0:T(8,128)(2,1)S(1)} %broadcast_select_fusion.3), channel_id=1, source_target_pairs={{0,8},{8,0},{16,24},{24,16},{1,9},{5,13},{9,1},{13,5},{17,25},{21,... | collective-permute-start | bytes 1572872 | tf_op jit(solution)/shard_map/ppermute | solution.py:218
  58.9 7.9 %collective-permute-done.15.refs_5_ = bf16[128,16,128]{2,1,0:T(8,128)(2,1)S(1)} collective-permute-done((bf16[128,16,128]{2,1,0:T(8,128)(2,1)S(1)}, bf16[128,16,128]{2,1,0:T(8,128)(2,1)S(1)}, u32[]{:S(2)}, u32[]{:S(2)}) %collective-permute-start.15) | collective-permute-done | bytes 524320 | tf_op jit(solution)/shard_map/ppermute | solution.py:218
  66.8 1.0 select_select_fusion
  67.8 11.5 %collective-permute-start.16 = (bf16[128,16,128]{2,1,0:T(8,128)(2,1)}, bf16[128,16,128]{2,1,0:T(8,128)(2,1)}, u32[]{:S(2)}, u32[]{:S(2)}) collective-permute-start(bf16[128,16,128]{2,1,0:T(8,128)(2,1)} %select_select_fusion), channel_id=1, source_target_pairs={{0,4},{4,0},{8,12},{12,8},{16,20},{20,16},{24,28},{28,24},{1,5},{5... | collective-permute-start | bytes 1572872 | tf_op jit(solution)/shard_map/ppermute | solution.py:218
  79.3 0.9 select_select_fusion.3
  80.3 0.8 copy-done.4
  81.1 4.7 %collective-permute-start.4 = (bf16[128,16,128]{2,1,0:T(8,128)(2,1)}, bf16[128,16,128]{2,1,0:T(8,128)(2,1)}, u32[]{:S(2)}, u32[]{:S(2)}) collective-permute-start(bf16[128,16,128]{2,1,0:T(8,128)(2,1)} %select_select_fusion.3), channel_id=1, source_target_pairs={{0,4},{4,0},{8,12},{12,8},{16,20},{20,16},{24,28},{28,24},{1,5},{5... | collective-permute-start | bytes 1572872 | tf_op jit(solution)/shard_map/ppermute | solution.py:218
  85.8 2.2 %select_select_fusion.2 = bf16[128,16,128]{2,1,0:T(8,128)(2,1)} fusion(bf16[128,16,128]{2,1,0:T(8,128)(2,1)} %collective-permute-done.5.refs_4_, bf16[128,16,128]{2,1,0:T(8,128)(2,1)S(1)} %collective-permute-done.7.refs_7_, bf16[128,16,128]{2,1,0:T(8,128)(2,1)S(1)} %collective-permute-done.9.refs_8_, ...), kind=kLoop, calls=%fused_computation.2 | loop fusion | flops 1310720 | bytes 3145732 | tf_op jit(solution)/shard_map/jit(_where)/select_n | solution.py:249
  88.0 0.8 copy-done.6
  89.1 1.2 copy-done.9
  90.2 17.1 %stack.40.refs_10_ = f32[64,64,256]{2,1,0:T(8,128)} custom-call(s32[6]{0:T(128)S(1)} %stack.39.place_ref, s32[64]{0:T(128)S(1)} %copy-done.15, bf16[128,16,128]{2,1,0:T(8,128)(2,1)S(1)} %whiten.1.refs_0_, bf16[128,16,128]{2,1,0:T(8,128)(2,1)} %collective-permute-done.12.refs_1_, bf16[128,16,128]{2,1,0:T(8,128)(2,1)S(1)} %collective-permute-done.11.refs_2_, ...), custom_call_target="tpu_custom_call" | custom-call | flops 536870912 | bytes 30000000 | tf_op jit(solution)/shard_map/stack/pallas_call | solution.py:191
  107.3 19.2 %stack.41 = f32[64,64,256]{2,1,0:T(8,128)} custom-call(s32[6]{0:T(128)S(1)} %stack.38.place_ref, s32[64]{0:T(128)S(1)} %copy-done.15, bf16[128,16,128]{2,1,0:T(8,128)(2,1)S(1)} %collective-permute-done.1.refs_0_, bf16[128,16,128]{2,1,0:T(8,128)(2,1)S(1)} %copy-done.5, bf16[128,16,128]{2,1,0:T(8,128)(2,1)S(1)} %collective-permute-done.2.refs_2_, ...), custom_call_target="tpu_custom_call" | custom-call | flops 536870912 | bytes 30000000 | tf_op jit(solution)/shard_map/stack/pallas_call | solution.py:191
  (47 shorter events, 2.5 us)
Async XLA Ops:
  0.0 1.2 copy-start.12
  1.2 0.9 copy-start.13
  5.0 12.8 %collective-permute-start = (bf16[128,16,128]{2,1,0:T(8,128)(2,1)S(1)}, bf16[128,16,128]{2,1,0:T(8,128)(2,1)S(1)}, u32[]{:S(2)}, u32[]{:S(2)}) collective-permute-start(bf16[128,16,128]{2,1,0:T(8,128)(2,1)S(1)} %whiten.1.refs_0_), channel_id=1, source_target_pairs={{0,1},{1,2},{2,3},{3,0},{4,5},{5,6},{6,7},{7,4},{8,9},{9,10},{10,1... | collective-permute-start | bytes 1572872 | tf_op jit(solution)/shard_map/ppermute | solution.py:315
  6.4 14.4 %collective-permute-start.11 = (bf16[128,16,128]{2,1,0:T(8,128)(2,1)S(1)}, bf16[128,16,128]{2,1,0:T(8,128)(2,1)S(1)}, u32[]{:S(2)}, u32[]{:S(2)}) collective-permute-start(bf16[128,16,128]{2,1,0:T(8,128)(2,1)S(1)} %whiten.1.refs_0_), channel_id=1, source_target_pairs={{0,16},{16,0},{1,17},{5,21},{17,1},{21,5},{2,18},{6,22},{10,26},{1... | collective-permute-start | bytes 1572872 | tf_op jit(solution)/shard_map/ppermute | solution.py:218
  17.9 13.5 %collective-permute-start.1 = (bf16[128,16,128]{2,1,0:T(8,128)(2,1)S(1)}, bf16[128,16,128]{2,1,0:T(8,128)(2,1)S(1)}, u32[]{:S(2)}, u32[]{:S(2)}) collective-permute-start(bf16[128,16,128]{2,1,0:T(8,128)(2,1)S(1)} %collective-permute-done.refs_4_), channel_id=1, source_target_pairs={{0,1},{1,2},{2,3},{3,0},{4,5},{5,6},{6,7},{7,4},{8,9},{9,10},{10,1... | collective-permute-start | bytes 1572872 | tf_op jit(solution)/shard_map/ppermute | solution.py:315
  21.6 15.1 %collective-permute-start.12 = (bf16[128,16,128]{2,1,0:T(8,128)(2,1)}, bf16[128,16,128]{2,1,0:T(8,128)(2,1)}, u32[]{:S(2)}, u32[]{:S(2)}) collective-permute-start(bf16[128,16,128]{2,1,0:T(8,128)(2,1)} %broadcast_select_fusion.2), channel_id=1, source_target_pairs={{0,8},{8,0},{16,24},{24,16},{1,9},{5,13},{9,1},{13,5},{17,25},{21,... | collective-permute-start | bytes 1572872 | tf_op jit(solution)/shard_map/ppermute | solution.py:218
  31.3 13.1 %collective-permute-start.5 = (bf16[128,16,128]{2,1,0:T(8,128)(2,1)S(1)}, bf16[128,16,128]{2,1,0:T(8,128)(2,1)}, u32[]{:S(2)}, u32[]{:S(2)}) collective-permute-start(bf16[128,16,128]{2,1,0:T(8,128)(2,1)S(1)} %collective-permute-done.1.refs_0_), channel_id=1, source_target_pairs={{0,1},{1,2},{2,3},{3,0},{4,5},{5,6},{6,7},{7,4},{8,9},{9,10},{10,1... | collective-permute-start | bytes 1572872 | tf_op jit(solution)/shard_map/ppermute | solution.py:315
  31.3 16.1 %collective-permute-start.14 = (bf16[128,16,128]{2,1,0:T(8,128)(2,1)S(1)}, bf16[128,16,128]{2,1,0:T(8,128)(2,1)S(1)}, u32[]{:S(2)}, u32[]{:S(2)}) collective-permute-start(bf16[128,16,128]{2,1,0:T(8,128)(2,1)S(1)} %collective-permute-done.refs_4_), channel_id=1, source_target_pairs={{0,16},{16,0},{1,17},{5,21},{17,1},{21,5},{2,18},{6,22},{10,26},{1... | collective-permute-start | bytes 1572872 | tf_op jit(solution)/shard_map/ppermute | solution.py:218
  34.3 21.1 %collective-permute-start.2 = (bf16[128,16,128]{2,1,0:T(8,128)(2,1)S(1)}, bf16[128,16,128]{2,1,0:T(8,128)(2,1)S(1)}, u32[]{:S(2)}, u32[]{:S(2)}) collective-permute-start(bf16[128,16,128]{2,1,0:T(8,128)(2,1)S(1)} %collective-permute-done.1.refs_0_), channel_id=1, source_target_pairs={{0,16},{16,0},{1,17},{5,21},{17,1},{21,5},{2,18},{6,22},{10,26},{1... | collective-permute-start | bytes 1572872 | tf_op jit(solution)/shard_map/ppermute | solution.py:218
  38.6 50.4 %collective-permute-start.13 = (bf16[128,16,128]{2,1,0:T(8,128)(2,1)}, bf16[128,16,128]{2,1,0:T(8,128)(2,1)}, u32[]{:S(2)}, u32[]{:S(2)}) collective-permute-start(bf16[128,16,128]{2,1,0:T(8,128)(2,1)} %select_select_fusion.1), channel_id=1, source_target_pairs={{0,4},{4,0},{8,12},{12,8},{16,20},{20,16},{24,28},{28,24},{1,5},{5... | collective-permute-start | bytes 1572872 | tf_op jit(solution)/shard_map/ppermute | solution.py:218
  44.4 13.0 %collective-permute-start.7 = (bf16[128,16,128]{2,1,0:T(8,128)(2,1)}, bf16[128,16,128]{2,1,0:T(8,128)(2,1)S(1)}, u32[]{:S(2)}, u32[]{:S(2)}) collective-permute-start(bf16[128,16,128]{2,1,0:T(8,128)(2,1)} %collective-permute-done.5.refs_4_), channel_id=1, source_target_pairs={{0,16},{16,0},{1,17},{17,1},{2,18},{18,2},{7,23},{15,31},{23,7},{3... | collective-permute-start | bytes 1572872 | tf_op jit(solution)/shard_map/ppermute | solution.py:218
  45.1 13.1 %collective-permute-start.6 = (bf16[128,16,128]{2,1,0:T(8,128)(2,1)}, bf16[128,16,128]{2,1,0:T(8,128)(2,1)S(1)}, u32[]{:S(2)}, u32[]{:S(2)}) collective-permute-start(bf16[128,16,128]{2,1,0:T(8,128)(2,1)} %collective-permute-done.5.refs_4_), channel_id=1, source_target_pairs={{8,0},{24,16},{5,13},{9,1},{13,5},{21,29},{25,17},{29,21},{6,14},{... | collective-permute-start | bytes 1572872 | tf_op jit(solution)/shard_map/ppermute | solution.py:218
  47.5 19.3 %collective-permute-start.15 = (bf16[128,16,128]{2,1,0:T(8,128)(2,1)S(1)}, bf16[128,16,128]{2,1,0:T(8,128)(2,1)S(1)}, u32[]{:S(2)}, u32[]{:S(2)}) collective-permute-start(bf16[128,16,128]{2,1,0:T(8,128)(2,1)S(1)} %broadcast_select_fusion.1), channel_id=1, source_target_pairs={{0,8},{8,0},{16,24},{24,16},{1,9},{5,13},{9,1},{13,5},{17,25},{21,... | collective-permute-start | bytes 1572872 | tf_op jit(solution)/shard_map/ppermute | solution.py:218
  55.5 33.5 %copy-start.15 = (s32[64]{0:T(128)S(1)}, s32[64]{0:T(128)}, u32[]{:S(2)}) copy-start(s32[64]{0:T(128)} %reach_ref.3) | copy-start | bytes 772
  55.5 23.8 %collective-permute-start.3 = (bf16[128,16,128]{2,1,0:T(8,128)(2,1)S(1)}, bf16[128,16,128]{2,1,0:T(8,128)(2,1)S(1)}, u32[]{:S(2)}, u32[]{:S(2)}) collective-permute-start(bf16[128,16,128]{2,1,0:T(8,128)(2,1)S(1)} %broadcast_select_fusion.3), channel_id=1, source_target_pairs={{0,8},{8,0},{16,24},{24,16},{1,9},{5,13},{9,1},{13,5},{17,25},{21,... | collective-permute-start | bytes 1572872 | tf_op jit(solution)/shard_map/ppermute | solution.py:218
  57.4 30.6 %copy-start = (bf16[128,16,128]{2,1,0:T(8,128)(2,1)}, bf16[128,16,128]{2,1,0:T(8,128)(2,1)S(1)}, u32[]{:S(2)}) copy-start(bf16[128,16,128]{2,1,0:T(8,128)(2,1)S(1)} %collective-permute-done.7.refs_7_) | copy-start | bytes 1572868
  57.5 28.3 %collective-permute-start.9 = (bf16[128,16,128]{2,1,0:T(8,128)(2,1)}, bf16[128,16,128]{2,1,0:T(8,128)(2,1)S(1)}, u32[]{:S(2)}, u32[]{:S(2)}) collective-permute-start(bf16[128,16,128]{2,1,0:T(8,128)(2,1)} %collective-permute-done.5.refs_4_), channel_id=1, source_target_pairs={{10,26},{26,10},{3,19},{11,27},{19,3},{27,11}} | collective-permute-start | bytes 1572872 | tf_op jit(solution)/shard_map/ppermute | solution.py:218
  58.2 29.8 %copy-start.2 = (bf16[128,16,128]{2,1,0:T(8,128)(2,1)}, bf16[128,16,128]{2,1,0:T(8,128)(2,1)S(1)}, u32[]{:S(2)}) copy-start(bf16[128,16,128]{2,1,0:T(8,128)(2,1)S(1)} %collective-permute-done.6.refs_5_) | copy-start | bytes 1572868
  58.2 27.5 %collective-permute-start.8 = (bf16[128,16,128]{2,1,0:T(8,128)(2,1)S(1)}, bf16[128,16,128]{2,1,0:T(8,128)(2,1)S(1)}, u32[]{:S(2)}, u32[]{:S(2)}) collective-permute-start(bf16[128,16,128]{2,1,0:T(8,128)(2,1)S(1)} %broadcast_select_fusion), channel_id=1, source_target_pairs={{0,8},{16,24},{1,9},{13,29},{17,25},{29,13},{2,10},{14,30},{18,26}... | collective-permute-start | bytes 1572872 | tf_op jit(solution)/shard_map/ppermute | solution.py:218
  66.8 18.9 %copy-start.8 = (bf16[128,16,128]{2,1,0:T(8,128)(2,1)}, bf16[128,16,128]{2,1,0:T(8,128)(2,1)S(1)}, u32[]{:S(2)}) copy-start(bf16[128,16,128]{2,1,0:T(8,128)(2,1)S(1)} %collective-permute-done.15.refs_5_) | copy-start | bytes 1572868
  67.8 21.2 %collective-permute-start.16 = (bf16[128,16,128]{2,1,0:T(8,128)(2,1)}, bf16[128,16,128]{2,1,0:T(8,128)(2,1)}, u32[]{:S(2)}, u32[]{:S(2)}) collective-permute-start(bf16[128,16,128]{2,1,0:T(8,128)(2,1)} %select_select_fusion), channel_id=1, source_target_pairs={{0,4},{4,0},{8,12},{12,8},{16,20},{20,16},{24,28},{28,24},{1,5},{5... | collective-permute-start | bytes 1572872 | tf_op jit(solution)/shard_map/ppermute | solution.py:218
  80.3 0.8 copy-start.4
  81.1 26.2 %collective-permute-start.4 = (bf16[128,16,128]{2,1,0:T(8,128)(2,1)}, bf16[128,16,128]{2,1,0:T(8,128)(2,1)}, u32[]{:S(2)}, u32[]{:S(2)}) collective-permute-start(bf16[128,16,128]{2,1,0:T(8,128)(2,1)} %select_select_fusion.3), channel_id=1, source_target_pairs={{0,4},{4,0},{8,12},{12,8},{16,20},{20,16},{24,28},{28,24},{1,5},{5... | collective-permute-start | bytes 1572872 | tf_op jit(solution)/shard_map/ppermute | solution.py:218
  85.7 2.3 %copy-start.10 = (bf16[128,16,128]{2,1,0:T(8,128)(2,1)}, bf16[128,16,128]{2,1,0:T(8,128)(2,1)S(1)}, u32[]{:S(2)}) copy-start(bf16[128,16,128]{2,1,0:T(8,128)(2,1)S(1)} %collective-permute-done.8.refs_6_) | copy-start | bytes 1572868
  88.0 0.8 copy-start.6
  88.8 18.5 %collective-permute-start.10 = (bf16[128,16,128]{2,1,0:T(8,128)(2,1)}, bf16[128,16,128]{2,1,0:T(8,128)(2,1)}, u32[]{:S(2)}, u32[]{:S(2)}) collective-permute-start(bf16[128,16,128]{2,1,0:T(8,128)(2,1)} %select_select_fusion.2), channel_id=1, source_target_pairs={{0,4},{4,0},{8,12},{12,8},{16,20},{20,16},{24,28},{28,24},{1,5},{5... | collective-permute-start | bytes 1572872 | tf_op jit(solution)/shard_map/ppermute | solution.py:218
  89.0 18.3 %copy-start.1 = (bf16[128,16,128]{2,1,0:T(8,128)(2,1)S(1)}, bf16[128,16,128]{2,1,0:T(8,128)(2,1)}, u32[]{:S(2)}) copy-start(bf16[128,16,128]{2,1,0:T(8,128)(2,1)} %copy-done) | copy-start | bytes 1572868
  89.0 18.3 %copy-start.3 = (bf16[128,16,128]{2,1,0:T(8,128)(2,1)S(1)}, bf16[128,16,128]{2,1,0:T(8,128)(2,1)}, u32[]{:S(2)}) copy-start(bf16[128,16,128]{2,1,0:T(8,128)(2,1)} %copy-done.2) | copy-start | bytes 1572868
  89.0 18.3 %copy-start.5 = (bf16[128,16,128]{2,1,0:T(8,128)(2,1)S(1)}, bf16[128,16,128]{2,1,0:T(8,128)(2,1)}, u32[]{:S(2)}) copy-start(bf16[128,16,128]{2,1,0:T(8,128)(2,1)} %copy-done.4) | copy-start | bytes 1572868
  89.0 18.3 %copy-start.7 = (bf16[128,16,128]{2,1,0:T(8,128)(2,1)S(1)}, bf16[128,16,128]{2,1,0:T(8,128)(2,1)}, u32[]{:S(2)}) copy-start(bf16[128,16,128]{2,1,0:T(8,128)(2,1)} %copy-done.6) | copy-start | bytes 1572868
  89.0 1.2 copy-start.9
  90.2 17.1 %copy-start.11 = (bf16[128,16,128]{2,1,0:T(8,128)(2,1)S(1)}, bf16[128,16,128]{2,1,0:T(8,128)(2,1)}, u32[]{:S(2)}) copy-start(bf16[128,16,128]{2,1,0:T(8,128)(2,1)} %copy-done.10) | copy-start | bytes 1572868
  (1 other events, 0.7 us)

commit v3 on v1

v3 whole, which is shorter than its diff:
```python
import functools
import math

import jax
import jax.numpy as jnp
import numpy as np
from jax import lax
from jax.experimental import pallas as pl
from jax.experimental.pallas import tpu as pltpu
from jax.sharding import PartitionSpec as P

F = 128
FIRST = 16
BAND = 256
AXES = ("chan", "win")
CHANNEL_BLOCK = 8
WHITEN_BLOCKS = 4
PITCH_PAD = 8
MIB = 1024 * 1024
VMEM = pl.BlockSpec(memory_space=pltpu.VMEM)
SMEM = pl.BlockSpec(memory_space=pltpu.SMEM)
SMALL = pl.CostEstimate(flops=1, bytes_accessed=1, transcendentals=0)
ANY = pl.BlockSpec(memory_space=pl.ANY)


def make_table(samples):
    t_int = np.arange(samples, dtype=np.int64)
    j_int = np.arange(F, dtype=np.int64) + FIRST
    angle = 2.0 * np.pi / samples * (j_int[:, None] * t_int[None, :] % samples)
    hann = 0.5 - 0.5 * np.cos(2.0 * np.pi / samples * t_int)
    rows = np.concatenate([hann * np.cos(angle), -hann * np.sin(angle)], axis=0)
    return jnp.asarray(rows.astype(np.float32)).astype(jnp.bfloat16)


def whiten_kernel(table_hbm, traces_hbm, valid_hbm, out_ref, table, traces, valid, rows, sems):
    windows, width, samples = traces.shape
    block = windows // WHITEN_BLOCKS if windows % (2 * WHITEN_BLOCKS) == 0 else windows
    copies = [
        pltpu.make_async_copy(table_hbm, table, sems.at[0]),
        pltpu.make_async_copy(valid_hbm, valid, sems.at[1]),
    ]
    for n in range(windows // block):
        part = pl.ds(n * block, block)
        copies.append(
            pltpu.make_async_copy(traces_hbm.at[part], traces.at[part], sems.at[2 + n])
        )
    for copy in copies:
        copy.start()
    copies[0].wait()
    copies[1].wait()
    for w in range(0, windows, 2):
        if w % block == 0:
            copies[2 + w // block].wait()
        spectra = lax.dot_general(
            table[...],
            traces[w : w + 2].reshape(2 * width, samples),
            (((1,), (1,)), ((), ())),
            preferred_element_type=jnp.float32,
        )
        re, im = spectra[:F], spectra[F:]
        power = re * re + im * im
        level = jnp.sqrt(jnp.mean(power, axis=0, keepdims=True) + 1e-06)
        usable = jnp.concatenate([valid[w : w + 1, :], valid[w + 1 : w + 2, :]], axis=1)
        factor = usable.astype(jnp.float32) / (jnp.sqrt(power) + 0.1 * level)
        re, im = re * factor, im * factor
        for k in range(2):
            half = slice(k * width, (k + 1) * width)
            rows[pl.ds(w + k, F, stride=windows), :] = jnp.concatenate(
                [re[:, half], im[:, half]], axis=1
            )
    out_ref[...] = rows[...].reshape(out_ref.shape).astype(jnp.bfloat16)


def whitened_chunk(traces, valid):
    windows, width, samples = traces.shape
    return pl.pallas_call(
        whiten_kernel,
        out_shape=jax.ShapeDtypeStruct((F, windows, 2 * width), jnp.bfloat16),
        in_specs=[ANY] * 3,
        out_specs=VMEM,
        scratch_shapes=[
            pltpu.VMEM((2 * F, samples), jnp.bfloat16),
            pltpu.VMEM(traces.shape, traces.dtype),
            pltpu.VMEM(valid.shape, valid.dtype),
            pltpu.VMEM((F * windows, 2 * width), jnp.float32),
            pltpu.SemaphoreType.DMA((2 + WHITEN_BLOCKS,)),
        ],
        compiler_params=pltpu.CompilerParams(vmem_limit_bytes=62 * MIB),
        cost_estimate=pl.CostEstimate(
            flops=4 * F * traces.size, bytes_accessed=2 * traces.size, transcendentals=0
        ),
        name="whiten",
    )(make_table(samples), traces, valid)


def copy_chosen(code, refs, put):
    for index, ref in enumerate(refs):

        @pl.when(code == index)
        def _(ref=ref):
            put(ref)


def choose_kernel(groups, per_group, codes_ref, *refs):
    out_ref = refs[-1]
    shared = refs[groups * per_group : -1]
    for which in range(out_ref.shape[0]):
        for g in range(groups):

            def put(ref, which=which, g=g):
                out_ref[which, g] = ref[...]

            candidates = list(refs[g * per_group : (g + 1) * per_group])
            candidates += [ref.at[g] for ref in shared]
            copy_chosen(codes_ref[which], candidates, put)


def choose(codes, groups, *shared):
    operands = [buffer for group in groups for buffer in group] + list(shared)
    return pl.pallas_call(
        functools.partial(choose_kernel, len(groups), len(groups[0])),
        out_shape=jax.ShapeDtypeStruct(
            (len(codes), len(groups), *groups[0][0].shape), jnp.bfloat16
        ),
        in_specs=[SMEM] + [VMEM] * len(operands),
        out_specs=VMEM,
        compiler_params=pltpu.CompilerParams(vmem_limit_bytes=4 * MIB),
        cost_estimate=SMALL,
        name="choose",
    )(jnp.stack([jnp.asarray(code, jnp.int32) for code in codes]), *operands)


def own_kernel(*refs):
    out_ref = refs[-1]
    width = out_ref.shape[1]

    def one_bin(f, carry):
        turned = jnp.concatenate([ref[f] for ref in refs[:-1]], axis=0).T
        out_ref[f] = jnp.concatenate([turned[:width], turned[width:]], axis=1)
        return carry

    lax.fori_loop(0, out_ref.shape[0], one_bin, 0, unroll=8)


def own_rows(pieces):
    bins, windows, lanes = pieces[0].shape
    return pl.pallas_call(
        own_kernel,
        out_shape=jax.ShapeDtypeStruct(
            (bins, lanes // 2, 2 * windows * len(pieces)), jnp.bfloat16
        ),
        in_specs=[VMEM] * len(pieces),
        out_specs=VMEM,
        compiler_params=pltpu.CompilerParams(vmem_limit_bytes=4 * MIB),
        cost_estimate=SMALL,
        name="own_rows",
    )(*pieces)


def stack_kernel(scale, place_ref, reach_ref, own_ref, early_ref, *refs):
    last_refs, (out_hbm, products, last, out, sems) = refs[:-5], refs[-5:]
    bins, width, _ = own_ref.shape
    lanes = 2 * width
    offsets = out_hbm.shape[0]
    pitch = products.shape[1] // bins
    for which in range(2):

        def put(ref, which=which):
            last[which] = ref[...]

        copy_chosen(place_ref[2 + which], last_refs, put)

    def one_bin(f, carry):
        tops = [
            jnp.concatenate(
                [early_ref[which, slot, f] for slot in range(early_ref.shape[1])]
                + [last[which, f]],
                axis=0,
            )
            for which in range(2)
        ]
        bottoms = [jnp.concatenate([b[:, width:], -b[:, :width]], axis=1) for b in tops]
        right = jnp.concatenate(
            [jnp.concatenate(tops, axis=1), jnp.concatenate(bottoms, axis=1)], axis=0
        )
        both = jnp.dot(own_ref[f], right, preferred_element_type=jnp.float32)
        row = pl.multiple_of(f * pitch, 8)
        for half in range(2):
            products[half, pl.ds(row, width), :] = both[:, half * lanes : (half + 1) * lanes]
        return carry

    lax.fori_loop(0, bins, one_bin, 0, unroll=8)

    lane = lax.broadcasted_iota(jnp.int32, (offsets, 2 * lanes), 1)
    k = lax.broadcasted_iota(jnp.int32, (offsets, 2 * lanes), 0)
    partner = lane % width + jnp.where(lane >= lanes, width, 0)
    is_real = lane % lanes < width
    far = 4 * lanes
    shift_re = jnp.where(is_real, partner - k, far)
    shift_im = jnp.where(is_real, far, partner - k)
    row_k = lax.broadcasted_iota(jnp.int32, (offsets, F), 0) + place_ref[0]

    def copies(block):
        columns = pl.ds(pl.multiple_of(block * CHANNEL_BLOCK, CHANNEL_BLOCK), CHANNEL_BLOCK)
        return [
            pltpu.make_async_copy(
                out.at[part].reshape(offsets, pitch, F).at[:, columns, :],
                out_hbm.at[:, columns, pl.ds(part * F, F)],
                sems.at[block, part],
            )
            for part in range(2)
        ]

    def one_block(block, carry):
        for il in range(CHANNEL_BLOCK):
            i = block * CHANNEL_BLOCK + il
            at = i + place_ref[1]
            pick = jnp.concatenate(
                [
                    jnp.where(shift_re == at, 1.0, 0.0),
                    jnp.where(shift_im == at, -1.0, 0.0),
                ],
                axis=0,
            ).astype(jnp.bfloat16)
            x = jnp.concatenate(
                [products[half, pl.ds(i, F, stride=pitch), :] for half in range(2)], axis=1
            ).astype(jnp.bfloat16)
            y = lax.dot_general(
                pick, x, (((1,), (1,)), ((), ())), preferred_element_type=jnp.float32
            )
            inside = jnp.where(row_k < reach_ref[i], scale, 0.0)
            for part in range(2):
                out[part, pl.ds(i, offsets, stride=pitch), :] = (
                    y[part * offsets : (part + 1) * offsets] * inside
                )
        for copy in copies(block):
            copy.start()
        return carry

    blocks = width // CHANNEL_BLOCK
    lax.fori_loop(0, blocks, one_block, 0)

    def finish(block, carry):
        for copy in copies(block):
            copy.wait()
        return carry

    lax.fori_loop(0, blocks, finish, 0)


def stacked(own, early, last, place, reach, offsets, windows):
    bins, width, _ = own.shape
    chunk_windows, lanes = last[0].shape[1:]
    pitch = width + PITCH_PAD
    return pl.pallas_call(
        functools.partial(stack_kernel, 1.0 / math.sqrt(windows)),
        out_shape=jax.ShapeDtypeStruct((offsets, width, 2 * F), jnp.float32),
        in_specs=[SMEM, SMEM] + [VMEM] * (2 + len(last)),
        out_specs=ANY,
        scratch_shapes=[
            pltpu.VMEM((2, bins * pitch, lanes), jnp.float32),
            pltpu.VMEM((2, bins, chunk_windows, lanes), jnp.bfloat16),
            pltpu.VMEM((2, offsets * pitch, F), jnp.float32),
            pltpu.SemaphoreType.DMA((width // CHANNEL_BLOCK, 2)),
        ],
        compiler_params=pltpu.CompilerParams(vmem_limit_bytes=24 * MIB),
        cost_estimate=pl.CostEstimate(
            flops=16 * bins * width * width * windows,
            bytes_accessed=30_000_000,
            transcendentals=0,
        ),
        name="stack",
    )(jnp.stack([jnp.asarray(v, jnp.int32) for v in place]), reach, own, early, *last)


def send(array, pairs):
    return lax.ppermute(array, AXES, pairs)


def pairs_of(n_win, n_chan, target):
    pairs = []
    for z in range(n_win):
        for c in range(n_chan):
            to = target(z, c)
            if to is not None:
                pairs.append((c * n_win + z, to * n_win + z))
    return pairs


def after(array, *others):
    return lax.optimization_barrier((array, *others))[0]


def direct_partners(pieces, hops, n_win, n_chan):
    groups = []
    for piece in pieces:
        first = send(piece, pairs_of(n_win, n_chan, lambda z, c: (c - hops[z]) % n_chan))
        second = send(piece, pairs_of(n_win, n_chan, lambda z, c: (c - hops[z] - 1) % n_chan))
        groups.append((first, second))
    return choose((0, 1), groups[:-1]), groups[-1], (0, 1)


def square_partners(pieces, own, n_win, n_chan):
    def pairs(target):
        return pairs_of(n_win, n_chan, lambda z, c: target(z, c, c % 2, c // 2 % 2))

    def first_target(z, c, core, x):
        if z == 3:
            return c ^ 4
        if z == 0:
            return c ^ 2 if core == 0 else None
        if core == 1:
            return c ^ 2
        return c ^ 4 if z == 2 or x == 0 else None

    def second_target(z, c, core, x):
        if z == 3:
            return c ^ 2 if core == 1 else None
        if z == 0:
            return c ^ 4 if core == 0 and x == 1 else None
        if core == 0:
            return c ^ 2
        return c ^ 4 if x == 1 else None

    z, c = lax.axis_index("win"), lax.axis_index("chan")
    core, x = c % 2, c // 2 % 2
    onward = jnp.where((z == 0) | (x == 0) | ((z < 3) & (core == 1)), 1, 0)
    odd_next = jnp.where(x == 0, 1, 2)
    even_next = jnp.where(z == 0, odd_next, 2)
    next_code = jnp.where(core == 0, even_next, jnp.where(z == 3, 2, odd_next))
    outgoing = jnp.where(
        core == 0, jnp.where(z < 2, next_code, 1), jnp.where(z < 2, 0, next_code)
    )
    first_code = jnp.where(z == 0, 0, jnp.where(z == 2, next_code, 3))
    second_code = jnp.where(z == 1, next_code, jnp.where(z == 3, 1, 3))

    held = []
    for slot, piece in enumerate(pieces):
        start = after(piece, held[slot - 2][2]) if slot >= 2 else piece
        moved = send(start, pairs(first_target))
        if slot:
            moved = after(moved, own if slot == len(pieces) - 1 else pieces[slot + 1])
        relay = choose((onward,), [(piece, moved)])[0, 0]
        if slot == len(pieces) - 1:
            held[-1] = (*held[-1][:2], after(held[-1][2], relay))
        held.append((piece, moved, send(relay, pairs(second_target))))

    def swap(groups):
        return send(choose((outgoing,), groups)[0], pairs(lambda z, c, core, x: c ^ 1))

    piece, moved, relayed = held[-1]
    early = choose((first_code, second_code), held[:-1], swap(held[:-1]))
    relayed = after(relayed, early)
    swapped = swap([(piece, moved, relayed)])[0]
    return early, (piece, moved, relayed, swapped), (first_code, second_code)


def on_device(traces, valid, reach):
    width = traces.shape[1]
    n_win, n_chan = lax.axis_size("win"), lax.axis_size("chan")
    offsets = BAND // n_win
    hops = [z * offsets // width for z in range(n_win)]
    first_offset = lax.axis_index("win") * offsets
    pieces = [whitened_chunk(traces, valid)]
    while len(pieces) < n_win:
        ring = [(z, (z + 1) % n_win) for z in range(n_win)]
        pieces.append(lax.ppermute(pieces[-1], "win", ring))
    own = own_rows(pieces)
    if n_chan == 8 and hops == list(range(4)):
        early, last, codes = square_partners(pieces, own, n_win, n_chan)
    else:
        early, last, codes = direct_partners(pieces, hops, n_win, n_chan)
    place = (first_offset, first_offset % width, *codes)
    return stacked(own, early, last, place, reach, offsets, traces.shape[0] * n_win)


def solution(mesh):
    in_specs = (P("win", "chan", None), P("win", "chan"), P("chan"))
    out_specs = P("win", "chan", None)
    return jax.shard_map(
        on_device, mesh=mesh, in_specs=in_specs, out_specs=out_specs, check_vma=False
    )
```

time: 98.8 us -> 99.3 us (level)
  the two profiles are of different devices: /device:TPU:11 before, /device:TPU:9 now
where the time goes in v3:
time: 99.3 us; the launch traced here: 98.5 us
  starting transfers between devices  34.4 us (35%)
  Pallas kernels  25 us (25%)
  waiting for transfers between devices  24.6 us (25%)
  local copies, waits for them, and re-layouts  14.1 us (14%)
    ppermute x10, starting transfers between devices, send(): return lax.ppermute(array, AXES, pairs)  30.2 us
    unnamed x38, local copies, waits for them, and re-layouts  14.1 us
    ppermute x3, waiting for transfers between devices, on_device(): pieces.append(lax.ppermute(pieces[-1], 'win', ring))  13.6 us
    ppermute x10, waiting for transfers between devices, send(): return lax.ppermute(array, AXES, pairs)  11 us
    pallas_call x1, Pallas kernels, stacked(): pl.pallas_call(functools.partial(stack_kernel, 1.0 / math.sqrt(windows)),...  10.5 us
    pallas_call x7, Pallas kernels, choose(): pl.pallas_call(functools.partial(choose_kernel, len(groups), len(groups[0...  7.09 us
    ppermute x3, starting transfers between devices, on_device(): pieces.append(lax.ppermute(pieces[-1], 'win', ring))  4.28 us
    pallas_call x1, Pallas kernels, whitened_chunk(): pl.pallas_call(whiten_kernel, out_shape=jax.ShapeDtypeStruct((F, windows,...  4 us
  transfers between devices with their start and end apart: 13, of which 7 were waited for; matrix products, arithmetic and copies ran while one was open for 0% of the time, Pallas kernels for 7%

profile of v3, /device:TPU:9, one launch (start us, length us, event | category | flops | bytes accessed | tf_op | source)
XLA Modules:
  0.0 98.5 jit_solution(4332003414699529452)
XLA Ops:
  0.0 4.0 %whiten.1.refs_0_ = bf16[128,16,128]{2,1,0:T(8,128)(2,1)} custom-call(bf16[256,512]{1,0:T(8,128)(2,1)} %constant.54.table_hbm, bf16[16,64,512]{2,1,0:T(8,128)(2,1)} %traces_hbm.1, s32[16,64]{1,0:T(8,128)} %valid_hbm.1), custom_call_target="tpu_custom_call" | custom-call | flops 268435456 | bytes 1048576 | tf_op jit(solution)/shard_map/whiten/pallas_call | solution.py:76
  4.0 1.3 %collective-permute-start = (bf16[128,16,128]{2,1,0:T(8,128)(2,1)}, bf16[128,16,128]{2,1,0:T(8,128)(2,1)S(1)}, u32[]{:S(2)}, u32[]{:S(2)}) collective-permute-start(bf16[128,16,128]{2,1,0:T(8,128)(2,1)} %whiten.1.refs_0_), channel_id=1, source_target_pairs={{0,1},{1,2},{2,3},{3,0},{4,5},{5,6},{6,7},{7,4},{8,9},{9,10},{10,1... | collective-permute-start | bytes 1572872 | tf_op jit(solution)/shard_map/ppermute | solution.py:367
  5.4 3.1 %collective-permute-start.3 = (bf16[128,16,128]{2,1,0:T(8,128)(2,1)}, bf16[128,16,128]{2,1,0:T(8,128)(2,1)S(1)}, u32[]{:S(2)}, u32[]{:S(2)}) collective-permute-start(bf16[128,16,128]{2,1,0:T(8,128)(2,1)} %whiten.1.refs_0_), channel_id=1, source_target_pairs={{0,8},{8,0},{16,24},{24,16},{1,17},{5,13},{13,5},{17,1},{21,29},{2... | collective-permute-start | bytes 1572872 | tf_op jit(solution)/shard_map/ppermute | solution.py:277
  8.5 8.5 %collective-permute-done.refs_1_.refs_0_.refs_3_ = bf16[128,16,128]{2,1,0:T(8,128)(2,1)S(1)} collective-permute-done((bf16[128,16,128]{2,1,0:T(8,128)(2,1)}, bf16[128,16,128]{2,1,0:T(8,128)(2,1)S(1)}, u32[]{:S(2)}, u32[]{:S(2)}) %collective-permute-start) | collective-permute-done | bytes 524320 | tf_op jit(solution)/shard_map/ppermute | solution.py:367
  17.1 3.1 %collective-permute-start.5 = (bf16[128,16,128]{2,1,0:T(8,128)(2,1)S(1)}, bf16[128,16,128]{2,1,0:T(8,128)(2,1)S(1)}, u32[]{:S(2)}, u32[]{:S(2)}) collective-permute-start(bf16[128,16,128]{2,1,0:T(8,128)(2,1)S(1)} %collective-permute-done.refs_1_.refs_0_.refs_3_), channel_id=1, source_target_pairs={{0,8},{8,0},{16,24},{24,16},{1,17},{5,13},{13,5},{17,1},{21,29},{2... | collective-permute-start | bytes 1572872 | tf_op jit(solution)/shard_map/ppermute | solution.py:277
  20.2 1.3 %collective-permute-start.1 = (bf16[128,16,128]{2,1,0:T(8,128)(2,1)S(1)}, bf16[128,16,128]{2,1,0:T(8,128)(2,1)S(1)}, u32[]{:S(2)}, u32[]{:S(2)}) collective-permute-start(bf16[128,16,128]{2,1,0:T(8,128)(2,1)S(1)} %collective-permute-done.refs_1_.refs_0_.refs_3_), channel_id=1, source_target_pairs={{0,1},{1,2},{2,3},{3,0},{4,5},{5,6},{6,7},{7,4},{8,9},{9,10},{10,1... | collective-permute-start | bytes 1572872 | tf_op jit(solution)/shard_map/ppermute | solution.py:367
  21.5 1.0 %copy-done = bf16[128,16,128]{2,1,0:T(8,128)(2,1)S(1)} copy-done((bf16[128,16,128]{2,1,0:T(8,128)(2,1)S(1)}, bf16[128,16,128]{2,1,0:T(8,128)(2,1)}, u32[]{:S(2)}) %copy-start) | copy-done | bytes 524312
  23.4 3.8 %collective-permute-done.5.refs_1_.refs_4_ = bf16[128,16,128]{2,1,0:T(8,128)(2,1)S(1)} collective-permute-done((bf16[128,16,128]{2,1,0:T(8,128)(2,1)S(1)}, bf16[128,16,128]{2,1,0:T(8,128)(2,1)S(1)}, u32[]{:S(2)}, u32[]{:S(2)}) %collective-permute-start.5) | collective-permute-done | bytes 524320 | tf_op jit(solution)/shard_map/ppermute | solution.py:277
  27.3 4.3 %collective-permute-done.1.refs_2_.refs_0_.refs_6_ = bf16[128,16,128]{2,1,0:T(8,128)(2,1)S(1)} collective-permute-done((bf16[128,16,128]{2,1,0:T(8,128)(2,1)S(1)}, bf16[128,16,128]{2,1,0:T(8,128)(2,1)S(1)}, u32[]{:S(2)}, u32[]{:S(2)}) %collective-permute-start.1) | collective-permute-done | bytes 524320 | tf_op jit(solution)/shard_map/ppermute | solution.py:367
  32.3 1.6 %collective-permute-start.2 = (bf16[128,16,128]{2,1,0:T(8,128)(2,1)S(1)}, bf16[128,16,128]{2,1,0:T(8,128)(2,1)S(1)}, u32[]{:S(2)}, u32[]{:S(2)}) collective-permute-start(bf16[128,16,128]{2,1,0:T(8,128)(2,1)S(1)} %collective-permute-done.1.refs_2_.refs_0_.refs_6_), channel_id=1, source_target_pairs={{0,1},{1,2},{2,3},{3,0},{4,5},{5,6},{6,7},{7,4},{8,9},{9,10},{10,1... | collective-permute-start | bytes 1572872 | tf_op jit(solution)/shard_map/ppermute | solution.py:367
  34.7 4.7 %collective-permute-start.7 = (bf16[128,16,128]{2,1,0:T(8,128)(2,1)S(1)}, bf16[128,16,128]{2,1,0:T(8,128)(2,1)S(1)}, u32[]{:S(2)}, u32[]{:S(2)}) collective-permute-start(bf16[128,16,128]{2,1,0:T(8,128)(2,1)S(1)} %collective-permute-done.1.refs_2_.refs_0_.refs_6_), channel_id=1, source_target_pairs={{0,8},{8,0},{16,24},{24,16},{1,17},{5,13},{13,5},{17,1},{21,29},{2... | collective-permute-start | bytes 1572872 | tf_op jit(solution)/shard_map/ppermute | solution.py:277
  41.0 5.8 %collective-permute-start.9 = (bf16[128,16,128]{2,1,0:T(8,128)(2,1)S(1)}, bf16[128,16,128]{2,1,0:T(8,128)(2,1)S(1)}, u32[]{:S(2)}, u32[]{:S(2)}) collective-permute-start(bf16[128,16,128]{2,1,0:T(8,128)(2,1)S(1)} %collective-permute-done.2.refs_3_.refs_0_), channel_id=1, source_target_pairs={{0,8},{8,0},{16,24},{24,16},{1,17},{5,13},{13,5},{17,1},{21,29},{2... | collective-permute-start | bytes 1572872 | tf_op jit(solution)/shard_map/ppermute | solution.py:277
  46.8 3.8 %collective-permute-done.7.refs_1_.refs_7_ = bf16[128,16,128]{2,1,0:T(8,128)(2,1)S(1)} collective-permute-done((bf16[128,16,128]{2,1,0:T(8,128)(2,1)S(1)}, bf16[128,16,128]{2,1,0:T(8,128)(2,1)S(1)}, u32[]{:S(2)}, u32[]{:S(2)}) %collective-permute-start.7) | collective-permute-done | bytes 524320 | tf_op jit(solution)/shard_map/ppermute | solution.py:277
  52.3 1.5 %collective-permute-start.8 = (bf16[128,16,128]{2,1,0:T(8,128)(2,1)}, bf16[128,16,128]{2,1,0:T(8,128)(2,1)}, u32[]{:S(2)}, u32[]{:S(2)}) collective-permute-start(bf16[128,16,128]{2,1,0:T(8,128)(2,1)} %bitcast.7), channel_id=1, source_target_pairs={{8,24},{24,8},{1,9},{9,1},{13,29},{17,25},{25,17},{29,13},{2,10},{... | collective-permute-start | bytes 1572872 | tf_op jit(solution)/shard_map/ppermute | solution.py:277
  53.7 3.4 %own_rows.1.own_ref = bf16[128,64,128]{2,1,0:T(8,128)(2,1)S(1)} custom-call(bf16[128,16,128]{2,1,0:T(8,128)(2,1)S(1)} %copy-done.1, bf16[128,16,128]{2,1,0:T(8,128)(2,1)S(1)} %collective-permute-done.refs_1_.refs_0_.refs_3_, bf16[128,16,128]{2,1,0:T(8,128)(2,1)S(1)} %collective-permute-done.1.refs_2_.refs_0_.refs_6_, ...), custom_call_target="tpu_custom_call" | custom-call | flops 1 | bytes 1 | tf_op jit(solution)/shard_map/own_rows/pallas_call | solution.py:147
  57.2 1.3 %copy-done.4 = bf16[128,64,128]{2,1,0:T(8,128)(2,1)} copy-done((bf16[128,64,128]{2,1,0:T(8,128)(2,1)}, bf16[128,64,128]{2,1,0:T(8,128)(2,1)S(1)}, u32[]{:S(2)}) %copy-start.4) | copy-done | bytes 2097176
  58.5 0.9 choose.10
  59.4 2.3 %choose.11 = bf16[1,3,128,16,128]{4,3,2,1,0:T(8,128)(2,1)} custom-call(s32[1]{0:T(128)} %bitcast.9.codes_ref, bf16[128,16,128]{2,1,0:T(8,128)(2,1)S(1)} %copy-done.1, bf16[128,16,128]{2,1,0:T(8,128)(2,1)S(1)} %collective-permute-done.3.refs_1_, bf16[128,16,128]{2,1,0:T(8,128)(2,1)S(1)} %copy-done.13, ...), custom_call_target="tpu_custom_call" | custom-call | flops 1 | bytes 1 | tf_op jit(solution)/shard_map/choose/pallas_call | solution.py:120
  61.7 8.6 %collective-permute-start.10 = (bf16[3,128,16,128]{3,2,1,0:T(8,128)(2,1)}, bf16[3,128,16,128]{3,2,1,0:T(8,128)(2,1)}, u32[]{:S(2)}, u32[]{:S(2)}) collective-permute-start(bf16[3,128,16,128]{3,2,1,0:T(8,128)(2,1)} %bitcast.10), channel_id=1, source_target_pairs={{0,4},{4,0},{8,12},{12,8},{16,20},{20,16},{24,28},{28,24},{1,5},{5... | collective-permute-start | bytes 4718600 | tf_op jit(solution)/shard_map/ppermute | solution.py:277
  70.3 1.5 %collective-permute-start.11 = (bf16[128,16,128]{2,1,0:T(8,128)(2,1)}, bf16[128,16,128]{2,1,0:T(8,128)(2,1)}, u32[]{:S(2)}, u32[]{:S(2)}) collective-permute-start(bf16[128,16,128]{2,1,0:T(8,128)(2,1)} %bitcast.8), channel_id=1, source_target_pairs={{8,24},{24,8},{1,9},{9,1},{13,29},{17,25},{25,17},{29,13},{2,10},{... | collective-permute-start | bytes 1572872 | tf_op jit(solution)/shard_map/ppermute | solution.py:277
  71.8 1.9 %collective-permute-done.10.refs_9_ = bf16[3,128,16,128]{3,2,1,0:T(8,128)(2,1)} collective-permute-done((bf16[3,128,16,128]{3,2,1,0:T(8,128)(2,1)}, bf16[3,128,16,128]{3,2,1,0:T(8,128)(2,1)}, u32[]{:S(2)}, u32[]{:S(2)}) %collective-permute-start.10) | collective-permute-done | bytes 1572896 | tf_op jit(solution)/shard_map/ppermute | solution.py:277
  73.7 1.0 %copy-done.8 = bf16[128,16,128]{2,1,0:T(8,128)(2,1)S(1)} copy-done((bf16[128,16,128]{2,1,0:T(8,128)(2,1)S(1)}, bf16[128,16,128]{2,1,0:T(8,128)(2,1)}, u32[]{:S(2)}) %copy-start.8) | copy-done | bytes 524312
  74.7 1.0 %copy-done.11 = bf16[128,16,128]{2,1,0:T(8,128)(2,1)S(1)} copy-done((bf16[128,16,128]{2,1,0:T(8,128)(2,1)S(1)}, bf16[128,16,128]{2,1,0:T(8,128)(2,1)}, u32[]{:S(2)}) %copy-start.11) | copy-done | bytes 524312
  75.8 1.0 %copy-done.14 = bf16[128,16,128]{2,1,0:T(8,128)(2,1)S(1)} copy-done((bf16[128,16,128]{2,1,0:T(8,128)(2,1)S(1)}, bf16[128,16,128]{2,1,0:T(8,128)(2,1)}, u32[]{:S(2)}) %copy-start.14) | copy-done | bytes 524312
  76.8 1.0 %copy-done.17 = bf16[128,16,128]{2,1,0:T(8,128)(2,1)S(1)} copy-done((bf16[128,16,128]{2,1,0:T(8,128)(2,1)S(1)}, bf16[128,16,128]{2,1,0:T(8,128)(2,1)}, u32[]{:S(2)}) %copy-start.17) | copy-done | bytes 524312
  77.8 1.9 %choose.12.early_ref = bf16[2,3,128,16,128]{4,3,2,1,0:T(8,128)(2,1)S(1)} custom-call(s32[2]{0:T(128)S(1)} %pad_add_fusion.1.codes_ref, bf16[128,16,128]{2,1,0:T(8,128)(2,1)S(1)} %copy-done.1, bf16[128,16,128]{2,1,0:T(8,128)(2,1)S(1)} %collective-permute-done.3.refs_1_, bf16[128,16,128]{2,1,0:T(8,128)(2,1)S(1)} %copy-done.14, ...), custom_call_target="tpu_custom_call" | custom-call | flops 1 | bytes 1 | tf_op jit(solution)/shard_map/choose/pallas_call | solution.py:120
  79.8 1.7 %copy-done.2 = bf16[2,3,128,16,128]{4,3,2,1,0:T(8,128)(2,1)} copy-done((bf16[2,3,128,16,128]{4,3,2,1,0:T(8,128)(2,1)}, bf16[2,3,128,16,128]{4,3,2,1,0:T(8,128)(2,1)S(1)}, u32[]{:S(2)}) %copy-start.2) | copy-done | bytes 3145752
  81.4 1.1 %choose.13 = bf16[1,1,128,16,128]{4,3,2,1,0:T(8,128)(2,1)S(1)} custom-call(s32[1]{0:T(128)} %bitcast.9.codes_ref, bf16[128,16,128]{2,1,0:T(8,128)(2,1)S(1)} %collective-permute-done.2.refs_3_.refs_0_, bf16[128,16,128]{2,1,0:T(8,128)(2,1)S(1)} %collective-permute-done.9.refs_1_, bf16[128,16,128]{2,1,0:T(8,128)(2,1)} %collective-permute-done.11.refs_2_), custom_call_target="tpu_custom_call" | custom-call | flops 1 | bytes 1 | tf_op jit(solution)/shard_map/choose/pallas_call | solution.py:120
  83.0 1.5 %collective-permute-done.12 = bf16[1,128,16,128]{3,2,1,0:T(8,128)(2,1)S(1)} collective-permute-done((bf16[1,128,16,128]{3,2,1,0:T(8,128)(2,1)S(1)}, bf16[1,128,16,128]{3,2,1,0:T(8,128)(2,1)S(1)}, u32[]{:S(2)}, u32[]{:S(2)}) %collective-permute-start.12) | collective-permute-done | bytes 524320 | tf_op jit(solution)/shard_map/ppermute | solution.py:277
  84.5 1.9 %copy-done.3 = bf16[2,3,128,16,128]{4,3,2,1,0:T(8,128)(2,1)S(1)} copy-done((bf16[2,3,128,16,128]{4,3,2,1,0:T(8,128)(2,1)S(1)}, bf16[2,3,128,16,128]{4,3,2,1,0:T(8,128)(2,1)}, u32[]{:S(2)}) %copy-start.3) | copy-done | bytes 3145752
  86.4 1.6 %copy-done.5 = bf16[128,64,128]{2,1,0:T(8,128)(2,1)S(1)} copy-done((bf16[128,64,128]{2,1,0:T(8,128)(2,1)S(1)}, bf16[128,64,128]{2,1,0:T(8,128)(2,1)}, u32[]{:S(2)}) %copy-start.5) | copy-done | bytes 2097176
  88.0 10.5 %stack.39 = f32[64,64,256]{2,1,0:T(8,128)} custom-call(s32[4]{0:T(128)S(1)} %pad_add_fusion.place_ref, s32[64]{0:T(128)S(1)} %copy-done.18, bf16[128,64,128]{2,1,0:T(8,128)(2,1)S(1)} %copy-done.5, bf16[2,3,128,16,128]{4,3,2,1,0:T(8,128)(2,1)S(1)} %copy-done.3, bf16[128,16,128]{2,1,0:T(8,128)(2,1)S(1)} %collective-permute-done.2.refs_3_.refs_0_, ...), custom_call_target="tpu_custom_call" | custom-call | flops 536870912 | bytes 30000000 | tf_op jit(solution)/shard_map/stack/pallas_call | solution.py:255
  (44 shorter events, 6.2 us)
Async XLA Ops:
  4.0 13.0 %collective-permute-start = (bf16[128,16,128]{2,1,0:T(8,128)(2,1)}, bf16[128,16,128]{2,1,0:T(8,128)(2,1)S(1)}, u32[]{:S(2)}, u32[]{:S(2)}) collective-permute-start(bf16[128,16,128]{2,1,0:T(8,128)(2,1)} %whiten.1.refs_0_), channel_id=1, source_target_pairs={{0,1},{1,2},{2,3},{3,0},{4,5},{5,6},{6,7},{7,4},{8,9},{9,10},{10,1... | collective-permute-start | bytes 1572872 | tf_op jit(solution)/shard_map/ppermute | solution.py:367
  5.4 16.2 %collective-permute-start.3 = (bf16[128,16,128]{2,1,0:T(8,128)(2,1)}, bf16[128,16,128]{2,1,0:T(8,128)(2,1)S(1)}, u32[]{:S(2)}, u32[]{:S(2)}) collective-permute-start(bf16[128,16,128]{2,1,0:T(8,128)(2,1)} %whiten.1.refs_0_), channel_id=1, source_target_pairs={{0,8},{8,0},{16,24},{24,16},{1,17},{5,13},{13,5},{17,1},{21,29},{2... | collective-permute-start | bytes 1572872 | tf_op jit(solution)/shard_map/ppermute | solution.py:277
  17.1 10.2 %collective-permute-start.5 = (bf16[128,16,128]{2,1,0:T(8,128)(2,1)S(1)}, bf16[128,16,128]{2,1,0:T(8,128)(2,1)S(1)}, u32[]{:S(2)}, u32[]{:S(2)}) collective-permute-start(bf16[128,16,128]{2,1,0:T(8,128)(2,1)S(1)} %collective-permute-done.refs_1_.refs_0_.refs_3_), channel_id=1, source_target_pairs={{0,8},{8,0},{16,24},{24,16},{1,17},{5,13},{13,5},{17,1},{21,29},{2... | collective-permute-start | bytes 1572872 | tf_op jit(solution)/shard_map/ppermute | solution.py:277
  20.2 11.4 %collective-permute-start.1 = (bf16[128,16,128]{2,1,0:T(8,128)(2,1)S(1)}, bf16[128,16,128]{2,1,0:T(8,128)(2,1)S(1)}, u32[]{:S(2)}, u32[]{:S(2)}) collective-permute-start(bf16[128,16,128]{2,1,0:T(8,128)(2,1)S(1)} %collective-permute-done.refs_1_.refs_0_.refs_3_), channel_id=1, source_target_pairs={{0,1},{1,2},{2,3},{3,0},{4,5},{5,6},{6,7},{7,4},{8,9},{9,10},{10,1... | collective-permute-start | bytes 1572872 | tf_op jit(solution)/shard_map/ppermute | solution.py:367
  21.5 1.0 %copy-start = (bf16[128,16,128]{2,1,0:T(8,128)(2,1)S(1)}, bf16[128,16,128]{2,1,0:T(8,128)(2,1)}, u32[]{:S(2)}) copy-start(bf16[128,16,128]{2,1,0:T(8,128)(2,1)} %whiten.1.refs_0_) | copy-start | bytes 1572868
  22.6 31.2 %copy-start.1 = (bf16[128,16,128]{2,1,0:T(8,128)(2,1)S(1)}, bf16[128,16,128]{2,1,0:T(8,128)(2,1)}, u32[]{:S(2)}) copy-start(bf16[128,16,128]{2,1,0:T(8,128)(2,1)} %whiten.1.refs_0_) | copy-start | bytes 1572868
  22.6 11.3 %collective-permute-start.4 = (bf16[128,16,128]{2,1,0:T(8,128)(2,1)S(1)}, bf16[128,16,128]{2,1,0:T(8,128)(2,1)S(1)}, u32[]{:S(2)}, u32[]{:S(2)}) collective-permute-start(bf16[128,16,128]{2,1,0:T(8,128)(2,1)S(1)} %bitcast.15), channel_id=1, source_target_pairs={{8,24},{24,8},{1,9},{9,1},{13,29},{17,25},{25,17},{29,13},{2,10},{... | collective-permute-start | bytes 1572872 | tf_op jit(solution)/shard_map/ppermute | solution.py:277
  27.3 4.3 %copy-start.6 = (bf16[128,16,128]{2,1,0:T(8,128)(2,1)}, bf16[128,16,128]{2,1,0:T(8,128)(2,1)S(1)}, u32[]{:S(2)}) copy-start(bf16[128,16,128]{2,1,0:T(8,128)(2,1)S(1)} %collective-permute-done.5.refs_1_.refs_4_) | copy-start | bytes 1572868
  31.6 7.8 %collective-permute-start.6 = (bf16[128,16,128]{2,1,0:T(8,128)(2,1)S(1)}, bf16[128,16,128]{2,1,0:T(8,128)(2,1)S(1)}, u32[]{:S(2)}, u32[]{:S(2)}) collective-permute-start(bf16[128,16,128]{2,1,0:T(8,128)(2,1)S(1)} %bitcast.16), channel_id=1, source_target_pairs={{8,24},{24,8},{1,9},{9,1},{13,29},{17,25},{25,17},{29,13},{2,10},{... | collective-permute-start | bytes 1572872 | tf_op jit(solution)/shard_map/ppermute | solution.py:277
  32.3 8.7 %collective-permute-start.2 = (bf16[128,16,128]{2,1,0:T(8,128)(2,1)S(1)}, bf16[128,16,128]{2,1,0:T(8,128)(2,1)S(1)}, u32[]{:S(2)}, u32[]{:S(2)}) collective-permute-start(bf16[128,16,128]{2,1,0:T(8,128)(2,1)S(1)} %collective-permute-done.1.refs_2_.refs_0_.refs_6_), channel_id=1, source_target_pairs={{0,1},{1,2},{2,3},{3,0},{4,5},{5,6},{6,7},{7,4},{8,9},{9,10},{10,1... | collective-permute-start | bytes 1572872 | tf_op jit(solution)/shard_map/ppermute | solution.py:367
  33.9 0.8 copy-start.12
  34.7 15.9 %collective-permute-start.7 = (bf16[128,16,128]{2,1,0:T(8,128)(2,1)S(1)}, bf16[128,16,128]{2,1,0:T(8,128)(2,1)S(1)}, u32[]{:S(2)}, u32[]{:S(2)}) collective-permute-start(bf16[128,16,128]{2,1,0:T(8,128)(2,1)S(1)} %collective-permute-done.1.refs_2_.refs_0_.refs_6_), channel_id=1, source_target_pairs={{0,8},{8,0},{16,24},{24,16},{1,17},{5,13},{13,5},{17,1},{21,29},{2... | collective-permute-start | bytes 1572872 | tf_op jit(solution)/shard_map/ppermute | solution.py:277
  39.4 0.8 copy-start.15
  41.0 17.6 %collective-permute-start.9 = (bf16[128,16,128]{2,1,0:T(8,128)(2,1)S(1)}, bf16[128,16,128]{2,1,0:T(8,128)(2,1)S(1)}, u32[]{:S(2)}, u32[]{:S(2)}) collective-permute-start(bf16[128,16,128]{2,1,0:T(8,128)(2,1)S(1)} %collective-permute-done.2.refs_3_.refs_0_), channel_id=1, source_target_pairs={{0,8},{8,0},{16,24},{24,16},{1,17},{5,13},{13,5},{17,1},{21,29},{2... | collective-permute-start | bytes 1572872 | tf_op jit(solution)/shard_map/ppermute | solution.py:277
  51.5 0.8 copy-start.9
  52.3 7.1 %collective-permute-start.8 = (bf16[128,16,128]{2,1,0:T(8,128)(2,1)}, bf16[128,16,128]{2,1,0:T(8,128)(2,1)}, u32[]{:S(2)}, u32[]{:S(2)}) collective-permute-start(bf16[128,16,128]{2,1,0:T(8,128)(2,1)} %bitcast.7), channel_id=1, source_target_pairs={{8,24},{24,8},{1,9},{9,1},{13,29},{17,25},{25,17},{29,13},{2,10},{... | collective-permute-start | bytes 1572872 | tf_op jit(solution)/shard_map/ppermute | solution.py:277
  53.7 5.6 %copy-start.7 = (bf16[128,16,128]{2,1,0:T(8,128)(2,1)S(1)}, bf16[128,16,128]{2,1,0:T(8,128)(2,1)}, u32[]{:S(2)}) copy-start(bf16[128,16,128]{2,1,0:T(8,128)(2,1)} %copy-done.6) | copy-start | bytes 1572868
  53.7 5.6 %copy-start.10 = (bf16[128,16,128]{2,1,0:T(8,128)(2,1)S(1)}, bf16[128,16,128]{2,1,0:T(8,128)(2,1)}, u32[]{:S(2)}) copy-start(bf16[128,16,128]{2,1,0:T(8,128)(2,1)} %copy-done.9) | copy-start | bytes 1572868
  53.7 5.6 %copy-start.13 = (bf16[128,16,128]{2,1,0:T(8,128)(2,1)S(1)}, bf16[128,16,128]{2,1,0:T(8,128)(2,1)}, u32[]{:S(2)}) copy-start(bf16[128,16,128]{2,1,0:T(8,128)(2,1)} %copy-done.12) | copy-start | bytes 1572868
  53.7 5.7 %copy-start.16 = (bf16[128,16,128]{2,1,0:T(8,128)(2,1)S(1)}, bf16[128,16,128]{2,1,0:T(8,128)(2,1)}, u32[]{:S(2)}) copy-start(bf16[128,16,128]{2,1,0:T(8,128)(2,1)} %copy-done.15) | copy-start | bytes 1572868
  57.2 1.3 %copy-start.4 = (bf16[128,64,128]{2,1,0:T(8,128)(2,1)}, bf16[128,64,128]{2,1,0:T(8,128)(2,1)S(1)}, u32[]{:S(2)}) copy-start(bf16[128,64,128]{2,1,0:T(8,128)(2,1)S(1)} %own_rows.1.own_ref) | copy-start | bytes 6291460
  61.7 12.0 %collective-permute-start.10 = (bf16[3,128,16,128]{3,2,1,0:T(8,128)(2,1)}, bf16[3,128,16,128]{3,2,1,0:T(8,128)(2,1)}, u32[]{:S(2)}, u32[]{:S(2)}) collective-permute-start(bf16[3,128,16,128]{3,2,1,0:T(8,128)(2,1)} %bitcast.10), channel_id=1, source_target_pairs={{0,4},{4,0},{8,12},{12,8},{16,20},{20,16},{24,28},{28,24},{1,5},{5... | collective-permute-start | bytes 4718600 | tf_op jit(solution)/shard_map/ppermute | solution.py:277
  70.3 11.1 %collective-permute-start.11 = (bf16[128,16,128]{2,1,0:T(8,128)(2,1)}, bf16[128,16,128]{2,1,0:T(8,128)(2,1)}, u32[]{:S(2)}, u32[]{:S(2)}) collective-permute-start(bf16[128,16,128]{2,1,0:T(8,128)(2,1)} %bitcast.8), channel_id=1, source_target_pairs={{8,24},{24,8},{1,9},{9,1},{13,29},{17,25},{25,17},{29,13},{2,10},{... | collective-permute-start | bytes 1572872 | tf_op jit(solution)/shard_map/ppermute | solution.py:277
  73.7 1.0 %copy-start.8 = (bf16[128,16,128]{2,1,0:T(8,128)(2,1)S(1)}, bf16[128,16,128]{2,1,0:T(8,128)(2,1)}, u32[]{:S(2)}) copy-start(bf16[128,16,128]{2,1,0:T(8,128)(2,1)} %copy-done.6) | copy-start | bytes 1572868
  74.7 1.0 %copy-start.11 = (bf16[128,16,128]{2,1,0:T(8,128)(2,1)S(1)}, bf16[128,16,128]{2,1,0:T(8,128)(2,1)}, u32[]{:S(2)}) copy-start(bf16[128,16,128]{2,1,0:T(8,128)(2,1)} %copy-done.9) | copy-start | bytes 1572868
  75.8 1.0 %copy-start.14 = (bf16[128,16,128]{2,1,0:T(8,128)(2,1)S(1)}, bf16[128,16,128]{2,1,0:T(8,128)(2,1)}, u32[]{:S(2)}) copy-start(bf16[128,16,128]{2,1,0:T(8,128)(2,1)} %copy-done.12) | copy-start | bytes 1572868
  76.8 1.0 %copy-start.17 = (bf16[128,16,128]{2,1,0:T(8,128)(2,1)S(1)}, bf16[128,16,128]{2,1,0:T(8,128)(2,1)}, u32[]{:S(2)}) copy-start(bf16[128,16,128]{2,1,0:T(8,128)(2,1)} %copy-done.15) | copy-start | bytes 1572868
  79.8 1.7 %copy-start.2 = (bf16[2,3,128,16,128]{4,3,2,1,0:T(8,128)(2,1)}, bf16[2,3,128,16,128]{4,3,2,1,0:T(8,128)(2,1)S(1)}, u32[]{:S(2)}) copy-start(bf16[2,3,128,16,128]{4,3,2,1,0:T(8,128)(2,1)S(1)} %choose.12.early_ref) | copy-start | bytes 9437188
  81.4 3.1 %copy-start.18 = (s32[64]{0:T(128)S(1)}, s32[64]{0:T(128)}, u32[]{:S(2)}) copy-start(s32[64]{0:T(128)} %reach_ref.1) | copy-start | bytes 772
  82.5 2.0 %collective-permute-start.12 = (bf16[1,128,16,128]{3,2,1,0:T(8,128)(2,1)S(1)}, bf16[1,128,16,128]{3,2,1,0:T(8,128)(2,1)S(1)}, u32[]{:S(2)}, u32[]{:S(2)}) collective-permute-start(bf16[1,128,16,128]{3,2,1,0:T(8,128)(2,1)S(1)} %bitcast.14), channel_id=1, source_target_pairs={{0,4},{4,0},{8,12},{12,8},{16,20},{20,16},{24,28},{28,24},{1,5},{5... | collective-permute-start | bytes 1572872 | tf_op jit(solution)/shard_map/ppermute | solution.py:277
  84.5 1.9 %copy-start.3 = (bf16[2,3,128,16,128]{4,3,2,1,0:T(8,128)(2,1)S(1)}, bf16[2,3,128,16,128]{4,3,2,1,0:T(8,128)(2,1)}, u32[]{:S(2)}) copy-start(bf16[2,3,128,16,128]{4,3,2,1,0:T(8,128)(2,1)} %copy-done.2) | copy-start | bytes 9437188
  86.4 1.6 %copy-start.5 = (bf16[128,64,128]{2,1,0:T(8,128)(2,1)S(1)}, bf16[128,64,128]{2,1,0:T(8,128)(2,1)}, u32[]{:S(2)}) copy-start(bf16[128,64,128]{2,1,0:T(8,128)(2,1)} %copy-done.4) | copy-start | bytes 6291460

commit v4 on v3

--- a/solution.py
+++ b/solution.py
@@ -17,7 +17,11 @@
 WHITEN_BLOCKS = 4
 PITCH_PAD = 8
 MIB = 1024 * 1024
+COPY_BLOCKS = 4
+WIDE_BYTES = 24 * MIB
 VMEM = pl.BlockSpec(memory_space=pltpu.VMEM)
+FEW_MIB = pltpu.CompilerParams(vmem_limit_bytes=4 * MIB)
+WHOLE_VMEM = pltpu.CompilerParams(vmem_limit_bytes=62 * MIB)
 SMEM = pl.BlockSpec(memory_space=pltpu.SMEM)
 SMALL = pl.CostEstimate(flops=1, bytes_accessed=1, transcendentals=0)
 ANY = pl.BlockSpec(memory_space=pl.ANY)
@@ -85,7 +89,7 @@
             pltpu.VMEM((F * windows, 2 * width), jnp.float32),
             pltpu.SemaphoreType.DMA((2 + WHITEN_BLOCKS,)),
         ],
-        compiler_params=pltpu.CompilerParams(vmem_limit_bytes=62 * MIB),
+        compiler_params=WHOLE_VMEM,
         cost_estimate=pl.CostEstimate(
             flops=4 * F * traces.size, bytes_accessed=2 * traces.size, transcendentals=0
         ),
@@ -101,95 +105,176 @@
             put(ref)
 
 
-def choose_kernel(groups, per_group, codes_ref, *refs):
+def choose_kernel(groups, code_ref, *refs):
     out_ref = refs[-1]
-    shared = refs[groups * per_group : -1]
-    for which in range(out_ref.shape[0]):
-        for g in range(groups):
-
-            def put(ref, which=which, g=g):
-                out_ref[which, g] = ref[...]
-
-            candidates = list(refs[g * per_group : (g + 1) * per_group])
-            candidates += [ref.at[g] for ref in shared]
-            copy_chosen(codes_ref[which], candidates, put)
-
-
-def choose(codes, groups, *shared):
-    operands = [buffer for group in groups for buffer in group] + list(shared)
+    per_group = (len(refs) - 1) // groups
+    for g in range(groups):
+
+        def put(ref, g=g):
+            out_ref[g] = ref[...]
+
+        copy_chosen(code_ref[0], refs[g * per_group : (g + 1) * per_group], put)
+
+
+def choose(code, groups):
+    operands = [buffer for group in groups for buffer in group]
     return pl.pallas_call(
-        functools.partial(choose_kernel, len(groups), len(groups[0])),
-        out_shape=jax.ShapeDtypeStruct(
-            (len(codes), len(groups), *groups[0][0].shape), jnp.bfloat16
-        ),
+        functools.partial(choose_kernel, len(groups)),
+        out_shape=jax.ShapeDtypeStruct((len(groups), *groups[0][0].shape), jnp.bfloat16),
         in_specs=[SMEM] + [VMEM] * len(operands),
         out_specs=VMEM,
-        compiler_params=pltpu.CompilerParams(vmem_limit_bytes=4 * MIB),
+        compiler_params=FEW_MIB,
         cost_estimate=SMALL,
         name="choose",
+    )(jnp.asarray(code, jnp.int32).reshape(1), *operands)
+
+
+def bank_kernel(slot, codes_ref, *refs):
+    store_ref, sems = refs[-2:]
+    candidates = refs[:-2]
+
+    def copy(candidate, to):
+        return pltpu.make_async_copy(candidates[candidate], store_ref.at[to, slot], sems.at[to])
+
+    copy(0, 0).start()
+    for which in range(2):
+        for candidate in range(len(candidates)):
+
+            @pl.when(codes_ref[which] == candidate)
+            def _(candidate=candidate, which=which):
+                copy(candidate, 1 + which).start()
+
+    for to in range(3):
+        copy(0, to).wait()
+
+
+def widened(places, shape):
+    return (max(places, WIDE_BYTES // (2 * math.prod(shape))), *shape)
+
+
+def bank(store, slot, slots, codes, candidates):
+    shape = widened(3, (slots, *candidates[0].shape))
+    operands = list(candidates)
+    aliases = {}
+    kernel = functools.partial(bank_kernel, slot)
+    if store is not None:
+        operands.append(store)
+        aliases = {len(operands): 0}
+
+        def kernel(codes_ref, *refs):
+            bank_kernel(slot, codes_ref, *refs[: len(candidates)], *refs[-2:])
+
+    return pl.pallas_call(
+        kernel,
+        out_shape=jax.ShapeDtypeStruct(shape, jnp.bfloat16),
+        in_specs=[SMEM] + [VMEM] * len(candidates) + [ANY] * len(aliases),
+        out_specs=ANY,
+        scratch_shapes=[pltpu.SemaphoreType.DMA((3,))],
+        input_output_aliases=aliases,
+        compiler_params=FEW_MIB,
+        cost_estimate=SMALL,
+        name="bank",
     )(jnp.stack([jnp.asarray(code, jnp.int32) for code in codes]), *operands)
 
 
-def own_kernel(*refs):
-    out_ref = refs[-1]
-    width = out_ref.shape[1]
+def own_kernel(early, store_ref, *refs):
+    late_refs, (out_hbm, pieces, out, sems) = refs[:-4], refs[-4:]
+    bins, width, _ = out.shape
+
+    def load(slot):
+        return pltpu.make_async_copy(store_ref.at[0, slot], pieces.at[slot], sems.at[slot])
+
+    for slot in range(early):
+        load(slot).start()
+    for slot in range(early):
+        load(slot).wait()
 
     def one_bin(f, carry):
-        turned = jnp.concatenate([ref[f] for ref in refs[:-1]], axis=0).T
-        out_ref[f] = jnp.concatenate([turned[:width], turned[width:]], axis=1)
+        rows = [pieces[slot, f] for slot in range(early)] + [ref[f] for ref in late_refs]
+        turned = jnp.concatenate(rows, axis=0).T
+        out[f] = jnp.concatenate([turned[:width], turned[width:]], axis=1)
         return carry
 
-    lax.fori_loop(0, out_ref.shape[0], one_bin, 0, unroll=8)
-
-
-def own_rows(pieces):
-    bins, windows, lanes = pieces[0].shape
+    lax.fori_loop(0, bins, one_bin, 0, unroll=8)
+    store = pltpu.make_async_copy(out, out_hbm.at[0], sems.at[0])
+    store.start()
+    store.wait()
+
+
+def own_rows(store, late):
+    bins, windows, lanes = late[0].shape
+    early = store.shape[1]
+    rows = (bins, lanes // 2, 2 * windows * (early + len(late)))
     return pl.pallas_call(
-        own_kernel,
-        out_shape=jax.ShapeDtypeStruct(
-            (bins, lanes // 2, 2 * windows * len(pieces)), jnp.bfloat16
-        ),
-        in_specs=[VMEM] * len(pieces),
-        out_specs=VMEM,
-        compiler_params=pltpu.CompilerParams(vmem_limit_bytes=4 * MIB),
+        functools.partial(own_kernel, early),
+        out_shape=jax.ShapeDtypeStruct(widened(1, rows), jnp.bfloat16),
+        in_specs=[ANY] + [VMEM] * len(late),
+        out_specs=ANY,
+        scratch_shapes=[
+            pltpu.VMEM((early, bins, windows, lanes), jnp.bfloat16),
+            pltpu.VMEM(rows, jnp.bfloat16),
+            pltpu.SemaphoreType.DMA((early,)),
+        ],
+        compiler_params=pltpu.CompilerParams(vmem_limit_bytes=12 * MIB),
         cost_estimate=SMALL,
         name="own_rows",
-    )(*pieces)
-
-
-def stack_kernel(scale, place_ref, reach_ref, own_ref, early_ref, *refs):
-    last_refs, (out_hbm, products, last, out, sems) = refs[:-5], refs[-5:]
-    bins, width, _ = own_ref.shape
+    )(store, *late)
+
+
+def stack_kernel(scale, groups, place_ref, reach_ref, own_hbm, store_ref, *refs):
+    buffers, (out_hbm, own, partners, products, out, in_sems, sems) = refs[:-7], refs[-7:]
+    bins, width, _ = own.shape
     lanes = 2 * width
     offsets = out_hbm.shape[0]
     pitch = products.shape[1] // bins
-    for which in range(2):
-
-        def put(ref, which=which):
-            last[which] = ref[...]
-
-        copy_chosen(place_ref[2 + which], last_refs, put)
+    slots = partners.shape[1]
+    early = slots - len(groups)
+    block_bins = bins // COPY_BLOCKS
+
+    def loads(n):
+        block = pl.ds(n * block_bins, block_bins)
+        yield pltpu.make_async_copy(own_hbm.at[0, block], own.at[block], in_sems.at[n, 0])
+        for which in range(2):
+            yield pltpu.make_async_copy(
+                store_ref.at[1 + which, :, block],
+                partners.at[which, 0:early, block],
+                in_sems.at[n, 1 + which],
+            )
+
+    for n in range(COPY_BLOCKS):
+        for copy in loads(n):
+            copy.start()
+    for late, group in enumerate(groups):
+        for which in range(2):
+            candidates = [
+                buffers[number] if index is None else buffers[number].at[index]
+                for number, index in group
+            ]
+
+            def put(ref, late=late, which=which):
+                partners[which, early + late] = ref[...]
+
+            copy_chosen(place_ref[2 + 2 * late + which], candidates, put)
 
     def one_bin(f, carry):
         tops = [
-            jnp.concatenate(
-                [early_ref[which, slot, f] for slot in range(early_ref.shape[1])]
-                + [last[which, f]],
-                axis=0,
-            )
+            jnp.concatenate([partners[which, slot, f] for slot in range(slots)], axis=0)
             for which in range(2)
         ]
         bottoms = [jnp.concatenate([b[:, width:], -b[:, :width]], axis=1) for b in tops]
         right = jnp.concatenate(
             [jnp.concatenate(tops, axis=1), jnp.concatenate(bottoms, axis=1)], axis=0
         )
-        both = jnp.dot(own_ref[f], right, preferred_element_type=jnp.float32)
+        both = jnp.dot(own[f], right, preferred_element_type=jnp.float32)
         row = pl.multiple_of(f * pitch, 8)
         for half in range(2):
             products[half, pl.ds(row, width), :] = both[:, half * lanes : (half + 1) * lanes]
         return carry
 
-    lax.fori_loop(0, bins, one_bin, 0, unroll=8)
+    for n in range(COPY_BLOCKS):
+        for copy in loads(n):
+            copy.wait()
+        lax.fori_loop(n * block_bins, (n + 1) * block_bins, one_bin, 0, unroll=8)
 
     lane = lax.broadcasted_iota(jnp.int32, (offsets, 2 * lanes), 1)
     k = lax.broadcasted_iota(jnp.int32, (offsets, 2 * lanes), 0)
@@ -248,29 +333,28 @@
     lax.fori_loop(0, blocks, finish, 0)
 
 
-def stacked(own, early, last, place, reach, offsets, windows):
-    bins, width, _ = own.shape
-    chunk_windows, lanes = last[0].shape[1:]
+def stacked(own, store, buffers, groups, place, reach, offsets, windows):
+    _, bins, width, depth = own.shape
+    chunk_windows, lanes = buffers[0].shape[-2:]
     pitch = width + PITCH_PAD
+    slots = store.shape[1] + len(groups)
     return pl.pallas_call(
-        functools.partial(stack_kernel, 1.0 / math.sqrt(windows)),
+        functools.partial(stack_kernel, 1.0 / math.sqrt(windows), groups),
         out_shape=jax.ShapeDtypeStruct((offsets, width, 2 * F), jnp.float32),
-        in_specs=[SMEM, SMEM] + [VMEM] * (2 + len(last)),
+        in_specs=[SMEM, SMEM, ANY, ANY] + [VMEM] * len(buffers),
         out_specs=ANY,
         scratch_shapes=[
+            pltpu.VMEM((bins, width, depth), own.dtype),
+            pltpu.VMEM((2, slots, bins, chunk_windows, lanes), jnp.bfloat16),
             pltpu.VMEM((2, bins * pitch, lanes), jnp.float32),
-            pltpu.VMEM((2, bins, chunk_windows, lanes), jnp.bfloat16),
             pltpu.VMEM((2, offsets * pitch, F), jnp.float32),
+            pltpu.SemaphoreType.DMA((COPY_BLOCKS, 3)),
             pltpu.SemaphoreType.DMA((width // CHANNEL_BLOCK, 2)),
         ],
-        compiler_params=pltpu.CompilerParams(vmem_limit_bytes=24 * MIB),
-        cost_estimate=pl.CostEstimate(
-            flops=16 * bins * width * width * windows,
-            bytes_accessed=30_000_000,
-            transcendentals=0,
-        ),
+        compiler_params=pltpu.CompilerParams(vmem_limit_bytes=32 * MIB),
+        cost_estimate=SMALL,
         name="stack",
-    )(jnp.stack([jnp.asarray(v, jnp.int32) for v in place]), reach, own, early, *last)
+    )(jnp.stack([jnp.asarray(v, jnp.int32) for v in place]), reach, own, store, *buffers)
 
 
 def send(array, pairs):
@@ -292,15 +376,21 @@
 
 
 def direct_partners(pieces, hops, n_win, n_chan):
-    groups = []
+    held = []
     for piece in pieces:
         first = send(piece, pairs_of(n_win, n_chan, lambda z, c: (c - hops[z]) % n_chan))
         second = send(piece, pairs_of(n_win, n_chan, lambda z, c: (c - hops[z] - 1) % n_chan))
-        groups.append((first, second))
-    return choose((0, 1), groups[:-1]), groups[-1], (0, 1)
-
-
-def square_partners(pieces, own, n_win, n_chan):
+        held.append((piece, first, second))
+    store = None
+    early = len(pieces) - 2
+    for slot in range(early):
+        store = bank(store, slot, early, (1, 2), held[slot])
+    buffers = [buffer for group in held[early:] for buffer in group]
+    groups = [[(3 * n, None), (3 * n + 1, None), (3 * n + 2, None)] for n in range(2)]
+    return own_rows(store, pieces[early:]), store, buffers, groups, (1, 2, 1, 2)
+
+
+def square_partners(pieces, n_win, n_chan):
     def pairs(target):
         return pairs_of(n_win, n_chan, lambda z, c: target(z, c, c % 2, c // 2 % 2))
 
@@ -328,31 +418,54 @@
     odd_next = jnp.where(x == 0, 1, 2)
     even_next = jnp.where(z == 0, odd_next, 2)
     next_code = jnp.where(core == 0, even_next, jnp.where(z == 3, 2, odd_next))
+    late_one = jnp.where((z == 3) & (core == 0), 4, 1)
     outgoing = jnp.where(
         core == 0, jnp.where(z < 2, next_code, 1), jnp.where(z < 2, 0, next_code)
     )
     first_code = jnp.where(z == 0, 0, jnp.where(z == 2, next_code, 3))
     second_code = jnp.where(z == 1, next_code, jnp.where(z == 3, 1, 3))
-
+    second_last = jnp.where(z == 1, next_code, jnp.where(z == 3, late_one, 3))
+
+    def swap(code, groups):
+        return send(choose(code, groups), pairs(lambda z, c, core, x: c ^ 1))
+
+    count = len(pieces)
+    early = count - 2
     held = []
+    store = None
     for slot, piece in enumerate(pieces):
-        start = after(piece, held[slot - 2][2]) if slot >= 2 else piece
-        moved = send(start, pairs(first_target))
-        if slot:
-            moved = after(moved, own if slot == len(pieces) - 1 else pieces[slot + 1])
-        relay = choose((onward,), [(piece, moved)])[0, 0]
-        if slot == len(pieces) - 1:
-            held[-1] = (*held[-1][:2], after(held[-1][2], relay))
+        last = slot == count - 1
+        if slot >= 2:
+            piece = after(piece, held[slot - 2][2])
+        moved = send(
+            piece,
+            pairs(
+                lambda z, c, core, x: (
+                    None if last and z == 3 and core == 0 else first_target(z, c, core, x)
+                )
+            ),
+        )
+        if slot >= 2:
+            group = held[slot - 2]
+            swapped = swap(outgoing, [group])[0]
+            store = bank(store, slot - 2, early, (first_code, second_code), (*group, swapped))
+        if last:
+            own = own_rows(store, pieces[early:])
+        arrived = after(moved, own if last else pieces[slot + 1]) if slot else moved
+        relay = choose(onward, [(piece, arrived)])[0]
         held.append((piece, moved, send(relay, pairs(second_target))))
-
-    def swap(groups):
-        return send(choose((outgoing,), groups)[0], pairs(lambda z, c, core, x: c ^ 1))
-
-    piece, moved, relayed = held[-1]
-    early = choose((first_code, second_code), held[:-1], swap(held[:-1]))
-    relayed = after(relayed, early)
-    swapped = swap([(piece, moved, relayed)])[0]
-    return early, (piece, moved, relayed, swapped), (first_code, second_code)
+    late = send(
+        after(pieces[-1], relay),
+        pairs(lambda z, c, core, x: c ^ 4 if z == 3 and core == 0 else None),
+    )
+    outgoing_late = jnp.where((outgoing == 1) & (late_one == 4), 3, outgoing)
+    swapped = swap(outgoing_late, [(*held[-2], held[-2][1]), (*held[-1], late)])
+    buffers = [*held[-2], *held[-1], swapped, late]
+    groups = [
+        [(0, None), (1, None), (2, None), (6, 0)],
+        [(3, None), (4, None), (5, None), (6, 1), (7, None)],
+    ]
+    return own, store, buffers, groups, (first_code, second_code, first_code, second_last)
 
 
 def on_device(traces, valid, reach):
@@ -365,13 +478,14 @@
     while len(pieces) < n_win:
         ring = [(z, (z + 1) % n_win) for z in range(n_win)]
         pieces.append(lax.ppermute(pieces[-1], "win", ring))
-    own = own_rows(pieces)
     if n_chan == 8 and hops == list(range(4)):
-        early, last, codes = square_partners(pieces, own, n_win, n_chan)
+        own, store, buffers, groups, codes = square_partners(pieces, n_win, n_chan)
     else:
-        early, last, codes = direct_partners(pieces, hops, n_win, n_chan)
+        own, store, buffers, groups, codes = direct_partners(pieces, hops, n_win, n_chan)
     place = (first_offset, first_offset % width, *codes)
-    return stacked(own, early, last, place, reach, offsets, traces.shape[0] * n_win)
+    return stacked(
+        own, store, buffers, groups, place, reach, offsets, traces.shape[0] * n_win
+    )
 
 
 def solution(mesh):

time: 99.3 us -> 118 us (1.19)
  the two profiles are of different devices: /device:TPU:9 before, /device:TPU:17 now
where the time goes in v4:
time: 118 us
  starting transfers between devices  45.8 us (39%)
  Pallas kernels  31.6 us (27%)
  local copies, waits for them, and re-layouts  23.9 us (20%)
  waiting for transfers between devices  15.8 us (13%)
    ppermute x12, starting transfers between devices, send(): return lax.ppermute(array, AXES, pairs)  36.6 us
    unnamed x22, local copies, waits for them, and re-layouts  23.8 us
    ppermute x3, waiting for transfers between devices, on_device(): pieces.append(lax.ppermute(pieces[-1], 'win', ring))  13.2 us
    pallas_call x1, Pallas kernels, stacked(): pl.pallas_call(functools.partial(stack_kernel, 1.0 / math.sqrt(windows),...  12.1 us
    ppermute x3, starting transfers between devices, on_device(): pieces.append(lax.ppermute(pieces[-1], 'win', ring))  9.18 us
    pallas_call x7, Pallas kernels, choose(): pl.pallas_call(functools.partial(choose_kernel, len(groups)), out_shape=j...  8.11 us
    pallas_call x1, Pallas kernels, own_rows(): pl.pallas_call(functools.partial(own_kernel, early), out_shape=jax.ShapeD...  4.79 us
    pallas_call x1, Pallas kernels, whitened_chunk(): pl.pallas_call(whiten_kernel, out_shape=jax.ShapeDtypeStruct((F, windows,...  4 us
  transfers between devices with their start and end apart: 15, of which 3 were waited for; matrix products, arithmetic and copies ran while one was open for 0% of the time, Pallas kernels for 11%

profile of v4, /device:TPU:17, one launch (start us, length us, event | category | flops | bytes accessed | tf_op | source)
XLA Modules:
  0.0 117.5 jit_solution(14038110580378711708)
XLA Ops:
  0.0 4.0 %whiten.1.refs_0_ = bf16[128,16,128]{2,1,0:T(8,128)(2,1)} custom-call(bf16[256,512]{1,0:T(8,128)(2,1)} %constant.56.table_hbm, bf16[16,64,512]{2,1,0:T(8,128)(2,1)} %traces_hbm.1, s32[16,64]{1,0:T(8,128)} %valid_hbm.1), custom_call_target="tpu_custom_call" | custom-call | flops 268435456 | bytes 1048576 | tf_op jit(solution)/shard_map/whiten/pallas_call | solution.py:80
  4.0 1.3 %collective-permute-start = (bf16[128,16,128]{2,1,0:T(8,128)(2,1)}, bf16[128,16,128]{2,1,0:T(8,128)(2,1)S(1)}, u32[]{:S(2)}, u32[]{:S(2)}) collective-permute-start(bf16[128,16,128]{2,1,0:T(8,128)(2,1)} %whiten.1.refs_0_), channel_id=1, source_target_pairs={{0,1},{1,2},{2,3},{3,0},{4,5},{5,6},{6,7},{7,4},{8,9},{9,10},{10,1... | collective-permute-start | bytes 1572872 | tf_op jit(solution)/shard_map/ppermute | solution.py:480
  5.4 3.1 %collective-permute-start.5 = (bf16[128,16,128]{2,1,0:T(8,128)(2,1)}, bf16[128,16,128]{2,1,0:T(8,128)(2,1)S(1)}, u32[]{:S(2)}, u32[]{:S(2)}) collective-permute-start(bf16[128,16,128]{2,1,0:T(8,128)(2,1)} %whiten.1.refs_0_), channel_id=1, source_target_pairs={{0,8},{8,0},{16,24},{24,16},{1,17},{5,13},{13,5},{17,1},{21,29},{2... | collective-permute-start | bytes 1572872 | tf_op jit(solution)/shard_map/ppermute | solution.py:361
  8.5 8.6 %collective-permute-done.refs_0_ = bf16[128,16,128]{2,1,0:T(8,128)(2,1)S(1)} collective-permute-done((bf16[128,16,128]{2,1,0:T(8,128)(2,1)}, bf16[128,16,128]{2,1,0:T(8,128)(2,1)S(1)}, u32[]{:S(2)}, u32[]{:S(2)}) %collective-permute-start) | collective-permute-done | bytes 524320 | tf_op jit(solution)/shard_map/ppermute | solution.py:480
  17.1 1.3 %collective-permute-start.2 = (bf16[128,16,128]{2,1,0:T(8,128)(2,1)S(1)}, bf16[128,16,128]{2,1,0:T(8,128)(2,1)S(1)}, u32[]{:S(2)}, u32[]{:S(2)}) collective-permute-start(bf16[128,16,128]{2,1,0:T(8,128)(2,1)S(1)} %collective-permute-done.refs_0_), channel_id=1, source_target_pairs={{0,1},{1,2},{2,3},{3,0},{4,5},{5,6},{6,7},{7,4},{8,9},{9,10},{10,1... | collective-permute-start | bytes 1572872 | tf_op jit(solution)/shard_map/ppermute | solution.py:480
  18.4 3.1 %collective-permute-start.1 = (bf16[128,16,128]{2,1,0:T(8,128)(2,1)S(1)}, bf16[128,16,128]{2,1,0:T(8,128)(2,1)S(1)}, u32[]{:S(2)}, u32[]{:S(2)}) collective-permute-start(bf16[128,16,128]{2,1,0:T(8,128)(2,1)S(1)} %collective-permute-done.refs_0_), channel_id=1, source_target_pairs={{0,8},{8,0},{16,24},{24,16},{1,17},{5,13},{13,5},{17,1},{21,29},{2... | collective-permute-start | bytes 1572872 | tf_op jit(solution)/shard_map/ppermute | solution.py:361
  21.6 1.2 %copy-done.2 = bf16[128,16,128]{2,1,0:T(8,128)(2,1)S(1)} copy-done((bf16[128,16,128]{2,1,0:T(8,128)(2,1)S(1)}, bf16[128,16,128]{2,1,0:T(8,128)(2,1)}, u32[]{:S(2)}) %copy-start.2) | copy-done | bytes 524312
  22.8 0.8 choose.9
  24.3 4.6 %collective-permute-done.2.refs_0_ = bf16[128,16,128]{2,1,0:T(8,128)(2,1)S(1)} collective-permute-done((bf16[128,16,128]{2,1,0:T(8,128)(2,1)S(1)}, bf16[128,16,128]{2,1,0:T(8,128)(2,1)S(1)}, u32[]{:S(2)}, u32[]{:S(2)}) %collective-permute-start.2) | collective-permute-done | bytes 524320 | tf_op jit(solution)/shard_map/ppermute | solution.py:480
  28.9 0.8 choose.7
  29.8 1.5 %collective-permute-start.3 = (bf16[128,16,128]{2,1,0:T(8,128)(2,1)}, bf16[128,16,128]{2,1,0:T(8,128)(2,1)}, u32[]{:S(2)}, u32[]{:S(2)}) collective-permute-start(bf16[128,16,128]{2,1,0:T(8,128)(2,1)} %bitcast.6), channel_id=1, source_target_pairs={{8,24},{24,8},{1,9},{9,1},{13,29},{17,25},{25,17},{29,13},{2,10},{... | collective-permute-start | bytes 1572872 | tf_op jit(solution)/shard_map/ppermute | solution.py:361
  31.2 6.5 %collective-permute-start.8 = (bf16[128,16,128]{2,1,0:T(8,128)(2,1)S(1)}, bf16[128,16,128]{2,1,0:T(8,128)(2,1)S(1)}, u32[]{:S(2)}, u32[]{:S(2)}) collective-permute-start(bf16[128,16,128]{2,1,0:T(8,128)(2,1)S(1)} %collective-permute-done.2.refs_0_), channel_id=1, source_target_pairs={{0,1},{1,2},{2,3},{3,0},{4,5},{5,6},{6,7},{7,4},{8,9},{9,10},{10,1... | collective-permute-start | bytes 1572872 | tf_op jit(solution)/shard_map/ppermute | solution.py:480
  38.6 2.6 %collective-permute-start.9 = (bf16[128,16,128]{2,1,0:T(8,128)(2,1)S(1)}, bf16[128,16,128]{2,1,0:T(8,128)(2,1)S(1)}, u32[]{:S(2)}, u32[]{:S(2)}) collective-permute-start(bf16[128,16,128]{2,1,0:T(8,128)(2,1)S(1)} %collective-permute-done.2.refs_0_), channel_id=1, source_target_pairs={{0,8},{8,0},{16,24},{24,16},{1,17},{5,13},{13,5},{17,1},{21,29},{2... | collective-permute-start | bytes 1572872 | tf_op jit(solution)/shard_map/ppermute | solution.py:361
  41.2 1.0 copy-done.3
  42.3 1.0 copy-done.8
  44.1 2.0 %collective-permute-start.7 = (bf16[1,128,16,128]{3,2,1,0:T(8,128)(2,1)}, bf16[1,128,16,128]{3,2,1,0:T(8,128)(2,1)}, u32[]{:S(2)}, u32[]{:S(2)}) collective-permute-start(bf16[1,128,16,128]{3,2,1,0:T(8,128)(2,1)} %choose.10), channel_id=1, source_target_pairs={{0,4},{4,0},{8,12},{12,8},{16,20},{20,16},{24,28},{28,24},{1,5},{5... | collective-permute-start | bytes 1572872 | tf_op jit(solution)/shard_map/ppermute | solution.py:361
  46.2 1.9 %choose.8 = bf16[1,128,16,128]{3,2,1,0:T(8,128)(2,1)} custom-call(s32[1]{0:T(128)} %bitcast.7.code_ref, bf16[128,16,128]{2,1,0:T(8,128)(2,1)S(1)} %collective-permute-done.refs_0_, bf16[128,16,128]{2,1,0:T(8,128)(2,1)S(1)} %collective-permute-done.1.refs_1_, bf16[128,16,128]{2,1,0:T(8,128)(2,1)} %collective-permute-done.3.refs_2_), custom_call_target="tpu_custom_call" | custom-call | flops 1 | bytes 1 | tf_op jit(solution)/shard_map/choose/pallas_call | solution.py:121
  48.1 3.1 %collective-permute-start.4 = (bf16[1,128,16,128]{3,2,1,0:T(8,128)(2,1)}, bf16[1,128,16,128]{3,2,1,0:T(8,128)(2,1)}, u32[]{:S(2)}, u32[]{:S(2)}) collective-permute-start(bf16[1,128,16,128]{3,2,1,0:T(8,128)(2,1)} %choose.8), channel_id=1, source_target_pairs={{0,4},{4,0},{8,12},{12,8},{16,20},{20,16},{24,28},{28,24},{1,5},{5... | collective-permute-start | bytes 1572872 | tf_op jit(solution)/shard_map/ppermute | solution.py:361
  51.2 4.1 %collective-permute-start.11 = (bf16[128,16,128]{2,1,0:T(8,128)(2,1)S(1)}, bf16[128,16,128]{2,1,0:T(8,128)(2,1)S(1)}, u32[]{:S(2)}, u32[]{:S(2)}) collective-permute-start(bf16[128,16,128]{2,1,0:T(8,128)(2,1)S(1)} %collective-permute-done.8.refs_1_.refs_0_.refs_4_.refs_3_), channel_id=1, source_target_pairs={{0,8},{8,0},{16,24},{24,16},{1,17},{5,13},{13,5},{17,1},{21,29},{2... | collective-permute-start | bytes 1572872 | tf_op jit(solution)/shard_map/ppermute | solution.py:361
  56.2 1.0 copy-done.4
  57.3 1.0 copy-done.6
  58.3 1.0 copy-done.9
  59.4 1.3 %bank.2.refs_4_ = bf16[24,2,128,16,128]{4,3,2,1,0:T(8,128)(2,1)S(1)} custom-call(s32[2]{0:T(128)S(1)} %pad_add_fusion.codes_ref, bf16[128,16,128]{2,1,0:T(8,128)(2,1)S(1)} %copy-done.4, bf16[128,16,128]{2,1,0:T(8,128)(2,1)S(1)} %copy-done.6, bf16[128,16,128]{2,1,0:T(8,128)(2,1)S(1)} %copy-done.9, bf16[128,16,128]{2,1,0:T(8,128)(2,1)} %bitcast.10.refs_3_), custom_call_target="tpu_custom_call" | custom-call | flops 1 | bytes 1 | tf_op jit(solution)/shard_map/bank/pallas_call | solution.py:167
  60.6 1.4 %bank.3.store_ref = bf16[24,2,128,16,128]{4,3,2,1,0:T(8,128)(2,1)S(1)} custom-call(s32[2]{0:T(128)S(1)} %pad_add_fusion.codes_ref, bf16[128,16,128]{2,1,0:T(8,128)(2,1)S(1)} %collective-permute-done.refs_0_, bf16[128,16,128]{2,1,0:T(8,128)(2,1)S(1)} %collective-permute-done.1.refs_1_, ...), custom_call_target="tpu_custom_call", output_to_operand_aliasing={{}: (5, {})} | custom-call | flops 1 | bytes 1 | tf_op jit(solution)/shard_map/bank/pallas_call | solution.py:167
  62.1 8.3 %copy-done = bf16[24,2,128,16,128]{4,3,2,1,0:T(8,128)(2,1)} copy-done((bf16[24,2,128,16,128]{4,3,2,1,0:T(8,128)(2,1)}, bf16[24,2,128,16,128]{4,3,2,1,0:T(8,128)(2,1)S(1)}, u32[]{:S(2)}) %copy-start) | copy-done | bytes 25165848
  71.2 4.8 %own_rows.1.own_hbm = bf16[12,128,64,128]{3,2,1,0:T(8,128)(2,1)S(1)} custom-call(bf16[24,2,128,16,128]{4,3,2,1,0:T(8,128)(2,1)} %copy-done, bf16[128,16,128]{2,1,0:T(8,128)(2,1)S(1)} %collective-permute-done.2.refs_0_, bf16[128,16,128]{2,1,0:T(8,128)(2,1)S(1)} %collective-permute-done.8.refs_1_.refs_0_.refs_4_.refs_3_), custom_call_target="tpu_custom_call" | custom-call | flops 1 | bytes 1 | tf_op jit(solution)/shard_map/own_rows/pallas_call | solution.py:208
  76.0 8.3 %copy-done.1 = bf16[12,128,64,128]{3,2,1,0:T(8,128)(2,1)} copy-done((bf16[12,128,64,128]{3,2,1,0:T(8,128)(2,1)}, bf16[12,128,64,128]{3,2,1,0:T(8,128)(2,1)S(1)}, u32[]{:S(2)}) %copy-start.1) | copy-done | bytes 25165848
  85.8 1.5 %collective-permute-start.12 = (bf16[128,16,128]{2,1,0:T(8,128)(2,1)}, bf16[128,16,128]{2,1,0:T(8,128)(2,1)}, u32[]{:S(2)}, u32[]{:S(2)}) collective-permute-start(bf16[128,16,128]{2,1,0:T(8,128)(2,1)} %bitcast.12), channel_id=1, source_target_pairs={{8,24},{24,8},{1,9},{9,1},{13,29},{17,25},{25,17},{29,13},{2,10},{... | collective-permute-start | bytes 1572872 | tf_op jit(solution)/shard_map/ppermute | solution.py:361
  87.3 2.1 %choose.13 = bf16[2,128,16,128]{3,2,1,0:T(8,128)(2,1)} custom-call(s32[1]{0:T(128)} %bitcast.13.code_ref, bf16[128,16,128]{2,1,0:T(8,128)(2,1)S(1)} %collective-permute-done.2.refs_0_, bf16[128,16,128]{2,1,0:T(8,128)(2,1)S(1)} %collective-permute-done.9.refs_1_.refs_3_, bf16[128,16,128]{2,1,0:T(8,128)(2,1)S(1)} %collective-permute-done.10.refs_2_, ...), custom_call_target="tpu_custom_call" | custom-call | flops 1 | bytes 1 | tf_op jit(solution)/shard_map/choose/pallas_call | solution.py:121
  89.4 13.4 %collective-permute-start.14 = (bf16[2,128,16,128]{3,2,1,0:T(8,128)(2,1)}, bf16[2,128,16,128]{3,2,1,0:T(8,128)(2,1)}, u32[]{:S(2)}, u32[]{:S(2)}) collective-permute-start(bf16[2,128,16,128]{3,2,1,0:T(8,128)(2,1)} %choose.13), channel_id=1, source_target_pairs={{0,4},{4,0},{8,12},{12,8},{16,20},{20,16},{24,28},{28,24},{1,5},{5... | collective-permute-start | bytes 3145736 | tf_op jit(solution)/shard_map/ppermute | solution.py:361
  102.9 2.5 %collective-permute-done.14.refs_6_ = bf16[2,128,16,128]{3,2,1,0:T(8,128)(2,1)} collective-permute-done((bf16[2,128,16,128]{3,2,1,0:T(8,128)(2,1)}, bf16[2,128,16,128]{3,2,1,0:T(8,128)(2,1)}, u32[]{:S(2)}, u32[]{:S(2)}) %collective-permute-start.14) | collective-permute-done | bytes 1048608 | tf_op jit(solution)/shard_map/ppermute | solution.py:361
  105.4 12.1 %stack.35 = f32[64,64,256]{2,1,0:T(8,128)} custom-call(s32[6]{0:T(128)S(1)} %stack.33.place_ref, s32[64]{0:T(128)S(1)} %copy-done.10, bf16[12,128,64,128]{3,2,1,0:T(8,128)(2,1)} %copy-done.1, bf16[24,2,128,16,128]{4,3,2,1,0:T(8,128)(2,1)} %copy-done, bf16[128,16,128]{2,1,0:T(8,128)(2,1)S(1)} %collective-permute-done.2.refs_0_, ...), custom_call_target="tpu_custom_call" | custom-call | flops 1 | bytes 1 | tf_op jit(solution)/shard_map/stack/pallas_call | solution.py:341
  (34 shorter events, 5.7 us)
Async XLA Ops:
  4.0 13.1 %collective-permute-start = (bf16[128,16,128]{2,1,0:T(8,128)(2,1)}, bf16[128,16,128]{2,1,0:T(8,128)(2,1)S(1)}, u32[]{:S(2)}, u32[]{:S(2)}) collective-permute-start(bf16[128,16,128]{2,1,0:T(8,128)(2,1)} %whiten.1.refs_0_), channel_id=1, source_target_pairs={{0,1},{1,2},{2,3},{3,0},{4,5},{5,6},{6,7},{7,4},{8,9},{9,10},{10,1... | collective-permute-start | bytes 1572872 | tf_op jit(solution)/shard_map/ppermute | solution.py:480
  5.4 16.2 %collective-permute-start.5 = (bf16[128,16,128]{2,1,0:T(8,128)(2,1)}, bf16[128,16,128]{2,1,0:T(8,128)(2,1)S(1)}, u32[]{:S(2)}, u32[]{:S(2)}) collective-permute-start(bf16[128,16,128]{2,1,0:T(8,128)(2,1)} %whiten.1.refs_0_), channel_id=1, source_target_pairs={{0,8},{8,0},{16,24},{24,16},{1,17},{5,13},{13,5},{17,1},{21,29},{2... | collective-permute-start | bytes 1572872 | tf_op jit(solution)/shard_map/ppermute | solution.py:361
  17.1 11.9 %collective-permute-start.2 = (bf16[128,16,128]{2,1,0:T(8,128)(2,1)S(1)}, bf16[128,16,128]{2,1,0:T(8,128)(2,1)S(1)}, u32[]{:S(2)}, u32[]{:S(2)}) collective-permute-start(bf16[128,16,128]{2,1,0:T(8,128)(2,1)S(1)} %collective-permute-done.refs_0_), channel_id=1, source_target_pairs={{0,1},{1,2},{2,3},{3,0},{4,5},{5,6},{6,7},{7,4},{8,9},{9,10},{10,1... | collective-permute-start | bytes 1572872 | tf_op jit(solution)/shard_map/ppermute | solution.py:480
  18.4 10.6 %collective-permute-start.1 = (bf16[128,16,128]{2,1,0:T(8,128)(2,1)S(1)}, bf16[128,16,128]{2,1,0:T(8,128)(2,1)S(1)}, u32[]{:S(2)}, u32[]{:S(2)}) collective-permute-start(bf16[128,16,128]{2,1,0:T(8,128)(2,1)S(1)} %collective-permute-done.refs_0_), channel_id=1, source_target_pairs={{0,8},{8,0},{16,24},{24,16},{1,17},{5,13},{13,5},{17,1},{21,29},{2... | collective-permute-start | bytes 1572872 | tf_op jit(solution)/shard_map/ppermute | solution.py:361
  21.5 29.7 %copy-start.5 = (bf16[128,16,128]{2,1,0:T(8,128)(2,1)}, bf16[128,16,128]{2,1,0:T(8,128)(2,1)S(1)}, u32[]{:S(2)}) copy-start(bf16[128,16,128]{2,1,0:T(8,128)(2,1)S(1)} %collective-permute-done.5.refs_1_) | copy-start | bytes 1572868
  21.5 1.2 %copy-start.2 = (bf16[128,16,128]{2,1,0:T(8,128)(2,1)S(1)}, bf16[128,16,128]{2,1,0:T(8,128)(2,1)}, u32[]{:S(2)}) copy-start(bf16[128,16,128]{2,1,0:T(8,128)(2,1)} %whiten.1.refs_0_) | copy-start | bytes 1572868
  23.6 14.2 %collective-permute-start.6 = (bf16[128,16,128]{2,1,0:T(8,128)(2,1)}, bf16[128,16,128]{2,1,0:T(8,128)(2,1)S(1)}, u32[]{:S(2)}, u32[]{:S(2)}) collective-permute-start(bf16[128,16,128]{2,1,0:T(8,128)(2,1)} %bitcast.9), channel_id=1, source_target_pairs={{8,24},{24,8},{1,9},{9,1},{13,29},{17,25},{25,17},{29,13},{2,10},{... | collective-permute-start | bytes 1572872 | tf_op jit(solution)/shard_map/ppermute | solution.py:361
  29.8 16.4 %collective-permute-start.3 = (bf16[128,16,128]{2,1,0:T(8,128)(2,1)}, bf16[128,16,128]{2,1,0:T(8,128)(2,1)}, u32[]{:S(2)}, u32[]{:S(2)}) collective-permute-start(bf16[128,16,128]{2,1,0:T(8,128)(2,1)} %bitcast.6), channel_id=1, source_target_pairs={{8,24},{24,8},{1,9},{9,1},{13,29},{17,25},{25,17},{29,13},{2,10},{... | collective-permute-start | bytes 1572872 | tf_op jit(solution)/shard_map/ppermute | solution.py:361
  31.2 20.0 %collective-permute-start.8 = (bf16[128,16,128]{2,1,0:T(8,128)(2,1)S(1)}, bf16[128,16,128]{2,1,0:T(8,128)(2,1)S(1)}, u32[]{:S(2)}, u32[]{:S(2)}) collective-permute-start(bf16[128,16,128]{2,1,0:T(8,128)(2,1)S(1)} %collective-permute-done.2.refs_0_), channel_id=1, source_target_pairs={{0,1},{1,2},{2,3},{3,0},{4,5},{5,6},{6,7},{7,4},{8,9},{9,10},{10,1... | collective-permute-start | bytes 1572872 | tf_op jit(solution)/shard_map/ppermute | solution.py:480
  37.8 0.8 copy-start.7
  38.6 16.8 %collective-permute-start.9 = (bf16[128,16,128]{2,1,0:T(8,128)(2,1)S(1)}, bf16[128,16,128]{2,1,0:T(8,128)(2,1)S(1)}, u32[]{:S(2)}, u32[]{:S(2)}) collective-permute-start(bf16[128,16,128]{2,1,0:T(8,128)(2,1)S(1)} %collective-permute-done.2.refs_0_), channel_id=1, source_target_pairs={{0,8},{8,0},{16,24},{24,16},{1,17},{5,13},{13,5},{17,1},{21,29},{2... | collective-permute-start | bytes 1572872 | tf_op jit(solution)/shard_map/ppermute | solution.py:361
  41.2 1.0 copy-start.3
  42.3 1.0 copy-start.8
  44.1 12.1 %collective-permute-start.7 = (bf16[1,128,16,128]{3,2,1,0:T(8,128)(2,1)}, bf16[1,128,16,128]{3,2,1,0:T(8,128)(2,1)}, u32[]{:S(2)}, u32[]{:S(2)}) collective-permute-start(bf16[1,128,16,128]{3,2,1,0:T(8,128)(2,1)} %choose.10), channel_id=1, source_target_pairs={{0,4},{4,0},{8,12},{12,8},{16,20},{20,16},{24,28},{28,24},{1,5},{5... | collective-permute-start | bytes 1572872 | tf_op jit(solution)/shard_map/ppermute | solution.py:361
  48.1 12.6 %collective-permute-start.4 = (bf16[1,128,16,128]{3,2,1,0:T(8,128)(2,1)}, bf16[1,128,16,128]{3,2,1,0:T(8,128)(2,1)}, u32[]{:S(2)}, u32[]{:S(2)}) collective-permute-start(bf16[1,128,16,128]{3,2,1,0:T(8,128)(2,1)} %choose.8), channel_id=1, source_target_pairs={{0,4},{4,0},{8,12},{12,8},{16,20},{20,16},{24,28},{28,24},{1,5},{5... | collective-permute-start | bytes 1572872 | tf_op jit(solution)/shard_map/ppermute | solution.py:361
  51.2 33.1 %collective-permute-start.11 = (bf16[128,16,128]{2,1,0:T(8,128)(2,1)S(1)}, bf16[128,16,128]{2,1,0:T(8,128)(2,1)S(1)}, u32[]{:S(2)}, u32[]{:S(2)}) collective-permute-start(bf16[128,16,128]{2,1,0:T(8,128)(2,1)S(1)} %collective-permute-done.8.refs_1_.refs_0_.refs_4_.refs_3_), channel_id=1, source_target_pairs={{0,8},{8,0},{16,24},{24,16},{1,17},{5,13},{13,5},{17,1},{21,29},{2... | collective-permute-start | bytes 1572872 | tf_op jit(solution)/shard_map/ppermute | solution.py:361
  56.2 1.0 copy-start.4
  57.3 1.0 copy-start.6
  58.3 1.0 copy-start.9
  62.0 8.3 %copy-start = (bf16[24,2,128,16,128]{4,3,2,1,0:T(8,128)(2,1)}, bf16[24,2,128,16,128]{4,3,2,1,0:T(8,128)(2,1)S(1)}, u32[]{:S(2)}) copy-start(bf16[24,2,128,16,128]{4,3,2,1,0:T(8,128)(2,1)S(1)} %bank.3.store_ref) | copy-start | bytes 75497472
  70.4 35.1 %copy-start.10 = (s32[64]{0:T(128)S(1)}, s32[64]{0:T(128)}, u32[]{:S(2)}) copy-start(s32[64]{0:T(128)} %reach_ref.1) | copy-start | bytes 772
  70.4 16.9 %collective-permute-start.10 = (bf16[128,16,128]{2,1,0:T(8,128)(2,1)}, bf16[128,16,128]{2,1,0:T(8,128)(2,1)S(1)}, u32[]{:S(2)}, u32[]{:S(2)}) collective-permute-start(bf16[128,16,128]{2,1,0:T(8,128)(2,1)} %bitcast.11), channel_id=1, source_target_pairs={{8,24},{24,8},{1,9},{9,1},{13,29},{17,25},{25,17},{29,13},{2,10},{... | collective-permute-start | bytes 1572872 | tf_op jit(solution)/shard_map/ppermute | solution.py:361
  76.0 8.3 %copy-start.1 = (bf16[12,128,64,128]{3,2,1,0:T(8,128)(2,1)}, bf16[12,128,64,128]{3,2,1,0:T(8,128)(2,1)S(1)}, u32[]{:S(2)}) copy-start(bf16[12,128,64,128]{3,2,1,0:T(8,128)(2,1)S(1)} %own_rows.1.own_hbm) | copy-start | bytes 75497472
  85.1 2.2 %collective-permute-start.13 = (bf16[128,16,128]{2,1,0:T(8,128)(2,1)S(1)}, bf16[128,16,128]{2,1,0:T(8,128)(2,1)S(1)}, u32[]{:S(2)}, u32[]{:S(2)}) collective-permute-start(bf16[128,16,128]{2,1,0:T(8,128)(2,1)S(1)} %collective-permute-done.8.refs_1_.refs_0_.refs_4_.refs_3_), channel_id=1, source_target_pairs={{3,19},{11,27},{19,3},{27,11}} | collective-permute-start | bytes 1572872 | tf_op jit(solution)/shard_map/ppermute | solution.py:361
  85.8 1.5 %collective-permute-start.12 = (bf16[128,16,128]{2,1,0:T(8,128)(2,1)}, bf16[128,16,128]{2,1,0:T(8,128)(2,1)}, u32[]{:S(2)}, u32[]{:S(2)}) collective-permute-start(bf16[128,16,128]{2,1,0:T(8,128)(2,1)} %bitcast.12), channel_id=1, source_target_pairs={{8,24},{24,8},{1,9},{9,1},{13,29},{17,25},{25,17},{29,13},{2,10},{... | collective-permute-start | bytes 1572872 | tf_op jit(solution)/shard_map/ppermute | solution.py:361
  89.4 16.0 %collective-permute-start.14 = (bf16[2,128,16,128]{3,2,1,0:T(8,128)(2,1)}, bf16[2,128,16,128]{3,2,1,0:T(8,128)(2,1)}, u32[]{:S(2)}, u32[]{:S(2)}) collective-permute-start(bf16[2,128,16,128]{3,2,1,0:T(8,128)(2,1)} %choose.13), channel_id=1, source_target_pairs={{0,4},{4,0},{8,12},{12,8},{16,20},{20,16},{24,28},{28,24},{1,5},{5... | collective-permute-start | bytes 3145736 | tf_op jit(solution)/shard_map/ppermute | solution.py:361

commit v5 on v3

--- a/solution.py
+++ b/solution.py
@@ -18,6 +18,8 @@
 PITCH_PAD = 8
 MIB = 1024 * 1024
 VMEM = pl.BlockSpec(memory_space=pltpu.VMEM)
+FEW_MIB = pltpu.CompilerParams(vmem_limit_bytes=4 * MIB)
+WHOLE_VMEM = pltpu.CompilerParams(vmem_limit_bytes=62 * MIB)
 SMEM = pl.BlockSpec(memory_space=pltpu.SMEM)
 SMALL = pl.CostEstimate(flops=1, bytes_accessed=1, transcendentals=0)
 ANY = pl.BlockSpec(memory_space=pl.ANY)
@@ -85,7 +87,7 @@
             pltpu.VMEM((F * windows, 2 * width), jnp.float32),
             pltpu.SemaphoreType.DMA((2 + WHITEN_BLOCKS,)),
         ],
-        compiler_params=pltpu.CompilerParams(vmem_limit_bytes=62 * MIB),
+        compiler_params=WHOLE_VMEM,
         cost_estimate=pl.CostEstimate(
             flops=4 * F * traces.size, bytes_accessed=2 * traces.size, transcendentals=0
         ),
@@ -101,33 +103,29 @@
             put(ref)
 
 
-def choose_kernel(groups, per_group, codes_ref, *refs):
+def choose_kernel(code_of, groups, *refs):
     out_ref = refs[-1]
-    shared = refs[groups * per_group : -1]
-    for which in range(out_ref.shape[0]):
-        for g in range(groups):
-
-            def put(ref, which=which, g=g):
-                out_ref[which, g] = ref[...]
-
-            candidates = list(refs[g * per_group : (g + 1) * per_group])
-            candidates += [ref.at[g] for ref in shared]
-            copy_chosen(codes_ref[which], candidates, put)
-
-
-def choose(codes, groups, *shared):
-    operands = [buffer for group in groups for buffer in group] + list(shared)
+    per_group = (len(refs) - 1) // groups
+    code = code_of()
+    for g in range(groups):
+
+        def put(ref, g=g):
+            out_ref[g] = ref[...]
+
+        copy_chosen(code, refs[g * per_group : (g + 1) * per_group], put)
+
+
+def choose(code_of, groups):
+    operands = [buffer for group in groups for buffer in group]
     return pl.pallas_call(
-        functools.partial(choose_kernel, len(groups), len(groups[0])),
-        out_shape=jax.ShapeDtypeStruct(
-            (len(codes), len(groups), *groups[0][0].shape), jnp.bfloat16
-        ),
-        in_specs=[SMEM] + [VMEM] * len(operands),
+        functools.partial(choose_kernel, code_of, len(groups)),
+        out_shape=jax.ShapeDtypeStruct((len(groups), *groups[0][0].shape), jnp.bfloat16),
+        in_specs=[VMEM] * len(operands),
         out_specs=VMEM,
-        compiler_params=pltpu.CompilerParams(vmem_limit_bytes=4 * MIB),
+        compiler_params=FEW_MIB,
         cost_estimate=SMALL,
         name="choose",
-    )(jnp.stack([jnp.asarray(code, jnp.int32) for code in codes]), *operands)
+    )(*operands)
 
 
 def own_kernel(*refs):
@@ -151,39 +149,43 @@
         ),
         in_specs=[VMEM] * len(pieces),
         out_specs=VMEM,
-        compiler_params=pltpu.CompilerParams(vmem_limit_bytes=4 * MIB),
+        compiler_params=FEW_MIB,
         cost_estimate=SMALL,
         name="own_rows",
     )(*pieces)
 
 
-def stack_kernel(scale, place_ref, reach_ref, own_ref, early_ref, *refs):
-    last_refs, (out_hbm, products, last, out, sems) = refs[:-5], refs[-5:]
-    bins, width, _ = own_ref.shape
+def stack_kernel(scale, groups, codes_of, reach_ref, own, *refs):
+    buffers, (out_hbm, partners, products, out, sems) = refs[:-5], refs[-5:]
+    bins, width, _ = own.shape
     lanes = 2 * width
     offsets = out_hbm.shape[0]
     pitch = products.shape[1] // bins
-    for which in range(2):
-
-        def put(ref, which=which):
-            last[which] = ref[...]
-
-        copy_chosen(place_ref[2 + which], last_refs, put)
+    slots = len(groups)
+    first_offset = lax.axis_index("win") * offsets
+    codes = codes_of()
+    for slot, group in enumerate(groups):
+        for which in range(2):
+            candidates = [
+                buffers[number] if index is None else buffers[number].at[index]
+                for number, index in group
+            ]
+
+            def put(ref, slot=slot, which=which):
+                partners[which, slot] = ref[...]
+
+            copy_chosen(codes[which if slot < slots - 1 else 2 + which], candidates, put)
 
     def one_bin(f, carry):
         tops = [
-            jnp.concatenate(
-                [early_ref[which, slot, f] for slot in range(early_ref.shape[1])]
-                + [last[which, f]],
-                axis=0,
-            )
+            jnp.concatenate([partners[which, slot, f] for slot in range(slots)], axis=0)
             for which in range(2)
         ]
         bottoms = [jnp.concatenate([b[:, width:], -b[:, :width]], axis=1) for b in tops]
         right = jnp.concatenate(
             [jnp.concatenate(tops, axis=1), jnp.concatenate(bottoms, axis=1)], axis=0
         )
-        both = jnp.dot(own_ref[f], right, preferred_element_type=jnp.float32)
+        both = jnp.dot(own[f], right, preferred_element_type=jnp.float32)
         row = pl.multiple_of(f * pitch, 8)
         for half in range(2):
             products[half, pl.ds(row, width), :] = both[:, half * lanes : (half + 1) * lanes]
@@ -198,7 +200,7 @@
     far = 4 * lanes
     shift_re = jnp.where(is_real, partner - k, far)
     shift_im = jnp.where(is_real, far, partner - k)
-    row_k = lax.broadcasted_iota(jnp.int32, (offsets, F), 0) + place_ref[0]
+    row_k = lax.broadcasted_iota(jnp.int32, (offsets, F), 0) + first_offset
 
     def copies(block):
         columns = pl.ds(pl.multiple_of(block * CHANNEL_BLOCK, CHANNEL_BLOCK), CHANNEL_BLOCK)
@@ -214,7 +216,7 @@
     def one_block(block, carry):
         for il in range(CHANNEL_BLOCK):
             i = block * CHANNEL_BLOCK + il
-            at = i + place_ref[1]
+            at = i + first_offset % width
             pick = jnp.concatenate(
                 [
                     jnp.where(shift_re == at, 1.0, 0.0),
@@ -248,29 +250,25 @@
     lax.fori_loop(0, blocks, finish, 0)
 
 
-def stacked(own, early, last, place, reach, offsets, windows):
+def stacked(own, buffers, groups, codes_of, reach, offsets, windows):
     bins, width, _ = own.shape
-    chunk_windows, lanes = last[0].shape[1:]
+    chunk_windows, lanes = buffers[0].shape[-2:]
     pitch = width + PITCH_PAD
     return pl.pallas_call(
-        functools.partial(stack_kernel, 1.0 / math.sqrt(windows)),
+        functools.partial(stack_kernel, 1.0 / math.sqrt(windows), groups, codes_of),
         out_shape=jax.ShapeDtypeStruct((offsets, width, 2 * F), jnp.float32),
-        in_specs=[SMEM, SMEM] + [VMEM] * (2 + len(last)),
+        in_specs=[SMEM] + [VMEM] * (1 + len(buffers)),
         out_specs=ANY,
         scratch_shapes=[
+            pltpu.VMEM((2, len(groups), bins, chunk_windows, lanes), jnp.bfloat16),
             pltpu.VMEM((2, bins * pitch, lanes), jnp.float32),
-            pltpu.VMEM((2, bins, chunk_windows, lanes), jnp.bfloat16),
             pltpu.VMEM((2, offsets * pitch, F), jnp.float32),
             pltpu.SemaphoreType.DMA((width // CHANNEL_BLOCK, 2)),
         ],
-        compiler_params=pltpu.CompilerParams(vmem_limit_bytes=24 * MIB),
-        cost_estimate=pl.CostEstimate(
-            flops=16 * bins * width * width * windows,
-            bytes_accessed=30_000_000,
-            transcendentals=0,
-        ),
+        compiler_params=pltpu.CompilerParams(vmem_limit_bytes=28 * MIB),
+        cost_estimate=SMALL,
         name="stack",
-    )(jnp.stack([jnp.asarray(v, jnp.int32) for v in place]), reach, own, early, *last)
+    )(reach, own, *buffers)
 
 
 def send(array, pairs):
@@ -292,15 +290,33 @@
 
 
 def direct_partners(pieces, hops, n_win, n_chan):
-    groups = []
+    buffers = []
     for piece in pieces:
-        first = send(piece, pairs_of(n_win, n_chan, lambda z, c: (c - hops[z]) % n_chan))
-        second = send(piece, pairs_of(n_win, n_chan, lambda z, c: (c - hops[z] - 1) % n_chan))
-        groups.append((first, second))
-    return choose((0, 1), groups[:-1]), groups[-1], (0, 1)
-
-
-def square_partners(pieces, own, n_win, n_chan):
+        buffers.append(send(piece, pairs_of(n_win, n_chan, lambda z, c: (c - hops[z]) % n_chan)))
+        buffers.append(
+            send(piece, pairs_of(n_win, n_chan, lambda z, c: (c - hops[z] - 1) % n_chan))
+        )
+    groups = [[(2 * n, None), (2 * n + 1, None)] for n in range(len(pieces))]
+    return own_rows(pieces), buffers, groups, lambda: (0, 1, 0, 1)
+
+
+def square_codes():
+    z, c = lax.axis_index("win"), lax.axis_index("chan")
+    core, x = c & 1, (c >> 1) & 1
+    onward = jnp.where((z == 0) | (x == 0) | ((z < 3) & (core == 1)), 1, 0)
+    odd_next = jnp.where(x == 0, 1, 2)
+    even_next = jnp.where(z == 0, odd_next, 2)
+    next_code = jnp.where(core == 0, even_next, jnp.where(z == 3, 2, odd_next))
+    outgoing = jnp.where(core == 0, jnp.where(z < 2, next_code, 1), jnp.where(z < 2, 0, next_code))
+    first = jnp.where(z == 0, 0, jnp.where(z == 2, next_code, 3))
+    second = jnp.where(z == 1, next_code, jnp.where(z == 3, 1, 3))
+    is_late = (z == 3) & (core == 0)
+    outgoing_late = jnp.where(is_late, 3, outgoing)
+    second_last = jnp.where(is_late, 4, second)
+    return onward, outgoing, outgoing_late, (first, second, first, second_last)
+
+
+def square_partners(pieces, n_win, n_chan):
     def pairs(target):
         return pairs_of(n_win, n_chan, lambda z, c: target(z, c, c % 2, c // 2 % 2))
 
@@ -322,37 +338,47 @@
             return c ^ 2
         return c ^ 4 if x == 1 else None
 
-    z, c = lax.axis_index("win"), lax.axis_index("chan")
-    core, x = c % 2, c // 2 % 2
-    onward = jnp.where((z == 0) | (x == 0) | ((z < 3) & (core == 1)), 1, 0)
-    odd_next = jnp.where(x == 0, 1, 2)
-    even_next = jnp.where(z == 0, odd_next, 2)
-    next_code = jnp.where(core == 0, even_next, jnp.where(z == 3, 2, odd_next))
-    outgoing = jnp.where(
-        core == 0, jnp.where(z < 2, next_code, 1), jnp.where(z < 2, 0, next_code)
-    )
-    first_code = jnp.where(z == 0, 0, jnp.where(z == 2, next_code, 3))
-    second_code = jnp.where(z == 1, next_code, jnp.where(z == 3, 1, 3))
-
+    def swap(code_of, groups):
+        return send(choose(code_of, groups), pairs(lambda z, c, core, x: c ^ 1))
+
+    count = len(pieces)
+    half = count // 2
     held = []
     for slot, piece in enumerate(pieces):
-        start = after(piece, held[slot - 2][2]) if slot >= 2 else piece
-        moved = send(start, pairs(first_target))
+        last = slot == count - 1
         if slot:
-            moved = after(moved, own if slot == len(pieces) - 1 else pieces[slot + 1])
-        relay = choose((onward,), [(piece, moved)])[0, 0]
-        if slot == len(pieces) - 1:
-            held[-1] = (*held[-1][:2], after(held[-1][2], relay))
+            piece = after(piece, held[slot - 1][1], *([held[slot - 2][2]] if slot >= 2 else []))
+        moved = send(
+            piece,
+            pairs(
+                lambda z, c, core, x: (
+                    None if last and z == 3 and core == 0 else first_target(z, c, core, x)
+                )
+            ),
+        )
+        arrived = moved
+        if last:
+            held[0] = (*held[0][:2], after(held[0][2], piece))
+            swapped_early = swap(lambda: square_codes()[1], held[:half])
+            own = own_rows([*pieces[:-1], after(piece, swapped_early)])
+            arrived = after(moved, own)
+        elif True:
+            arrived = after(moved, pieces[slot + 1])
+        relay = choose(lambda: square_codes()[0], [(piece, arrived)])[0]
         held.append((piece, moved, send(relay, pairs(second_target))))
-
-    def swap(groups):
-        return send(choose((outgoing,), groups)[0], pairs(lambda z, c, core, x: c ^ 1))
-
-    piece, moved, relayed = held[-1]
-    early = choose((first_code, second_code), held[:-1], swap(held[:-1]))
-    relayed = after(relayed, early)
-    swapped = swap([(piece, moved, relayed)])[0]
-    return early, (piece, moved, relayed, swapped), (first_code, second_code)
+    late = send(
+        after(pieces[-1], relay),
+        pairs(lambda z, c, core, x: c ^ 4 if z == 3 and core == 0 else None),
+    )
+    late_groups = [(*group, group[1]) for group in held[half:-1]] + [(*held[-1], late)]
+    swapped_late = swap(lambda: square_codes()[2], late_groups)
+    buffers = [buffer for group in held for buffer in group] + [swapped_early, swapped_late, late]
+    groups = []
+    for n in range(count):
+        swapped = (3 * count, n) if n < half else (3 * count + 1, n - half)
+        groups.append([(3 * n, None), (3 * n + 1, None), (3 * n + 2, None), swapped])
+    groups[-1].append((3 * count + 2, None))
+    return own, buffers, groups, lambda: square_codes()[3]
 
 
 def on_device(traces, valid, reach):
@@ -360,18 +386,15 @@
     n_win, n_chan = lax.axis_size("win"), lax.axis_size("chan")
     offsets = BAND // n_win
     hops = [z * offsets // width for z in range(n_win)]
-    first_offset = lax.axis_index("win") * offsets
     pieces = [whitened_chunk(traces, valid)]
     while len(pieces) < n_win:
         ring = [(z, (z + 1) % n_win) for z in range(n_win)]
         pieces.append(lax.ppermute(pieces[-1], "win", ring))
-    own = own_rows(pieces)
     if n_chan == 8 and hops == list(range(4)):
-        early, last, codes = square_partners(pieces, own, n_win, n_chan)
+        own, buffers, groups, codes_of = square_partners(pieces, n_win, n_chan)
     else:
-        early, last, codes = direct_partners(pieces, hops, n_win, n_chan)
-    place = (first_offset, first_offset % width, *codes)
-    return stacked(own, early, last, place, reach, offsets, traces.shape[0] * n_win)
+        own, buffers, groups, codes_of = direct_partners(pieces, hops, n_win, n_chan)
+    return stacked(own, buffers, groups, codes_of, reach, offsets, traces.shape[0] * n_win)
 
 
 def solution(mesh):

time: 99.3 us -> 96.5 us (0.972)
  the two profiles are of different devices: /device:TPU:9 before, /device:TPU:19 now
where the time goes in v5:
time: 96.5 us; the launch traced here: 96.1 us
  waiting for transfers between devices  46.3 us (48%)
  starting transfers between devices  29.5 us (31%)
  Pallas kernels  18 us (19%)
  local copies, waits for them, and re-layouts  2.1 us (2%)
    ppermute x11, waiting for transfers between devices, send(): return lax.ppermute(array, AXES, pairs)  37.7 us
    ppermute x11, starting transfers between devices, send(): return lax.ppermute(array, AXES, pairs)  25.7 us
    pallas_call x1, Pallas kernels, stacked(): pl.pallas_call(functools.partial(stack_kernel, 1.0 / math.sqrt(windows),...  10.3 us
    ppermute x3, waiting for transfers between devices, on_device(): pieces.append(lax.ppermute(pieces[-1], 'win', ring))  8.6 us
    pallas_call x1, Pallas kernels, whitened_chunk(): pl.pallas_call(whiten_kernel, out_shape=jax.ShapeDtypeStruct((F, windows,...  4 us
    ppermute x3, starting transfers between devices, on_device(): pieces.append(lax.ppermute(pieces[-1], 'win', ring))  3.79 us
    pallas_call x1, Pallas kernels, own_rows(): pl.pallas_call(own_kernel, out_shape=jax.ShapeDtypeStruct((bins, lanes //...  3.41 us
    unnamed x8, local copies, waits for them, and re-layouts  2.1 us
  transfers between devices with their start and end apart: 14, of which 11 were waited for; matrix products, arithmetic and copies ran while one was open for 0% of the time, Pallas kernels for 4%

profile of v5, /device:TPU:19, one launch (start us, length us, event | category | flops | bytes accessed | tf_op | source)
XLA Modules:
  0.0 96.1 jit_solution(5008381524475870850)
XLA Ops:
  0.0 4.0 %whiten.1.refs_0_ = bf16[128,16,128]{2,1,0:T(8,128)(2,1)} custom-call(bf16[256,512]{1,0:T(8,128)(2,1)} %constant.3.table_hbm, bf16[16,64,512]{2,1,0:T(8,128)(2,1)} %traces_hbm.1, s32[16,64]{1,0:T(8,128)} %valid_hbm.1), custom_call_target="tpu_custom_call" | custom-call | flops 268435456 | bytes 1048576 | tf_op jit(solution)/shard_map/whiten/pallas_call | solution.py:78
  4.0 2.2 %collective-permute-start.3 = (bf16[128,16,128]{2,1,0:T(8,128)(2,1)}, bf16[128,16,128]{2,1,0:T(8,128)(2,1)S(1)}, u32[]{:S(2)}, u32[]{:S(2)}) collective-permute-start(bf16[128,16,128]{2,1,0:T(8,128)(2,1)} %whiten.1.refs_0_), channel_id=1, source_target_pairs={{0,8},{8,0},{16,24},{24,16},{1,17},{5,13},{13,5},{17,1},{21,29},{2... | collective-permute-start | bytes 1572872 | tf_op jit(solution)/shard_map/ppermute | solution.py:275
  6.2 2.3 %collective-permute-start = (bf16[128,16,128]{2,1,0:T(8,128)(2,1)}, bf16[128,16,128]{2,1,0:T(8,128)(2,1)S(1)}, u32[]{:S(2)}, u32[]{:S(2)}) collective-permute-start(bf16[128,16,128]{2,1,0:T(8,128)(2,1)} %whiten.1.refs_0_), channel_id=1, source_target_pairs={{0,1},{1,2},{2,3},{3,0},{4,5},{5,6},{6,7},{7,4},{8,9},{9,10},{10,1... | collective-permute-start | bytes 1572872 | tf_op jit(solution)/shard_map/ppermute | solution.py:392
  8.5 5.9 %collective-permute-done.3.refs_1_ = bf16[128,16,128]{2,1,0:T(8,128)(2,1)S(1)} collective-permute-done((bf16[128,16,128]{2,1,0:T(8,128)(2,1)}, bf16[128,16,128]{2,1,0:T(8,128)(2,1)S(1)}, u32[]{:S(2)}, u32[]{:S(2)}) %collective-permute-start.3) | collective-permute-done | bytes 524320 | tf_op jit(solution)/shard_map/ppermute | solution.py:275
  14.4 4.7 %collective-permute-done.refs_0_.refs_3_.refs_1_ = bf16[128,16,128]{2,1,0:T(8,128)(2,1)S(1)} collective-permute-done((bf16[128,16,128]{2,1,0:T(8,128)(2,1)}, bf16[128,16,128]{2,1,0:T(8,128)(2,1)S(1)}, u32[]{:S(2)}, u32[]{:S(2)}) %collective-permute-start) | collective-permute-done | bytes 524320 | tf_op jit(solution)/shard_map/ppermute | solution.py:392
  19.1 2.9 %collective-permute-start.4 = (bf16[128,16,128]{2,1,0:T(8,128)(2,1)S(1)}, bf16[128,16,128]{2,1,0:T(8,128)(2,1)S(1)}, u32[]{:S(2)}, u32[]{:S(2)}) collective-permute-start(bf16[128,16,128]{2,1,0:T(8,128)(2,1)S(1)} %collective-permute-done.refs_0_.refs_3_.refs_1_), channel_id=1, source_target_pairs={{0,8},{8,0},{16,24},{24,16},{1,17},{5,13},{13,5},{17,1},{21,29},{2... | collective-permute-start | bytes 1572872 | tf_op jit(solution)/shard_map/ppermute | solution.py:275
  22.0 1.4 %collective-permute-start.1 = (bf16[128,16,128]{2,1,0:T(8,128)(2,1)S(1)}, bf16[128,16,128]{2,1,0:T(8,128)(2,1)S(1)}, u32[]{:S(2)}, u32[]{:S(2)}) collective-permute-start(bf16[128,16,128]{2,1,0:T(8,128)(2,1)S(1)} %collective-permute-done.refs_0_.refs_3_.refs_1_), channel_id=1, source_target_pairs={{0,1},{1,2},{2,3},{3,0},{4,5},{5,6},{6,7},{7,4},{8,9},{9,10},{10,1... | collective-permute-start | bytes 1572872 | tf_op jit(solution)/shard_map/ppermute | solution.py:392
  23.4 1.0 %copy-done = bf16[128,16,128]{2,1,0:T(8,128)(2,1)S(1)} copy-done((bf16[128,16,128]{2,1,0:T(8,128)(2,1)S(1)}, bf16[128,16,128]{2,1,0:T(8,128)(2,1)}, u32[]{:S(2)}) %copy-start) | copy-done | bytes 524312
  24.5 3.1 %collective-permute-start.5 = (bf16[128,16,128]{2,1,0:T(8,128)(2,1)S(1)}, bf16[128,16,128]{2,1,0:T(8,128)(2,1)S(1)}, u32[]{:S(2)}, u32[]{:S(2)}) collective-permute-start(bf16[128,16,128]{2,1,0:T(8,128)(2,1)S(1)} %bitcast.7), channel_id=1, source_target_pairs={{8,24},{24,8},{1,9},{9,1},{13,29},{17,25},{25,17},{29,13},{2,10},{... | collective-permute-start | bytes 1572872 | tf_op jit(solution)/shard_map/ppermute | solution.py:275
  27.6 1.7 %collective-permute-done.4.refs_1_.refs_4_ = bf16[128,16,128]{2,1,0:T(8,128)(2,1)S(1)} collective-permute-done((bf16[128,16,128]{2,1,0:T(8,128)(2,1)S(1)}, bf16[128,16,128]{2,1,0:T(8,128)(2,1)S(1)}, u32[]{:S(2)}, u32[]{:S(2)}) %collective-permute-start.4) | collective-permute-done | bytes 524320 | tf_op jit(solution)/shard_map/ppermute | solution.py:275
  29.3 3.9 %collective-permute-done.1.refs_2_.refs_0_.refs_6_ = bf16[128,16,128]{2,1,0:T(8,128)(2,1)S(1)} collective-permute-done((bf16[128,16,128]{2,1,0:T(8,128)(2,1)S(1)}, bf16[128,16,128]{2,1,0:T(8,128)(2,1)S(1)}, u32[]{:S(2)}, u32[]{:S(2)}) %collective-permute-start.1) | collective-permute-done | bytes 524320 | tf_op jit(solution)/shard_map/ppermute | solution.py:392
  33.2 4.0 %collective-permute-done.5.refs_2_ = bf16[128,16,128]{2,1,0:T(8,128)(2,1)S(1)} collective-permute-done((bf16[128,16,128]{2,1,0:T(8,128)(2,1)S(1)}, bf16[128,16,128]{2,1,0:T(8,128)(2,1)S(1)}, u32[]{:S(2)}, u32[]{:S(2)}) %collective-permute-start.5) | collective-permute-done | bytes 524320 | tf_op jit(solution)/shard_map/ppermute | solution.py:275
  37.3 3.0 %collective-permute-start.7 = (bf16[128,16,128]{2,1,0:T(8,128)(2,1)S(1)}, bf16[128,16,128]{2,1,0:T(8,128)(2,1)S(1)}, u32[]{:S(2)}, u32[]{:S(2)}) collective-permute-start(bf16[128,16,128]{2,1,0:T(8,128)(2,1)S(1)} %bitcast.6), channel_id=1, source_target_pairs={{8,24},{24,8},{1,9},{9,1},{13,29},{17,25},{25,17},{29,13},{2,10},{... | collective-permute-start | bytes 1572872 | tf_op jit(solution)/shard_map/ppermute | solution.py:275
  40.3 1.9 %collective-permute-start.6 = (bf16[128,16,128]{2,1,0:T(8,128)(2,1)S(1)}, bf16[128,16,128]{2,1,0:T(8,128)(2,1)S(1)}, u32[]{:S(2)}, u32[]{:S(2)}) collective-permute-start(bf16[128,16,128]{2,1,0:T(8,128)(2,1)S(1)} %collective-permute-done.1.refs_2_.refs_0_.refs_6_), channel_id=1, source_target_pairs={{0,8},{8,0},{16,24},{24,16},{1,17},{5,13},{13,5},{17,1},{21,29},{2... | collective-permute-start | bytes 1572872 | tf_op jit(solution)/shard_map/ppermute | solution.py:275
  42.2 0.1 collective-permute-start.2
  42.3 7.2 %collective-permute-done.7.refs_5_ = bf16[128,16,128]{2,1,0:T(8,128)(2,1)S(1)} collective-permute-done((bf16[128,16,128]{2,1,0:T(8,128)(2,1)S(1)}, bf16[128,16,128]{2,1,0:T(8,128)(2,1)S(1)}, u32[]{:S(2)}, u32[]{:S(2)}) %collective-permute-start.7) | collective-permute-done | bytes 524320 | tf_op jit(solution)/shard_map/ppermute | solution.py:275
  49.4 4.9 %collective-permute-done.6.refs_1_.refs_3_.refs_7_ = bf16[128,16,128]{2,1,0:T(8,128)(2,1)S(1)} collective-permute-done((bf16[128,16,128]{2,1,0:T(8,128)(2,1)S(1)}, bf16[128,16,128]{2,1,0:T(8,128)(2,1)S(1)}, u32[]{:S(2)}, u32[]{:S(2)}) %collective-permute-start.6) | collective-permute-done | bytes 524320 | tf_op jit(solution)/shard_map/ppermute | solution.py:275
  54.3 1.0 %copy-done.1 = bf16[128,16,128]{2,1,0:T(8,128)(2,1)S(1)} copy-done((bf16[128,16,128]{2,1,0:T(8,128)(2,1)S(1)}, bf16[128,16,128]{2,1,0:T(8,128)(2,1)}, u32[]{:S(2)}) %copy-start.1) | copy-done | bytes 524312
  55.4 0.1 choose.8
  55.4 2.3 %collective-permute-start.8 = (bf16[2,128,16,128]{3,2,1,0:T(8,128)(2,1)S(1)}, bf16[2,128,16,128]{3,2,1,0:T(8,128)(2,1)S(1)}, u32[]{:S(2)}, u32[]{:S(2)}) collective-permute-start(bf16[2,128,16,128]{3,2,1,0:T(8,128)(2,1)S(1)} %choose.8), channel_id=1, source_target_pairs={{0,4},{4,0},{8,12},{12,8},{16,20},{20,16},{24,28},{28,24},{1,5},{5... | collective-permute-start | bytes 3145736 | tf_op jit(solution)/shard_map/ppermute | solution.py:275
  57.8 3.4 %collective-permute-start.10 = (bf16[128,16,128]{2,1,0:T(8,128)(2,1)S(1)}, bf16[128,16,128]{2,1,0:T(8,128)(2,1)S(1)}, u32[]{:S(2)}, u32[]{:S(2)}) collective-permute-start(bf16[128,16,128]{2,1,0:T(8,128)(2,1)S(1)} %collective-permute-done.2.refs_3_.refs_0_.refs_4_.refs_9_), channel_id=1, source_target_pairs={{0,8},{8,0},{16,24},{24,16},{1,17},{5,13},{13,5},{17,1},{21,29},{2... | collective-permute-start | bytes 1572872 | tf_op jit(solution)/shard_map/ppermute | solution.py:275
  61.2 2.3 %collective-permute-start.9 = (bf16[128,16,128]{2,1,0:T(8,128)(2,1)S(1)}, bf16[128,16,128]{2,1,0:T(8,128)(2,1)S(1)}, u32[]{:S(2)}, u32[]{:S(2)}) collective-permute-start(bf16[128,16,128]{2,1,0:T(8,128)(2,1)S(1)} %bitcast.4), channel_id=1, source_target_pairs={{8,24},{24,8},{1,9},{9,1},{13,29},{17,25},{25,17},{29,13},{2,10},{... | collective-permute-start | bytes 1572872 | tf_op jit(solution)/shard_map/ppermute | solution.py:275
  63.5 3.4 %own_rows.1.own = bf16[128,64,128]{2,1,0:T(8,128)(2,1)S(1)} custom-call(bf16[128,16,128]{2,1,0:T(8,128)(2,1)S(1)} %copy-done.1, bf16[128,16,128]{2,1,0:T(8,128)(2,1)S(1)} %collective-permute-done.refs_0_.refs_3_.refs_1_, bf16[128,16,128]{2,1,0:T(8,128)(2,1)S(1)} %collective-permute-done.1.refs_2_.refs_0_.refs_6_, ...), custom_call_target="tpu_custom_call" | custom-call | flops 1 | bytes 1 | tf_op jit(solution)/shard_map/own_rows/pallas_call | solution.py:145
  67.0 3.4 %collective-permute-done.10.refs_1_.refs_5_.refs_10_ = bf16[128,16,128]{2,1,0:T(8,128)(2,1)S(1)} collective-permute-done((bf16[128,16,128]{2,1,0:T(8,128)(2,1)S(1)}, bf16[128,16,128]{2,1,0:T(8,128)(2,1)S(1)}, u32[]{:S(2)}, u32[]{:S(2)}) %collective-permute-start.10) | collective-permute-done | bytes 524320 | tf_op jit(solution)/shard_map/ppermute | solution.py:275
  70.4 0.7 collective-permute-start.12
  71.1 1.9 %collective-permute-start.11 = (bf16[128,16,128]{2,1,0:T(8,128)(2,1)S(1)}, bf16[128,16,128]{2,1,0:T(8,128)(2,1)S(1)}, u32[]{:S(2)}, u32[]{:S(2)}) collective-permute-start(bf16[128,16,128]{2,1,0:T(8,128)(2,1)S(1)} %bitcast.5), channel_id=1, source_target_pairs={{8,24},{24,8},{1,9},{9,1},{13,29},{17,25},{25,17},{29,13},{2,10},{... | collective-permute-start | bytes 1572872 | tf_op jit(solution)/shard_map/ppermute | solution.py:275
  73.0 0.7 collective-permute-done.9.refs_2_.refs_8_
  73.8 7.5 %collective-permute-done.11.refs_6_.refs_11_ = bf16[128,16,128]{2,1,0:T(8,128)(2,1)S(1)} collective-permute-done((bf16[128,16,128]{2,1,0:T(8,128)(2,1)S(1)}, bf16[128,16,128]{2,1,0:T(8,128)(2,1)S(1)}, u32[]{:S(2)}, u32[]{:S(2)}) %collective-permute-start.11) | collective-permute-done | bytes 524320 | tf_op jit(solution)/shard_map/ppermute | solution.py:275
  81.3 0.1 choose.11
  81.4 2.0 %collective-permute-start.13 = (bf16[2,128,16,128]{3,2,1,0:T(8,128)(2,1)S(1)}, bf16[2,128,16,128]{3,2,1,0:T(8,128)(2,1)S(1)}, u32[]{:S(2)}, u32[]{:S(2)}) collective-permute-start(bf16[2,128,16,128]{3,2,1,0:T(8,128)(2,1)S(1)} %choose.11), channel_id=1, source_target_pairs={{0,4},{4,0},{8,12},{12,8},{16,20},{20,16},{24,28},{28,24},{1,5},{5... | collective-permute-start | bytes 3145736 | tf_op jit(solution)/shard_map/ppermute | solution.py:275
  83.4 2.3 %collective-permute-done.13.refs_13_ = bf16[2,128,16,128]{3,2,1,0:T(8,128)(2,1)S(1)} collective-permute-done((bf16[2,128,16,128]{3,2,1,0:T(8,128)(2,1)S(1)}, bf16[2,128,16,128]{3,2,1,0:T(8,128)(2,1)S(1)}, u32[]{:S(2)}, u32[]{:S(2)}) %collective-permute-start.13) | collective-permute-done | bytes 1048608 | tf_op jit(solution)/shard_map/ppermute | solution.py:275
  85.7 10.3 %stack.1 = f32[64,64,256]{2,1,0:T(8,128)} custom-call(s32[64]{0:T(128)S(1)} %copy-done.3, bf16[128,64,128]{2,1,0:T(8,128)(2,1)S(1)} %own_rows.1.own, bf16[128,16,128]{2,1,0:T(8,128)(2,1)S(1)} %copy-done.2, bf16[128,16,128]{2,1,0:T(8,128)(2,1)S(1)} %collective-permute-done.3.refs_1_, bf16[128,16,128]{2,1,0:T(8,128)(2,1)S(1)} %collective-permute-done.5.refs_2_, ...), custom_call_target="tpu_custom_call" | custom-call | flops 1 | bytes 1 | tf_op jit(solution)/shard_map/stack/pallas_call | solution.py:257
  (13 shorter events, 0.2 us)
Async XLA Ops:
  4.0 10.4 %collective-permute-start.3 = (bf16[128,16,128]{2,1,0:T(8,128)(2,1)}, bf16[128,16,128]{2,1,0:T(8,128)(2,1)S(1)}, u32[]{:S(2)}, u32[]{:S(2)}) collective-permute-start(bf16[128,16,128]{2,1,0:T(8,128)(2,1)} %whiten.1.refs_0_), channel_id=1, source_target_pairs={{0,8},{8,0},{16,24},{24,16},{1,17},{5,13},{13,5},{17,1},{21,29},{2... | collective-permute-start | bytes 1572872 | tf_op jit(solution)/shard_map/ppermute | solution.py:275
  6.2 12.9 %collective-permute-start = (bf16[128,16,128]{2,1,0:T(8,128)(2,1)}, bf16[128,16,128]{2,1,0:T(8,128)(2,1)S(1)}, u32[]{:S(2)}, u32[]{:S(2)}) collective-permute-start(bf16[128,16,128]{2,1,0:T(8,128)(2,1)} %whiten.1.refs_0_), channel_id=1, source_target_pairs={{0,1},{1,2},{2,3},{3,0},{4,5},{5,6},{6,7},{7,4},{8,9},{9,10},{10,1... | collective-permute-start | bytes 1572872 | tf_op jit(solution)/shard_map/ppermute | solution.py:392
  19.1 10.2 %collective-permute-start.4 = (bf16[128,16,128]{2,1,0:T(8,128)(2,1)S(1)}, bf16[128,16,128]{2,1,0:T(8,128)(2,1)S(1)}, u32[]{:S(2)}, u32[]{:S(2)}) collective-permute-start(bf16[128,16,128]{2,1,0:T(8,128)(2,1)S(1)} %collective-permute-done.refs_0_.refs_3_.refs_1_), channel_id=1, source_target_pairs={{0,8},{8,0},{16,24},{24,16},{1,17},{5,13},{13,5},{17,1},{21,29},{2... | collective-permute-start | bytes 1572872 | tf_op jit(solution)/shard_map/ppermute | solution.py:275
  22.0 11.3 %collective-permute-start.1 = (bf16[128,16,128]{2,1,0:T(8,128)(2,1)S(1)}, bf16[128,16,128]{2,1,0:T(8,128)(2,1)S(1)}, u32[]{:S(2)}, u32[]{:S(2)}) collective-permute-start(bf16[128,16,128]{2,1,0:T(8,128)(2,1)S(1)} %collective-permute-done.refs_0_.refs_3_.refs_1_), channel_id=1, source_target_pairs={{0,1},{1,2},{2,3},{3,0},{4,5},{5,6},{6,7},{7,4},{8,9},{9,10},{10,1... | collective-permute-start | bytes 1572872 | tf_op jit(solution)/shard_map/ppermute | solution.py:392
  23.4 1.0 %copy-start = (bf16[128,16,128]{2,1,0:T(8,128)(2,1)S(1)}, bf16[128,16,128]{2,1,0:T(8,128)(2,1)}, u32[]{:S(2)}) copy-start(bf16[128,16,128]{2,1,0:T(8,128)(2,1)} %whiten.1.refs_0_) | copy-start | bytes 1572868
  24.5 12.8 %collective-permute-start.5 = (bf16[128,16,128]{2,1,0:T(8,128)(2,1)S(1)}, bf16[128,16,128]{2,1,0:T(8,128)(2,1)S(1)}, u32[]{:S(2)}, u32[]{:S(2)}) collective-permute-start(bf16[128,16,128]{2,1,0:T(8,128)(2,1)S(1)} %bitcast.7), channel_id=1, source_target_pairs={{8,24},{24,8},{1,9},{9,1},{13,29},{17,25},{25,17},{29,13},{2,10},{... | collective-permute-start | bytes 1572872 | tf_op jit(solution)/shard_map/ppermute | solution.py:275
  37.3 12.2 %collective-permute-start.7 = (bf16[128,16,128]{2,1,0:T(8,128)(2,1)S(1)}, bf16[128,16,128]{2,1,0:T(8,128)(2,1)S(1)}, u32[]{:S(2)}, u32[]{:S(2)}) collective-permute-start(bf16[128,16,128]{2,1,0:T(8,128)(2,1)S(1)} %bitcast.6), channel_id=1, source_target_pairs={{8,24},{24,8},{1,9},{9,1},{13,29},{17,25},{25,17},{29,13},{2,10},{... | collective-permute-start | bytes 1572872 | tf_op jit(solution)/shard_map/ppermute | solution.py:275
  40.3 14.0 %collective-permute-start.6 = (bf16[128,16,128]{2,1,0:T(8,128)(2,1)S(1)}, bf16[128,16,128]{2,1,0:T(8,128)(2,1)S(1)}, u32[]{:S(2)}, u32[]{:S(2)}) collective-permute-start(bf16[128,16,128]{2,1,0:T(8,128)(2,1)S(1)} %collective-permute-done.1.refs_2_.refs_0_.refs_6_), channel_id=1, source_target_pairs={{0,8},{8,0},{16,24},{24,16},{1,17},{5,13},{13,5},{17,1},{21,29},{2... | collective-permute-start | bytes 1572872 | tf_op jit(solution)/shard_map/ppermute | solution.py:275
  42.2 12.1 %collective-permute-start.2 = (bf16[128,16,128]{2,1,0:T(8,128)(2,1)S(1)}, bf16[128,16,128]{2,1,0:T(8,128)(2,1)S(1)}, u32[]{:S(2)}, u32[]{:S(2)}) collective-permute-start(bf16[128,16,128]{2,1,0:T(8,128)(2,1)S(1)} %collective-permute-done.1.refs_2_.refs_0_.refs_6_), channel_id=1, source_target_pairs={{0,1},{1,2},{2,3},{3,0},{4,5},{5,6},{6,7},{7,4},{8,9},{9,10},{10,1... | collective-permute-start | bytes 1572872 | tf_op jit(solution)/shard_map/ppermute | solution.py:392
  54.3 1.0 %copy-start.1 = (bf16[128,16,128]{2,1,0:T(8,128)(2,1)S(1)}, bf16[128,16,128]{2,1,0:T(8,128)(2,1)}, u32[]{:S(2)}) copy-start(bf16[128,16,128]{2,1,0:T(8,128)(2,1)} %whiten.1.refs_0_) | copy-start | bytes 1572868
  55.4 8.1 %collective-permute-start.8 = (bf16[2,128,16,128]{3,2,1,0:T(8,128)(2,1)S(1)}, bf16[2,128,16,128]{3,2,1,0:T(8,128)(2,1)S(1)}, u32[]{:S(2)}, u32[]{:S(2)}) collective-permute-start(bf16[2,128,16,128]{3,2,1,0:T(8,128)(2,1)S(1)} %choose.8), channel_id=1, source_target_pairs={{0,4},{4,0},{8,12},{12,8},{16,20},{20,16},{24,28},{28,24},{1,5},{5... | collective-permute-start | bytes 3145736 | tf_op jit(solution)/shard_map/ppermute | solution.py:275
  57.8 12.6 %collective-permute-start.10 = (bf16[128,16,128]{2,1,0:T(8,128)(2,1)S(1)}, bf16[128,16,128]{2,1,0:T(8,128)(2,1)S(1)}, u32[]{:S(2)}, u32[]{:S(2)}) collective-permute-start(bf16[128,16,128]{2,1,0:T(8,128)(2,1)S(1)} %collective-permute-done.2.refs_3_.refs_0_.refs_4_.refs_9_), channel_id=1, source_target_pairs={{0,8},{8,0},{16,24},{24,16},{1,17},{5,13},{13,5},{17,1},{21,29},{2... | collective-permute-start | bytes 1572872 | tf_op jit(solution)/shard_map/ppermute | solution.py:275
  61.2 12.6 %collective-permute-start.9 = (bf16[128,16,128]{2,1,0:T(8,128)(2,1)S(1)}, bf16[128,16,128]{2,1,0:T(8,128)(2,1)S(1)}, u32[]{:S(2)}, u32[]{:S(2)}) collective-permute-start(bf16[128,16,128]{2,1,0:T(8,128)(2,1)S(1)} %bitcast.4), channel_id=1, source_target_pairs={{8,24},{24,8},{1,9},{9,1},{13,29},{17,25},{25,17},{29,13},{2,10},{... | collective-permute-start | bytes 1572872 | tf_op jit(solution)/shard_map/ppermute | solution.py:275
  66.9 18.8 %copy-start.2 = (bf16[128,16,128]{2,1,0:T(8,128)(2,1)S(1)}, bf16[128,16,128]{2,1,0:T(8,128)(2,1)}, u32[]{:S(2)}) copy-start(bf16[128,16,128]{2,1,0:T(8,128)(2,1)} %whiten.1.refs_0_) | copy-start | bytes 1572868
  67.0 18.8 %copy-start.3 = (s32[64]{0:T(128)S(1)}, s32[64]{0:T(128)}, u32[]{:S(2)}) copy-start(s32[64]{0:T(128)} %reach_ref.1) | copy-start | bytes 772
  70.4 3.4 %collective-permute-start.12 = (bf16[128,16,128]{2,1,0:T(8,128)(2,1)S(1)}, bf16[128,16,128]{2,1,0:T(8,128)(2,1)S(1)}, u32[]{:S(2)}, u32[]{:S(2)}) collective-permute-start(bf16[128,16,128]{2,1,0:T(8,128)(2,1)S(1)} %collective-permute-done.2.refs_3_.refs_0_.refs_4_.refs_9_), channel_id=1, source_target_pairs={{3,19},{11,27},{19,3},{27,11}} | collective-permute-start | bytes 1572872 | tf_op jit(solution)/shard_map/ppermute | solution.py:275
  71.1 10.2 %collective-permute-start.11 = (bf16[128,16,128]{2,1,0:T(8,128)(2,1)S(1)}, bf16[128,16,128]{2,1,0:T(8,128)(2,1)S(1)}, u32[]{:S(2)}, u32[]{:S(2)}) collective-permute-start(bf16[128,16,128]{2,1,0:T(8,128)(2,1)S(1)} %bitcast.5), channel_id=1, source_target_pairs={{8,24},{24,8},{1,9},{9,1},{13,29},{17,25},{25,17},{29,13},{2,10},{... | collective-permute-start | bytes 1572872 | tf_op jit(solution)/shard_map/ppermute | solution.py:275
  81.4 4.3 %collective-permute-start.13 = (bf16[2,128,16,128]{3,2,1,0:T(8,128)(2,1)S(1)}, bf16[2,128,16,128]{3,2,1,0:T(8,128)(2,1)S(1)}, u32[]{:S(2)}, u32[]{:S(2)}) collective-permute-start(bf16[2,128,16,128]{3,2,1,0:T(8,128)(2,1)S(1)} %choose.11), channel_id=1, source_target_pairs={{0,4},{4,0},{8,12},{12,8},{16,20},{20,16},{24,28},{28,24},{1,5},{5... | collective-permute-start | bytes 3145736 | tf_op jit(solution)/shard_map/ppermute | solution.py:275

commit v6 on v5

--- a/solution.py
+++ b/solution.py
@@ -343,29 +343,38 @@
 
     count = len(pieces)
     half = count // 2
-    held = []
+    firsts, seconds = [], []
+
+    def second_move(slot, arrived):
+        relay = choose(lambda: square_codes()[0], [(pieces[slot], arrived)])[0]
+        seconds.append(send(relay, pairs(second_target)))
+        return relay
+
     for slot, piece in enumerate(pieces):
         last = slot == count - 1
+        if slot >= 2:
+            piece = after(piece, firsts[slot - 2])
+        firsts.append(
+            send(
+                piece,
+                pairs(
+                    lambda z, c, core, x: (
+                        None if last and z == 3 and core == 0 else first_target(z, c, core, x)
+                    )
+                ),
+            )
+        )
         if slot:
-            piece = after(piece, held[slot - 1][1], *([held[slot - 2][2]] if slot >= 2 else []))
-        moved = send(
-            piece,
-            pairs(
-                lambda z, c, core, x: (
-                    None if last and z == 3 and core == 0 else first_target(z, c, core, x)
-                )
-            ),
-        )
-        arrived = moved
-        if last:
-            held[0] = (*held[0][:2], after(held[0][2], piece))
-            swapped_early = swap(lambda: square_codes()[1], held[:half])
-            own = own_rows([*pieces[:-1], after(piece, swapped_early)])
-            arrived = after(moved, own)
-        elif True:
-            arrived = after(moved, pieces[slot + 1])
-        relay = choose(lambda: square_codes()[0], [(piece, arrived)])[0]
-        held.append((piece, moved, send(relay, pairs(second_target))))
+            arrived = firsts[slot - 1]
+            arrived = after(arrived, *seconds[-1:])
+            second_move(slot - 1, arrived)
+    held = list(zip(pieces, firsts, seconds))
+    own = own_rows(pieces)
+    held[0] = (*held[0][:2], after(held[0][2], firsts[-1]))
+    swapped_early = swap(lambda: square_codes()[1], held[:half])
+    arrived = after(firsts[-1], own)
+    relay = second_move(count - 1, arrived)
+    held.append((pieces[-1], firsts[-1], seconds[-1]))
     late = send(
         after(pieces[-1], relay),
         pairs(lambda z, c, core, x: c ^ 4 if z == 3 and core == 0 else None),

time: 96.5 us -> 86.4 us (0.90)
  the two profiles are of different devices: /device:TPU:19 before, /device:TPU:11 now
where the time goes in v6:
time: 86.4 us; the launch traced here: 86 us
  waiting for transfers between devices  41.3 us (48%)
  starting transfers between devices  25.3 us (29%)
  Pallas kernels  18.1 us (21%)
  local copies, waits for them, and re-layouts  1.05 us (1%)
    ppermute x11, waiting for transfers between devices, send(): return lax.ppermute(array, AXES, pairs)  26.3 us
    ppermute x11, starting transfers between devices, send(): return lax.ppermute(array, AXES, pairs)  22.4 us
    ppermute x3, waiting for transfers between devices, on_device(): pieces.append(lax.ppermute(pieces[-1], 'win', ring))  15 us
    pallas_call x1, Pallas kernels, stacked(): pl.pallas_call(functools.partial(stack_kernel, 1.0 / math.sqrt(windows),...  10.3 us
    pallas_call x1, Pallas kernels, whitened_chunk(): pl.pallas_call(whiten_kernel, out_shape=jax.ShapeDtypeStruct((F, windows,...  4 us
    pallas_call x1, Pallas kernels, own_rows(): pl.pallas_call(own_kernel, out_shape=jax.ShapeDtypeStruct((bins, lanes //...  3.44 us
    ppermute x3, starting transfers between devices, on_device(): pieces.append(lax.ppermute(pieces[-1], 'win', ring))  2.93 us
  transfers between devices with their start and end apart: 14, of which 9 were waited for; matrix products, arithmetic and copies ran while one was open for 0% of the time, Pallas kernels for 4%

profile of v6, /device:TPU:11, one launch (start us, length us, event | category | flops | bytes accessed | tf_op | source)
XLA Modules:
  0.0 86.0 jit_solution(7791570686117774134)
XLA Ops:
  0.0 4.0 %whiten.1.refs_0_ = bf16[128,16,128]{2,1,0:T(8,128)(2,1)} custom-call(bf16[256,512]{1,0:T(8,128)(2,1)} %constant.3.table_hbm, bf16[16,64,512]{2,1,0:T(8,128)(2,1)} %traces_hbm.1, s32[16,64]{1,0:T(8,128)} %valid_hbm.1), custom_call_target="tpu_custom_call" | custom-call | flops 268435456 | bytes 1048576 | tf_op jit(solution)/shard_map/whiten/pallas_call | solution.py:78
  4.0 1.3 %collective-permute-start = (bf16[128,16,128]{2,1,0:T(8,128)(2,1)}, bf16[128,16,128]{2,1,0:T(8,128)(2,1)S(1)}, u32[]{:S(2)}, u32[]{:S(2)}) collective-permute-start(bf16[128,16,128]{2,1,0:T(8,128)(2,1)} %whiten.1.refs_0_), channel_id=1, source_target_pairs={{0,1},{1,2},{2,3},{3,0},{4,5},{5,6},{6,7},{7,4},{8,9},{9,10},{10,1... | collective-permute-start | bytes 1572872 | tf_op jit(solution)/shard_map/ppermute | solution.py:401
  5.4 2.2 %collective-permute-start.3 = (bf16[128,16,128]{2,1,0:T(8,128)(2,1)}, bf16[128,16,128]{2,1,0:T(8,128)(2,1)S(1)}, u32[]{:S(2)}, u32[]{:S(2)}) collective-permute-start(bf16[128,16,128]{2,1,0:T(8,128)(2,1)} %whiten.1.refs_0_), channel_id=1, source_target_pairs={{0,8},{8,0},{16,24},{24,16},{1,17},{5,13},{13,5},{17,1},{21,29},{2... | collective-permute-start | bytes 1572872 | tf_op jit(solution)/shard_map/ppermute | solution.py:275
  7.5 9.5 %collective-permute-done.refs_1_.refs_0_.refs_3_ = bf16[128,16,128]{2,1,0:T(8,128)(2,1)S(1)} collective-permute-done((bf16[128,16,128]{2,1,0:T(8,128)(2,1)}, bf16[128,16,128]{2,1,0:T(8,128)(2,1)S(1)}, u32[]{:S(2)}, u32[]{:S(2)}) %collective-permute-start) | collective-permute-done | bytes 524320 | tf_op jit(solution)/shard_map/ppermute | solution.py:401
  17.1 1.3 %collective-permute-start.1 = (bf16[128,16,128]{2,1,0:T(8,128)(2,1)S(1)}, bf16[128,16,128]{2,1,0:T(8,128)(2,1)S(1)}, u32[]{:S(2)}, u32[]{:S(2)}) collective-permute-start(bf16[128,16,128]{2,1,0:T(8,128)(2,1)S(1)} %collective-permute-done.refs_1_.refs_0_.refs_3_), channel_id=1, source_target_pairs={{0,1},{1,2},{2,3},{3,0},{4,5},{5,6},{6,7},{7,4},{8,9},{9,10},{10,1... | collective-permute-start | bytes 1572872 | tf_op jit(solution)/shard_map/ppermute | solution.py:401
  18.4 0.0 collective-permute-done.3.refs_1_
  18.4 1.0 %copy-done = bf16[128,16,128]{2,1,0:T(8,128)(2,1)S(1)} copy-done((bf16[128,16,128]{2,1,0:T(8,128)(2,1)S(1)}, bf16[128,16,128]{2,1,0:T(8,128)(2,1)}, u32[]{:S(2)}) %copy-start) | copy-done | bytes 524312
  19.4 3.3 %collective-permute-start.4 = (bf16[128,16,128]{2,1,0:T(8,128)(2,1)S(1)}, bf16[128,16,128]{2,1,0:T(8,128)(2,1)S(1)}, u32[]{:S(2)}, u32[]{:S(2)}) collective-permute-start(bf16[128,16,128]{2,1,0:T(8,128)(2,1)S(1)} %bitcast.6), channel_id=1, source_target_pairs={{8,24},{24,8},{1,9},{9,1},{13,29},{17,25},{25,17},{29,13},{2,10},{... | collective-permute-start | bytes 1572872 | tf_op jit(solution)/shard_map/ppermute | solution.py:275
  22.7 1.9 %collective-permute-start.5 = (bf16[128,16,128]{2,1,0:T(8,128)(2,1)S(1)}, bf16[128,16,128]{2,1,0:T(8,128)(2,1)S(1)}, u32[]{:S(2)}, u32[]{:S(2)}) collective-permute-start(bf16[128,16,128]{2,1,0:T(8,128)(2,1)S(1)} %collective-permute-done.refs_1_.refs_0_.refs_3_), channel_id=1, source_target_pairs={{0,8},{8,0},{16,24},{24,16},{1,17},{5,13},{13,5},{17,1},{21,29},{2... | collective-permute-start | bytes 1572872 | tf_op jit(solution)/shard_map/ppermute | solution.py:275
  24.7 5.3 %collective-permute-done.1.refs_2_.refs_0_.refs_6_ = bf16[128,16,128]{2,1,0:T(8,128)(2,1)S(1)} collective-permute-done((bf16[128,16,128]{2,1,0:T(8,128)(2,1)S(1)}, bf16[128,16,128]{2,1,0:T(8,128)(2,1)S(1)}, u32[]{:S(2)}, u32[]{:S(2)}) %collective-permute-start.1) | collective-permute-done | bytes 524320 | tf_op jit(solution)/shard_map/ppermute | solution.py:401
  29.9 0.3 collective-permute-start.2
  30.2 7.5 %collective-permute-done.5.refs_1_.refs_4_ = bf16[128,16,128]{2,1,0:T(8,128)(2,1)S(1)} collective-permute-done((bf16[128,16,128]{2,1,0:T(8,128)(2,1)S(1)}, bf16[128,16,128]{2,1,0:T(8,128)(2,1)S(1)}, u32[]{:S(2)}, u32[]{:S(2)}) %collective-permute-start.5) | collective-permute-done | bytes 524320 | tf_op jit(solution)/shard_map/ppermute | solution.py:275
  37.7 2.8 %collective-permute-start.7 = (bf16[128,16,128]{2,1,0:T(8,128)(2,1)S(1)}, bf16[128,16,128]{2,1,0:T(8,128)(2,1)S(1)}, u32[]{:S(2)}, u32[]{:S(2)}) collective-permute-start(bf16[128,16,128]{2,1,0:T(8,128)(2,1)S(1)} %bitcast.7), channel_id=1, source_target_pairs={{8,24},{24,8},{1,9},{9,1},{13,29},{17,25},{25,17},{29,13},{2,10},{... | collective-permute-start | bytes 1572872 | tf_op jit(solution)/shard_map/ppermute | solution.py:275
  40.6 1.9 %collective-permute-start.8 = (bf16[128,16,128]{2,1,0:T(8,128)(2,1)S(1)}, bf16[128,16,128]{2,1,0:T(8,128)(2,1)S(1)}, u32[]{:S(2)}, u32[]{:S(2)}) collective-permute-start(bf16[128,16,128]{2,1,0:T(8,128)(2,1)S(1)} %collective-permute-done.1.refs_2_.refs_0_.refs_6_), channel_id=1, source_target_pairs={{0,8},{8,0},{16,24},{24,16},{1,17},{5,13},{13,5},{17,1},{21,29},{2... | collective-permute-start | bytes 1572872 | tf_op jit(solution)/shard_map/ppermute | solution.py:275
  42.5 0.2 collective-permute-done.2.refs_3_.refs_0_.refs_4_.refs_9_
  42.7 3.1 %collective-permute-start.6 = (bf16[128,16,128]{2,1,0:T(8,128)(2,1)S(1)}, bf16[128,16,128]{2,1,0:T(8,128)(2,1)S(1)}, u32[]{:S(2)}, u32[]{:S(2)}) collective-permute-start(bf16[128,16,128]{2,1,0:T(8,128)(2,1)S(1)} %collective-permute-done.2.refs_3_.refs_0_.refs_4_.refs_9_), channel_id=1, source_target_pairs={{0,8},{8,0},{16,24},{24,16},{1,17},{5,13},{13,5},{17,1},{21,29},{2... | collective-permute-start | bytes 1572872 | tf_op jit(solution)/shard_map/ppermute | solution.py:275
  45.9 2.1 %collective-permute-done.7.refs_5_ = bf16[128,16,128]{2,1,0:T(8,128)(2,1)S(1)} collective-permute-done((bf16[128,16,128]{2,1,0:T(8,128)(2,1)S(1)}, bf16[128,16,128]{2,1,0:T(8,128)(2,1)S(1)}, u32[]{:S(2)}, u32[]{:S(2)}) %collective-permute-start.7) | collective-permute-done | bytes 524320 | tf_op jit(solution)/shard_map/ppermute | solution.py:275
  48.0 5.3 %collective-permute-done.8.refs_1_.refs_3_.refs_7_ = bf16[128,16,128]{2,1,0:T(8,128)(2,1)S(1)} collective-permute-done((bf16[128,16,128]{2,1,0:T(8,128)(2,1)S(1)}, bf16[128,16,128]{2,1,0:T(8,128)(2,1)S(1)}, u32[]{:S(2)}, u32[]{:S(2)}) %collective-permute-start.8) | collective-permute-done | bytes 524320 | tf_op jit(solution)/shard_map/ppermute | solution.py:275
  53.3 3.8 %collective-permute-start.9 = (bf16[128,16,128]{2,1,0:T(8,128)(2,1)S(1)}, bf16[128,16,128]{2,1,0:T(8,128)(2,1)S(1)}, u32[]{:S(2)}, u32[]{:S(2)}) collective-permute-start(bf16[128,16,128]{2,1,0:T(8,128)(2,1)S(1)} %bitcast.4), channel_id=1, source_target_pairs={{8,24},{24,8},{1,9},{9,1},{13,29},{17,25},{25,17},{29,13},{2,10},{... | collective-permute-start | bytes 1572872 | tf_op jit(solution)/shard_map/ppermute | solution.py:275
  57.2 3.4 %own_rows.1.own = bf16[128,64,128]{2,1,0:T(8,128)(2,1)S(1)} custom-call(bf16[128,16,128]{2,1,0:T(8,128)(2,1)S(1)} %copy-done.1, bf16[128,16,128]{2,1,0:T(8,128)(2,1)S(1)} %collective-permute-done.refs_1_.refs_0_.refs_3_, bf16[128,16,128]{2,1,0:T(8,128)(2,1)S(1)} %collective-permute-done.1.refs_2_.refs_0_.refs_6_, ...), custom_call_target="tpu_custom_call" | custom-call | flops 1 | bytes 1 | tf_op jit(solution)/shard_map/own_rows/pallas_call | solution.py:145
  60.6 1.5 %collective-permute-done.6.refs_1_.refs_5_.refs_10_ = bf16[128,16,128]{2,1,0:T(8,128)(2,1)S(1)} collective-permute-done((bf16[128,16,128]{2,1,0:T(8,128)(2,1)S(1)}, bf16[128,16,128]{2,1,0:T(8,128)(2,1)S(1)}, u32[]{:S(2)}, u32[]{:S(2)}) %collective-permute-start.6) | collective-permute-done | bytes 524320 | tf_op jit(solution)/shard_map/ppermute | solution.py:275
  62.2 0.0 copy-start.2
  62.2 0.7 collective-permute-start.12
  62.9 2.4 %collective-permute-start.10 = (bf16[128,16,128]{2,1,0:T(8,128)(2,1)S(1)}, bf16[128,16,128]{2,1,0:T(8,128)(2,1)S(1)}, u32[]{:S(2)}, u32[]{:S(2)}) collective-permute-start(bf16[128,16,128]{2,1,0:T(8,128)(2,1)S(1)} %bitcast.5), channel_id=1, source_target_pairs={{8,24},{24,8},{1,9},{9,1},{13,29},{17,25},{25,17},{29,13},{2,10},{... | collective-permute-start | bytes 1572872 | tf_op jit(solution)/shard_map/ppermute | solution.py:275
  65.4 0.1 choose.10
  65.5 0.1 collective-permute-start.11
  65.5 0.0 collective-permute-done.9.refs_2_.refs_8_
  65.6 7.3 %collective-permute-done.10.refs_6_.refs_11_ = bf16[128,16,128]{2,1,0:T(8,128)(2,1)S(1)} collective-permute-done((bf16[128,16,128]{2,1,0:T(8,128)(2,1)S(1)}, bf16[128,16,128]{2,1,0:T(8,128)(2,1)S(1)}, u32[]{:S(2)}, u32[]{:S(2)}) %collective-permute-start.10) | collective-permute-done | bytes 524320 | tf_op jit(solution)/shard_map/ppermute | solution.py:275
  72.8 0.1 choose.11
  72.9 0.1 collective-permute-start.13
  73.0 2.6 %collective-permute-done.13.refs_13_ = bf16[2,128,16,128]{3,2,1,0:T(8,128)(2,1)S(1)} collective-permute-done((bf16[2,128,16,128]{3,2,1,0:T(8,128)(2,1)S(1)}, bf16[2,128,16,128]{3,2,1,0:T(8,128)(2,1)S(1)}, u32[]{:S(2)}, u32[]{:S(2)}) %collective-permute-start.13) | collective-permute-done | bytes 1048608 | tf_op jit(solution)/shard_map/ppermute | solution.py:275
  75.7 10.3 %stack.1 = f32[64,64,256]{2,1,0:T(8,128)} custom-call(s32[64]{0:T(128)S(1)} %copy-done.2, bf16[128,64,128]{2,1,0:T(8,128)(2,1)S(1)} %own_rows.1.own, bf16[128,16,128]{2,1,0:T(8,128)(2,1)S(1)} %copy-done.1, bf16[128,16,128]{2,1,0:T(8,128)(2,1)S(1)} %collective-permute-done.3.refs_1_, bf16[128,16,128]{2,1,0:T(8,128)(2,1)S(1)} %collective-permute-done.4.refs_2_, ...), custom_call_target="tpu_custom_call" | custom-call | flops 1 | bytes 1 | tf_op jit(solution)/shard_map/stack/pallas_call | solution.py:257
  (11 shorter events, 0.2 us)
Async XLA Ops:
  4.0 13.1 %collective-permute-start = (bf16[128,16,128]{2,1,0:T(8,128)(2,1)}, bf16[128,16,128]{2,1,0:T(8,128)(2,1)S(1)}, u32[]{:S(2)}, u32[]{:S(2)}) collective-permute-start(bf16[128,16,128]{2,1,0:T(8,128)(2,1)} %whiten.1.refs_0_), channel_id=1, source_target_pairs={{0,1},{1,2},{2,3},{3,0},{4,5},{5,6},{6,7},{7,4},{8,9},{9,10},{10,1... | collective-permute-start | bytes 1572872 | tf_op jit(solution)/shard_map/ppermute | solution.py:401
  5.4 13.0 %collective-permute-start.3 = (bf16[128,16,128]{2,1,0:T(8,128)(2,1)}, bf16[128,16,128]{2,1,0:T(8,128)(2,1)S(1)}, u32[]{:S(2)}, u32[]{:S(2)}) collective-permute-start(bf16[128,16,128]{2,1,0:T(8,128)(2,1)} %whiten.1.refs_0_), channel_id=1, source_target_pairs={{0,8},{8,0},{16,24},{24,16},{1,17},{5,13},{13,5},{17,1},{21,29},{2... | collective-permute-start | bytes 1572872 | tf_op jit(solution)/shard_map/ppermute | solution.py:275
  17.1 12.9 %collective-permute-start.1 = (bf16[128,16,128]{2,1,0:T(8,128)(2,1)S(1)}, bf16[128,16,128]{2,1,0:T(8,128)(2,1)S(1)}, u32[]{:S(2)}, u32[]{:S(2)}) collective-permute-start(bf16[128,16,128]{2,1,0:T(8,128)(2,1)S(1)} %collective-permute-done.refs_1_.refs_0_.refs_3_), channel_id=1, source_target_pairs={{0,1},{1,2},{2,3},{3,0},{4,5},{5,6},{6,7},{7,4},{8,9},{9,10},{10,1... | collective-permute-start | bytes 1572872 | tf_op jit(solution)/shard_map/ppermute | solution.py:401
  18.4 1.0 %copy-start = (bf16[128,16,128]{2,1,0:T(8,128)(2,1)S(1)}, bf16[128,16,128]{2,1,0:T(8,128)(2,1)}, u32[]{:S(2)}) copy-start(bf16[128,16,128]{2,1,0:T(8,128)(2,1)} %whiten.1.refs_0_) | copy-start | bytes 1572868
  19.4 37.8 %copy-start.1 = (bf16[128,16,128]{2,1,0:T(8,128)(2,1)S(1)}, bf16[128,16,128]{2,1,0:T(8,128)(2,1)}, u32[]{:S(2)}) copy-start(bf16[128,16,128]{2,1,0:T(8,128)(2,1)} %whiten.1.refs_0_) | copy-start | bytes 1572868
  19.4 10.8 %collective-permute-start.4 = (bf16[128,16,128]{2,1,0:T(8,128)(2,1)S(1)}, bf16[128,16,128]{2,1,0:T(8,128)(2,1)S(1)}, u32[]{:S(2)}, u32[]{:S(2)}) collective-permute-start(bf16[128,16,128]{2,1,0:T(8,128)(2,1)S(1)} %bitcast.6), channel_id=1, source_target_pairs={{8,24},{24,8},{1,9},{9,1},{13,29},{17,25},{25,17},{29,13},{2,10},{... | collective-permute-start | bytes 1572872 | tf_op jit(solution)/shard_map/ppermute | solution.py:275
  22.7 15.0 %collective-permute-start.5 = (bf16[128,16,128]{2,1,0:T(8,128)(2,1)S(1)}, bf16[128,16,128]{2,1,0:T(8,128)(2,1)S(1)}, u32[]{:S(2)}, u32[]{:S(2)}) collective-permute-start(bf16[128,16,128]{2,1,0:T(8,128)(2,1)S(1)} %collective-permute-done.refs_1_.refs_0_.refs_3_), channel_id=1, source_target_pairs={{0,8},{8,0},{16,24},{24,16},{1,17},{5,13},{13,5},{17,1},{21,29},{2... | collective-permute-start | bytes 1572872 | tf_op jit(solution)/shard_map/ppermute | solution.py:275
  29.9 12.8 %collective-permute-start.2 = (bf16[128,16,128]{2,1,0:T(8,128)(2,1)S(1)}, bf16[128,16,128]{2,1,0:T(8,128)(2,1)S(1)}, u32[]{:S(2)}, u32[]{:S(2)}) collective-permute-start(bf16[128,16,128]{2,1,0:T(8,128)(2,1)S(1)} %collective-permute-done.1.refs_2_.refs_0_.refs_6_), channel_id=1, source_target_pairs={{0,1},{1,2},{2,3},{3,0},{4,5},{5,6},{6,7},{7,4},{8,9},{9,10},{10,1... | collective-permute-start | bytes 1572872 | tf_op jit(solution)/shard_map/ppermute | solution.py:401
  37.7 10.2 %collective-permute-start.7 = (bf16[128,16,128]{2,1,0:T(8,128)(2,1)S(1)}, bf16[128,16,128]{2,1,0:T(8,128)(2,1)S(1)}, u32[]{:S(2)}, u32[]{:S(2)}) collective-permute-start(bf16[128,16,128]{2,1,0:T(8,128)(2,1)S(1)} %bitcast.7), channel_id=1, source_target_pairs={{8,24},{24,8},{1,9},{9,1},{13,29},{17,25},{25,17},{29,13},{2,10},{... | collective-permute-start | bytes 1572872 | tf_op jit(solution)/shard_map/ppermute | solution.py:275
  40.6 12.7 %collective-permute-start.8 = (bf16[128,16,128]{2,1,0:T(8,128)(2,1)S(1)}, bf16[128,16,128]{2,1,0:T(8,128)(2,1)S(1)}, u32[]{:S(2)}, u32[]{:S(2)}) collective-permute-start(bf16[128,16,128]{2,1,0:T(8,128)(2,1)S(1)} %collective-permute-done.1.refs_2_.refs_0_.refs_6_), channel_id=1, source_target_pairs={{0,8},{8,0},{16,24},{24,16},{1,17},{5,13},{13,5},{17,1},{21,29},{2... | collective-permute-start | bytes 1572872 | tf_op jit(solution)/shard_map/ppermute | solution.py:275
  42.7 19.4 %collective-permute-start.6 = (bf16[128,16,128]{2,1,0:T(8,128)(2,1)S(1)}, bf16[128,16,128]{2,1,0:T(8,128)(2,1)S(1)}, u32[]{:S(2)}, u32[]{:S(2)}) collective-permute-start(bf16[128,16,128]{2,1,0:T(8,128)(2,1)S(1)} %collective-permute-done.2.refs_3_.refs_0_.refs_4_.refs_9_), channel_id=1, source_target_pairs={{0,8},{8,0},{16,24},{24,16},{1,17},{5,13},{13,5},{17,1},{21,29},{2... | collective-permute-start | bytes 1572872 | tf_op jit(solution)/shard_map/ppermute | solution.py:275
  53.3 12.2 %collective-permute-start.9 = (bf16[128,16,128]{2,1,0:T(8,128)(2,1)S(1)}, bf16[128,16,128]{2,1,0:T(8,128)(2,1)S(1)}, u32[]{:S(2)}, u32[]{:S(2)}) collective-permute-start(bf16[128,16,128]{2,1,0:T(8,128)(2,1)S(1)} %bitcast.4), channel_id=1, source_target_pairs={{8,24},{24,8},{1,9},{9,1},{13,29},{17,25},{25,17},{29,13},{2,10},{... | collective-permute-start | bytes 1572872 | tf_op jit(solution)/shard_map/ppermute | solution.py:275
  62.2 13.5 %copy-start.2 = (s32[64]{0:T(128)S(1)}, s32[64]{0:T(128)}, u32[]{:S(2)}) copy-start(s32[64]{0:T(128)} %reach_ref.1) | copy-start | bytes 772
  62.2 3.4 %collective-permute-start.12 = (bf16[128,16,128]{2,1,0:T(8,128)(2,1)S(1)}, bf16[128,16,128]{2,1,0:T(8,128)(2,1)S(1)}, u32[]{:S(2)}, u32[]{:S(2)}) collective-permute-start(bf16[128,16,128]{2,1,0:T(8,128)(2,1)S(1)} %collective-permute-done.2.refs_3_.refs_0_.refs_4_.refs_9_), channel_id=1, source_target_pairs={{3,19},{11,27},{19,3},{27,11}} | collective-permute-start | bytes 1572872 | tf_op jit(solution)/shard_map/ppermute | solution.py:275
  62.9 9.9 %collective-permute-start.10 = (bf16[128,16,128]{2,1,0:T(8,128)(2,1)S(1)}, bf16[128,16,128]{2,1,0:T(8,128)(2,1)S(1)}, u32[]{:S(2)}, u32[]{:S(2)}) collective-permute-start(bf16[128,16,128]{2,1,0:T(8,128)(2,1)S(1)} %bitcast.5), channel_id=1, source_target_pairs={{8,24},{24,8},{1,9},{9,1},{13,29},{17,25},{25,17},{29,13},{2,10},{... | collective-permute-start | bytes 1572872 | tf_op jit(solution)/shard_map/ppermute | solution.py:275
  65.5 7.5 %collective-permute-start.11 = (bf16[2,128,16,128]{3,2,1,0:T(8,128)(2,1)S(1)}, bf16[2,128,16,128]{3,2,1,0:T(8,128)(2,1)S(1)}, u32[]{:S(2)}, u32[]{:S(2)}) collective-permute-start(bf16[2,128,16,128]{3,2,1,0:T(8,128)(2,1)S(1)} %choose.10), channel_id=1, source_target_pairs={{0,4},{4,0},{8,12},{12,8},{16,20},{20,16},{24,28},{28,24},{1,5},{5... | collective-permute-start | bytes 3145736 | tf_op jit(solution)/shard_map/ppermute | solution.py:275
  72.9 2.7 %collective-permute-start.13 = (bf16[2,128,16,128]{3,2,1,0:T(8,128)(2,1)S(1)}, bf16[2,128,16,128]{3,2,1,0:T(8,128)(2,1)S(1)}, u32[]{:S(2)}, u32[]{:S(2)}) collective-permute-start(bf16[2,128,16,128]{3,2,1,0:T(8,128)(2,1)S(1)} %choose.11), channel_id=1, source_target_pairs={{0,4},{4,0},{8,12},{12,8},{16,20},{20,16},{24,28},{28,24},{1,5},{5... | collective-permute-start | bytes 3145736 | tf_op jit(solution)/shard_map/ppermute | solution.py:275

commit v7 on v6

--- a/solution.py
+++ b/solution.py
@@ -345,15 +345,15 @@
     half = count // 2
     firsts, seconds = [], []
 
-    def second_move(slot, arrived):
+    def second_move(slot, arrived, *others):
         relay = choose(lambda: square_codes()[0], [(pieces[slot], arrived)])[0]
+        relay = after(relay, *others)
         seconds.append(send(relay, pairs(second_target)))
         return relay
 
     for slot, piece in enumerate(pieces):
         last = slot == count - 1
-        if slot >= 2:
-            piece = after(piece, firsts[slot - 2])
+
         firsts.append(
             send(
                 piece,
@@ -365,15 +365,12 @@
             )
         )
         if slot:
-            arrived = firsts[slot - 1]
-            arrived = after(arrived, *seconds[-1:])
-            second_move(slot - 1, arrived)
+            second_move(slot - 1, after(firsts[slot - 1], pieces[slot]), *seconds[-1:])
     held = list(zip(pieces, firsts, seconds))
     own = own_rows(pieces)
     held[0] = (*held[0][:2], after(held[0][2], firsts[-1]))
     swapped_early = swap(lambda: square_codes()[1], held[:half])
-    arrived = after(firsts[-1], own)
-    relay = second_move(count - 1, arrived)
+    relay = second_move(count - 1, after(firsts[-1], own))
     held.append((pieces[-1], firsts[-1], seconds[-1]))
     late = send(
         after(pieces[-1], relay),

time: 86.4 us -> 87.6 us (1.014)
  the two profiles are of different devices: /device:TPU:11 before, /device:TPU:17 now
where the time goes in v7:
time: 87.6 us; the launch traced here: 87.3 us
  starting transfers between devices  37.8 us (43%)
  waiting for transfers between devices  30.1 us (34%)
  Pallas kernels  18.2 us (21%)
  local copies, waits for them, and re-layouts  1.05 us (1%)
    ppermute x11, starting transfers between devices, send(): return lax.ppermute(array, AXES, pairs)  33.6 us
    ppermute x3, waiting for transfers between devices, on_device(): pieces.append(lax.ppermute(pieces[-1], 'win', ring))  20.3 us
    pallas_call x1, Pallas kernels, stacked(): pl.pallas_call(functools.partial(stack_kernel, 1.0 / math.sqrt(windows),...  10.3 us
    ppermute x11, waiting for transfers between devices, send(): return lax.ppermute(array, AXES, pairs)  9.8 us
    ppermute x3, starting transfers between devices, on_device(): pieces.append(lax.ppermute(pieces[-1], 'win', ring))  4.16 us
    pallas_call x1, Pallas kernels, whitened_chunk(): pl.pallas_call(whiten_kernel, out_shape=jax.ShapeDtypeStruct((F, windows,...  4 us
    pallas_call x1, Pallas kernels, own_rows(): pl.pallas_call(own_kernel, out_shape=jax.ShapeDtypeStruct((bins, lanes //...  3.44 us
  transfers between devices with their start and end apart: 14, of which 5 were waited for; matrix products, arithmetic and copies ran while one was open for 0% of the time, Pallas kernels for 4%

profile of v7, /device:TPU:17, one launch (start us, length us, event | category | flops | bytes accessed | tf_op | source)
XLA Modules:
  0.0 87.3 jit_solution(13735520203908712444)
XLA Ops:
  0.0 4.0 %whiten.1.refs_0_ = bf16[128,16,128]{2,1,0:T(8,128)(2,1)} custom-call(bf16[256,512]{1,0:T(8,128)(2,1)} %constant.3.table_hbm, bf16[16,64,512]{2,1,0:T(8,128)(2,1)} %traces_hbm.1, s32[16,64]{1,0:T(8,128)} %valid_hbm.1), custom_call_target="tpu_custom_call" | custom-call | flops 268435456 | bytes 1048576 | tf_op jit(solution)/shard_map/whiten/pallas_call | solution.py:78
  4.0 1.3 %collective-permute-start = (bf16[128,16,128]{2,1,0:T(8,128)(2,1)}, bf16[128,16,128]{2,1,0:T(8,128)(2,1)S(1)}, u32[]{:S(2)}, u32[]{:S(2)}) collective-permute-start(bf16[128,16,128]{2,1,0:T(8,128)(2,1)} %whiten.1.refs_0_), channel_id=1, source_target_pairs={{0,1},{1,2},{2,3},{3,0},{4,5},{5,6},{6,7},{7,4},{8,9},{9,10},{10,1... | collective-permute-start | bytes 1572872 | tf_op jit(solution)/shard_map/ppermute | solution.py:398
  5.4 3.1 %collective-permute-start.3 = (bf16[128,16,128]{2,1,0:T(8,128)(2,1)}, bf16[128,16,128]{2,1,0:T(8,128)(2,1)S(1)}, u32[]{:S(2)}, u32[]{:S(2)}) collective-permute-start(bf16[128,16,128]{2,1,0:T(8,128)(2,1)} %whiten.1.refs_0_), channel_id=1, source_target_pairs={{0,8},{8,0},{16,24},{24,16},{1,17},{5,13},{13,5},{17,1},{21,29},{2... | collective-permute-start | bytes 1572872 | tf_op jit(solution)/shard_map/ppermute | solution.py:275
  8.5 8.6 %collective-permute-done.refs_1_.refs_0_.refs_3_ = bf16[128,16,128]{2,1,0:T(8,128)(2,1)S(1)} collective-permute-done((bf16[128,16,128]{2,1,0:T(8,128)(2,1)}, bf16[128,16,128]{2,1,0:T(8,128)(2,1)S(1)}, u32[]{:S(2)}, u32[]{:S(2)}) %collective-permute-start) | collective-permute-done | bytes 524320 | tf_op jit(solution)/shard_map/ppermute | solution.py:398
  17.1 1.3 %collective-permute-start.1 = (bf16[128,16,128]{2,1,0:T(8,128)(2,1)S(1)}, bf16[128,16,128]{2,1,0:T(8,128)(2,1)S(1)}, u32[]{:S(2)}, u32[]{:S(2)}) collective-permute-start(bf16[128,16,128]{2,1,0:T(8,128)(2,1)S(1)} %collective-permute-done.refs_1_.refs_0_.refs_3_), channel_id=1, source_target_pairs={{0,1},{1,2},{2,3},{3,0},{4,5},{5,6},{6,7},{7,4},{8,9},{9,10},{10,1... | collective-permute-start | bytes 1572872 | tf_op jit(solution)/shard_map/ppermute | solution.py:398
  18.4 3.1 %collective-permute-start.6 = (bf16[128,16,128]{2,1,0:T(8,128)(2,1)S(1)}, bf16[128,16,128]{2,1,0:T(8,128)(2,1)S(1)}, u32[]{:S(2)}, u32[]{:S(2)}) collective-permute-start(bf16[128,16,128]{2,1,0:T(8,128)(2,1)S(1)} %collective-permute-done.refs_1_.refs_0_.refs_3_), channel_id=1, source_target_pairs={{0,8},{8,0},{16,24},{24,16},{1,17},{5,13},{13,5},{17,1},{21,29},{2... | collective-permute-start | bytes 1572872 | tf_op jit(solution)/shard_map/ppermute | solution.py:275
  21.5 0.0 collective-permute-done.3.refs_1_
  21.5 0.0 copy-start
  21.5 1.0 %copy-done = bf16[128,16,128]{2,1,0:T(8,128)(2,1)S(1)} copy-done((bf16[128,16,128]{2,1,0:T(8,128)(2,1)S(1)}, bf16[128,16,128]{2,1,0:T(8,128)(2,1)}, u32[]{:S(2)}) %copy-start) | copy-done | bytes 524312
  22.6 0.8 collective-permute-start.4
  23.4 5.5 %collective-permute-done.1.refs_2_.refs_0_.refs_6_ = bf16[128,16,128]{2,1,0:T(8,128)(2,1)S(1)} collective-permute-done((bf16[128,16,128]{2,1,0:T(8,128)(2,1)S(1)}, bf16[128,16,128]{2,1,0:T(8,128)(2,1)S(1)}, u32[]{:S(2)}, u32[]{:S(2)}) %collective-permute-start.1) | collective-permute-done | bytes 524320 | tf_op jit(solution)/shard_map/ppermute | solution.py:398
  28.9 1.5 %collective-permute-start.2 = (bf16[128,16,128]{2,1,0:T(8,128)(2,1)S(1)}, bf16[128,16,128]{2,1,0:T(8,128)(2,1)S(1)}, u32[]{:S(2)}, u32[]{:S(2)}) collective-permute-start(bf16[128,16,128]{2,1,0:T(8,128)(2,1)S(1)} %collective-permute-done.1.refs_2_.refs_0_.refs_6_), channel_id=1, source_target_pairs={{0,1},{1,2},{2,3},{3,0},{4,5},{5,6},{6,7},{7,4},{8,9},{9,10},{10,1... | collective-permute-start | bytes 1572872 | tf_op jit(solution)/shard_map/ppermute | solution.py:398
  30.5 0.0 collective-permute-done.6.refs_1_.refs_4_
  30.5 2.9 %collective-permute-start.8 = (bf16[128,16,128]{2,1,0:T(8,128)(2,1)S(1)}, bf16[128,16,128]{2,1,0:T(8,128)(2,1)S(1)}, u32[]{:S(2)}, u32[]{:S(2)}) collective-permute-start(bf16[128,16,128]{2,1,0:T(8,128)(2,1)S(1)} %collective-permute-done.1.refs_2_.refs_0_.refs_6_), channel_id=1, source_target_pairs={{0,8},{8,0},{16,24},{24,16},{1,17},{5,13},{13,5},{17,1},{21,29},{2... | collective-permute-start | bytes 1572872 | tf_op jit(solution)/shard_map/ppermute | solution.py:275
  33.3 0.1 choose.7
  33.4 0.7 collective-permute-start.7
  34.1 6.1 %collective-permute-done.2.refs_3_.refs_0_.refs_4_.refs_9_ = bf16[128,16,128]{2,1,0:T(8,128)(2,1)S(1)} collective-permute-done((bf16[128,16,128]{2,1,0:T(8,128)(2,1)S(1)}, bf16[128,16,128]{2,1,0:T(8,128)(2,1)S(1)}, u32[]{:S(2)}, u32[]{:S(2)}) %collective-permute-start.2) | collective-permute-done | bytes 524320 | tf_op jit(solution)/shard_map/ppermute | solution.py:398
  40.3 2.7 %collective-permute-start.5 = (bf16[128,16,128]{2,1,0:T(8,128)(2,1)S(1)}, bf16[128,16,128]{2,1,0:T(8,128)(2,1)S(1)}, u32[]{:S(2)}, u32[]{:S(2)}) collective-permute-start(bf16[128,16,128]{2,1,0:T(8,128)(2,1)S(1)} %collective-permute-done.2.refs_3_.refs_0_.refs_4_.refs_9_), channel_id=1, source_target_pairs={{0,8},{8,0},{16,24},{24,16},{1,17},{5,13},{13,5},{17,1},{21,29},{2... | collective-permute-start | bytes 1572872 | tf_op jit(solution)/shard_map/ppermute | solution.py:275
  43.0 0.1 choose.8
  43.1 0.7 collective-permute-start.9
  43.8 3.4 %own_rows.1.own = bf16[128,64,128]{2,1,0:T(8,128)(2,1)S(1)} custom-call(bf16[128,16,128]{2,1,0:T(8,128)(2,1)S(1)} %copy-done.1, bf16[128,16,128]{2,1,0:T(8,128)(2,1)S(1)} %collective-permute-done.refs_1_.refs_0_.refs_3_, bf16[128,16,128]{2,1,0:T(8,128)(2,1)S(1)} %collective-permute-done.1.refs_2_.refs_0_.refs_6_, ...), custom_call_target="tpu_custom_call" | custom-call | flops 1 | bytes 1 | tf_op jit(solution)/shard_map/own_rows/pallas_call | solution.py:145
  47.2 7.5 %collective-permute-done.5.refs_1_.refs_5_.refs_10_ = bf16[128,16,128]{2,1,0:T(8,128)(2,1)S(1)} collective-permute-done((bf16[128,16,128]{2,1,0:T(8,128)(2,1)S(1)}, bf16[128,16,128]{2,1,0:T(8,128)(2,1)S(1)}, u32[]{:S(2)}, u32[]{:S(2)}) %collective-permute-start.5) | collective-permute-done | bytes 524320 | tf_op jit(solution)/shard_map/ppermute | solution.py:275
  54.8 0.0 copy-start.2
  54.8 0.7 collective-permute-start.12
  55.5 0.7 collective-permute-start.10
  56.2 0.1 choose.10
  56.3 9.2 %collective-permute-start.11 = (bf16[2,128,16,128]{3,2,1,0:T(8,128)(2,1)S(1)}, bf16[2,128,16,128]{3,2,1,0:T(8,128)(2,1)S(1)}, u32[]{:S(2)}, u32[]{:S(2)}) collective-permute-start(bf16[2,128,16,128]{3,2,1,0:T(8,128)(2,1)S(1)} %choose.10), channel_id=1, source_target_pairs={{0,4},{4,0},{8,12},{12,8},{16,20},{20,16},{24,28},{28,24},{1,5},{5... | collective-permute-start | bytes 3145736 | tf_op jit(solution)/shard_map/ppermute | solution.py:275
  65.5 0.0 collective-permute-done.9.refs_2_.refs_8_
  65.5 0.1 choose.11
  65.6 9.0 %collective-permute-start.13 = (bf16[2,128,16,128]{3,2,1,0:T(8,128)(2,1)S(1)}, bf16[2,128,16,128]{3,2,1,0:T(8,128)(2,1)S(1)}, u32[]{:S(2)}, u32[]{:S(2)}) collective-permute-start(bf16[2,128,16,128]{3,2,1,0:T(8,128)(2,1)S(1)} %choose.11), channel_id=1, source_target_pairs={{0,4},{4,0},{8,12},{12,8},{16,20},{20,16},{24,28},{28,24},{1,5},{5... | collective-permute-start | bytes 3145736 | tf_op jit(solution)/shard_map/ppermute | solution.py:275
  74.6 2.3 %collective-permute-done.13.refs_13_ = bf16[2,128,16,128]{3,2,1,0:T(8,128)(2,1)S(1)} collective-permute-done((bf16[2,128,16,128]{3,2,1,0:T(8,128)(2,1)S(1)}, bf16[2,128,16,128]{3,2,1,0:T(8,128)(2,1)S(1)}, u32[]{:S(2)}, u32[]{:S(2)}) %collective-permute-start.13) | collective-permute-done | bytes 1048608 | tf_op jit(solution)/shard_map/ppermute | solution.py:275
  76.9 10.3 %stack.1 = f32[64,64,256]{2,1,0:T(8,128)} custom-call(s32[64]{0:T(128)S(1)} %copy-done.2, bf16[128,64,128]{2,1,0:T(8,128)(2,1)S(1)} %own_rows.1.own, bf16[128,16,128]{2,1,0:T(8,128)(2,1)S(1)} %copy-done.1, bf16[128,16,128]{2,1,0:T(8,128)(2,1)S(1)} %collective-permute-done.3.refs_1_, bf16[128,16,128]{2,1,0:T(8,128)(2,1)S(1)} %collective-permute-done.4.refs_2_, ...), custom_call_target="tpu_custom_call" | custom-call | flops 1 | bytes 1 | tf_op jit(solution)/shard_map/stack/pallas_call | solution.py:257
  (11 shorter events, 0.1 us)
Async XLA Ops:
  4.0 13.1 %collective-permute-start = (bf16[128,16,128]{2,1,0:T(8,128)(2,1)}, bf16[128,16,128]{2,1,0:T(8,128)(2,1)S(1)}, u32[]{:S(2)}, u32[]{:S(2)}) collective-permute-start(bf16[128,16,128]{2,1,0:T(8,128)(2,1)} %whiten.1.refs_0_), channel_id=1, source_target_pairs={{0,1},{1,2},{2,3},{3,0},{4,5},{5,6},{6,7},{7,4},{8,9},{9,10},{10,1... | collective-permute-start | bytes 1572872 | tf_op jit(solution)/shard_map/ppermute | solution.py:398
  5.4 16.1 %collective-permute-start.3 = (bf16[128,16,128]{2,1,0:T(8,128)(2,1)}, bf16[128,16,128]{2,1,0:T(8,128)(2,1)S(1)}, u32[]{:S(2)}, u32[]{:S(2)}) collective-permute-start(bf16[128,16,128]{2,1,0:T(8,128)(2,1)} %whiten.1.refs_0_), channel_id=1, source_target_pairs={{0,8},{8,0},{16,24},{24,16},{1,17},{5,13},{13,5},{17,1},{21,29},{2... | collective-permute-start | bytes 1572872 | tf_op jit(solution)/shard_map/ppermute | solution.py:275
  17.1 11.9 %collective-permute-start.1 = (bf16[128,16,128]{2,1,0:T(8,128)(2,1)S(1)}, bf16[128,16,128]{2,1,0:T(8,128)(2,1)S(1)}, u32[]{:S(2)}, u32[]{:S(2)}) collective-permute-start(bf16[128,16,128]{2,1,0:T(8,128)(2,1)S(1)} %collective-permute-done.refs_1_.refs_0_.refs_3_), channel_id=1, source_target_pairs={{0,1},{1,2},{2,3},{3,0},{4,5},{5,6},{6,7},{7,4},{8,9},{9,10},{10,1... | collective-permute-start | bytes 1572872 | tf_op jit(solution)/shard_map/ppermute | solution.py:398
  18.4 12.1 %collective-permute-start.6 = (bf16[128,16,128]{2,1,0:T(8,128)(2,1)S(1)}, bf16[128,16,128]{2,1,0:T(8,128)(2,1)S(1)}, u32[]{:S(2)}, u32[]{:S(2)}) collective-permute-start(bf16[128,16,128]{2,1,0:T(8,128)(2,1)S(1)} %collective-permute-done.refs_1_.refs_0_.refs_3_), channel_id=1, source_target_pairs={{0,8},{8,0},{16,24},{24,16},{1,17},{5,13},{13,5},{17,1},{21,29},{2... | collective-permute-start | bytes 1572872 | tf_op jit(solution)/shard_map/ppermute | solution.py:275
  21.5 1.0 %copy-start = (bf16[128,16,128]{2,1,0:T(8,128)(2,1)S(1)}, bf16[128,16,128]{2,1,0:T(8,128)(2,1)}, u32[]{:S(2)}) copy-start(bf16[128,16,128]{2,1,0:T(8,128)(2,1)} %whiten.1.refs_0_) | copy-start | bytes 1572868
  22.5 21.2 %copy-start.1 = (bf16[128,16,128]{2,1,0:T(8,128)(2,1)S(1)}, bf16[128,16,128]{2,1,0:T(8,128)(2,1)}, u32[]{:S(2)}) copy-start(bf16[128,16,128]{2,1,0:T(8,128)(2,1)} %whiten.1.refs_0_) | copy-start | bytes 1572868
  22.6 10.8 %collective-permute-start.4 = (bf16[128,16,128]{2,1,0:T(8,128)(2,1)S(1)}, bf16[128,16,128]{2,1,0:T(8,128)(2,1)S(1)}, u32[]{:S(2)}, u32[]{:S(2)}) collective-permute-start(bf16[128,16,128]{2,1,0:T(8,128)(2,1)S(1)} %bitcast.6), channel_id=1, source_target_pairs={{8,24},{24,8},{1,9},{9,1},{13,29},{17,25},{25,17},{29,13},{2,10},{... | collective-permute-start | bytes 1572872 | tf_op jit(solution)/shard_map/ppermute | solution.py:275
  28.9 11.3 %collective-permute-start.2 = (bf16[128,16,128]{2,1,0:T(8,128)(2,1)S(1)}, bf16[128,16,128]{2,1,0:T(8,128)(2,1)S(1)}, u32[]{:S(2)}, u32[]{:S(2)}) collective-permute-start(bf16[128,16,128]{2,1,0:T(8,128)(2,1)S(1)} %collective-permute-done.1.refs_2_.refs_0_.refs_6_), channel_id=1, source_target_pairs={{0,1},{1,2},{2,3},{3,0},{4,5},{5,6},{6,7},{7,4},{8,9},{9,10},{10,1... | collective-permute-start | bytes 1572872 | tf_op jit(solution)/shard_map/ppermute | solution.py:398
  30.5 12.5 %collective-permute-start.8 = (bf16[128,16,128]{2,1,0:T(8,128)(2,1)S(1)}, bf16[128,16,128]{2,1,0:T(8,128)(2,1)S(1)}, u32[]{:S(2)}, u32[]{:S(2)}) collective-permute-start(bf16[128,16,128]{2,1,0:T(8,128)(2,1)S(1)} %collective-permute-done.1.refs_2_.refs_0_.refs_6_), channel_id=1, source_target_pairs={{0,8},{8,0},{16,24},{24,16},{1,17},{5,13},{13,5},{17,1},{21,29},{2... | collective-permute-start | bytes 1572872 | tf_op jit(solution)/shard_map/ppermute | solution.py:275
  33.4 9.6 %collective-permute-start.7 = (bf16[128,16,128]{2,1,0:T(8,128)(2,1)S(1)}, bf16[128,16,128]{2,1,0:T(8,128)(2,1)S(1)}, u32[]{:S(2)}, u32[]{:S(2)}) collective-permute-start(bf16[128,16,128]{2,1,0:T(8,128)(2,1)S(1)} %bitcast.7), channel_id=1, source_target_pairs={{8,24},{24,8},{1,9},{9,1},{13,29},{17,25},{25,17},{29,13},{2,10},{... | collective-permute-start | bytes 1572872 | tf_op jit(solution)/shard_map/ppermute | solution.py:275
  40.3 14.5 %collective-permute-start.5 = (bf16[128,16,128]{2,1,0:T(8,128)(2,1)S(1)}, bf16[128,16,128]{2,1,0:T(8,128)(2,1)S(1)}, u32[]{:S(2)}, u32[]{:S(2)}) collective-permute-start(bf16[128,16,128]{2,1,0:T(8,128)(2,1)S(1)} %collective-permute-done.2.refs_3_.refs_0_.refs_4_.refs_9_), channel_id=1, source_target_pairs={{0,8},{8,0},{16,24},{24,16},{1,17},{5,13},{13,5},{17,1},{21,29},{2... | collective-permute-start | bytes 1572872 | tf_op jit(solution)/shard_map/ppermute | solution.py:275
  43.1 22.5 %collective-permute-start.9 = (bf16[128,16,128]{2,1,0:T(8,128)(2,1)S(1)}, bf16[128,16,128]{2,1,0:T(8,128)(2,1)S(1)}, u32[]{:S(2)}, u32[]{:S(2)}) collective-permute-start(bf16[128,16,128]{2,1,0:T(8,128)(2,1)S(1)} %bitcast.4), channel_id=1, source_target_pairs={{8,24},{24,8},{1,9},{9,1},{13,29},{17,25},{25,17},{29,13},{2,10},{... | collective-permute-start | bytes 1572872 | tf_op jit(solution)/shard_map/ppermute | solution.py:275
  54.8 22.2 %copy-start.2 = (s32[64]{0:T(128)S(1)}, s32[64]{0:T(128)}, u32[]{:S(2)}) copy-start(s32[64]{0:T(128)} %reach_ref.1) | copy-start | bytes 772
  54.8 10.8 %collective-permute-start.12 = (bf16[128,16,128]{2,1,0:T(8,128)(2,1)S(1)}, bf16[128,16,128]{2,1,0:T(8,128)(2,1)S(1)}, u32[]{:S(2)}, u32[]{:S(2)}) collective-permute-start(bf16[128,16,128]{2,1,0:T(8,128)(2,1)S(1)} %collective-permute-done.2.refs_3_.refs_0_.refs_4_.refs_9_), channel_id=1, source_target_pairs={{3,19},{11,27},{19,3},{27,11}} | collective-permute-start | bytes 1572872 | tf_op jit(solution)/shard_map/ppermute | solution.py:275
  55.5 10.1 %collective-permute-start.10 = (bf16[128,16,128]{2,1,0:T(8,128)(2,1)S(1)}, bf16[128,16,128]{2,1,0:T(8,128)(2,1)S(1)}, u32[]{:S(2)}, u32[]{:S(2)}) collective-permute-start(bf16[128,16,128]{2,1,0:T(8,128)(2,1)S(1)} %bitcast.5), channel_id=1, source_target_pairs={{8,24},{24,8},{1,9},{9,1},{13,29},{17,25},{25,17},{29,13},{2,10},{... | collective-permute-start | bytes 1572872 | tf_op jit(solution)/shard_map/ppermute | solution.py:275
  56.3 18.4 %collective-permute-start.11 = (bf16[2,128,16,128]{3,2,1,0:T(8,128)(2,1)S(1)}, bf16[2,128,16,128]{3,2,1,0:T(8,128)(2,1)S(1)}, u32[]{:S(2)}, u32[]{:S(2)}) collective-permute-start(bf16[2,128,16,128]{3,2,1,0:T(8,128)(2,1)S(1)} %choose.10), channel_id=1, source_target_pairs={{0,4},{4,0},{8,12},{12,8},{16,20},{20,16},{24,28},{28,24},{1,5},{5... | collective-permute-start | bytes 3145736 | tf_op jit(solution)/shard_map/ppermute | solution.py:275
  65.6 11.3 %collective-permute-start.13 = (bf16[2,128,16,128]{3,2,1,0:T(8,128)(2,1)S(1)}, bf16[2,128,16,128]{3,2,1,0:T(8,128)(2,1)S(1)}, u32[]{:S(2)}, u32[]{:S(2)}) collective-permute-start(bf16[2,128,16,128]{3,2,1,0:T(8,128)(2,1)S(1)} %choose.11), channel_id=1, source_target_pairs={{0,4},{4,0},{8,12},{12,8},{16,20},{20,16},{24,28},{28,24},{1,5},{5... | collective-permute-start | bytes 3145736 | tf_op jit(solution)/shard_map/ppermute | solution.py:275

commit v8 on v7

--- a/solution.py
+++ b/solution.py
@@ -106,13 +106,13 @@
 def choose_kernel(code_of, groups, *refs):
     out_ref = refs[-1]
     per_group = (len(refs) - 1) // groups
-    code = code_of()
+    codes = code_of()
     for g in range(groups):
 
         def put(ref, g=g):
             out_ref[g] = ref[...]
 
-        copy_chosen(code, refs[g * per_group : (g + 1) * per_group], put)
+        copy_chosen(codes[g], refs[g * per_group : (g + 1) * per_group], put)
 
 
 def choose(code_of, groups):
@@ -300,36 +300,53 @@
     return own_rows(pieces), buffers, groups, lambda: (0, 1, 0, 1)
 
 
-def square_codes():
+def square_codes(last):
     z, c = lax.axis_index("win"), lax.axis_index("chan")
     core, x = c & 1, (c >> 1) & 1
-    onward = jnp.where((z == 0) | (x == 0) | ((z < 3) & (core == 1)), 1, 0)
-    odd_next = jnp.where(x == 0, 1, 2)
-    even_next = jnp.where(z == 0, odd_next, 2)
-    next_code = jnp.where(core == 0, even_next, jnp.where(z == 3, 2, odd_next))
-    outgoing = jnp.where(core == 0, jnp.where(z < 2, next_code, 1), jnp.where(z < 2, 0, next_code))
+    if last:
+        onward = jnp.where((z == 0) | (x == 0) | ((z < 3) & (core == 1)), 1, 0)
+        odd_next = jnp.where(x == 0, 1, 2)
+        even_next = jnp.where(z == 0, odd_next, 2)
+        next_code = jnp.where(core == 0, even_next, jnp.where(z == 3, 2, odd_next))
+        is_late = (z == 3) & (core == 0)
+    else:
+        onward = jnp.where(x == 0, 1, 0)
+        next_code = jnp.int32(2)
+        is_late = jnp.bool_(False)
+    outgoing = jnp.where(
+        core == 0,
+        jnp.where(z < 2, next_code, jnp.where(is_late, 3, 1)),
+        jnp.where(z < 2, 0, next_code),
+    )
     first = jnp.where(z == 0, 0, jnp.where(z == 2, next_code, 3))
-    second = jnp.where(z == 1, next_code, jnp.where(z == 3, 1, 3))
-    is_late = (z == 3) & (core == 0)
-    outgoing_late = jnp.where(is_late, 3, outgoing)
-    second_last = jnp.where(is_late, 4, second)
-    return onward, outgoing, outgoing_late, (first, second, first, second_last)
+    second = jnp.where(z == 1, next_code, jnp.where(z == 3, jnp.where(is_late, 4, 1), 3))
+    return onward, outgoing, first, second
 
 
 def square_partners(pieces, n_win, n_chan):
     def pairs(target):
         return pairs_of(n_win, n_chan, lambda z, c: target(z, c, c % 2, c // 2 % 2))
 
+    def crosses(z, core):
+        return core == 0 if z == 0 else core == 1 if z == 3 else True
+
     def first_target(z, c, core, x):
+        needed = z == 3 or (z == 2 and core == 0) or (x == 0 and crosses(z, core))
+        return c ^ 4 if needed else None
+
+    def second_target(z, c, core, x):
+        return c ^ 2 if crosses(z, core) else None
+
+    def first_target_last(z, c, core, x):
         if z == 3:
-            return c ^ 4
+            return c ^ 4 if core == 1 else None
         if z == 0:
             return c ^ 2 if core == 0 else None
         if core == 1:
             return c ^ 2
         return c ^ 4 if z == 2 or x == 0 else None
 
-    def second_target(z, c, core, x):
+    def second_target_last(z, c, core, x):
         if z == 3:
             return c ^ 2 if core == 1 else None
         if z == 0:
@@ -346,45 +363,41 @@
     firsts, seconds = [], []
 
     def second_move(slot, arrived, *others):
-        relay = choose(lambda: square_codes()[0], [(pieces[slot], arrived)])[0]
-        relay = after(relay, *others)
-        seconds.append(send(relay, pairs(second_target)))
+        last = slot == count - 1
+        relay = choose(lambda: (square_codes(last)[0],), [(pieces[slot], arrived)])[0]
+        target = second_target_last if last else second_target
+        seconds.append(send(after(relay, *others), pairs(target)))
         return relay
 
     for slot, piece in enumerate(pieces):
-        last = slot == count - 1
-
-        firsts.append(
-            send(
-                piece,
-                pairs(
-                    lambda z, c, core, x: (
-                        None if last and z == 3 and core == 0 else first_target(z, c, core, x)
-                    )
-                ),
-            )
-        )
+        target = first_target_last if slot == count - 1 else first_target
+        firsts.append(send(piece, pairs(target)))
         if slot:
-            second_move(slot - 1, after(firsts[slot - 1], pieces[slot]), *seconds[-1:])
+            second_move(slot - 1, after(firsts[slot - 1], piece), *seconds[-1:])
     held = list(zip(pieces, firsts, seconds))
     own = own_rows(pieces)
     held[0] = (*held[0][:2], after(held[0][2], firsts[-1]))
-    swapped_early = swap(lambda: square_codes()[1], held[:half])
+    swapped_early = swap(lambda: (square_codes(False)[1],) * half, held[:half])
     relay = second_move(count - 1, after(firsts[-1], own))
     held.append((pieces[-1], firsts[-1], seconds[-1]))
     late = send(
         after(pieces[-1], relay),
         pairs(lambda z, c, core, x: c ^ 4 if z == 3 and core == 0 else None),
     )
+
+    def late_codes():
+        plain = square_codes(False)[1]
+        return (plain,) * (count - half - 1) + (square_codes(True)[1],)
+
     late_groups = [(*group, group[1]) for group in held[half:-1]] + [(*held[-1], late)]
-    swapped_late = swap(lambda: square_codes()[2], late_groups)
+    swapped_late = swap(late_codes, late_groups)
     buffers = [buffer for group in held for buffer in group] + [swapped_early, swapped_late, late]
     groups = []
     for n in range(count):
         swapped = (3 * count, n) if n < half else (3 * count + 1, n - half)
         groups.append([(3 * n, None), (3 * n + 1, None), (3 * n + 2, None), swapped])
     groups[-1].append((3 * count + 2, None))
-    return own, buffers, groups, lambda: square_codes()[3]
+    return own, buffers, groups, lambda: square_codes(False)[2:] + square_codes(True)[2:]
 
 
 def on_device(traces, valid, reach):

time: 87.6 us -> 87.8 us (level)
  the two profiles are of different devices: /device:TPU:17 before, /device:TPU:11 now
where the time goes in v8:
time: 87.8 us; the launch traced here: 86.5 us
  waiting for transfers between devices  33.6 us (38%)
  starting transfers between devices  33.5 us (38%)
  Pallas kernels  18.1 us (21%)
  local copies, waits for them, and re-layouts  1.05 us (1%)
    ppermute x11, starting transfers between devices, send(): return lax.ppermute(array, AXES, pairs)  30.6 us
    ppermute x3, waiting for transfers between devices, on_device(): pieces.append(lax.ppermute(pieces[-1], 'win', ring))  20.7 us
    ppermute x11, waiting for transfers between devices, send(): return lax.ppermute(array, AXES, pairs)  12.9 us
    pallas_call x1, Pallas kernels, stacked(): pl.pallas_call(functools.partial(stack_kernel, 1.0 / math.sqrt(windows),...  10.3 us
    pallas_call x1, Pallas kernels, whitened_chunk(): pl.pallas_call(whiten_kernel, out_shape=jax.ShapeDtypeStruct((F, windows,...  4 us
    pallas_call x1, Pallas kernels, own_rows(): pl.pallas_call(own_kernel, out_shape=jax.ShapeDtypeStruct((bins, lanes //...  3.44 us
    ppermute x3, starting transfers between devices, on_device(): pieces.append(lax.ppermute(pieces[-1], 'win', ring))  2.93 us
  transfers between devices with their start and end apart: 14, of which 8 were waited for; matrix products, arithmetic and copies ran while one was open for 0% of the time, Pallas kernels for 4%

profile of v8, /device:TPU:11, one launch (start us, length us, event | category | flops | bytes accessed | tf_op | source)
XLA Modules:
  0.0 86.5 jit_solution(17428860684487168407)
XLA Ops:
  0.0 4.0 %whiten.1.refs_0_ = bf16[128,16,128]{2,1,0:T(8,128)(2,1)} custom-call(bf16[256,512]{1,0:T(8,128)(2,1)} %constant.3.table_hbm, bf16[16,64,512]{2,1,0:T(8,128)(2,1)} %traces_hbm.1, s32[16,64]{1,0:T(8,128)} %valid_hbm.1), custom_call_target="tpu_custom_call" | custom-call | flops 268435456 | bytes 1048576 | tf_op jit(solution)/shard_map/whiten/pallas_call | solution.py:78
  4.0 1.3 %collective-permute-start = (bf16[128,16,128]{2,1,0:T(8,128)(2,1)}, bf16[128,16,128]{2,1,0:T(8,128)(2,1)S(1)}, u32[]{:S(2)}, u32[]{:S(2)}) collective-permute-start(bf16[128,16,128]{2,1,0:T(8,128)(2,1)} %whiten.1.refs_0_), channel_id=1, source_target_pairs={{0,1},{1,2},{2,3},{3,0},{4,5},{5,6},{6,7},{7,4},{8,9},{9,10},{10,1... | collective-permute-start | bytes 1572872 | tf_op jit(solution)/shard_map/ppermute | solution.py:411
  5.4 0.7 collective-permute-start.3
  6.0 11.0 %collective-permute-done.refs_1_.refs_0_.refs_3_ = bf16[128,16,128]{2,1,0:T(8,128)(2,1)S(1)} collective-permute-done((bf16[128,16,128]{2,1,0:T(8,128)(2,1)}, bf16[128,16,128]{2,1,0:T(8,128)(2,1)S(1)}, u32[]{:S(2)}, u32[]{:S(2)}) %collective-permute-start) | collective-permute-done | bytes 524320 | tf_op jit(solution)/shard_map/ppermute | solution.py:411
  17.1 1.3 %collective-permute-start.1 = (bf16[128,16,128]{2,1,0:T(8,128)(2,1)S(1)}, bf16[128,16,128]{2,1,0:T(8,128)(2,1)S(1)}, u32[]{:S(2)}, u32[]{:S(2)}) collective-permute-start(bf16[128,16,128]{2,1,0:T(8,128)(2,1)S(1)} %collective-permute-done.refs_1_.refs_0_.refs_3_), channel_id=1, source_target_pairs={{0,1},{1,2},{2,3},{3,0},{4,5},{5,6},{6,7},{7,4},{8,9},{9,10},{10,1... | collective-permute-start | bytes 1572872 | tf_op jit(solution)/shard_map/ppermute | solution.py:411
  18.4 0.7 collective-permute-start.6
  19.1 0.0 copy-start
  19.1 1.0 %copy-done = bf16[128,16,128]{2,1,0:T(8,128)(2,1)S(1)} copy-done((bf16[128,16,128]{2,1,0:T(8,128)(2,1)S(1)}, bf16[128,16,128]{2,1,0:T(8,128)(2,1)}, u32[]{:S(2)}) %copy-start) | copy-done | bytes 524312
  20.1 4.7 %collective-permute-start.4 = (bf16[128,16,128]{2,1,0:T(8,128)(2,1)S(1)}, bf16[128,16,128]{2,1,0:T(8,128)(2,1)S(1)}, u32[]{:S(2)}, u32[]{:S(2)}) collective-permute-start(bf16[128,16,128]{2,1,0:T(8,128)(2,1)S(1)} %bitcast.6), channel_id=1, source_target_pairs={{0,8},{8,0},{16,24},{24,16},{1,9},{5,13},{9,1},{13,5},{17,25},{21,... | collective-permute-start | bytes 1572872 | tf_op jit(solution)/shard_map/ppermute | solution.py:275
  24.9 5.0 %collective-permute-done.1.refs_2_.refs_0_.refs_6_ = bf16[128,16,128]{2,1,0:T(8,128)(2,1)S(1)} collective-permute-done((bf16[128,16,128]{2,1,0:T(8,128)(2,1)S(1)}, bf16[128,16,128]{2,1,0:T(8,128)(2,1)S(1)}, u32[]{:S(2)}, u32[]{:S(2)}) %collective-permute-start.1) | collective-permute-done | bytes 524320 | tf_op jit(solution)/shard_map/ppermute | solution.py:411
  29.9 0.3 collective-permute-start.2
  30.2 0.7 collective-permute-start.8
  30.9 0.1 choose.7
  31.0 4.0 %collective-permute-done.4.refs_2_ = bf16[128,16,128]{2,1,0:T(8,128)(2,1)S(1)} collective-permute-done((bf16[128,16,128]{2,1,0:T(8,128)(2,1)S(1)}, bf16[128,16,128]{2,1,0:T(8,128)(2,1)S(1)}, u32[]{:S(2)}, u32[]{:S(2)}) %collective-permute-start.4) | collective-permute-done | bytes 524320 | tf_op jit(solution)/shard_map/ppermute | solution.py:275
  35.0 3.1 %collective-permute-start.7 = (bf16[128,16,128]{2,1,0:T(8,128)(2,1)S(1)}, bf16[128,16,128]{2,1,0:T(8,128)(2,1)S(1)}, u32[]{:S(2)}, u32[]{:S(2)}) collective-permute-start(bf16[128,16,128]{2,1,0:T(8,128)(2,1)S(1)} %bitcast.7), channel_id=1, source_target_pairs={{0,8},{8,0},{16,24},{24,16},{1,9},{5,13},{9,1},{13,5},{17,25},{21,... | collective-permute-start | bytes 1572872 | tf_op jit(solution)/shard_map/ppermute | solution.py:275
  38.1 4.7 %collective-permute-done.2.refs_3_.refs_0_.refs_4_.refs_9_ = bf16[128,16,128]{2,1,0:T(8,128)(2,1)S(1)} collective-permute-done((bf16[128,16,128]{2,1,0:T(8,128)(2,1)S(1)}, bf16[128,16,128]{2,1,0:T(8,128)(2,1)S(1)}, u32[]{:S(2)}, u32[]{:S(2)}) %collective-permute-start.2) | collective-permute-done | bytes 524320 | tf_op jit(solution)/shard_map/ppermute | solution.py:411
  42.7 2.9 %collective-permute-start.5 = (bf16[128,16,128]{2,1,0:T(8,128)(2,1)S(1)}, bf16[128,16,128]{2,1,0:T(8,128)(2,1)S(1)}, u32[]{:S(2)}, u32[]{:S(2)}) collective-permute-start(bf16[128,16,128]{2,1,0:T(8,128)(2,1)S(1)} %collective-permute-done.2.refs_3_.refs_0_.refs_4_.refs_9_), channel_id=1, source_target_pairs={{0,8},{8,0},{16,24},{24,16},{1,17},{5,13},{13,5},{17,1},{21,29},{2... | collective-permute-start | bytes 1572872 | tf_op jit(solution)/shard_map/ppermute | solution.py:275
  45.6 0.1 choose.8
  45.7 1.9 %collective-permute-done.7.refs_5_ = bf16[128,16,128]{2,1,0:T(8,128)(2,1)S(1)} collective-permute-done((bf16[128,16,128]{2,1,0:T(8,128)(2,1)S(1)}, bf16[128,16,128]{2,1,0:T(8,128)(2,1)S(1)}, u32[]{:S(2)}, u32[]{:S(2)}) %collective-permute-start.7) | collective-permute-done | bytes 524320 | tf_op jit(solution)/shard_map/ppermute | solution.py:275
  47.5 2.8 %collective-permute-start.9 = (bf16[128,16,128]{2,1,0:T(8,128)(2,1)S(1)}, bf16[128,16,128]{2,1,0:T(8,128)(2,1)S(1)}, u32[]{:S(2)}, u32[]{:S(2)}) collective-permute-start(bf16[128,16,128]{2,1,0:T(8,128)(2,1)S(1)} %bitcast.4), channel_id=1, source_target_pairs={{0,8},{8,0},{16,24},{24,16},{1,9},{5,13},{9,1},{13,5},{17,25},{21,... | collective-permute-start | bytes 1572872 | tf_op jit(solution)/shard_map/ppermute | solution.py:275
  50.4 3.4 %own_rows.1.own = bf16[128,64,128]{2,1,0:T(8,128)(2,1)S(1)} custom-call(bf16[128,16,128]{2,1,0:T(8,128)(2,1)S(1)} %copy-done.1, bf16[128,16,128]{2,1,0:T(8,128)(2,1)S(1)} %collective-permute-done.refs_1_.refs_0_.refs_3_, bf16[128,16,128]{2,1,0:T(8,128)(2,1)S(1)} %collective-permute-done.1.refs_2_.refs_0_.refs_6_, ...), custom_call_target="tpu_custom_call" | custom-call | flops 1 | bytes 1 | tf_op jit(solution)/shard_map/own_rows/pallas_call | solution.py:145
  53.8 2.3 %collective-permute-done.5.refs_1_.refs_5_.refs_10_ = bf16[128,16,128]{2,1,0:T(8,128)(2,1)S(1)} collective-permute-done((bf16[128,16,128]{2,1,0:T(8,128)(2,1)S(1)}, bf16[128,16,128]{2,1,0:T(8,128)(2,1)S(1)}, u32[]{:S(2)}, u32[]{:S(2)}) %collective-permute-start.5) | collective-permute-done | bytes 524320 | tf_op jit(solution)/shard_map/ppermute | solution.py:275
  56.2 0.0 copy-start.2
  56.2 0.7 collective-permute-start.12
  56.9 2.1 %collective-permute-start.10 = (bf16[128,16,128]{2,1,0:T(8,128)(2,1)S(1)}, bf16[128,16,128]{2,1,0:T(8,128)(2,1)S(1)}, u32[]{:S(2)}, u32[]{:S(2)}) collective-permute-start(bf16[128,16,128]{2,1,0:T(8,128)(2,1)S(1)} %bitcast.5), channel_id=1, source_target_pairs={{8,24},{24,8},{1,9},{9,1},{13,29},{17,25},{25,17},{29,13},{2,10},{... | collective-permute-start | bytes 1572872 | tf_op jit(solution)/shard_map/ppermute | solution.py:275
  59.1 0.1 choose.10
  59.2 5.6 %collective-permute-start.11 = (bf16[2,128,16,128]{3,2,1,0:T(8,128)(2,1)S(1)}, bf16[2,128,16,128]{3,2,1,0:T(8,128)(2,1)S(1)}, u32[]{:S(2)}, u32[]{:S(2)}) collective-permute-start(bf16[2,128,16,128]{3,2,1,0:T(8,128)(2,1)S(1)} %choose.10), channel_id=1, source_target_pairs={{0,4},{4,0},{8,12},{12,8},{16,20},{20,16},{24,28},{28,24},{1,5},{5... | collective-permute-start | bytes 3145736 | tf_op jit(solution)/shard_map/ppermute | solution.py:275
  64.8 2.4 %collective-permute-done.10.refs_6_.refs_11_ = bf16[128,16,128]{2,1,0:T(8,128)(2,1)S(1)} collective-permute-done((bf16[128,16,128]{2,1,0:T(8,128)(2,1)S(1)}, bf16[128,16,128]{2,1,0:T(8,128)(2,1)S(1)}, u32[]{:S(2)}, u32[]{:S(2)}) %collective-permute-start.10) | collective-permute-done | bytes 524320 | tf_op jit(solution)/shard_map/ppermute | solution.py:275
  67.1 0.1 choose.11
  67.2 6.6 %collective-permute-start.13 = (bf16[2,128,16,128]{3,2,1,0:T(8,128)(2,1)S(1)}, bf16[2,128,16,128]{3,2,1,0:T(8,128)(2,1)S(1)}, u32[]{:S(2)}, u32[]{:S(2)}) collective-permute-start(bf16[2,128,16,128]{3,2,1,0:T(8,128)(2,1)S(1)} %choose.11), channel_id=1, source_target_pairs={{0,4},{4,0},{8,12},{12,8},{16,20},{20,16},{24,28},{28,24},{1,5},{5... | collective-permute-start | bytes 3145736 | tf_op jit(solution)/shard_map/ppermute | solution.py:275
  73.9 2.3 %collective-permute-done.13.refs_13_ = bf16[2,128,16,128]{3,2,1,0:T(8,128)(2,1)S(1)} collective-permute-done((bf16[2,128,16,128]{3,2,1,0:T(8,128)(2,1)S(1)}, bf16[2,128,16,128]{3,2,1,0:T(8,128)(2,1)S(1)}, u32[]{:S(2)}, u32[]{:S(2)}) %collective-permute-start.13) | collective-permute-done | bytes 1048608 | tf_op jit(solution)/shard_map/ppermute | solution.py:275
  76.1 10.3 %stack.1 = f32[64,64,256]{2,1,0:T(8,128)} custom-call(s32[64]{0:T(128)S(1)} %copy-done.2, bf16[128,64,128]{2,1,0:T(8,128)(2,1)S(1)} %own_rows.1.own, bf16[128,16,128]{2,1,0:T(8,128)(2,1)S(1)} %copy-done.1, bf16[128,16,128]{2,1,0:T(8,128)(2,1)S(1)} %collective-permute-done.3.refs_1_, bf16[128,16,128]{2,1,0:T(8,128)(2,1)S(1)} %collective-permute-done.4.refs_2_, ...), custom_call_target="tpu_custom_call" | custom-call | flops 1 | bytes 1 | tf_op jit(solution)/shard_map/stack/pallas_call | solution.py:257
  (11 shorter events, 0.1 us)
Async XLA Ops:
  4.0 13.1 %collective-permute-start = (bf16[128,16,128]{2,1,0:T(8,128)(2,1)}, bf16[128,16,128]{2,1,0:T(8,128)(2,1)S(1)}, u32[]{:S(2)}, u32[]{:S(2)}) collective-permute-start(bf16[128,16,128]{2,1,0:T(8,128)(2,1)} %whiten.1.refs_0_), channel_id=1, source_target_pairs={{0,1},{1,2},{2,3},{3,0},{4,5},{5,6},{6,7},{7,4},{8,9},{9,10},{10,1... | collective-permute-start | bytes 1572872 | tf_op jit(solution)/shard_map/ppermute | solution.py:411
  5.4 13.7 %collective-permute-start.3 = (bf16[128,16,128]{2,1,0:T(8,128)(2,1)}, bf16[128,16,128]{2,1,0:T(8,128)(2,1)S(1)}, u32[]{:S(2)}, u32[]{:S(2)}) collective-permute-start(bf16[128,16,128]{2,1,0:T(8,128)(2,1)} %whiten.1.refs_0_), channel_id=1, source_target_pairs={{0,16},{16,0},{1,17},{5,21},{17,1},{21,5},{2,18},{6,22},{10,26},{1... | collective-permute-start | bytes 1572872 | tf_op jit(solution)/shard_map/ppermute | solution.py:275
  17.1 12.9 %collective-permute-start.1 = (bf16[128,16,128]{2,1,0:T(8,128)(2,1)S(1)}, bf16[128,16,128]{2,1,0:T(8,128)(2,1)S(1)}, u32[]{:S(2)}, u32[]{:S(2)}) collective-permute-start(bf16[128,16,128]{2,1,0:T(8,128)(2,1)S(1)} %collective-permute-done.refs_1_.refs_0_.refs_3_), channel_id=1, source_target_pairs={{0,1},{1,2},{2,3},{3,0},{4,5},{5,6},{6,7},{7,4},{8,9},{9,10},{10,1... | collective-permute-start | bytes 1572872 | tf_op jit(solution)/shard_map/ppermute | solution.py:411
  18.4 11.9 %collective-permute-start.6 = (bf16[128,16,128]{2,1,0:T(8,128)(2,1)S(1)}, bf16[128,16,128]{2,1,0:T(8,128)(2,1)S(1)}, u32[]{:S(2)}, u32[]{:S(2)}) collective-permute-start(bf16[128,16,128]{2,1,0:T(8,128)(2,1)S(1)} %collective-permute-done.refs_1_.refs_0_.refs_3_), channel_id=1, source_target_pairs={{0,16},{16,0},{1,17},{5,21},{17,1},{21,5},{2,18},{6,22},{10,26},{1... | collective-permute-start | bytes 1572872 | tf_op jit(solution)/shard_map/ppermute | solution.py:275
  19.1 1.0 %copy-start = (bf16[128,16,128]{2,1,0:T(8,128)(2,1)S(1)}, bf16[128,16,128]{2,1,0:T(8,128)(2,1)}, u32[]{:S(2)}) copy-start(bf16[128,16,128]{2,1,0:T(8,128)(2,1)} %whiten.1.refs_0_) | copy-start | bytes 1572868
  20.1 30.3 %copy-start.1 = (bf16[128,16,128]{2,1,0:T(8,128)(2,1)S(1)}, bf16[128,16,128]{2,1,0:T(8,128)(2,1)}, u32[]{:S(2)}) copy-start(bf16[128,16,128]{2,1,0:T(8,128)(2,1)} %whiten.1.refs_0_) | copy-start | bytes 1572868
  20.1 14.9 %collective-permute-start.4 = (bf16[128,16,128]{2,1,0:T(8,128)(2,1)S(1)}, bf16[128,16,128]{2,1,0:T(8,128)(2,1)S(1)}, u32[]{:S(2)}, u32[]{:S(2)}) collective-permute-start(bf16[128,16,128]{2,1,0:T(8,128)(2,1)S(1)} %bitcast.6), channel_id=1, source_target_pairs={{0,8},{8,0},{16,24},{24,16},{1,9},{5,13},{9,1},{13,5},{17,25},{21,... | collective-permute-start | bytes 1572872 | tf_op jit(solution)/shard_map/ppermute | solution.py:275
  29.9 12.8 %collective-permute-start.2 = (bf16[128,16,128]{2,1,0:T(8,128)(2,1)S(1)}, bf16[128,16,128]{2,1,0:T(8,128)(2,1)S(1)}, u32[]{:S(2)}, u32[]{:S(2)}) collective-permute-start(bf16[128,16,128]{2,1,0:T(8,128)(2,1)S(1)} %collective-permute-done.1.refs_2_.refs_0_.refs_6_), channel_id=1, source_target_pairs={{0,1},{1,2},{2,3},{3,0},{4,5},{5,6},{6,7},{7,4},{8,9},{9,10},{10,1... | collective-permute-start | bytes 1572872 | tf_op jit(solution)/shard_map/ppermute | solution.py:411
  30.2 15.4 %collective-permute-start.8 = (bf16[128,16,128]{2,1,0:T(8,128)(2,1)S(1)}, bf16[128,16,128]{2,1,0:T(8,128)(2,1)S(1)}, u32[]{:S(2)}, u32[]{:S(2)}) collective-permute-start(bf16[128,16,128]{2,1,0:T(8,128)(2,1)S(1)} %collective-permute-done.1.refs_2_.refs_0_.refs_6_), channel_id=1, source_target_pairs={{0,16},{16,0},{1,17},{5,21},{17,1},{21,5},{2,18},{6,22},{10,26},{1... | collective-permute-start | bytes 1572872 | tf_op jit(solution)/shard_map/ppermute | solution.py:275
  35.0 12.5 %collective-permute-start.7 = (bf16[128,16,128]{2,1,0:T(8,128)(2,1)S(1)}, bf16[128,16,128]{2,1,0:T(8,128)(2,1)S(1)}, u32[]{:S(2)}, u32[]{:S(2)}) collective-permute-start(bf16[128,16,128]{2,1,0:T(8,128)(2,1)S(1)} %bitcast.7), channel_id=1, source_target_pairs={{0,8},{8,0},{16,24},{24,16},{1,9},{5,13},{9,1},{13,5},{17,25},{21,... | collective-permute-start | bytes 1572872 | tf_op jit(solution)/shard_map/ppermute | solution.py:275
  42.7 13.4 %collective-permute-start.5 = (bf16[128,16,128]{2,1,0:T(8,128)(2,1)S(1)}, bf16[128,16,128]{2,1,0:T(8,128)(2,1)S(1)}, u32[]{:S(2)}, u32[]{:S(2)}) collective-permute-start(bf16[128,16,128]{2,1,0:T(8,128)(2,1)S(1)} %collective-permute-done.2.refs_3_.refs_0_.refs_4_.refs_9_), channel_id=1, source_target_pairs={{0,8},{8,0},{16,24},{24,16},{1,17},{5,13},{13,5},{17,1},{21,29},{2... | collective-permute-start | bytes 1572872 | tf_op jit(solution)/shard_map/ppermute | solution.py:275
  47.5 17.2 %collective-permute-start.9 = (bf16[128,16,128]{2,1,0:T(8,128)(2,1)S(1)}, bf16[128,16,128]{2,1,0:T(8,128)(2,1)S(1)}, u32[]{:S(2)}, u32[]{:S(2)}) collective-permute-start(bf16[128,16,128]{2,1,0:T(8,128)(2,1)S(1)} %bitcast.4), channel_id=1, source_target_pairs={{0,8},{8,0},{16,24},{24,16},{1,9},{5,13},{9,1},{13,5},{17,25},{21,... | collective-permute-start | bytes 1572872 | tf_op jit(solution)/shard_map/ppermute | solution.py:275
  56.2 20.0 %copy-start.2 = (s32[64]{0:T(128)S(1)}, s32[64]{0:T(128)}, u32[]{:S(2)}) copy-start(s32[64]{0:T(128)} %reach_ref.1) | copy-start | bytes 772
  56.2 8.6 %collective-permute-start.12 = (bf16[128,16,128]{2,1,0:T(8,128)(2,1)S(1)}, bf16[128,16,128]{2,1,0:T(8,128)(2,1)S(1)}, u32[]{:S(2)}, u32[]{:S(2)}) collective-permute-start(bf16[128,16,128]{2,1,0:T(8,128)(2,1)S(1)} %collective-permute-done.2.refs_3_.refs_0_.refs_4_.refs_9_), channel_id=1, source_target_pairs={{3,19},{11,27},{19,3},{27,11}} | collective-permute-start | bytes 1572872 | tf_op jit(solution)/shard_map/ppermute | solution.py:275
  56.9 10.2 %collective-permute-start.10 = (bf16[128,16,128]{2,1,0:T(8,128)(2,1)S(1)}, bf16[128,16,128]{2,1,0:T(8,128)(2,1)S(1)}, u32[]{:S(2)}, u32[]{:S(2)}) collective-permute-start(bf16[128,16,128]{2,1,0:T(8,128)(2,1)S(1)} %bitcast.5), channel_id=1, source_target_pairs={{8,24},{24,8},{1,9},{9,1},{13,29},{17,25},{25,17},{29,13},{2,10},{... | collective-permute-start | bytes 1572872 | tf_op jit(solution)/shard_map/ppermute | solution.py:275
  59.2 14.7 %collective-permute-start.11 = (bf16[2,128,16,128]{3,2,1,0:T(8,128)(2,1)S(1)}, bf16[2,128,16,128]{3,2,1,0:T(8,128)(2,1)S(1)}, u32[]{:S(2)}, u32[]{:S(2)}) collective-permute-start(bf16[2,128,16,128]{3,2,1,0:T(8,128)(2,1)S(1)} %choose.10), channel_id=1, source_target_pairs={{0,4},{4,0},{8,12},{12,8},{16,20},{20,16},{24,28},{28,24},{1,5},{5... | collective-permute-start | bytes 3145736 | tf_op jit(solution)/shard_map/ppermute | solution.py:275
  67.2 8.9 %collective-permute-start.13 = (bf16[2,128,16,128]{3,2,1,0:T(8,128)(2,1)S(1)}, bf16[2,128,16,128]{3,2,1,0:T(8,128)(2,1)S(1)}, u32[]{:S(2)}, u32[]{:S(2)}) collective-permute-start(bf16[2,128,16,128]{3,2,1,0:T(8,128)(2,1)S(1)} %choose.11), channel_id=1, source_target_pairs={{0,4},{4,0},{8,12},{12,8},{16,20},{20,16},{24,28},{28,24},{1,5},{5... | collective-permute-start | bytes 3145736 | tf_op jit(solution)/shard_map/ppermute | solution.py:275

commit v9 on v5

--- a/solution.py
+++ b/solution.py
@@ -106,13 +106,13 @@
 def choose_kernel(code_of, groups, *refs):
     out_ref = refs[-1]
     per_group = (len(refs) - 1) // groups
-    code = code_of()
+    codes = code_of()
     for g in range(groups):
 
         def put(ref, g=g):
             out_ref[g] = ref[...]
 
-        copy_chosen(code, refs[g * per_group : (g + 1) * per_group], put)
+        copy_chosen(codes[g], refs[g * per_group : (g + 1) * per_group], put)
 
 
 def choose(code_of, groups):
@@ -289,7 +289,11 @@
     return lax.optimization_barrier((array, *others))[0]
 
 
-def direct_partners(pieces, hops, n_win, n_chan):
+def direct_partners(piece, hops, n_win, n_chan):
+    pieces = [piece]
+    while len(pieces) < n_win:
+        ring = [(z, (z + 1) % n_win) for z in range(n_win)]
+        pieces.append(lax.ppermute(pieces[-1], "win", ring))
     buffers = []
     for piece in pieces:
         buffers.append(send(piece, pairs_of(n_win, n_chan, lambda z, c: (c - hops[z]) % n_chan)))
@@ -307,22 +311,22 @@
     odd_next = jnp.where(x == 0, 1, 2)
     even_next = jnp.where(z == 0, odd_next, 2)
     next_code = jnp.where(core == 0, even_next, jnp.where(z == 3, 2, odd_next))
-    outgoing = jnp.where(core == 0, jnp.where(z < 2, next_code, 1), jnp.where(z < 2, 0, next_code))
-    first = jnp.where(z == 0, 0, jnp.where(z == 2, next_code, 3))
-    second = jnp.where(z == 1, next_code, jnp.where(z == 3, 1, 3))
-    is_late = (z == 3) & (core == 0)
-    outgoing_late = jnp.where(is_late, 3, outgoing)
-    second_last = jnp.where(is_late, 4, second)
-    return onward, outgoing, outgoing_late, (first, second, first, second_last)
-
-
-def square_partners(pieces, n_win, n_chan):
+    across = jnp.where((z == 3) & (core == 0), 3, 1)
+    outgoing = jnp.where(
+        core == 0, jnp.where(z < 2, next_code, across), jnp.where(z < 2, 0, next_code)
+    )
+    first = jnp.where(z == 0, 0, jnp.where(z == 2, next_code, 4))
+    second = jnp.where(z == 1, next_code, jnp.where(z == 3, across, 4))
+    return onward, outgoing, first, second
+
+
+def square_partners(piece_zero, n_win, n_chan):
     def pairs(target):
         return pairs_of(n_win, n_chan, lambda z, c: target(z, c, c % 2, c // 2 % 2))
 
     def first_target(z, c, core, x):
         if z == 3:
-            return c ^ 4
+            return c ^ 4 if core == 1 else None
         if z == 0:
             return c ^ 2 if core == 0 else None
         if core == 1:
@@ -338,47 +342,41 @@
             return c ^ 2
         return c ^ 4 if x == 1 else None
 
+    def late_target(z, c, core, x):
+        return c ^ 4 if z == 3 and core == 0 else None
+
     def swap(code_of, groups):
         return send(choose(code_of, groups), pairs(lambda z, c, core, x: c ^ 1))
 
-    count = len(pieces)
+    count = n_win
     half = count // 2
-    held = []
-    for slot, piece in enumerate(pieces):
+    pieces = []
+    held, relays = [], []
+    piece = piece_zero
+    for slot in range(count):
         last = slot == count - 1
         if slot:
-            piece = after(piece, held[slot - 1][1], *([held[slot - 2][2]] if slot >= 2 else []))
-        moved = send(
-            piece,
-            pairs(
-                lambda z, c, core, x: (
-                    None if last and z == 3 and core == 0 else first_target(z, c, core, x)
-                )
-            ),
-        )
-        arrived = moved
+            piece = lax.ppermute(piece, "win", [(z, (z + 1) % n_win) for z in range(n_win)])
+        pieces.append(piece)
+        moved = send(after(piece, *[]), pairs(first_target))
+        arrived = after(moved, *(held[-1][2:] if held else []))
         if last:
-            held[0] = (*held[0][:2], after(held[0][2], piece))
-            swapped_early = swap(lambda: square_codes()[1], held[:half])
-            own = own_rows([*pieces[:-1], after(piece, swapped_early)])
-            arrived = after(moved, own)
-        elif True:
-            arrived = after(moved, pieces[slot + 1])
-        relay = choose(lambda: square_codes()[0], [(piece, arrived)])[0]
-        held.append((piece, moved, send(relay, pairs(second_target))))
-    late = send(
-        after(pieces[-1], relay),
-        pairs(lambda z, c, core, x: c ^ 4 if z == 3 and core == 0 else None),
-    )
-    late_groups = [(*group, group[1]) for group in held[half:-1]] + [(*held[-1], late)]
-    swapped_late = swap(lambda: square_codes()[2], late_groups)
-    buffers = [buffer for group in held for buffer in group] + [swapped_early, swapped_late, late]
+            own = own_rows(pieces)
+            held[0] = (*held[0][:2], after(held[0][2], moved), held[0][3])
+            swapped_early = swap(lambda: square_codes()[1:2] * half, held[:half])
+            arrived = after(arrived, own)
+        relay = choose(lambda: square_codes()[:1], [(piece, arrived)])[0]
+        relays.append(relay)
+        relayed = send(after(relay, *(held[-1][2:] if held else [])), pairs(second_target))
+        late = send(after(piece, relay), pairs(late_target))
+        held.append((piece, moved, relayed, late))
+    swapped_late = swap(lambda: square_codes()[1:2] * (count - half), held[half:])
+    buffers = [buffer for group in held for buffer in group] + [swapped_early, swapped_late]
     groups = []
     for n in range(count):
-        swapped = (3 * count, n) if n < half else (3 * count + 1, n - half)
-        groups.append([(3 * n, None), (3 * n + 1, None), (3 * n + 2, None), swapped])
-    groups[-1].append((3 * count + 2, None))
-    return own, buffers, groups, lambda: square_codes()[3]
+        swapped = (4 * count, n) if n < half else (4 * count + 1, n - half)
+        groups.append([*((4 * n + k, None) for k in range(4)), swapped])
+    return own, buffers, groups, lambda: square_codes()[2:] * 2
 
 
 def on_device(traces, valid, reach):
@@ -386,14 +384,11 @@
     n_win, n_chan = lax.axis_size("win"), lax.axis_size("chan")
     offsets = BAND // n_win
     hops = [z * offsets // width for z in range(n_win)]
-    pieces = [whitened_chunk(traces, valid)]
-    while len(pieces) < n_win:
-        ring = [(z, (z + 1) % n_win) for z in range(n_win)]
-        pieces.append(lax.ppermute(pieces[-1], "win", ring))
+    piece = whitened_chunk(traces, valid)
     if n_chan == 8 and hops == list(range(4)):
-        own, buffers, groups, codes_of = square_partners(pieces, n_win, n_chan)
+        own, buffers, groups, codes_of = square_partners(piece, n_win, n_chan)
     else:
-        own, buffers, groups, codes_of = direct_partners(pieces, hops, n_win, n_chan)
+        own, buffers, groups, codes_of = direct_partners(piece, hops, n_win, n_chan)
     return stacked(own, buffers, groups, codes_of, reach, offsets, traces.shape[0] * n_win)
 
 

time: 96.5 us -> 90.9 us (0.942)
  the two profiles are of different devices: /device:TPU:19 before, /device:TPU:17 now
where the time goes in v9:
time: 90.9 us; the launch traced here: 90.5 us
  waiting for transfers between devices  39.1 us (43%)
  starting transfers between devices  32.1 us (35%)
  Pallas kernels  18.1 us (20%)
  local copies, waits for them, and re-layouts  1.05 us (1%)
    ppermute x14, waiting for transfers between devices, send(): return lax.ppermute(array, AXES, pairs)  31 us
    ppermute x14, starting transfers between devices, send(): return lax.ppermute(array, AXES, pairs)  29.3 us
    pallas_call x1, Pallas kernels, stacked(): pl.pallas_call(functools.partial(stack_kernel, 1.0 / math.sqrt(windows),...  10.3 us
    ppermute x3, waiting for transfers between devices, square_partners(): lax.ppermute(piece, 'win', [(z, (z + 1) % n_win) for z in range(n_win)])  8.11 us
    pallas_call x1, Pallas kernels, whitened_chunk(): pl.pallas_call(whiten_kernel, out_shape=jax.ShapeDtypeStruct((F, windows,...  4 us
    pallas_call x1, Pallas kernels, own_rows(): pl.pallas_call(own_kernel, out_shape=jax.ShapeDtypeStruct((bins, lanes //...  3.44 us
    ppermute x3, starting transfers between devices, square_partners(): lax.ppermute(piece, 'win', [(z, (z + 1) % n_win) for z in range(n_win)])  2.84 us
  transfers between devices with their start and end apart: 17, of which 8 were waited for; matrix products, arithmetic and copies ran while one was open for 0% of the time, Pallas kernels for 4%

profile of v9, /device:TPU:17, one launch (start us, length us, event | category | flops | bytes accessed | tf_op | source)
XLA Modules:
  0.0 90.5 jit_solution(12172798175535429866)
XLA Ops:
  0.0 4.0 %whiten.1.refs_0_ = bf16[128,16,128]{2,1,0:T(8,128)(2,1)} custom-call(bf16[256,512]{1,0:T(8,128)(2,1)} %constant.3.table_hbm, bf16[16,64,512]{2,1,0:T(8,128)(2,1)} %traces_hbm.1, s32[16,64]{1,0:T(8,128)} %valid_hbm.1), custom_call_target="tpu_custom_call" | custom-call | flops 268435456 | bytes 1048576 | tf_op jit(solution)/shard_map/whiten/pallas_call | solution.py:78
  4.0 3.1 %collective-permute-start.3 = (bf16[128,16,128]{2,1,0:T(8,128)(2,1)}, bf16[128,16,128]{2,1,0:T(8,128)(2,1)S(1)}, u32[]{:S(2)}, u32[]{:S(2)}) collective-permute-start(bf16[128,16,128]{2,1,0:T(8,128)(2,1)} %whiten.1.refs_0_), channel_id=1, source_target_pairs={{0,8},{8,0},{16,24},{24,16},{1,17},{5,13},{13,5},{17,1},{21,29},{2... | collective-permute-start | bytes 1572872 | tf_op jit(solution)/shard_map/ppermute | solution.py:275
  7.1 1.4 %collective-permute-start = (bf16[128,16,128]{2,1,0:T(8,128)(2,1)}, bf16[128,16,128]{2,1,0:T(8,128)(2,1)S(1)}, u32[]{:S(2)}, u32[]{:S(2)}) collective-permute-start(bf16[128,16,128]{2,1,0:T(8,128)(2,1)} %whiten.1.refs_0_), channel_id=1, source_target_pairs={{0,1},{1,2},{2,3},{3,0},{4,5},{5,6},{6,7},{7,4},{8,9},{9,10},{10,1... | collective-permute-start | bytes 1572872 | tf_op jit(solution)/shard_map/ppermute | solution.py:359
  8.5 5.9 %collective-permute-done.3.refs_1_ = bf16[128,16,128]{2,1,0:T(8,128)(2,1)S(1)} collective-permute-done((bf16[128,16,128]{2,1,0:T(8,128)(2,1)}, bf16[128,16,128]{2,1,0:T(8,128)(2,1)S(1)}, u32[]{:S(2)}, u32[]{:S(2)}) %collective-permute-start.3) | collective-permute-done | bytes 524320 | tf_op jit(solution)/shard_map/ppermute | solution.py:275
  14.4 1.0 %copy-done = bf16[128,16,128]{2,1,0:T(8,128)(2,1)S(1)} copy-done((bf16[128,16,128]{2,1,0:T(8,128)(2,1)S(1)}, bf16[128,16,128]{2,1,0:T(8,128)(2,1)}, u32[]{:S(2)}) %copy-start) | copy-done | bytes 524312
  15.5 0.8 collective-permute-start.6
  16.4 0.7 collective-permute-start.4
  17.1 3.4 %collective-permute-done.refs_1_.refs_0_.refs_4_ = bf16[128,16,128]{2,1,0:T(8,128)(2,1)S(1)} collective-permute-done((bf16[128,16,128]{2,1,0:T(8,128)(2,1)}, bf16[128,16,128]{2,1,0:T(8,128)(2,1)S(1)}, u32[]{:S(2)}, u32[]{:S(2)}) %collective-permute-start) | collective-permute-done | bytes 524320 | tf_op jit(solution)/shard_map/ppermute | solution.py:359
  20.4 3.1 %collective-permute-start.7 = (bf16[128,16,128]{2,1,0:T(8,128)(2,1)S(1)}, bf16[128,16,128]{2,1,0:T(8,128)(2,1)S(1)}, u32[]{:S(2)}, u32[]{:S(2)}) collective-permute-start(bf16[128,16,128]{2,1,0:T(8,128)(2,1)S(1)} %collective-permute-done.refs_1_.refs_0_.refs_4_), channel_id=1, source_target_pairs={{0,8},{8,0},{16,24},{24,16},{1,17},{5,13},{13,5},{17,1},{21,29},{2... | collective-permute-start | bytes 1572872 | tf_op jit(solution)/shard_map/ppermute | solution.py:275
  23.5 1.2 %collective-permute-start.1 = (bf16[128,16,128]{2,1,0:T(8,128)(2,1)S(1)}, bf16[128,16,128]{2,1,0:T(8,128)(2,1)S(1)}, u32[]{:S(2)}, u32[]{:S(2)}) collective-permute-start(bf16[128,16,128]{2,1,0:T(8,128)(2,1)S(1)} %collective-permute-done.refs_1_.refs_0_.refs_4_), channel_id=1, source_target_pairs={{0,1},{1,2},{2,3},{3,0},{4,5},{5,6},{6,7},{7,4},{8,9},{9,10},{10,1... | collective-permute-start | bytes 1572872 | tf_op jit(solution)/shard_map/ppermute | solution.py:359
  24.7 9.5 %collective-permute-done.7.refs_1_.refs_5_ = bf16[128,16,128]{2,1,0:T(8,128)(2,1)S(1)} collective-permute-done((bf16[128,16,128]{2,1,0:T(8,128)(2,1)S(1)}, bf16[128,16,128]{2,1,0:T(8,128)(2,1)S(1)}, u32[]{:S(2)}, u32[]{:S(2)}) %collective-permute-start.7) | collective-permute-done | bytes 524320 | tf_op jit(solution)/shard_map/ppermute | solution.py:275
  34.2 0.7 collective-permute-start.8
  34.9 0.7 collective-permute-start.9
  35.6 0.1 collective-permute-done.1.refs_2_.refs_0_.refs_8_
  35.8 5.4 %collective-permute-start.10 = (bf16[128,16,128]{2,1,0:T(8,128)(2,1)S(1)}, bf16[128,16,128]{2,1,0:T(8,128)(2,1)S(1)}, u32[]{:S(2)}, u32[]{:S(2)}) collective-permute-start(bf16[128,16,128]{2,1,0:T(8,128)(2,1)S(1)} %collective-permute-done.1.refs_2_.refs_0_.refs_8_), channel_id=1, source_target_pairs={{0,8},{8,0},{16,24},{24,16},{1,17},{5,13},{13,5},{17,1},{21,29},{2... | collective-permute-start | bytes 1572872 | tf_op jit(solution)/shard_map/ppermute | solution.py:275
  41.2 0.3 collective-permute-start.2
  41.5 7.6 %collective-permute-done.10.refs_1_.refs_9_ = bf16[128,16,128]{2,1,0:T(8,128)(2,1)S(1)} collective-permute-done((bf16[128,16,128]{2,1,0:T(8,128)(2,1)S(1)}, bf16[128,16,128]{2,1,0:T(8,128)(2,1)S(1)}, u32[]{:S(2)}, u32[]{:S(2)}) %collective-permute-start.10) | collective-permute-done | bytes 524320 | tf_op jit(solution)/shard_map/ppermute | solution.py:275
  49.2 0.7 collective-permute-start.11
  49.9 0.7 collective-permute-start.12
  50.6 4.6 %collective-permute-done.2.refs_3_.refs_0_.refs_4_.refs_12_ = bf16[128,16,128]{2,1,0:T(8,128)(2,1)S(1)} collective-permute-done((bf16[128,16,128]{2,1,0:T(8,128)(2,1)S(1)}, bf16[128,16,128]{2,1,0:T(8,128)(2,1)S(1)}, u32[]{:S(2)}, u32[]{:S(2)}) %collective-permute-start.2) | collective-permute-done | bytes 524320 | tf_op jit(solution)/shard_map/ppermute | solution.py:359
  55.2 1.9 %collective-permute-start.5 = (bf16[128,16,128]{2,1,0:T(8,128)(2,1)S(1)}, bf16[128,16,128]{2,1,0:T(8,128)(2,1)S(1)}, u32[]{:S(2)}, u32[]{:S(2)}) collective-permute-start(bf16[128,16,128]{2,1,0:T(8,128)(2,1)S(1)} %collective-permute-done.2.refs_3_.refs_0_.refs_4_.refs_12_), channel_id=1, source_target_pairs={{0,8},{8,0},{16,24},{24,16},{1,17},{5,13},{13,5},{17,1},{21,29},{2... | collective-permute-start | bytes 1572872 | tf_op jit(solution)/shard_map/ppermute | solution.py:275
  57.1 3.4 %own_rows.1.own = bf16[128,64,128]{2,1,0:T(8,128)(2,1)S(1)} custom-call(bf16[128,16,128]{2,1,0:T(8,128)(2,1)S(1)} %copy-done.1, bf16[128,16,128]{2,1,0:T(8,128)(2,1)S(1)} %collective-permute-done.refs_1_.refs_0_.refs_4_, bf16[128,16,128]{2,1,0:T(8,128)(2,1)S(1)} %collective-permute-done.1.refs_2_.refs_0_.refs_8_, ...), custom_call_target="tpu_custom_call" | custom-call | flops 1 | bytes 1 | tf_op jit(solution)/shard_map/own_rows/pallas_call | solution.py:145
  60.6 5.6 %collective-permute-done.5.refs_1_.refs_5_.refs_13_ = bf16[128,16,128]{2,1,0:T(8,128)(2,1)S(1)} collective-permute-done((bf16[128,16,128]{2,1,0:T(8,128)(2,1)S(1)}, bf16[128,16,128]{2,1,0:T(8,128)(2,1)S(1)}, u32[]{:S(2)}, u32[]{:S(2)}) %collective-permute-start.5) | collective-permute-done | bytes 524320 | tf_op jit(solution)/shard_map/ppermute | solution.py:275
  66.3 0.0 copy-start.2
  66.3 0.7 collective-permute-start.13
  67.0 0.7 collective-permute-start.14
  67.7 0.1 choose.10
  67.8 2.0 %collective-permute-start.15 = (bf16[2,128,16,128]{3,2,1,0:T(8,128)(2,1)S(1)}, bf16[2,128,16,128]{3,2,1,0:T(8,128)(2,1)S(1)}, u32[]{:S(2)}, u32[]{:S(2)}) collective-permute-start(bf16[2,128,16,128]{3,2,1,0:T(8,128)(2,1)S(1)} %choose.10), channel_id=1, source_target_pairs={{0,4},{4,0},{8,12},{12,8},{16,20},{20,16},{24,28},{28,24},{1,5},{5... | collective-permute-start | bytes 3145736 | tf_op jit(solution)/shard_map/ppermute | solution.py:275
  69.8 0.1 choose.11
  69.9 8.0 %collective-permute-start.16 = (bf16[2,128,16,128]{3,2,1,0:T(8,128)(2,1)S(1)}, bf16[2,128,16,128]{3,2,1,0:T(8,128)(2,1)S(1)}, u32[]{:S(2)}, u32[]{:S(2)}) collective-permute-start(bf16[2,128,16,128]{3,2,1,0:T(8,128)(2,1)S(1)} %choose.11), channel_id=1, source_target_pairs={{0,4},{4,0},{8,12},{12,8},{16,20},{20,16},{24,28},{28,24},{1,5},{5... | collective-permute-start | bytes 3145736 | tf_op jit(solution)/shard_map/ppermute | solution.py:275
  77.9 2.3 %collective-permute-done.16.refs_17_ = bf16[2,128,16,128]{3,2,1,0:T(8,128)(2,1)S(1)} collective-permute-done((bf16[2,128,16,128]{3,2,1,0:T(8,128)(2,1)S(1)}, bf16[2,128,16,128]{3,2,1,0:T(8,128)(2,1)S(1)}, u32[]{:S(2)}, u32[]{:S(2)}) %collective-permute-start.16) | collective-permute-done | bytes 1048608 | tf_op jit(solution)/shard_map/ppermute | solution.py:275
  80.2 10.3 %stack.1 = f32[64,64,256]{2,1,0:T(8,128)} custom-call(s32[64]{0:T(128)S(1)} %copy-done.2, bf16[128,64,128]{2,1,0:T(8,128)(2,1)S(1)} %own_rows.1.own, bf16[128,16,128]{2,1,0:T(8,128)(2,1)S(1)} %copy-done.1, bf16[128,16,128]{2,1,0:T(8,128)(2,1)S(1)} %collective-permute-done.3.refs_1_, bf16[128,16,128]{2,1,0:T(8,128)(2,1)S(1)} %collective-permute-done.4.refs_2_, ...), custom_call_target="tpu_custom_call" | custom-call | flops 1 | bytes 1 | tf_op jit(solution)/shard_map/stack/pallas_call | solution.py:257
  (17 shorter events, 0.2 us)
Async XLA Ops:
  4.0 10.4 %collective-permute-start.3 = (bf16[128,16,128]{2,1,0:T(8,128)(2,1)}, bf16[128,16,128]{2,1,0:T(8,128)(2,1)S(1)}, u32[]{:S(2)}, u32[]{:S(2)}) collective-permute-start(bf16[128,16,128]{2,1,0:T(8,128)(2,1)} %whiten.1.refs_0_), channel_id=1, source_target_pairs={{0,8},{8,0},{16,24},{24,16},{1,17},{5,13},{13,5},{17,1},{21,29},{2... | collective-permute-start | bytes 1572872 | tf_op jit(solution)/shard_map/ppermute | solution.py:275
  7.1 13.3 %collective-permute-start = (bf16[128,16,128]{2,1,0:T(8,128)(2,1)}, bf16[128,16,128]{2,1,0:T(8,128)(2,1)S(1)}, u32[]{:S(2)}, u32[]{:S(2)}) collective-permute-start(bf16[128,16,128]{2,1,0:T(8,128)(2,1)} %whiten.1.refs_0_), channel_id=1, source_target_pairs={{0,1},{1,2},{2,3},{3,0},{4,5},{5,6},{6,7},{7,4},{8,9},{9,10},{10,1... | collective-permute-start | bytes 1572872 | tf_op jit(solution)/shard_map/ppermute | solution.py:359
  14.4 1.0 %copy-start = (bf16[128,16,128]{2,1,0:T(8,128)(2,1)S(1)}, bf16[128,16,128]{2,1,0:T(8,128)(2,1)}, u32[]{:S(2)}) copy-start(bf16[128,16,128]{2,1,0:T(8,128)(2,1)} %whiten.1.refs_0_) | copy-start | bytes 1572868
  15.5 41.6 %copy-start.1 = (bf16[128,16,128]{2,1,0:T(8,128)(2,1)S(1)}, bf16[128,16,128]{2,1,0:T(8,128)(2,1)}, u32[]{:S(2)}) copy-start(bf16[128,16,128]{2,1,0:T(8,128)(2,1)} %whiten.1.refs_0_) | copy-start | bytes 1572868
  15.5 9.2 %collective-permute-start.6 = (bf16[128,16,128]{2,1,0:T(8,128)(2,1)S(1)}, bf16[128,16,128]{2,1,0:T(8,128)(2,1)S(1)}, u32[]{:S(2)}, u32[]{:S(2)}) collective-permute-start(bf16[128,16,128]{2,1,0:T(8,128)(2,1)S(1)} %copy-done), channel_id=1, source_target_pairs={{3,19},{11,27},{19,3},{27,11}} | collective-permute-start | bytes 1572872 | tf_op jit(solution)/shard_map/ppermute | solution.py:275
  16.4 8.3 %collective-permute-start.4 = (bf16[128,16,128]{2,1,0:T(8,128)(2,1)S(1)}, bf16[128,16,128]{2,1,0:T(8,128)(2,1)S(1)}, u32[]{:S(2)}, u32[]{:S(2)}) collective-permute-start(bf16[128,16,128]{2,1,0:T(8,128)(2,1)S(1)} %bitcast.4), channel_id=1, source_target_pairs={{8,24},{24,8},{1,9},{9,1},{13,29},{17,25},{25,17},{29,13},{2,10},{... | collective-permute-start | bytes 1572872 | tf_op jit(solution)/shard_map/ppermute | solution.py:275
  20.4 13.8 %collective-permute-start.7 = (bf16[128,16,128]{2,1,0:T(8,128)(2,1)S(1)}, bf16[128,16,128]{2,1,0:T(8,128)(2,1)S(1)}, u32[]{:S(2)}, u32[]{:S(2)}) collective-permute-start(bf16[128,16,128]{2,1,0:T(8,128)(2,1)S(1)} %collective-permute-done.refs_1_.refs_0_.refs_4_), channel_id=1, source_target_pairs={{0,8},{8,0},{16,24},{24,16},{1,17},{5,13},{13,5},{17,1},{21,29},{2... | collective-permute-start | bytes 1572872 | tf_op jit(solution)/shard_map/ppermute | solution.py:275
  23.5 12.2 %collective-permute-start.1 = (bf16[128,16,128]{2,1,0:T(8,128)(2,1)S(1)}, bf16[128,16,128]{2,1,0:T(8,128)(2,1)S(1)}, u32[]{:S(2)}, u32[]{:S(2)}) collective-permute-start(bf16[128,16,128]{2,1,0:T(8,128)(2,1)S(1)} %collective-permute-done.refs_1_.refs_0_.refs_4_), channel_id=1, source_target_pairs={{0,1},{1,2},{2,3},{3,0},{4,5},{5,6},{6,7},{7,4},{8,9},{9,10},{10,1... | collective-permute-start | bytes 1572872 | tf_op jit(solution)/shard_map/ppermute | solution.py:359
  34.2 7.3 %collective-permute-start.8 = (bf16[128,16,128]{2,1,0:T(8,128)(2,1)S(1)}, bf16[128,16,128]{2,1,0:T(8,128)(2,1)S(1)}, u32[]{:S(2)}, u32[]{:S(2)}) collective-permute-start(bf16[128,16,128]{2,1,0:T(8,128)(2,1)S(1)} %bitcast.5), channel_id=1, source_target_pairs={{8,24},{24,8},{1,9},{9,1},{13,29},{17,25},{25,17},{29,13},{2,10},{... | collective-permute-start | bytes 1572872 | tf_op jit(solution)/shard_map/ppermute | solution.py:275
  34.9 6.6 %collective-permute-start.9 = (bf16[128,16,128]{2,1,0:T(8,128)(2,1)S(1)}, bf16[128,16,128]{2,1,0:T(8,128)(2,1)S(1)}, u32[]{:S(2)}, u32[]{:S(2)}) collective-permute-start(bf16[128,16,128]{2,1,0:T(8,128)(2,1)S(1)} %collective-permute-done.refs_1_.refs_0_.refs_4_), channel_id=1, source_target_pairs={{3,19},{11,27},{19,3},{27,11}} | collective-permute-start | bytes 1572872 | tf_op jit(solution)/shard_map/ppermute | solution.py:275
  35.8 13.4 %collective-permute-start.10 = (bf16[128,16,128]{2,1,0:T(8,128)(2,1)S(1)}, bf16[128,16,128]{2,1,0:T(8,128)(2,1)S(1)}, u32[]{:S(2)}, u32[]{:S(2)}) collective-permute-start(bf16[128,16,128]{2,1,0:T(8,128)(2,1)S(1)} %collective-permute-done.1.refs_2_.refs_0_.refs_8_), channel_id=1, source_target_pairs={{0,8},{8,0},{16,24},{24,16},{1,17},{5,13},{13,5},{17,1},{21,29},{2... | collective-permute-start | bytes 1572872 | tf_op jit(solution)/shard_map/ppermute | solution.py:275
  41.2 14.0 %collective-permute-start.2 = (bf16[128,16,128]{2,1,0:T(8,128)(2,1)S(1)}, bf16[128,16,128]{2,1,0:T(8,128)(2,1)S(1)}, u32[]{:S(2)}, u32[]{:S(2)}) collective-permute-start(bf16[128,16,128]{2,1,0:T(8,128)(2,1)S(1)} %collective-permute-done.1.refs_2_.refs_0_.refs_8_), channel_id=1, source_target_pairs={{0,1},{1,2},{2,3},{3,0},{4,5},{5,6},{6,7},{7,4},{8,9},{9,10},{10,1... | collective-permute-start | bytes 1572872 | tf_op jit(solution)/shard_map/ppermute | solution.py:359
  49.2 11.4 %collective-permute-start.11 = (bf16[128,16,128]{2,1,0:T(8,128)(2,1)S(1)}, bf16[128,16,128]{2,1,0:T(8,128)(2,1)S(1)}, u32[]{:S(2)}, u32[]{:S(2)}) collective-permute-start(bf16[128,16,128]{2,1,0:T(8,128)(2,1)S(1)} %bitcast.6), channel_id=1, source_target_pairs={{8,24},{24,8},{1,9},{9,1},{13,29},{17,25},{25,17},{29,13},{2,10},{... | collective-permute-start | bytes 1572872 | tf_op jit(solution)/shard_map/ppermute | solution.py:275
  49.9 10.7 %collective-permute-start.12 = (bf16[128,16,128]{2,1,0:T(8,128)(2,1)S(1)}, bf16[128,16,128]{2,1,0:T(8,128)(2,1)S(1)}, u32[]{:S(2)}, u32[]{:S(2)}) collective-permute-start(bf16[128,16,128]{2,1,0:T(8,128)(2,1)S(1)} %collective-permute-done.1.refs_2_.refs_0_.refs_8_), channel_id=1, source_target_pairs={{3,19},{11,27},{19,3},{27,11}} | collective-permute-start | bytes 1572872 | tf_op jit(solution)/shard_map/ppermute | solution.py:275
  55.2 11.0 %collective-permute-start.5 = (bf16[128,16,128]{2,1,0:T(8,128)(2,1)S(1)}, bf16[128,16,128]{2,1,0:T(8,128)(2,1)S(1)}, u32[]{:S(2)}, u32[]{:S(2)}) collective-permute-start(bf16[128,16,128]{2,1,0:T(8,128)(2,1)S(1)} %collective-permute-done.2.refs_3_.refs_0_.refs_4_.refs_12_), channel_id=1, source_target_pairs={{0,8},{8,0},{16,24},{24,16},{1,17},{5,13},{13,5},{17,1},{21,29},{2... | collective-permute-start | bytes 1572872 | tf_op jit(solution)/shard_map/ppermute | solution.py:275
  66.3 13.9 %copy-start.2 = (s32[64]{0:T(128)S(1)}, s32[64]{0:T(128)}, u32[]{:S(2)}) copy-start(s32[64]{0:T(128)} %reach_ref.1) | copy-start | bytes 772
  66.3 3.6 %collective-permute-start.13 = (bf16[128,16,128]{2,1,0:T(8,128)(2,1)S(1)}, bf16[128,16,128]{2,1,0:T(8,128)(2,1)S(1)}, u32[]{:S(2)}, u32[]{:S(2)}) collective-permute-start(bf16[128,16,128]{2,1,0:T(8,128)(2,1)S(1)} %bitcast.7), channel_id=1, source_target_pairs={{8,24},{24,8},{1,9},{9,1},{13,29},{17,25},{25,17},{29,13},{2,10},{... | collective-permute-start | bytes 1572872 | tf_op jit(solution)/shard_map/ppermute | solution.py:275
  67.0 2.9 %collective-permute-start.14 = (bf16[128,16,128]{2,1,0:T(8,128)(2,1)S(1)}, bf16[128,16,128]{2,1,0:T(8,128)(2,1)S(1)}, u32[]{:S(2)}, u32[]{:S(2)}) collective-permute-start(bf16[128,16,128]{2,1,0:T(8,128)(2,1)S(1)} %collective-permute-done.2.refs_3_.refs_0_.refs_4_.refs_12_), channel_id=1, source_target_pairs={{3,19},{11,27},{19,3},{27,11}} | collective-permute-start | bytes 1572872 | tf_op jit(solution)/shard_map/ppermute | solution.py:275
  67.8 10.1 %collective-permute-start.15 = (bf16[2,128,16,128]{3,2,1,0:T(8,128)(2,1)S(1)}, bf16[2,128,16,128]{3,2,1,0:T(8,128)(2,1)S(1)}, u32[]{:S(2)}, u32[]{:S(2)}) collective-permute-start(bf16[2,128,16,128]{3,2,1,0:T(8,128)(2,1)S(1)} %choose.10), channel_id=1, source_target_pairs={{0,4},{4,0},{8,12},{12,8},{16,20},{20,16},{24,28},{28,24},{1,5},{5... | collective-permute-start | bytes 3145736 | tf_op jit(solution)/shard_map/ppermute | solution.py:275
  69.9 10.3 %collective-permute-start.16 = (bf16[2,128,16,128]{3,2,1,0:T(8,128)(2,1)S(1)}, bf16[2,128,16,128]{3,2,1,0:T(8,128)(2,1)S(1)}, u32[]{:S(2)}, u32[]{:S(2)}) collective-permute-start(bf16[2,128,16,128]{3,2,1,0:T(8,128)(2,1)S(1)} %choose.11), channel_id=1, source_target_pairs={{0,4},{4,0},{8,12},{12,8},{16,20},{20,16},{24,28},{28,24},{1,5},{5... | collective-permute-start | bytes 3145736 | tf_op jit(solution)/shard_map/ppermute | solution.py:275

commit v10 on v6

--- a/solution.py
+++ b/solution.py
@@ -160,7 +160,7 @@
     bins, width, _ = own.shape
     lanes = 2 * width
     offsets = out_hbm.shape[0]
-    pitch = products.shape[1] // bins
+    pitch = products.shape[0] // bins
     slots = len(groups)
     first_offset = lax.axis_index("win") * offsets
     codes = codes_of()
@@ -175,6 +175,10 @@
                 partners[which, slot] = ref[...]
 
             copy_chosen(codes[which if slot < slots - 1 else 2 + which], candidates, put)
+
+    first = first_offset % width
+    lane = lax.broadcasted_iota(jnp.int32, (width, lanes), 1)
+    in_first = lane % width >= lax.broadcasted_iota(jnp.int32, (width, lanes), 0) + first
 
     def one_bin(f, carry):
         tops = [
@@ -187,19 +191,15 @@
         )
         both = jnp.dot(own[f], right, preferred_element_type=jnp.float32)
         row = pl.multiple_of(f * pitch, 8)
-        for half in range(2):
-            products[half, pl.ds(row, width), :] = both[:, half * lanes : (half + 1) * lanes]
+        products[pl.ds(row, width), :] = jnp.where(in_first, both[:, :lanes], both[:, lanes:])
         return carry
 
     lax.fori_loop(0, bins, one_bin, 0, unroll=8)
 
-    lane = lax.broadcasted_iota(jnp.int32, (offsets, 2 * lanes), 1)
-    k = lax.broadcasted_iota(jnp.int32, (offsets, 2 * lanes), 0)
-    partner = lane % width + jnp.where(lane >= lanes, width, 0)
-    is_real = lane % lanes < width
-    far = 4 * lanes
-    shift_re = jnp.where(is_real, partner - k, far)
-    shift_im = jnp.where(is_real, far, partner - k)
+    lane = lax.broadcasted_iota(jnp.int32, (offsets, lanes), 1)
+    shift = (lane + offsets * width - lax.broadcasted_iota(jnp.int32, (offsets, lanes), 0)) % width
+    shift_re = jnp.where(lane < width, shift, width)
+    shift_im = jnp.where(lane < width, width, shift)
     row_k = lax.broadcasted_iota(jnp.int32, (offsets, F), 0) + first_offset
 
     def copies(block):
@@ -216,7 +216,7 @@
     def one_block(block, carry):
         for il in range(CHANNEL_BLOCK):
             i = block * CHANNEL_BLOCK + il
-            at = i + first_offset % width
+            at = (i + first) % width
             pick = jnp.concatenate(
                 [
                     jnp.where(shift_re == at, 1.0, 0.0),
@@ -224,9 +224,7 @@
                 ],
                 axis=0,
             ).astype(jnp.bfloat16)
-            x = jnp.concatenate(
-                [products[half, pl.ds(i, F, stride=pitch), :] for half in range(2)], axis=1
-            ).astype(jnp.bfloat16)
+            x = products[pl.ds(i, F, stride=pitch), :].astype(jnp.bfloat16)
             y = lax.dot_general(
                 pick, x, (((1,), (1,)), ((), ())), preferred_element_type=jnp.float32
             )
@@ -261,7 +259,7 @@
         out_specs=ANY,
         scratch_shapes=[
             pltpu.VMEM((2, len(groups), bins, chunk_windows, lanes), jnp.bfloat16),
-            pltpu.VMEM((2, bins * pitch, lanes), jnp.float32),
+            pltpu.VMEM((bins * pitch, lanes), jnp.float32),
             pltpu.VMEM((2, offsets * pitch, F), jnp.float32),
             pltpu.SemaphoreType.DMA((width // CHANNEL_BLOCK, 2)),
         ],

time: 86.4 us -> 86.3 us (level)
  no operation moved by 1% of the time
where the time goes in v10:
time: 86.3 us; the launch traced here: 85.9 us
  waiting for transfers between devices  41.3 us (48%)
  starting transfers between devices  25.3 us (29%)
  Pallas kernels  18 us (21%)
  local copies, waits for them, and re-layouts  1.05 us (1%)
    ppermute x11, waiting for transfers between devices, send(): return lax.ppermute(array, AXES, pairs)  26.3 us
    ppermute x11, starting transfers between devices, send(): return lax.ppermute(array, AXES, pairs)  22.4 us
    ppermute x3, waiting for transfers between devices, on_device(): pieces.append(lax.ppermute(pieces[-1], 'win', ring))  15 us
    pallas_call x1, Pallas kernels, stacked(): pl.pallas_call(functools.partial(stack_kernel, 1.0 / math.sqrt(windows),...  10.2 us
    pallas_call x1, Pallas kernels, whitened_chunk(): pl.pallas_call(whiten_kernel, out_shape=jax.ShapeDtypeStruct((F, windows,...  4 us
    pallas_call x1, Pallas kernels, own_rows(): pl.pallas_call(own_kernel, out_shape=jax.ShapeDtypeStruct((bins, lanes //...  3.44 us
    ppermute x3, starting transfers between devices, on_device(): pieces.append(lax.ppermute(pieces[-1], 'win', ring))  2.93 us
  transfers between devices with their start and end apart: 14, of which 9 were waited for; matrix products, arithmetic and copies ran while one was open for 0% of the time, Pallas kernels for 4%

profile of v10, /device:TPU:11, one launch (start us, length us, event | category | flops | bytes accessed | tf_op | source)
XLA Modules:
  0.0 85.9 jit_solution(18194271150458547774)
XLA Ops:
  0.0 4.0 %whiten.1.refs_0_ = bf16[128,16,128]{2,1,0:T(8,128)(2,1)} custom-call(bf16[256,512]{1,0:T(8,128)(2,1)} %constant.3.table_hbm, bf16[16,64,512]{2,1,0:T(8,128)(2,1)} %traces_hbm.1, s32[16,64]{1,0:T(8,128)} %valid_hbm.1), custom_call_target="tpu_custom_call" | custom-call | flops 268435456 | bytes 1048576 | tf_op jit(solution)/shard_map/whiten/pallas_call | solution.py:78
  4.0 1.3 %collective-permute-start = (bf16[128,16,128]{2,1,0:T(8,128)(2,1)}, bf16[128,16,128]{2,1,0:T(8,128)(2,1)S(1)}, u32[]{:S(2)}, u32[]{:S(2)}) collective-permute-start(bf16[128,16,128]{2,1,0:T(8,128)(2,1)} %whiten.1.refs_0_), channel_id=1, source_target_pairs={{0,1},{1,2},{2,3},{3,0},{4,5},{5,6},{6,7},{7,4},{8,9},{9,10},{10,1... | collective-permute-start | bytes 1572872 | tf_op jit(solution)/shard_map/ppermute | solution.py:399
  5.4 2.2 %collective-permute-start.3 = (bf16[128,16,128]{2,1,0:T(8,128)(2,1)}, bf16[128,16,128]{2,1,0:T(8,128)(2,1)S(1)}, u32[]{:S(2)}, u32[]{:S(2)}) collective-permute-start(bf16[128,16,128]{2,1,0:T(8,128)(2,1)} %whiten.1.refs_0_), channel_id=1, source_target_pairs={{0,8},{8,0},{16,24},{24,16},{1,17},{5,13},{13,5},{17,1},{21,29},{2... | collective-permute-start | bytes 1572872 | tf_op jit(solution)/shard_map/ppermute | solution.py:273
  7.5 9.5 %collective-permute-done.refs_1_.refs_0_.refs_3_ = bf16[128,16,128]{2,1,0:T(8,128)(2,1)S(1)} collective-permute-done((bf16[128,16,128]{2,1,0:T(8,128)(2,1)}, bf16[128,16,128]{2,1,0:T(8,128)(2,1)S(1)}, u32[]{:S(2)}, u32[]{:S(2)}) %collective-permute-start) | collective-permute-done | bytes 524320 | tf_op jit(solution)/shard_map/ppermute | solution.py:399
  17.1 1.3 %collective-permute-start.1 = (bf16[128,16,128]{2,1,0:T(8,128)(2,1)S(1)}, bf16[128,16,128]{2,1,0:T(8,128)(2,1)S(1)}, u32[]{:S(2)}, u32[]{:S(2)}) collective-permute-start(bf16[128,16,128]{2,1,0:T(8,128)(2,1)S(1)} %collective-permute-done.refs_1_.refs_0_.refs_3_), channel_id=1, source_target_pairs={{0,1},{1,2},{2,3},{3,0},{4,5},{5,6},{6,7},{7,4},{8,9},{9,10},{10,1... | collective-permute-start | bytes 1572872 | tf_op jit(solution)/shard_map/ppermute | solution.py:399
  18.4 1.0 %copy-done = bf16[128,16,128]{2,1,0:T(8,128)(2,1)S(1)} copy-done((bf16[128,16,128]{2,1,0:T(8,128)(2,1)S(1)}, bf16[128,16,128]{2,1,0:T(8,128)(2,1)}, u32[]{:S(2)}) %copy-start) | copy-done | bytes 524312
  19.4 3.3 %collective-permute-start.4 = (bf16[128,16,128]{2,1,0:T(8,128)(2,1)S(1)}, bf16[128,16,128]{2,1,0:T(8,128)(2,1)S(1)}, u32[]{:S(2)}, u32[]{:S(2)}) collective-permute-start(bf16[128,16,128]{2,1,0:T(8,128)(2,1)S(1)} %bitcast.6), channel_id=1, source_target_pairs={{8,24},{24,8},{1,9},{9,1},{13,29},{17,25},{25,17},{29,13},{2,10},{... | collective-permute-start | bytes 1572872 | tf_op jit(solution)/shard_map/ppermute | solution.py:273
  22.7 1.9 %collective-permute-start.5 = (bf16[128,16,128]{2,1,0:T(8,128)(2,1)S(1)}, bf16[128,16,128]{2,1,0:T(8,128)(2,1)S(1)}, u32[]{:S(2)}, u32[]{:S(2)}) collective-permute-start(bf16[128,16,128]{2,1,0:T(8,128)(2,1)S(1)} %collective-permute-done.refs_1_.refs_0_.refs_3_), channel_id=1, source_target_pairs={{0,8},{8,0},{16,24},{24,16},{1,17},{5,13},{13,5},{17,1},{21,29},{2... | collective-permute-start | bytes 1572872 | tf_op jit(solution)/shard_map/ppermute | solution.py:273
  24.7 5.3 %collective-permute-done.1.refs_2_.refs_0_.refs_6_ = bf16[128,16,128]{2,1,0:T(8,128)(2,1)S(1)} collective-permute-done((bf16[128,16,128]{2,1,0:T(8,128)(2,1)S(1)}, bf16[128,16,128]{2,1,0:T(8,128)(2,1)S(1)}, u32[]{:S(2)}, u32[]{:S(2)}) %collective-permute-start.1) | collective-permute-done | bytes 524320 | tf_op jit(solution)/shard_map/ppermute | solution.py:399
  29.9 0.3 collective-permute-start.2
  30.2 0.0 collective-permute-done.4.refs_2_
  30.2 7.5 %collective-permute-done.5.refs_1_.refs_4_ = bf16[128,16,128]{2,1,0:T(8,128)(2,1)S(1)} collective-permute-done((bf16[128,16,128]{2,1,0:T(8,128)(2,1)S(1)}, bf16[128,16,128]{2,1,0:T(8,128)(2,1)S(1)}, u32[]{:S(2)}, u32[]{:S(2)}) %collective-permute-start.5) | collective-permute-done | bytes 524320 | tf_op jit(solution)/shard_map/ppermute | solution.py:273
  37.7 2.8 %collective-permute-start.7 = (bf16[128,16,128]{2,1,0:T(8,128)(2,1)S(1)}, bf16[128,16,128]{2,1,0:T(8,128)(2,1)S(1)}, u32[]{:S(2)}, u32[]{:S(2)}) collective-permute-start(bf16[128,16,128]{2,1,0:T(8,128)(2,1)S(1)} %bitcast.7), channel_id=1, source_target_pairs={{8,24},{24,8},{1,9},{9,1},{13,29},{17,25},{25,17},{29,13},{2,10},{... | collective-permute-start | bytes 1572872 | tf_op jit(solution)/shard_map/ppermute | solution.py:273
  40.6 1.9 %collective-permute-start.8 = (bf16[128,16,128]{2,1,0:T(8,128)(2,1)S(1)}, bf16[128,16,128]{2,1,0:T(8,128)(2,1)S(1)}, u32[]{:S(2)}, u32[]{:S(2)}) collective-permute-start(bf16[128,16,128]{2,1,0:T(8,128)(2,1)S(1)} %collective-permute-done.1.refs_2_.refs_0_.refs_6_), channel_id=1, source_target_pairs={{0,8},{8,0},{16,24},{24,16},{1,17},{5,13},{13,5},{17,1},{21,29},{2... | collective-permute-start | bytes 1572872 | tf_op jit(solution)/shard_map/ppermute | solution.py:273
  42.5 0.2 collective-permute-done.2.refs_3_.refs_0_.refs_4_.refs_9_
  42.7 3.1 %collective-permute-start.6 = (bf16[128,16,128]{2,1,0:T(8,128)(2,1)S(1)}, bf16[128,16,128]{2,1,0:T(8,128)(2,1)S(1)}, u32[]{:S(2)}, u32[]{:S(2)}) collective-permute-start(bf16[128,16,128]{2,1,0:T(8,128)(2,1)S(1)} %collective-permute-done.2.refs_3_.refs_0_.refs_4_.refs_9_), channel_id=1, source_target_pairs={{0,8},{8,0},{16,24},{24,16},{1,17},{5,13},{13,5},{17,1},{21,29},{2... | collective-permute-start | bytes 1572872 | tf_op jit(solution)/shard_map/ppermute | solution.py:273
  45.9 2.1 %collective-permute-done.7.refs_5_ = bf16[128,16,128]{2,1,0:T(8,128)(2,1)S(1)} collective-permute-done((bf16[128,16,128]{2,1,0:T(8,128)(2,1)S(1)}, bf16[128,16,128]{2,1,0:T(8,128)(2,1)S(1)}, u32[]{:S(2)}, u32[]{:S(2)}) %collective-permute-start.7) | collective-permute-done | bytes 524320 | tf_op jit(solution)/shard_map/ppermute | solution.py:273
  48.0 5.3 %collective-permute-done.8.refs_1_.refs_3_.refs_7_ = bf16[128,16,128]{2,1,0:T(8,128)(2,1)S(1)} collective-permute-done((bf16[128,16,128]{2,1,0:T(8,128)(2,1)S(1)}, bf16[128,16,128]{2,1,0:T(8,128)(2,1)S(1)}, u32[]{:S(2)}, u32[]{:S(2)}) %collective-permute-start.8) | collective-permute-done | bytes 524320 | tf_op jit(solution)/shard_map/ppermute | solution.py:273
  53.3 3.8 %collective-permute-start.9 = (bf16[128,16,128]{2,1,0:T(8,128)(2,1)S(1)}, bf16[128,16,128]{2,1,0:T(8,128)(2,1)S(1)}, u32[]{:S(2)}, u32[]{:S(2)}) collective-permute-start(bf16[128,16,128]{2,1,0:T(8,128)(2,1)S(1)} %bitcast.4), channel_id=1, source_target_pairs={{8,24},{24,8},{1,9},{9,1},{13,29},{17,25},{25,17},{29,13},{2,10},{... | collective-permute-start | bytes 1572872 | tf_op jit(solution)/shard_map/ppermute | solution.py:273
  57.2 3.4 %own_rows.1.own = bf16[128,64,128]{2,1,0:T(8,128)(2,1)S(1)} custom-call(bf16[128,16,128]{2,1,0:T(8,128)(2,1)S(1)} %copy-done.1, bf16[128,16,128]{2,1,0:T(8,128)(2,1)S(1)} %collective-permute-done.refs_1_.refs_0_.refs_3_, bf16[128,16,128]{2,1,0:T(8,128)(2,1)S(1)} %collective-permute-done.1.refs_2_.refs_0_.refs_6_, ...), custom_call_target="tpu_custom_call" | custom-call | flops 1 | bytes 1 | tf_op jit(solution)/shard_map/own_rows/pallas_call | solution.py:145
  60.6 1.5 %collective-permute-done.6.refs_1_.refs_5_.refs_10_ = bf16[128,16,128]{2,1,0:T(8,128)(2,1)S(1)} collective-permute-done((bf16[128,16,128]{2,1,0:T(8,128)(2,1)S(1)}, bf16[128,16,128]{2,1,0:T(8,128)(2,1)S(1)}, u32[]{:S(2)}, u32[]{:S(2)}) %collective-permute-start.6) | collective-permute-done | bytes 524320 | tf_op jit(solution)/shard_map/ppermute | solution.py:273
  62.2 0.0 copy-start.2
  62.2 0.7 collective-permute-start.12
  62.9 2.4 %collective-permute-start.10 = (bf16[128,16,128]{2,1,0:T(8,128)(2,1)S(1)}, bf16[128,16,128]{2,1,0:T(8,128)(2,1)S(1)}, u32[]{:S(2)}, u32[]{:S(2)}) collective-permute-start(bf16[128,16,128]{2,1,0:T(8,128)(2,1)S(1)} %bitcast.5), channel_id=1, source_target_pairs={{8,24},{24,8},{1,9},{9,1},{13,29},{17,25},{25,17},{29,13},{2,10},{... | collective-permute-start | bytes 1572872 | tf_op jit(solution)/shard_map/ppermute | solution.py:273
  65.4 0.1 choose.10
  65.5 0.1 collective-permute-start.11
  65.6 0.0 collective-permute-done.12.refs_7_.refs_14_
  65.6 7.3 %collective-permute-done.10.refs_6_.refs_11_ = bf16[128,16,128]{2,1,0:T(8,128)(2,1)S(1)} collective-permute-done((bf16[128,16,128]{2,1,0:T(8,128)(2,1)S(1)}, bf16[128,16,128]{2,1,0:T(8,128)(2,1)S(1)}, u32[]{:S(2)}, u32[]{:S(2)}) %collective-permute-start.10) | collective-permute-done | bytes 524320 | tf_op jit(solution)/shard_map/ppermute | solution.py:273
  72.8 0.1 choose.11
  72.9 0.1 collective-permute-start.13
  73.0 2.6 %collective-permute-done.13.refs_13_ = bf16[2,128,16,128]{3,2,1,0:T(8,128)(2,1)S(1)} collective-permute-done((bf16[2,128,16,128]{3,2,1,0:T(8,128)(2,1)S(1)}, bf16[2,128,16,128]{3,2,1,0:T(8,128)(2,1)S(1)}, u32[]{:S(2)}, u32[]{:S(2)}) %collective-permute-start.13) | collective-permute-done | bytes 1048608 | tf_op jit(solution)/shard_map/ppermute | solution.py:273
  75.7 10.2 %stack.1 = f32[64,64,256]{2,1,0:T(8,128)} custom-call(s32[64]{0:T(128)S(1)} %copy-done.2, bf16[128,64,128]{2,1,0:T(8,128)(2,1)S(1)} %own_rows.1.own, bf16[128,16,128]{2,1,0:T(8,128)(2,1)S(1)} %copy-done.1, bf16[128,16,128]{2,1,0:T(8,128)(2,1)S(1)} %collective-permute-done.3.refs_1_, bf16[128,16,128]{2,1,0:T(8,128)(2,1)S(1)} %collective-permute-done.4.refs_2_, ...), custom_call_target="tpu_custom_call" | custom-call | flops 1 | bytes 1 | tf_op jit(solution)/shard_map/stack/pallas_call | solution.py:255
  (11 shorter events, 0.2 us)
Async XLA Ops:
  4.0 13.1 %collective-permute-start = (bf16[128,16,128]{2,1,0:T(8,128)(2,1)}, bf16[128,16,128]{2,1,0:T(8,128)(2,1)S(1)}, u32[]{:S(2)}, u32[]{:S(2)}) collective-permute-start(bf16[128,16,128]{2,1,0:T(8,128)(2,1)} %whiten.1.refs_0_), channel_id=1, source_target_pairs={{0,1},{1,2},{2,3},{3,0},{4,5},{5,6},{6,7},{7,4},{8,9},{9,10},{10,1... | collective-permute-start | bytes 1572872 | tf_op jit(solution)/shard_map/ppermute | solution.py:399
  5.4 13.0 %collective-permute-start.3 = (bf16[128,16,128]{2,1,0:T(8,128)(2,1)}, bf16[128,16,128]{2,1,0:T(8,128)(2,1)S(1)}, u32[]{:S(2)}, u32[]{:S(2)}) collective-permute-start(bf16[128,16,128]{2,1,0:T(8,128)(2,1)} %whiten.1.refs_0_), channel_id=1, source_target_pairs={{0,8},{8,0},{16,24},{24,16},{1,17},{5,13},{13,5},{17,1},{21,29},{2... | collective-permute-start | bytes 1572872 | tf_op jit(solution)/shard_map/ppermute | solution.py:273
  17.1 12.9 %collective-permute-start.1 = (bf16[128,16,128]{2,1,0:T(8,128)(2,1)S(1)}, bf16[128,16,128]{2,1,0:T(8,128)(2,1)S(1)}, u32[]{:S(2)}, u32[]{:S(2)}) collective-permute-start(bf16[128,16,128]{2,1,0:T(8,128)(2,1)S(1)} %collective-permute-done.refs_1_.refs_0_.refs_3_), channel_id=1, source_target_pairs={{0,1},{1,2},{2,3},{3,0},{4,5},{5,6},{6,7},{7,4},{8,9},{9,10},{10,1... | collective-permute-start | bytes 1572872 | tf_op jit(solution)/shard_map/ppermute | solution.py:399
  18.4 1.0 %copy-start = (bf16[128,16,128]{2,1,0:T(8,128)(2,1)S(1)}, bf16[128,16,128]{2,1,0:T(8,128)(2,1)}, u32[]{:S(2)}) copy-start(bf16[128,16,128]{2,1,0:T(8,128)(2,1)} %whiten.1.refs_0_) | copy-start | bytes 1572868
  19.4 37.8 %copy-start.1 = (bf16[128,16,128]{2,1,0:T(8,128)(2,1)S(1)}, bf16[128,16,128]{2,1,0:T(8,128)(2,1)}, u32[]{:S(2)}) copy-start(bf16[128,16,128]{2,1,0:T(8,128)(2,1)} %whiten.1.refs_0_) | copy-start | bytes 1572868
  19.4 10.8 %collective-permute-start.4 = (bf16[128,16,128]{2,1,0:T(8,128)(2,1)S(1)}, bf16[128,16,128]{2,1,0:T(8,128)(2,1)S(1)}, u32[]{:S(2)}, u32[]{:S(2)}) collective-permute-start(bf16[128,16,128]{2,1,0:T(8,128)(2,1)S(1)} %bitcast.6), channel_id=1, source_target_pairs={{8,24},{24,8},{1,9},{9,1},{13,29},{17,25},{25,17},{29,13},{2,10},{... | collective-permute-start | bytes 1572872 | tf_op jit(solution)/shard_map/ppermute | solution.py:273
  22.7 15.0 %collective-permute-start.5 = (bf16[128,16,128]{2,1,0:T(8,128)(2,1)S(1)}, bf16[128,16,128]{2,1,0:T(8,128)(2,1)S(1)}, u32[]{:S(2)}, u32[]{:S(2)}) collective-permute-start(bf16[128,16,128]{2,1,0:T(8,128)(2,1)S(1)} %collective-permute-done.refs_1_.refs_0_.refs_3_), channel_id=1, source_target_pairs={{0,8},{8,0},{16,24},{24,16},{1,17},{5,13},{13,5},{17,1},{21,29},{2... | collective-permute-start | bytes 1572872 | tf_op jit(solution)/shard_map/ppermute | solution.py:273
  29.9 12.8 %collective-permute-start.2 = (bf16[128,16,128]{2,1,0:T(8,128)(2,1)S(1)}, bf16[128,16,128]{2,1,0:T(8,128)(2,1)S(1)}, u32[]{:S(2)}, u32[]{:S(2)}) collective-permute-start(bf16[128,16,128]{2,1,0:T(8,128)(2,1)S(1)} %collective-permute-done.1.refs_2_.refs_0_.refs_6_), channel_id=1, source_target_pairs={{0,1},{1,2},{2,3},{3,0},{4,5},{5,6},{6,7},{7,4},{8,9},{9,10},{10,1... | collective-permute-start | bytes 1572872 | tf_op jit(solution)/shard_map/ppermute | solution.py:399
  37.7 10.2 %collective-permute-start.7 = (bf16[128,16,128]{2,1,0:T(8,128)(2,1)S(1)}, bf16[128,16,128]{2,1,0:T(8,128)(2,1)S(1)}, u32[]{:S(2)}, u32[]{:S(2)}) collective-permute-start(bf16[128,16,128]{2,1,0:T(8,128)(2,1)S(1)} %bitcast.7), channel_id=1, source_target_pairs={{8,24},{24,8},{1,9},{9,1},{13,29},{17,25},{25,17},{29,13},{2,10},{... | collective-permute-start | bytes 1572872 | tf_op jit(solution)/shard_map/ppermute | solution.py:273
  40.6 12.7 %collective-permute-start.8 = (bf16[128,16,128]{2,1,0:T(8,128)(2,1)S(1)}, bf16[128,16,128]{2,1,0:T(8,128)(2,1)S(1)}, u32[]{:S(2)}, u32[]{:S(2)}) collective-permute-start(bf16[128,16,128]{2,1,0:T(8,128)(2,1)S(1)} %collective-permute-done.1.refs_2_.refs_0_.refs_6_), channel_id=1, source_target_pairs={{0,8},{8,0},{16,24},{24,16},{1,17},{5,13},{13,5},{17,1},{21,29},{2... | collective-permute-start | bytes 1572872 | tf_op jit(solution)/shard_map/ppermute | solution.py:273
  42.7 19.4 %collective-permute-start.6 = (bf16[128,16,128]{2,1,0:T(8,128)(2,1)S(1)}, bf16[128,16,128]{2,1,0:T(8,128)(2,1)S(1)}, u32[]{:S(2)}, u32[]{:S(2)}) collective-permute-start(bf16[128,16,128]{2,1,0:T(8,128)(2,1)S(1)} %collective-permute-done.2.refs_3_.refs_0_.refs_4_.refs_9_), channel_id=1, source_target_pairs={{0,8},{8,0},{16,24},{24,16},{1,17},{5,13},{13,5},{17,1},{21,29},{2... | collective-permute-start | bytes 1572872 | tf_op jit(solution)/shard_map/ppermute | solution.py:273
  53.3 12.2 %collective-permute-start.9 = (bf16[128,16,128]{2,1,0:T(8,128)(2,1)S(1)}, bf16[128,16,128]{2,1,0:T(8,128)(2,1)S(1)}, u32[]{:S(2)}, u32[]{:S(2)}) collective-permute-start(bf16[128,16,128]{2,1,0:T(8,128)(2,1)S(1)} %bitcast.4), channel_id=1, source_target_pairs={{8,24},{24,8},{1,9},{9,1},{13,29},{17,25},{25,17},{29,13},{2,10},{... | collective-permute-start | bytes 1572872 | tf_op jit(solution)/shard_map/ppermute | solution.py:273
  62.2 13.5 %copy-start.2 = (s32[64]{0:T(128)S(1)}, s32[64]{0:T(128)}, u32[]{:S(2)}) copy-start(s32[64]{0:T(128)} %reach_ref.1) | copy-start | bytes 772
  62.2 3.4 %collective-permute-start.12 = (bf16[128,16,128]{2,1,0:T(8,128)(2,1)S(1)}, bf16[128,16,128]{2,1,0:T(8,128)(2,1)S(1)}, u32[]{:S(2)}, u32[]{:S(2)}) collective-permute-start(bf16[128,16,128]{2,1,0:T(8,128)(2,1)S(1)} %collective-permute-done.2.refs_3_.refs_0_.refs_4_.refs_9_), channel_id=1, source_target_pairs={{3,19},{11,27},{19,3},{27,11}} | collective-permute-start | bytes 1572872 | tf_op jit(solution)/shard_map/ppermute | solution.py:273
  62.9 9.9 %collective-permute-start.10 = (bf16[128,16,128]{2,1,0:T(8,128)(2,1)S(1)}, bf16[128,16,128]{2,1,0:T(8,128)(2,1)S(1)}, u32[]{:S(2)}, u32[]{:S(2)}) collective-permute-start(bf16[128,16,128]{2,1,0:T(8,128)(2,1)S(1)} %bitcast.5), channel_id=1, source_target_pairs={{8,24},{24,8},{1,9},{9,1},{13,29},{17,25},{25,17},{29,13},{2,10},{... | collective-permute-start | bytes 1572872 | tf_op jit(solution)/shard_map/ppermute | solution.py:273
  65.5 7.5 %collective-permute-start.11 = (bf16[2,128,16,128]{3,2,1,0:T(8,128)(2,1)S(1)}, bf16[2,128,16,128]{3,2,1,0:T(8,128)(2,1)S(1)}, u32[]{:S(2)}, u32[]{:S(2)}) collective-permute-start(bf16[2,128,16,128]{3,2,1,0:T(8,128)(2,1)S(1)} %choose.10), channel_id=1, source_target_pairs={{0,4},{4,0},{8,12},{12,8},{16,20},{20,16},{24,28},{28,24},{1,5},{5... | collective-permute-start | bytes 3145736 | tf_op jit(solution)/shard_map/ppermute | solution.py:273
  72.9 2.7 %collective-permute-start.13 = (bf16[2,128,16,128]{3,2,1,0:T(8,128)(2,1)S(1)}, bf16[2,128,16,128]{3,2,1,0:T(8,128)(2,1)S(1)}, u32[]{:S(2)}, u32[]{:S(2)}) collective-permute-start(bf16[2,128,16,128]{3,2,1,0:T(8,128)(2,1)S(1)} %choose.11), channel_id=1, source_target_pairs={{0,4},{4,0},{8,12},{12,8},{16,20},{20,16},{24,28},{28,24},{1,5},{5... | collective-permute-start | bytes 3145736 | tf_op jit(solution)/shard_map/ppermute | solution.py:273

commit v11 on v10

--- a/solution.py
+++ b/solution.py
@@ -13,7 +13,8 @@
 FIRST = 16
 BAND = 256
 AXES = ("chan", "win")
-CHANNEL_BLOCK = 8
+SUBLANES = 8
+BLOCK_TILES = 2
 WHITEN_BLOCKS = 4
 PITCH_PAD = 8
 MIB = 1024 * 1024
@@ -194,7 +195,7 @@
         products[pl.ds(row, width), :] = jnp.where(in_first, both[:, :lanes], both[:, lanes:])
         return carry
 
-    lax.fori_loop(0, bins, one_bin, 0, unroll=8)
+    lax.fori_loop(0, bins, one_bin, 0, unroll=16)
 
     lane = lax.broadcasted_iota(jnp.int32, (offsets, lanes), 1)
     shift = (lane + offsets * width - lax.broadcasted_iota(jnp.int32, (offsets, lanes), 0)) % width
@@ -202,47 +203,43 @@
     shift_im = jnp.where(lane < width, width, shift)
     row_k = lax.broadcasted_iota(jnp.int32, (offsets, F), 0) + first_offset
 
-    def copies(block):
-        columns = pl.ds(pl.multiple_of(block * CHANNEL_BLOCK, CHANNEL_BLOCK), CHANNEL_BLOCK)
-        return [
-            pltpu.make_async_copy(
-                out.at[part].reshape(offsets, pitch, F).at[:, columns, :],
-                out_hbm.at[:, columns, pl.ds(part * F, F)],
-                sems.at[block, part],
-            )
-            for part in range(2)
-        ]
+    tiles = out.shape[1]
+    rows = out.reshape(offsets * tiles * 2 * SUBLANES, F)
+
+    def copy(block):
+        part = pl.ds(block * BLOCK_TILES, BLOCK_TILES)
+        return pltpu.make_async_copy(out.at[:, part], out_hbm.at[:, part], sems.at[block])
 
     def one_block(block, carry):
-        for il in range(CHANNEL_BLOCK):
-            i = block * CHANNEL_BLOCK + il
-            at = (i + first) % width
-            pick = jnp.concatenate(
-                [
-                    jnp.where(shift_re == at, 1.0, 0.0),
-                    jnp.where(shift_im == at, -1.0, 0.0),
-                ],
-                axis=0,
-            ).astype(jnp.bfloat16)
-            x = products[pl.ds(i, F, stride=pitch), :].astype(jnp.bfloat16)
-            y = lax.dot_general(
-                pick, x, (((1,), (1,)), ((), ())), preferred_element_type=jnp.float32
-            )
-            inside = jnp.where(row_k < reach_ref[i], scale, 0.0)
-            for part in range(2):
-                out[part, pl.ds(i, offsets, stride=pitch), :] = (
-                    y[part * offsets : (part + 1) * offsets] * inside
+        for tile in range(BLOCK_TILES):
+            for sublane in range(SUBLANES):
+                i = (block * BLOCK_TILES + tile) * SUBLANES + sublane
+                at = (i + first) % width
+                pick = jnp.concatenate(
+                    [
+                        jnp.where(shift_re == at, 1.0, 0.0),
+                        jnp.where(shift_im == at, -1.0, 0.0),
+                    ],
+                    axis=0,
+                ).astype(jnp.bfloat16)
+                x = products[pl.ds(i, F, stride=pitch), :].astype(jnp.bfloat16)
+                y = lax.dot_general(
+                    pick, x, (((1,), (1,)), ((), ())), preferred_element_type=jnp.float32
                 )
-        for copy in copies(block):
-            copy.start()
+                inside = jnp.where(row_k < reach_ref[i], scale, 0.0)
+                for part in range(2):
+                    row = ((block * BLOCK_TILES + tile) * 2 + part) * SUBLANES + sublane
+                    rows[pl.ds(row, offsets, stride=tiles * 2 * SUBLANES), :] = (
+                        y[part * offsets : (part + 1) * offsets] * inside
+                    )
+        copy(block).start()
         return carry
 
-    blocks = width // CHANNEL_BLOCK
+    blocks = tiles // BLOCK_TILES
     lax.fori_loop(0, blocks, one_block, 0)
 
     def finish(block, carry):
-        for copy in copies(block):
-            copy.wait()
+        copy(block).wait()
         return carry
 
     lax.fori_loop(0, blocks, finish, 0)
@@ -252,21 +249,24 @@
     bins, width, _ = own.shape
     chunk_windows, lanes = buffers[0].shape[-2:]
     pitch = width + PITCH_PAD
-    return pl.pallas_call(
+    tiles = width // SUBLANES
+    out = (offsets, tiles, 2, SUBLANES, F)
+    result = pl.pallas_call(
         functools.partial(stack_kernel, 1.0 / math.sqrt(windows), groups, codes_of),
-        out_shape=jax.ShapeDtypeStruct((offsets, width, 2 * F), jnp.float32),
+        out_shape=jax.ShapeDtypeStruct(out, jnp.float32),
         in_specs=[SMEM] + [VMEM] * (1 + len(buffers)),
         out_specs=ANY,
         scratch_shapes=[
             pltpu.VMEM((2, len(groups), bins, chunk_windows, lanes), jnp.bfloat16),
             pltpu.VMEM((bins * pitch, lanes), jnp.float32),
-            pltpu.VMEM((2, offsets * pitch, F), jnp.float32),
-            pltpu.SemaphoreType.DMA((width // CHANNEL_BLOCK, 2)),
+            pltpu.VMEM(out, jnp.float32),
+            pltpu.SemaphoreType.DMA((tiles // BLOCK_TILES,)),
         ],
         compiler_params=pltpu.CompilerParams(vmem_limit_bytes=28 * MIB),
         cost_estimate=SMALL,
         name="stack",
     )(reach, own, *buffers)
+    return result.transpose(0, 1, 3, 2, 4).reshape(offsets, width, 2 * F)
 
 
 def send(array, pairs):

time: 86.3 us -> 87.1 us (level)
  no operation moved by 1% of the time
where the time goes in v11:
time: 87.1 us; the launch traced here: 86.7 us
  waiting for transfers between devices  41.3 us (47%)
  starting transfers between devices  25.3 us (29%)
  Pallas kernels  18.8 us (22%)
  local copies, waits for them, and re-layouts  1.05 us (1%)
    ppermute x11, waiting for transfers between devices, send(): return lax.ppermute(array, AXES, pairs)  26.3 us
    ppermute x11, starting transfers between devices, send(): return lax.ppermute(array, AXES, pairs)  22.4 us
    ppermute x3, waiting for transfers between devices, on_device(): pieces.append(lax.ppermute(pieces[-1], 'win', ring))  15 us
    pallas_call x1, Pallas kernels, stacked(): pl.pallas_call(functools.partial(stack_kernel, 1.0 / math.sqrt(windows),...  11 us
    pallas_call x1, Pallas kernels, whitened_chunk(): pl.pallas_call(whiten_kernel, out_shape=jax.ShapeDtypeStruct((F, windows,...  4 us
    pallas_call x1, Pallas kernels, own_rows(): pl.pallas_call(own_kernel, out_shape=jax.ShapeDtypeStruct((bins, lanes //...  3.44 us
    ppermute x3, starting transfers between devices, on_device(): pieces.append(lax.ppermute(pieces[-1], 'win', ring))  2.93 us
  transfers between devices with their start and end apart: 14, of which 9 were waited for; matrix products, arithmetic and copies ran while one was open for 0% of the time, Pallas kernels for 4%

profile of v11, /device:TPU:11, one launch (start us, length us, event | category | flops | bytes accessed | tf_op | source)
XLA Modules:
  0.0 86.7 jit_solution(4287160139865258633)
XLA Ops:
  0.0 4.0 %whiten.1.refs_0_ = bf16[128,16,128]{2,1,0:T(8,128)(2,1)} custom-call(bf16[256,512]{1,0:T(8,128)(2,1)} %constant.3.table_hbm, bf16[16,64,512]{2,1,0:T(8,128)(2,1)} %traces_hbm.1, s32[16,64]{1,0:T(8,128)} %valid_hbm.1), custom_call_target="tpu_custom_call" | custom-call | flops 268435456 | bytes 1048576 | tf_op jit(solution)/shard_map/whiten/pallas_call | solution.py:79
  4.0 1.3 %collective-permute-start = (bf16[128,16,128]{2,1,0:T(8,128)(2,1)}, bf16[128,16,128]{2,1,0:T(8,128)(2,1)S(1)}, u32[]{:S(2)}, u32[]{:S(2)}) collective-permute-start(bf16[128,16,128]{2,1,0:T(8,128)(2,1)} %whiten.1.refs_0_), channel_id=1, source_target_pairs={{0,1},{1,2},{2,3},{3,0},{4,5},{5,6},{6,7},{7,4},{8,9},{9,10},{10,1... | collective-permute-start | bytes 1572872 | tf_op jit(solution)/shard_map/ppermute | solution.py:399
  5.4 2.2 %collective-permute-start.3 = (bf16[128,16,128]{2,1,0:T(8,128)(2,1)}, bf16[128,16,128]{2,1,0:T(8,128)(2,1)S(1)}, u32[]{:S(2)}, u32[]{:S(2)}) collective-permute-start(bf16[128,16,128]{2,1,0:T(8,128)(2,1)} %whiten.1.refs_0_), channel_id=1, source_target_pairs={{0,8},{8,0},{16,24},{24,16},{1,17},{5,13},{13,5},{17,1},{21,29},{2... | collective-permute-start | bytes 1572872 | tf_op jit(solution)/shard_map/ppermute | solution.py:273
  7.5 9.5 %collective-permute-done.refs_1_.refs_0_.refs_3_ = bf16[128,16,128]{2,1,0:T(8,128)(2,1)S(1)} collective-permute-done((bf16[128,16,128]{2,1,0:T(8,128)(2,1)}, bf16[128,16,128]{2,1,0:T(8,128)(2,1)S(1)}, u32[]{:S(2)}, u32[]{:S(2)}) %collective-permute-start) | collective-permute-done | bytes 524320 | tf_op jit(solution)/shard_map/ppermute | solution.py:399
  17.1 1.3 %collective-permute-start.1 = (bf16[128,16,128]{2,1,0:T(8,128)(2,1)S(1)}, bf16[128,16,128]{2,1,0:T(8,128)(2,1)S(1)}, u32[]{:S(2)}, u32[]{:S(2)}) collective-permute-start(bf16[128,16,128]{2,1,0:T(8,128)(2,1)S(1)} %collective-permute-done.refs_1_.refs_0_.refs_3_), channel_id=1, source_target_pairs={{0,1},{1,2},{2,3},{3,0},{4,5},{5,6},{6,7},{7,4},{8,9},{9,10},{10,1... | collective-permute-start | bytes 1572872 | tf_op jit(solution)/shard_map/ppermute | solution.py:399
  18.4 1.0 %copy-done = bf16[128,16,128]{2,1,0:T(8,128)(2,1)S(1)} copy-done((bf16[128,16,128]{2,1,0:T(8,128)(2,1)S(1)}, bf16[128,16,128]{2,1,0:T(8,128)(2,1)}, u32[]{:S(2)}) %copy-start) | copy-done | bytes 524312
  19.4 3.3 %collective-permute-start.4 = (bf16[128,16,128]{2,1,0:T(8,128)(2,1)S(1)}, bf16[128,16,128]{2,1,0:T(8,128)(2,1)S(1)}, u32[]{:S(2)}, u32[]{:S(2)}) collective-permute-start(bf16[128,16,128]{2,1,0:T(8,128)(2,1)S(1)} %bitcast.9), channel_id=1, source_target_pairs={{8,24},{24,8},{1,9},{9,1},{13,29},{17,25},{25,17},{29,13},{2,10},{... | collective-permute-start | bytes 1572872 | tf_op jit(solution)/shard_map/ppermute | solution.py:273
  22.7 1.9 %collective-permute-start.5 = (bf16[128,16,128]{2,1,0:T(8,128)(2,1)S(1)}, bf16[128,16,128]{2,1,0:T(8,128)(2,1)S(1)}, u32[]{:S(2)}, u32[]{:S(2)}) collective-permute-start(bf16[128,16,128]{2,1,0:T(8,128)(2,1)S(1)} %collective-permute-done.refs_1_.refs_0_.refs_3_), channel_id=1, source_target_pairs={{0,8},{8,0},{16,24},{24,16},{1,17},{5,13},{13,5},{17,1},{21,29},{2... | collective-permute-start | bytes 1572872 | tf_op jit(solution)/shard_map/ppermute | solution.py:273
  24.7 5.3 %collective-permute-done.1.refs_2_.refs_0_.refs_6_ = bf16[128,16,128]{2,1,0:T(8,128)(2,1)S(1)} collective-permute-done((bf16[128,16,128]{2,1,0:T(8,128)(2,1)S(1)}, bf16[128,16,128]{2,1,0:T(8,128)(2,1)S(1)}, u32[]{:S(2)}, u32[]{:S(2)}) %collective-permute-start.1) | collective-permute-done | bytes 524320 | tf_op jit(solution)/shard_map/ppermute | solution.py:399
  29.9 0.3 collective-permute-start.2
  30.2 0.0 collective-permute-done.4.refs_2_
  30.2 7.5 %collective-permute-done.5.refs_1_.refs_4_ = bf16[128,16,128]{2,1,0:T(8,128)(2,1)S(1)} collective-permute-done((bf16[128,16,128]{2,1,0:T(8,128)(2,1)S(1)}, bf16[128,16,128]{2,1,0:T(8,128)(2,1)S(1)}, u32[]{:S(2)}, u32[]{:S(2)}) %collective-permute-start.5) | collective-permute-done | bytes 524320 | tf_op jit(solution)/shard_map/ppermute | solution.py:273
  37.7 2.8 %collective-permute-start.7 = (bf16[128,16,128]{2,1,0:T(8,128)(2,1)S(1)}, bf16[128,16,128]{2,1,0:T(8,128)(2,1)S(1)}, u32[]{:S(2)}, u32[]{:S(2)}) collective-permute-start(bf16[128,16,128]{2,1,0:T(8,128)(2,1)S(1)} %bitcast.10), channel_id=1, source_target_pairs={{8,24},{24,8},{1,9},{9,1},{13,29},{17,25},{25,17},{29,13},{2,10},{... | collective-permute-start | bytes 1572872 | tf_op jit(solution)/shard_map/ppermute | solution.py:273
  40.6 1.9 %collective-permute-start.8 = (bf16[128,16,128]{2,1,0:T(8,128)(2,1)S(1)}, bf16[128,16,128]{2,1,0:T(8,128)(2,1)S(1)}, u32[]{:S(2)}, u32[]{:S(2)}) collective-permute-start(bf16[128,16,128]{2,1,0:T(8,128)(2,1)S(1)} %collective-permute-done.1.refs_2_.refs_0_.refs_6_), channel_id=1, source_target_pairs={{0,8},{8,0},{16,24},{24,16},{1,17},{5,13},{13,5},{17,1},{21,29},{2... | collective-permute-start | bytes 1572872 | tf_op jit(solution)/shard_map/ppermute | solution.py:273
  42.5 0.2 collective-permute-done.2.refs_3_.refs_0_.refs_4_.refs_9_
  42.7 3.1 %collective-permute-start.6 = (bf16[128,16,128]{2,1,0:T(8,128)(2,1)S(1)}, bf16[128,16,128]{2,1,0:T(8,128)(2,1)S(1)}, u32[]{:S(2)}, u32[]{:S(2)}) collective-permute-start(bf16[128,16,128]{2,1,0:T(8,128)(2,1)S(1)} %collective-permute-done.2.refs_3_.refs_0_.refs_4_.refs_9_), channel_id=1, source_target_pairs={{0,8},{8,0},{16,24},{24,16},{1,17},{5,13},{13,5},{17,1},{21,29},{2... | collective-permute-start | bytes 1572872 | tf_op jit(solution)/shard_map/ppermute | solution.py:273
  45.9 2.1 %collective-permute-done.7.refs_5_ = bf16[128,16,128]{2,1,0:T(8,128)(2,1)S(1)} collective-permute-done((bf16[128,16,128]{2,1,0:T(8,128)(2,1)S(1)}, bf16[128,16,128]{2,1,0:T(8,128)(2,1)S(1)}, u32[]{:S(2)}, u32[]{:S(2)}) %collective-permute-start.7) | collective-permute-done | bytes 524320 | tf_op jit(solution)/shard_map/ppermute | solution.py:273
  48.0 5.3 %collective-permute-done.8.refs_1_.refs_3_.refs_7_ = bf16[128,16,128]{2,1,0:T(8,128)(2,1)S(1)} collective-permute-done((bf16[128,16,128]{2,1,0:T(8,128)(2,1)S(1)}, bf16[128,16,128]{2,1,0:T(8,128)(2,1)S(1)}, u32[]{:S(2)}, u32[]{:S(2)}) %collective-permute-start.8) | collective-permute-done | bytes 524320 | tf_op jit(solution)/shard_map/ppermute | solution.py:273
  53.3 3.8 %collective-permute-start.9 = (bf16[128,16,128]{2,1,0:T(8,128)(2,1)S(1)}, bf16[128,16,128]{2,1,0:T(8,128)(2,1)S(1)}, u32[]{:S(2)}, u32[]{:S(2)}) collective-permute-start(bf16[128,16,128]{2,1,0:T(8,128)(2,1)S(1)} %bitcast.7), channel_id=1, source_target_pairs={{8,24},{24,8},{1,9},{9,1},{13,29},{17,25},{25,17},{29,13},{2,10},{... | collective-permute-start | bytes 1572872 | tf_op jit(solution)/shard_map/ppermute | solution.py:273
  57.2 3.4 %own_rows.1.own = bf16[128,64,128]{2,1,0:T(8,128)(2,1)S(1)} custom-call(bf16[128,16,128]{2,1,0:T(8,128)(2,1)S(1)} %copy-done.1, bf16[128,16,128]{2,1,0:T(8,128)(2,1)S(1)} %collective-permute-done.refs_1_.refs_0_.refs_3_, bf16[128,16,128]{2,1,0:T(8,128)(2,1)S(1)} %collective-permute-done.1.refs_2_.refs_0_.refs_6_, ...), custom_call_target="tpu_custom_call" | custom-call | flops 1 | bytes 1 | tf_op jit(solution)/shard_map/own_rows/pallas_call | solution.py:146
  60.6 1.5 %collective-permute-done.6.refs_1_.refs_5_.refs_10_ = bf16[128,16,128]{2,1,0:T(8,128)(2,1)S(1)} collective-permute-done((bf16[128,16,128]{2,1,0:T(8,128)(2,1)S(1)}, bf16[128,16,128]{2,1,0:T(8,128)(2,1)S(1)}, u32[]{:S(2)}, u32[]{:S(2)}) %collective-permute-start.6) | collective-permute-done | bytes 524320 | tf_op jit(solution)/shard_map/ppermute | solution.py:273
  62.2 0.0 copy-start.2
  62.2 0.7 collective-permute-start.12
  62.9 2.4 %collective-permute-start.10 = (bf16[128,16,128]{2,1,0:T(8,128)(2,1)S(1)}, bf16[128,16,128]{2,1,0:T(8,128)(2,1)S(1)}, u32[]{:S(2)}, u32[]{:S(2)}) collective-permute-start(bf16[128,16,128]{2,1,0:T(8,128)(2,1)S(1)} %bitcast.8), channel_id=1, source_target_pairs={{8,24},{24,8},{1,9},{9,1},{13,29},{17,25},{25,17},{29,13},{2,10},{... | collective-permute-start | bytes 1572872 | tf_op jit(solution)/shard_map/ppermute | solution.py:273
  65.4 0.1 choose.10
  65.5 0.1 collective-permute-start.11
  65.5 0.0 collective-permute-done.9.refs_2_.refs_8_
  65.6 7.3 %collective-permute-done.10.refs_6_.refs_11_ = bf16[128,16,128]{2,1,0:T(8,128)(2,1)S(1)} collective-permute-done((bf16[128,16,128]{2,1,0:T(8,128)(2,1)S(1)}, bf16[128,16,128]{2,1,0:T(8,128)(2,1)S(1)}, u32[]{:S(2)}, u32[]{:S(2)}) %collective-permute-start.10) | collective-permute-done | bytes 524320 | tf_op jit(solution)/shard_map/ppermute | solution.py:273
  72.8 0.1 choose.11
  72.9 0.1 collective-permute-start.13
  73.0 2.6 %collective-permute-done.13.refs_13_ = bf16[2,128,16,128]{3,2,1,0:T(8,128)(2,1)S(1)} collective-permute-done((bf16[2,128,16,128]{3,2,1,0:T(8,128)(2,1)S(1)}, bf16[2,128,16,128]{3,2,1,0:T(8,128)(2,1)S(1)}, u32[]{:S(2)}, u32[]{:S(2)}) %collective-permute-start.13) | collective-permute-done | bytes 1048608 | tf_op jit(solution)/shard_map/ppermute | solution.py:273
  75.7 11.0 %stack.1 = f32[64,8,2,8,128]{4,3,2,1,0:T(8,128)} custom-call(s32[64]{0:T(128)S(1)} %copy-done.2, bf16[128,64,128]{2,1,0:T(8,128)(2,1)S(1)} %own_rows.1.own, bf16[128,16,128]{2,1,0:T(8,128)(2,1)S(1)} %copy-done.1, bf16[128,16,128]{2,1,0:T(8,128)(2,1)S(1)} %collective-permute-done.3.refs_1_, bf16[128,16,128]{2,1,0:T(8,128)(2,1)S(1)} %collective-permute-done.4.refs_2_, ...), custom_call_target="tpu_custom_call" | custom-call | flops 1 | bytes 1 | tf_op jit(solution)/shard_map/stack/pallas_call | solution.py:254
  (11 shorter events, 0.2 us)
Async XLA Ops:
  4.0 13.1 %collective-permute-start = (bf16[128,16,128]{2,1,0:T(8,128)(2,1)}, bf16[128,16,128]{2,1,0:T(8,128)(2,1)S(1)}, u32[]{:S(2)}, u32[]{:S(2)}) collective-permute-start(bf16[128,16,128]{2,1,0:T(8,128)(2,1)} %whiten.1.refs_0_), channel_id=1, source_target_pairs={{0,1},{1,2},{2,3},{3,0},{4,5},{5,6},{6,7},{7,4},{8,9},{9,10},{10,1... | collective-permute-start | bytes 1572872 | tf_op jit(solution)/shard_map/ppermute | solution.py:399
  5.4 13.0 %collective-permute-start.3 = (bf16[128,16,128]{2,1,0:T(8,128)(2,1)}, bf16[128,16,128]{2,1,0:T(8,128)(2,1)S(1)}, u32[]{:S(2)}, u32[]{:S(2)}) collective-permute-start(bf16[128,16,128]{2,1,0:T(8,128)(2,1)} %whiten.1.refs_0_), channel_id=1, source_target_pairs={{0,8},{8,0},{16,24},{24,16},{1,17},{5,13},{13,5},{17,1},{21,29},{2... | collective-permute-start | bytes 1572872 | tf_op jit(solution)/shard_map/ppermute | solution.py:273
  17.1 12.9 %collective-permute-start.1 = (bf16[128,16,128]{2,1,0:T(8,128)(2,1)S(1)}, bf16[128,16,128]{2,1,0:T(8,128)(2,1)S(1)}, u32[]{:S(2)}, u32[]{:S(2)}) collective-permute-start(bf16[128,16,128]{2,1,0:T(8,128)(2,1)S(1)} %collective-permute-done.refs_1_.refs_0_.refs_3_), channel_id=1, source_target_pairs={{0,1},{1,2},{2,3},{3,0},{4,5},{5,6},{6,7},{7,4},{8,9},{9,10},{10,1... | collective-permute-start | bytes 1572872 | tf_op jit(solution)/shard_map/ppermute | solution.py:399
  18.4 1.0 %copy-start = (bf16[128,16,128]{2,1,0:T(8,128)(2,1)S(1)}, bf16[128,16,128]{2,1,0:T(8,128)(2,1)}, u32[]{:S(2)}) copy-start(bf16[128,16,128]{2,1,0:T(8,128)(2,1)} %whiten.1.refs_0_) | copy-start | bytes 1572868
  19.4 37.8 %copy-start.1 = (bf16[128,16,128]{2,1,0:T(8,128)(2,1)S(1)}, bf16[128,16,128]{2,1,0:T(8,128)(2,1)}, u32[]{:S(2)}) copy-start(bf16[128,16,128]{2,1,0:T(8,128)(2,1)} %whiten.1.refs_0_) | copy-start | bytes 1572868
  19.4 10.8 %collective-permute-start.4 = (bf16[128,16,128]{2,1,0:T(8,128)(2,1)S(1)}, bf16[128,16,128]{2,1,0:T(8,128)(2,1)S(1)}, u32[]{:S(2)}, u32[]{:S(2)}) collective-permute-start(bf16[128,16,128]{2,1,0:T(8,128)(2,1)S(1)} %bitcast.9), channel_id=1, source_target_pairs={{8,24},{24,8},{1,9},{9,1},{13,29},{17,25},{25,17},{29,13},{2,10},{... | collective-permute-start | bytes 1572872 | tf_op jit(solution)/shard_map/ppermute | solution.py:273
  22.7 15.0 %collective-permute-start.5 = (bf16[128,16,128]{2,1,0:T(8,128)(2,1)S(1)}, bf16[128,16,128]{2,1,0:T(8,128)(2,1)S(1)}, u32[]{:S(2)}, u32[]{:S(2)}) collective-permute-start(bf16[128,16,128]{2,1,0:T(8,128)(2,1)S(1)} %collective-permute-done.refs_1_.refs_0_.refs_3_), channel_id=1, source_target_pairs={{0,8},{8,0},{16,24},{24,16},{1,17},{5,13},{13,5},{17,1},{21,29},{2... | collective-permute-start | bytes 1572872 | tf_op jit(solution)/shard_map/ppermute | solution.py:273
  29.9 12.8 %collective-permute-start.2 = (bf16[128,16,128]{2,1,0:T(8,128)(2,1)S(1)}, bf16[128,16,128]{2,1,0:T(8,128)(2,1)S(1)}, u32[]{:S(2)}, u32[]{:S(2)}) collective-permute-start(bf16[128,16,128]{2,1,0:T(8,128)(2,1)S(1)} %collective-permute-done.1.refs_2_.refs_0_.refs_6_), channel_id=1, source_target_pairs={{0,1},{1,2},{2,3},{3,0},{4,5},{5,6},{6,7},{7,4},{8,9},{9,10},{10,1... | collective-permute-start | bytes 1572872 | tf_op jit(solution)/shard_map/ppermute | solution.py:399
  37.7 10.2 %collective-permute-start.7 = (bf16[128,16,128]{2,1,0:T(8,128)(2,1)S(1)}, bf16[128,16,128]{2,1,0:T(8,128)(2,1)S(1)}, u32[]{:S(2)}, u32[]{:S(2)}) collective-permute-start(bf16[128,16,128]{2,1,0:T(8,128)(2,1)S(1)} %bitcast.10), channel_id=1, source_target_pairs={{8,24},{24,8},{1,9},{9,1},{13,29},{17,25},{25,17},{29,13},{2,10},{... | collective-permute-start | bytes 1572872 | tf_op jit(solution)/shard_map/ppermute | solution.py:273
  40.6 12.7 %collective-permute-start.8 = (bf16[128,16,128]{2,1,0:T(8,128)(2,1)S(1)}, bf16[128,16,128]{2,1,0:T(8,128)(2,1)S(1)}, u32[]{:S(2)}, u32[]{:S(2)}) collective-permute-start(bf16[128,16,128]{2,1,0:T(8,128)(2,1)S(1)} %collective-permute-done.1.refs_2_.refs_0_.refs_6_), channel_id=1, source_target_pairs={{0,8},{8,0},{16,24},{24,16},{1,17},{5,13},{13,5},{17,1},{21,29},{2... | collective-permute-start | bytes 1572872 | tf_op jit(solution)/shard_map/ppermute | solution.py:273
  42.7 19.4 %collective-permute-start.6 = (bf16[128,16,128]{2,1,0:T(8,128)(2,1)S(1)}, bf16[128,16,128]{2,1,0:T(8,128)(2,1)S(1)}, u32[]{:S(2)}, u32[]{:S(2)}) collective-permute-start(bf16[128,16,128]{2,1,0:T(8,128)(2,1)S(1)} %collective-permute-done.2.refs_3_.refs_0_.refs_4_.refs_9_), channel_id=1, source_target_pairs={{0,8},{8,0},{16,24},{24,16},{1,17},{5,13},{13,5},{17,1},{21,29},{2... | collective-permute-start | bytes 1572872 | tf_op jit(solution)/shard_map/ppermute | solution.py:273
  53.3 12.2 %collective-permute-start.9 = (bf16[128,16,128]{2,1,0:T(8,128)(2,1)S(1)}, bf16[128,16,128]{2,1,0:T(8,128)(2,1)S(1)}, u32[]{:S(2)}, u32[]{:S(2)}) collective-permute-start(bf16[128,16,128]{2,1,0:T(8,128)(2,1)S(1)} %bitcast.7), channel_id=1, source_target_pairs={{8,24},{24,8},{1,9},{9,1},{13,29},{17,25},{25,17},{29,13},{2,10},{... | collective-permute-start | bytes 1572872 | tf_op jit(solution)/shard_map/ppermute | solution.py:273
  62.2 13.5 %copy-start.2 = (s32[64]{0:T(128)S(1)}, s32[64]{0:T(128)}, u32[]{:S(2)}) copy-start(s32[64]{0:T(128)} %reach_ref.1) | copy-start | bytes 772
  62.2 3.4 %collective-permute-start.12 = (bf16[128,16,128]{2,1,0:T(8,128)(2,1)S(1)}, bf16[128,16,128]{2,1,0:T(8,128)(2,1)S(1)}, u32[]{:S(2)}, u32[]{:S(2)}) collective-permute-start(bf16[128,16,128]{2,1,0:T(8,128)(2,1)S(1)} %collective-permute-done.2.refs_3_.refs_0_.refs_4_.refs_9_), channel_id=1, source_target_pairs={{3,19},{11,27},{19,3},{27,11}} | collective-permute-start | bytes 1572872 | tf_op jit(solution)/shard_map/ppermute | solution.py:273
  62.9 9.9 %collective-permute-start.10 = (bf16[128,16,128]{2,1,0:T(8,128)(2,1)S(1)}, bf16[128,16,128]{2,1,0:T(8,128)(2,1)S(1)}, u32[]{:S(2)}, u32[]{:S(2)}) collective-permute-start(bf16[128,16,128]{2,1,0:T(8,128)(2,1)S(1)} %bitcast.8), channel_id=1, source_target_pairs={{8,24},{24,8},{1,9},{9,1},{13,29},{17,25},{25,17},{29,13},{2,10},{... | collective-permute-start | bytes 1572872 | tf_op jit(solution)/shard_map/ppermute | solution.py:273
  65.5 7.5 %collective-permute-start.11 = (bf16[2,128,16,128]{3,2,1,0:T(8,128)(2,1)S(1)}, bf16[2,128,16,128]{3,2,1,0:T(8,128)(2,1)S(1)}, u32[]{:S(2)}, u32[]{:S(2)}) collective-permute-start(bf16[2,128,16,128]{3,2,1,0:T(8,128)(2,1)S(1)} %choose.10), channel_id=1, source_target_pairs={{0,4},{4,0},{8,12},{12,8},{16,20},{20,16},{24,28},{28,24},{1,5},{5... | collective-permute-start | bytes 3145736 | tf_op jit(solution)/shard_map/ppermute | solution.py:273
  72.9 2.7 %collective-permute-start.13 = (bf16[2,128,16,128]{3,2,1,0:T(8,128)(2,1)S(1)}, bf16[2,128,16,128]{3,2,1,0:T(8,128)(2,1)S(1)}, u32[]{:S(2)}, u32[]{:S(2)}) collective-permute-start(bf16[2,128,16,128]{3,2,1,0:T(8,128)(2,1)S(1)} %choose.11), channel_id=1, source_target_pairs={{0,4},{4,0},{8,12},{12,8},{16,20},{20,16},{24,28},{28,24},{1,5},{5... | collective-permute-start | bytes 3145736 | tf_op jit(solution)/shard_map/ppermute | solution.py:273

commit v12 on v10

--- a/solution.py
+++ b/solution.py
@@ -14,6 +14,7 @@
 BAND = 256
 AXES = ("chan", "win")
 CHANNEL_BLOCK = 8
+GROUP = 4
 WHITEN_BLOCKS = 4
 PITCH_PAD = 8
 MIB = 1024 * 1024
@@ -180,7 +181,7 @@
     lane = lax.broadcasted_iota(jnp.int32, (width, lanes), 1)
     in_first = lane % width >= lax.broadcasted_iota(jnp.int32, (width, lanes), 0) + first
 
-    def one_bin(f, carry):
+    def products_of(f):
         tops = [
             jnp.concatenate([partners[which, slot, f] for slot in range(slots)], axis=0)
             for which in range(2)
@@ -190,11 +191,16 @@
             [jnp.concatenate(tops, axis=1), jnp.concatenate(bottoms, axis=1)], axis=0
         )
         both = jnp.dot(own[f], right, preferred_element_type=jnp.float32)
-        row = pl.multiple_of(f * pitch, 8)
-        products[pl.ds(row, width), :] = jnp.where(in_first, both[:, :lanes], both[:, lanes:])
+        return jnp.where(in_first, both[:, :lanes], both[:, lanes:])
+
+    def one_group(group, carry):
+        results = [products_of(group * GROUP + n) for n in range(GROUP)]
+        for n, result in enumerate(results):
+            row = pl.multiple_of((group * GROUP + n) * pitch, 8)
+            products[pl.ds(row, width), :] = result
         return carry
 
-    lax.fori_loop(0, bins, one_bin, 0, unroll=8)
+    lax.fori_loop(0, bins // GROUP, one_group, 0, unroll=2)
 
     lane = lax.broadcasted_iota(jnp.int32, (offsets, lanes), 1)
     shift = (lane + offsets * width - lax.broadcasted_iota(jnp.int32, (offsets, lanes), 0)) % width
@@ -213,26 +219,25 @@
             for part in range(2)
         ]
 
+    def picked(i):
+        at = (i + first) % width
+        pick = jnp.concatenate(
+            [jnp.where(shift_re == at, 1.0, 0.0), jnp.where(shift_im == at, -1.0, 0.0)], axis=0
+        ).astype(jnp.bfloat16)
+        x = products[pl.ds(i, F, stride=pitch), :].astype(jnp.bfloat16)
+        y = lax.dot_general(
+            pick, x, (((1,), (1,)), ((), ())), preferred_element_type=jnp.float32
+        )
+        inside = jnp.where(row_k < reach_ref[i], scale, 0.0)
+        return [y[part * offsets : (part + 1) * offsets] * inside for part in range(2)]
+
     def one_block(block, carry):
-        for il in range(CHANNEL_BLOCK):
-            i = block * CHANNEL_BLOCK + il
-            at = (i + first) % width
-            pick = jnp.concatenate(
-                [
-                    jnp.where(shift_re == at, 1.0, 0.0),
-                    jnp.where(shift_im == at, -1.0, 0.0),
-                ],
-                axis=0,
-            ).astype(jnp.bfloat16)
-            x = products[pl.ds(i, F, stride=pitch), :].astype(jnp.bfloat16)
-            y = lax.dot_general(
-                pick, x, (((1,), (1,)), ((), ())), preferred_element_type=jnp.float32
-            )
-            inside = jnp.where(row_k < reach_ref[i], scale, 0.0)
-            for part in range(2):
-                out[part, pl.ds(i, offsets, stride=pitch), :] = (
-                    y[part * offsets : (part + 1) * offsets] * inside
-                )
+        for begin in range(0, CHANNEL_BLOCK, GROUP):
+            channels = [block * CHANNEL_BLOCK + begin + n for n in range(GROUP)]
+            results = [picked(i) for i in channels]
+            for i, result in zip(channels, results):
+                for part in range(2):
+                    out[part, pl.ds(i, offsets, stride=pitch), :] = result[part]
         for copy in copies(block):
             copy.start()
         return carry

time: 86.3 us -> 86.3 us (level)
  no operation moved by 1% of the time
where the time goes in v12:
time: 86.3 us; the launch traced here: 85.9 us
  waiting for transfers between devices  41.3 us (48%)
  starting transfers between devices  25.3 us (29%)
  Pallas kernels  18 us (21%)
  local copies, waits for them, and re-layouts  1.05 us (1%)
    ppermute x11, waiting for transfers between devices, send(): return lax.ppermute(array, AXES, pairs)  26.3 us
    ppermute x11, starting transfers between devices, send(): return lax.ppermute(array, AXES, pairs)  22.4 us
    ppermute x3, waiting for transfers between devices, on_device(): pieces.append(lax.ppermute(pieces[-1], 'win', ring))  15 us
    pallas_call x1, Pallas kernels, stacked(): pl.pallas_call(functools.partial(stack_kernel, 1.0 / math.sqrt(windows),...  10.2 us
    pallas_call x1, Pallas kernels, whitened_chunk(): pl.pallas_call(whiten_kernel, out_shape=jax.ShapeDtypeStruct((F, windows,...  4 us
    pallas_call x1, Pallas kernels, own_rows(): pl.pallas_call(own_kernel, out_shape=jax.ShapeDtypeStruct((bins, lanes //...  3.44 us
    ppermute x3, starting transfers between devices, on_device(): pieces.append(lax.ppermute(pieces[-1], 'win', ring))  2.93 us
  transfers between devices with their start and end apart: 14, of which 9 were waited for; matrix products, arithmetic and copies ran while one was open for 0% of the time, Pallas kernels for 4%

profile of v12, /device:TPU:11, one launch (start us, length us, event | category | flops | bytes accessed | tf_op | source)
XLA Modules:
  0.0 85.9 jit_solution(10854721527162508082)
XLA Ops:
  0.0 4.0 %whiten.1.refs_0_ = bf16[128,16,128]{2,1,0:T(8,128)(2,1)} custom-call(bf16[256,512]{1,0:T(8,128)(2,1)} %constant.3.table_hbm, bf16[16,64,512]{2,1,0:T(8,128)(2,1)} %traces_hbm.1, s32[16,64]{1,0:T(8,128)} %valid_hbm.1), custom_call_target="tpu_custom_call" | custom-call | flops 268435456 | bytes 1048576 | tf_op jit(solution)/shard_map/whiten/pallas_call | solution.py:79
  4.0 1.3 %collective-permute-start = (bf16[128,16,128]{2,1,0:T(8,128)(2,1)}, bf16[128,16,128]{2,1,0:T(8,128)(2,1)S(1)}, u32[]{:S(2)}, u32[]{:S(2)}) collective-permute-start(bf16[128,16,128]{2,1,0:T(8,128)(2,1)} %whiten.1.refs_0_), channel_id=1, source_target_pairs={{0,1},{1,2},{2,3},{3,0},{4,5},{5,6},{6,7},{7,4},{8,9},{9,10},{10,1... | collective-permute-start | bytes 1572872 | tf_op jit(solution)/shard_map/ppermute | solution.py:404
  5.4 2.2 %collective-permute-start.3 = (bf16[128,16,128]{2,1,0:T(8,128)(2,1)}, bf16[128,16,128]{2,1,0:T(8,128)(2,1)S(1)}, u32[]{:S(2)}, u32[]{:S(2)}) collective-permute-start(bf16[128,16,128]{2,1,0:T(8,128)(2,1)} %whiten.1.refs_0_), channel_id=1, source_target_pairs={{0,8},{8,0},{16,24},{24,16},{1,17},{5,13},{13,5},{17,1},{21,29},{2... | collective-permute-start | bytes 1572872 | tf_op jit(solution)/shard_map/ppermute | solution.py:278
  7.5 9.5 %collective-permute-done.refs_1_.refs_0_.refs_3_ = bf16[128,16,128]{2,1,0:T(8,128)(2,1)S(1)} collective-permute-done((bf16[128,16,128]{2,1,0:T(8,128)(2,1)}, bf16[128,16,128]{2,1,0:T(8,128)(2,1)S(1)}, u32[]{:S(2)}, u32[]{:S(2)}) %collective-permute-start) | collective-permute-done | bytes 524320 | tf_op jit(solution)/shard_map/ppermute | solution.py:404
  17.1 1.3 %collective-permute-start.1 = (bf16[128,16,128]{2,1,0:T(8,128)(2,1)S(1)}, bf16[128,16,128]{2,1,0:T(8,128)(2,1)S(1)}, u32[]{:S(2)}, u32[]{:S(2)}) collective-permute-start(bf16[128,16,128]{2,1,0:T(8,128)(2,1)S(1)} %collective-permute-done.refs_1_.refs_0_.refs_3_), channel_id=1, source_target_pairs={{0,1},{1,2},{2,3},{3,0},{4,5},{5,6},{6,7},{7,4},{8,9},{9,10},{10,1... | collective-permute-start | bytes 1572872 | tf_op jit(solution)/shard_map/ppermute | solution.py:404
  18.4 1.0 %copy-done = bf16[128,16,128]{2,1,0:T(8,128)(2,1)S(1)} copy-done((bf16[128,16,128]{2,1,0:T(8,128)(2,1)S(1)}, bf16[128,16,128]{2,1,0:T(8,128)(2,1)}, u32[]{:S(2)}) %copy-start) | copy-done | bytes 524312
  19.4 3.3 %collective-permute-start.4 = (bf16[128,16,128]{2,1,0:T(8,128)(2,1)S(1)}, bf16[128,16,128]{2,1,0:T(8,128)(2,1)S(1)}, u32[]{:S(2)}, u32[]{:S(2)}) collective-permute-start(bf16[128,16,128]{2,1,0:T(8,128)(2,1)S(1)} %bitcast.6), channel_id=1, source_target_pairs={{8,24},{24,8},{1,9},{9,1},{13,29},{17,25},{25,17},{29,13},{2,10},{... | collective-permute-start | bytes 1572872 | tf_op jit(solution)/shard_map/ppermute | solution.py:278
  22.7 1.9 %collective-permute-start.5 = (bf16[128,16,128]{2,1,0:T(8,128)(2,1)S(1)}, bf16[128,16,128]{2,1,0:T(8,128)(2,1)S(1)}, u32[]{:S(2)}, u32[]{:S(2)}) collective-permute-start(bf16[128,16,128]{2,1,0:T(8,128)(2,1)S(1)} %collective-permute-done.refs_1_.refs_0_.refs_3_), channel_id=1, source_target_pairs={{0,8},{8,0},{16,24},{24,16},{1,17},{5,13},{13,5},{17,1},{21,29},{2... | collective-permute-start | bytes 1572872 | tf_op jit(solution)/shard_map/ppermute | solution.py:278
  24.7 5.3 %collective-permute-done.1.refs_2_.refs_0_.refs_6_ = bf16[128,16,128]{2,1,0:T(8,128)(2,1)S(1)} collective-permute-done((bf16[128,16,128]{2,1,0:T(8,128)(2,1)S(1)}, bf16[128,16,128]{2,1,0:T(8,128)(2,1)S(1)}, u32[]{:S(2)}, u32[]{:S(2)}) %collective-permute-start.1) | collective-permute-done | bytes 524320 | tf_op jit(solution)/shard_map/ppermute | solution.py:404
  29.9 0.3 collective-permute-start.2
  30.2 0.0 collective-permute-done.4.refs_2_
  30.2 7.5 %collective-permute-done.5.refs_1_.refs_4_ = bf16[128,16,128]{2,1,0:T(8,128)(2,1)S(1)} collective-permute-done((bf16[128,16,128]{2,1,0:T(8,128)(2,1)S(1)}, bf16[128,16,128]{2,1,0:T(8,128)(2,1)S(1)}, u32[]{:S(2)}, u32[]{:S(2)}) %collective-permute-start.5) | collective-permute-done | bytes 524320 | tf_op jit(solution)/shard_map/ppermute | solution.py:278
  37.7 2.8 %collective-permute-start.7 = (bf16[128,16,128]{2,1,0:T(8,128)(2,1)S(1)}, bf16[128,16,128]{2,1,0:T(8,128)(2,1)S(1)}, u32[]{:S(2)}, u32[]{:S(2)}) collective-permute-start(bf16[128,16,128]{2,1,0:T(8,128)(2,1)S(1)} %bitcast.7), channel_id=1, source_target_pairs={{8,24},{24,8},{1,9},{9,1},{13,29},{17,25},{25,17},{29,13},{2,10},{... | collective-permute-start | bytes 1572872 | tf_op jit(solution)/shard_map/ppermute | solution.py:278
  40.6 1.9 %collective-permute-start.8 = (bf16[128,16,128]{2,1,0:T(8,128)(2,1)S(1)}, bf16[128,16,128]{2,1,0:T(8,128)(2,1)S(1)}, u32[]{:S(2)}, u32[]{:S(2)}) collective-permute-start(bf16[128,16,128]{2,1,0:T(8,128)(2,1)S(1)} %collective-permute-done.1.refs_2_.refs_0_.refs_6_), channel_id=1, source_target_pairs={{0,8},{8,0},{16,24},{24,16},{1,17},{5,13},{13,5},{17,1},{21,29},{2... | collective-permute-start | bytes 1572872 | tf_op jit(solution)/shard_map/ppermute | solution.py:278
  42.5 0.2 collective-permute-done.2.refs_3_.refs_0_.refs_4_.refs_9_
  42.7 3.1 %collective-permute-start.6 = (bf16[128,16,128]{2,1,0:T(8,128)(2,1)S(1)}, bf16[128,16,128]{2,1,0:T(8,128)(2,1)S(1)}, u32[]{:S(2)}, u32[]{:S(2)}) collective-permute-start(bf16[128,16,128]{2,1,0:T(8,128)(2,1)S(1)} %collective-permute-done.2.refs_3_.refs_0_.refs_4_.refs_9_), channel_id=1, source_target_pairs={{0,8},{8,0},{16,24},{24,16},{1,17},{5,13},{13,5},{17,1},{21,29},{2... | collective-permute-start | bytes 1572872 | tf_op jit(solution)/shard_map/ppermute | solution.py:278
  45.9 2.1 %collective-permute-done.7.refs_5_ = bf16[128,16,128]{2,1,0:T(8,128)(2,1)S(1)} collective-permute-done((bf16[128,16,128]{2,1,0:T(8,128)(2,1)S(1)}, bf16[128,16,128]{2,1,0:T(8,128)(2,1)S(1)}, u32[]{:S(2)}, u32[]{:S(2)}) %collective-permute-start.7) | collective-permute-done | bytes 524320 | tf_op jit(solution)/shard_map/ppermute | solution.py:278
  48.0 5.3 %collective-permute-done.8.refs_1_.refs_3_.refs_7_ = bf16[128,16,128]{2,1,0:T(8,128)(2,1)S(1)} collective-permute-done((bf16[128,16,128]{2,1,0:T(8,128)(2,1)S(1)}, bf16[128,16,128]{2,1,0:T(8,128)(2,1)S(1)}, u32[]{:S(2)}, u32[]{:S(2)}) %collective-permute-start.8) | collective-permute-done | bytes 524320 | tf_op jit(solution)/shard_map/ppermute | solution.py:278
  53.3 3.8 %collective-permute-start.9 = (bf16[128,16,128]{2,1,0:T(8,128)(2,1)S(1)}, bf16[128,16,128]{2,1,0:T(8,128)(2,1)S(1)}, u32[]{:S(2)}, u32[]{:S(2)}) collective-permute-start(bf16[128,16,128]{2,1,0:T(8,128)(2,1)S(1)} %bitcast.4), channel_id=1, source_target_pairs={{8,24},{24,8},{1,9},{9,1},{13,29},{17,25},{25,17},{29,13},{2,10},{... | collective-permute-start | bytes 1572872 | tf_op jit(solution)/shard_map/ppermute | solution.py:278
  57.2 3.4 %own_rows.1.own = bf16[128,64,128]{2,1,0:T(8,128)(2,1)S(1)} custom-call(bf16[128,16,128]{2,1,0:T(8,128)(2,1)S(1)} %copy-done.1, bf16[128,16,128]{2,1,0:T(8,128)(2,1)S(1)} %collective-permute-done.refs_1_.refs_0_.refs_3_, bf16[128,16,128]{2,1,0:T(8,128)(2,1)S(1)} %collective-permute-done.1.refs_2_.refs_0_.refs_6_, ...), custom_call_target="tpu_custom_call" | custom-call | flops 1 | bytes 1 | tf_op jit(solution)/shard_map/own_rows/pallas_call | solution.py:146
  60.6 1.5 %collective-permute-done.6.refs_1_.refs_5_.refs_10_ = bf16[128,16,128]{2,1,0:T(8,128)(2,1)S(1)} collective-permute-done((bf16[128,16,128]{2,1,0:T(8,128)(2,1)S(1)}, bf16[128,16,128]{2,1,0:T(8,128)(2,1)S(1)}, u32[]{:S(2)}, u32[]{:S(2)}) %collective-permute-start.6) | collective-permute-done | bytes 524320 | tf_op jit(solution)/shard_map/ppermute | solution.py:278
  62.2 0.0 copy-start.2
  62.2 0.7 collective-permute-start.12
  62.9 2.4 %collective-permute-start.10 = (bf16[128,16,128]{2,1,0:T(8,128)(2,1)S(1)}, bf16[128,16,128]{2,1,0:T(8,128)(2,1)S(1)}, u32[]{:S(2)}, u32[]{:S(2)}) collective-permute-start(bf16[128,16,128]{2,1,0:T(8,128)(2,1)S(1)} %bitcast.5), channel_id=1, source_target_pairs={{8,24},{24,8},{1,9},{9,1},{13,29},{17,25},{25,17},{29,13},{2,10},{... | collective-permute-start | bytes 1572872 | tf_op jit(solution)/shard_map/ppermute | solution.py:278
  65.4 0.1 choose.10
  65.5 0.1 collective-permute-start.11
  65.6 0.0 collective-permute-done.12.refs_7_.refs_14_
  65.6 7.3 %collective-permute-done.10.refs_6_.refs_11_ = bf16[128,16,128]{2,1,0:T(8,128)(2,1)S(1)} collective-permute-done((bf16[128,16,128]{2,1,0:T(8,128)(2,1)S(1)}, bf16[128,16,128]{2,1,0:T(8,128)(2,1)S(1)}, u32[]{:S(2)}, u32[]{:S(2)}) %collective-permute-start.10) | collective-permute-done | bytes 524320 | tf_op jit(solution)/shard_map/ppermute | solution.py:278
  72.8 0.1 choose.11
  72.9 0.1 collective-permute-start.13
  73.0 2.6 %collective-permute-done.13.refs_13_ = bf16[2,128,16,128]{3,2,1,0:T(8,128)(2,1)S(1)} collective-permute-done((bf16[2,128,16,128]{3,2,1,0:T(8,128)(2,1)S(1)}, bf16[2,128,16,128]{3,2,1,0:T(8,128)(2,1)S(1)}, u32[]{:S(2)}, u32[]{:S(2)}) %collective-permute-start.13) | collective-permute-done | bytes 1048608 | tf_op jit(solution)/shard_map/ppermute | solution.py:278
  75.7 10.2 %stack.1 = f32[64,64,256]{2,1,0:T(8,128)} custom-call(s32[64]{0:T(128)S(1)} %copy-done.2, bf16[128,64,128]{2,1,0:T(8,128)(2,1)S(1)} %own_rows.1.own, bf16[128,16,128]{2,1,0:T(8,128)(2,1)S(1)} %copy-done.1, bf16[128,16,128]{2,1,0:T(8,128)(2,1)S(1)} %collective-permute-done.3.refs_1_, bf16[128,16,128]{2,1,0:T(8,128)(2,1)S(1)} %collective-permute-done.4.refs_2_, ...), custom_call_target="tpu_custom_call" | custom-call | flops 1 | bytes 1 | tf_op jit(solution)/shard_map/stack/pallas_call | solution.py:260
  (11 shorter events, 0.2 us)
Async XLA Ops:
  4.0 13.1 %collective-permute-start = (bf16[128,16,128]{2,1,0:T(8,128)(2,1)}, bf16[128,16,128]{2,1,0:T(8,128)(2,1)S(1)}, u32[]{:S(2)}, u32[]{:S(2)}) collective-permute-start(bf16[128,16,128]{2,1,0:T(8,128)(2,1)} %whiten.1.refs_0_), channel_id=1, source_target_pairs={{0,1},{1,2},{2,3},{3,0},{4,5},{5,6},{6,7},{7,4},{8,9},{9,10},{10,1... | collective-permute-start | bytes 1572872 | tf_op jit(solution)/shard_map/ppermute | solution.py:404
  5.4 13.0 %collective-permute-start.3 = (bf16[128,16,128]{2,1,0:T(8,128)(2,1)}, bf16[128,16,128]{2,1,0:T(8,128)(2,1)S(1)}, u32[]{:S(2)}, u32[]{:S(2)}) collective-permute-start(bf16[128,16,128]{2,1,0:T(8,128)(2,1)} %whiten.1.refs_0_), channel_id=1, source_target_pairs={{0,8},{8,0},{16,24},{24,16},{1,17},{5,13},{13,5},{17,1},{21,29},{2... | collective-permute-start | bytes 1572872 | tf_op jit(solution)/shard_map/ppermute | solution.py:278
  17.1 12.9 %collective-permute-start.1 = (bf16[128,16,128]{2,1,0:T(8,128)(2,1)S(1)}, bf16[128,16,128]{2,1,0:T(8,128)(2,1)S(1)}, u32[]{:S(2)}, u32[]{:S(2)}) collective-permute-start(bf16[128,16,128]{2,1,0:T(8,128)(2,1)S(1)} %collective-permute-done.refs_1_.refs_0_.refs_3_), channel_id=1, source_target_pairs={{0,1},{1,2},{2,3},{3,0},{4,5},{5,6},{6,7},{7,4},{8,9},{9,10},{10,1... | collective-permute-start | bytes 1572872 | tf_op jit(solution)/shard_map/ppermute | solution.py:404
  18.4 1.0 %copy-start = (bf16[128,16,128]{2,1,0:T(8,128)(2,1)S(1)}, bf16[128,16,128]{2,1,0:T(8,128)(2,1)}, u32[]{:S(2)}) copy-start(bf16[128,16,128]{2,1,0:T(8,128)(2,1)} %whiten.1.refs_0_) | copy-start | bytes 1572868
  19.4 37.8 %copy-start.1 = (bf16[128,16,128]{2,1,0:T(8,128)(2,1)S(1)}, bf16[128,16,128]{2,1,0:T(8,128)(2,1)}, u32[]{:S(2)}) copy-start(bf16[128,16,128]{2,1,0:T(8,128)(2,1)} %whiten.1.refs_0_) | copy-start | bytes 1572868
  19.4 10.8 %collective-permute-start.4 = (bf16[128,16,128]{2,1,0:T(8,128)(2,1)S(1)}, bf16[128,16,128]{2,1,0:T(8,128)(2,1)S(1)}, u32[]{:S(2)}, u32[]{:S(2)}) collective-permute-start(bf16[128,16,128]{2,1,0:T(8,128)(2,1)S(1)} %bitcast.6), channel_id=1, source_target_pairs={{8,24},{24,8},{1,9},{9,1},{13,29},{17,25},{25,17},{29,13},{2,10},{... | collective-permute-start | bytes 1572872 | tf_op jit(solution)/shard_map/ppermute | solution.py:278
  22.7 15.0 %collective-permute-start.5 = (bf16[128,16,128]{2,1,0:T(8,128)(2,1)S(1)}, bf16[128,16,128]{2,1,0:T(8,128)(2,1)S(1)}, u32[]{:S(2)}, u32[]{:S(2)}) collective-permute-start(bf16[128,16,128]{2,1,0:T(8,128)(2,1)S(1)} %collective-permute-done.refs_1_.refs_0_.refs_3_), channel_id=1, source_target_pairs={{0,8},{8,0},{16,24},{24,16},{1,17},{5,13},{13,5},{17,1},{21,29},{2... | collective-permute-start | bytes 1572872 | tf_op jit(solution)/shard_map/ppermute | solution.py:278
  29.9 12.8 %collective-permute-start.2 = (bf16[128,16,128]{2,1,0:T(8,128)(2,1)S(1)}, bf16[128,16,128]{2,1,0:T(8,128)(2,1)S(1)}, u32[]{:S(2)}, u32[]{:S(2)}) collective-permute-start(bf16[128,16,128]{2,1,0:T(8,128)(2,1)S(1)} %collective-permute-done.1.refs_2_.refs_0_.refs_6_), channel_id=1, source_target_pairs={{0,1},{1,2},{2,3},{3,0},{4,5},{5,6},{6,7},{7,4},{8,9},{9,10},{10,1... | collective-permute-start | bytes 1572872 | tf_op jit(solution)/shard_map/ppermute | solution.py:404
  37.7 10.2 %collective-permute-start.7 = (bf16[128,16,128]{2,1,0:T(8,128)(2,1)S(1)}, bf16[128,16,128]{2,1,0:T(8,128)(2,1)S(1)}, u32[]{:S(2)}, u32[]{:S(2)}) collective-permute-start(bf16[128,16,128]{2,1,0:T(8,128)(2,1)S(1)} %bitcast.7), channel_id=1, source_target_pairs={{8,24},{24,8},{1,9},{9,1},{13,29},{17,25},{25,17},{29,13},{2,10},{... | collective-permute-start | bytes 1572872 | tf_op jit(solution)/shard_map/ppermute | solution.py:278
  40.6 12.7 %collective-permute-start.8 = (bf16[128,16,128]{2,1,0:T(8,128)(2,1)S(1)}, bf16[128,16,128]{2,1,0:T(8,128)(2,1)S(1)}, u32[]{:S(2)}, u32[]{:S(2)}) collective-permute-start(bf16[128,16,128]{2,1,0:T(8,128)(2,1)S(1)} %collective-permute-done.1.refs_2_.refs_0_.refs_6_), channel_id=1, source_target_pairs={{0,8},{8,0},{16,24},{24,16},{1,17},{5,13},{13,5},{17,1},{21,29},{2... | collective-permute-start | bytes 1572872 | tf_op jit(solution)/shard_map/ppermute | solution.py:278
  42.7 19.4 %collective-permute-start.6 = (bf16[128,16,128]{2,1,0:T(8,128)(2,1)S(1)}, bf16[128,16,128]{2,1,0:T(8,128)(2,1)S(1)}, u32[]{:S(2)}, u32[]{:S(2)}) collective-permute-start(bf16[128,16,128]{2,1,0:T(8,128)(2,1)S(1)} %collective-permute-done.2.refs_3_.refs_0_.refs_4_.refs_9_), channel_id=1, source_target_pairs={{0,8},{8,0},{16,24},{24,16},{1,17},{5,13},{13,5},{17,1},{21,29},{2... | collective-permute-start | bytes 1572872 | tf_op jit(solution)/shard_map/ppermute | solution.py:278
  53.3 12.2 %collective-permute-start.9 = (bf16[128,16,128]{2,1,0:T(8,128)(2,1)S(1)}, bf16[128,16,128]{2,1,0:T(8,128)(2,1)S(1)}, u32[]{:S(2)}, u32[]{:S(2)}) collective-permute-start(bf16[128,16,128]{2,1,0:T(8,128)(2,1)S(1)} %bitcast.4), channel_id=1, source_target_pairs={{8,24},{24,8},{1,9},{9,1},{13,29},{17,25},{25,17},{29,13},{2,10},{... | collective-permute-start | bytes 1572872 | tf_op jit(solution)/shard_map/ppermute | solution.py:278
  62.2 13.5 %copy-start.2 = (s32[64]{0:T(128)S(1)}, s32[64]{0:T(128)}, u32[]{:S(2)}) copy-start(s32[64]{0:T(128)} %reach_ref.1) | copy-start | bytes 772
  62.2 3.4 %collective-permute-start.12 = (bf16[128,16,128]{2,1,0:T(8,128)(2,1)S(1)}, bf16[128,16,128]{2,1,0:T(8,128)(2,1)S(1)}, u32[]{:S(2)}, u32[]{:S(2)}) collective-permute-start(bf16[128,16,128]{2,1,0:T(8,128)(2,1)S(1)} %collective-permute-done.2.refs_3_.refs_0_.refs_4_.refs_9_), channel_id=1, source_target_pairs={{3,19},{11,27},{19,3},{27,11}} | collective-permute-start | bytes 1572872 | tf_op jit(solution)/shard_map/ppermute | solution.py:278
  62.9 9.9 %collective-permute-start.10 = (bf16[128,16,128]{2,1,0:T(8,128)(2,1)S(1)}, bf16[128,16,128]{2,1,0:T(8,128)(2,1)S(1)}, u32[]{:S(2)}, u32[]{:S(2)}) collective-permute-start(bf16[128,16,128]{2,1,0:T(8,128)(2,1)S(1)} %bitcast.5), channel_id=1, source_target_pairs={{8,24},{24,8},{1,9},{9,1},{13,29},{17,25},{25,17},{29,13},{2,10},{... | collective-permute-start | bytes 1572872 | tf_op jit(solution)/shard_map/ppermute | solution.py:278
  65.5 7.5 %collective-permute-start.11 = (bf16[2,128,16,128]{3,2,1,0:T(8,128)(2,1)S(1)}, bf16[2,128,16,128]{3,2,1,0:T(8,128)(2,1)S(1)}, u32[]{:S(2)}, u32[]{:S(2)}) collective-permute-start(bf16[2,128,16,128]{3,2,1,0:T(8,128)(2,1)S(1)} %choose.10), channel_id=1, source_target_pairs={{0,4},{4,0},{8,12},{12,8},{16,20},{20,16},{24,28},{28,24},{1,5},{5... | collective-permute-start | bytes 3145736 | tf_op jit(solution)/shard_map/ppermute | solution.py:278
  72.9 2.7 %collective-permute-start.13 = (bf16[2,128,16,128]{3,2,1,0:T(8,128)(2,1)S(1)}, bf16[2,128,16,128]{3,2,1,0:T(8,128)(2,1)S(1)}, u32[]{:S(2)}, u32[]{:S(2)}) collective-permute-start(bf16[2,128,16,128]{3,2,1,0:T(8,128)(2,1)S(1)} %choose.11), channel_id=1, source_target_pairs={{0,4},{4,0},{8,12},{12,8},{16,20},{20,16},{24,28},{28,24},{1,5},{5... | collective-permute-start | bytes 3145736 | tf_op jit(solution)/shard_map/ppermute | solution.py:278

commit v13 on v12

--- a/solution.py
+++ b/solution.py
@@ -107,13 +107,13 @@
 def choose_kernel(code_of, groups, *refs):
     out_ref = refs[-1]
     per_group = (len(refs) - 1) // groups
-    code = code_of()
+    codes = code_of()
     for g in range(groups):
 
         def put(ref, g=g):
             out_ref[g] = ref[...]
 
-        copy_chosen(code, refs[g * per_group : (g + 1) * per_group], put)
+        copy_chosen(codes[g], refs[g * per_group : (g + 1) * per_group], put)
 
 
 def choose(code_of, groups):
@@ -292,7 +292,11 @@
     return lax.optimization_barrier((array, *others))[0]
 
 
-def direct_partners(pieces, hops, n_win, n_chan):
+def direct_partners(piece, hops, n_win, n_chan):
+    pieces = [piece]
+    while len(pieces) < n_win:
+        ring = [(z, (z + 1) % n_win) for z in range(n_win)]
+        pieces.append(lax.ppermute(pieces[-1], "win", ring))
     buffers = []
     for piece in pieces:
         buffers.append(send(piece, pairs_of(n_win, n_chan, lambda z, c: (c - hops[z]) % n_chan)))
@@ -310,16 +314,16 @@
     odd_next = jnp.where(x == 0, 1, 2)
     even_next = jnp.where(z == 0, odd_next, 2)
     next_code = jnp.where(core == 0, even_next, jnp.where(z == 3, 2, odd_next))
-    outgoing = jnp.where(core == 0, jnp.where(z < 2, next_code, 1), jnp.where(z < 2, 0, next_code))
-    first = jnp.where(z == 0, 0, jnp.where(z == 2, next_code, 3))
-    second = jnp.where(z == 1, next_code, jnp.where(z == 3, 1, 3))
-    is_late = (z == 3) & (core == 0)
-    outgoing_late = jnp.where(is_late, 3, outgoing)
-    second_last = jnp.where(is_late, 4, second)
-    return onward, outgoing, outgoing_late, (first, second, first, second_last)
-
-
-def square_partners(pieces, n_win, n_chan):
+    across = jnp.where((z == 3) & (core == 0), 3, 1)
+    outgoing = jnp.where(
+        core == 0, jnp.where(z < 2, next_code, across), jnp.where(z < 2, 0, next_code)
+    )
+    first = jnp.where(z == 0, 0, jnp.where(z == 2, next_code, 4))
+    second = jnp.where(z == 1, next_code, jnp.where(z == 3, across, 4))
+    return onward, outgoing, first, second
+
+
+def square_partners(piece_zero, n_win, n_chan):
     def pairs(target):
         return pairs_of(n_win, n_chan, lambda z, c: target(z, c, c % 2, c // 2 % 2))
 
@@ -332,6 +336,9 @@
             return c ^ 2
         return c ^ 4 if z == 2 or x == 0 else None
 
+    def early_target(z, c, core, x):
+        return None if z == 3 and core == 0 else first_target(z, c, core, x)
+
     def second_target(z, c, core, x):
         if z == 3:
             return c ^ 2 if core == 1 else None
@@ -341,56 +348,53 @@
             return c ^ 2
         return c ^ 4 if x == 1 else None
 
+    def late_target(z, c, core, x):
+        return c ^ 4 if z == 3 and core == 0 else None
+
     def swap(code_of, groups):
         return send(choose(code_of, groups), pairs(lambda z, c, core, x: c ^ 1))
 
-    count = len(pieces)
+    count = n_win
     half = count // 2
-    firsts, seconds = [], []
-
-    def second_move(slot, arrived):
-        relay = choose(lambda: square_codes()[0], [(pieces[slot], arrived)])[0]
-        seconds.append(send(relay, pairs(second_target)))
+    pieces = [piece_zero]
+    for slot in range(1, count):
+        ring = [(z, (z + 1) % n_win) for z in range(n_win)]
+        pieces.append(lax.ppermute(pieces[-1], "win", ring))
+    firsts, seconds, lates = [], [], []
+
+    def first_move(slot, *others):
+        in_parts = slot in (0, count - 1)
+        target = early_target if in_parts else first_target
+        firsts.append(send(after(pieces[slot], *others), pairs(target)))
+
+    def second_move(slot, arrived, *others):
+        relay = choose(lambda: square_codes()[:1], [(pieces[slot], arrived)])[0]
+        seconds.append(send(after(relay, *others), pairs(second_target)))
+        if slot in (0, count - 1):
+            lates.append(send(after(pieces[slot], relay), pairs(late_target)))
+        else:
+            lates.append(firsts[slot])
         return relay
 
-    for slot, piece in enumerate(pieces):
-        last = slot == count - 1
-        if slot >= 2:
-            piece = after(piece, firsts[slot - 2])
-        firsts.append(
-            send(
-                piece,
-                pairs(
-                    lambda z, c, core, x: (
-                        None if last and z == 3 and core == 0 else first_target(z, c, core, x)
-                    )
-                ),
-            )
-        )
-        if slot:
-            arrived = firsts[slot - 1]
-            arrived = after(arrived, *seconds[-1:])
-            second_move(slot - 1, arrived)
-    held = list(zip(pieces, firsts, seconds))
+    first_move(0)
+    relay = second_move(0, firsts[0])
+    first_move(1, *(seconds[0], lates[0]))
+    for slot in range(2, count):
+        first_move(slot, *())
+        second_move(slot - 1, after(firsts[slot - 1], pieces[slot]), seconds[-1])
     own = own_rows(pieces)
-    held[0] = (*held[0][:2], after(held[0][2], firsts[-1]))
-    swapped_early = swap(lambda: square_codes()[1], held[:half])
-    arrived = after(firsts[-1], own)
-    relay = second_move(count - 1, arrived)
-    held.append((pieces[-1], firsts[-1], seconds[-1]))
-    late = send(
-        after(pieces[-1], relay),
-        pairs(lambda z, c, core, x: c ^ 4 if z == 3 and core == 0 else None),
-    )
-    late_groups = [(*group, group[1]) for group in held[half:-1]] + [(*held[-1], late)]
-    swapped_late = swap(lambda: square_codes()[2], late_groups)
-    buffers = [buffer for group in held for buffer in group] + [swapped_early, swapped_late, late]
+    held = list(zip(pieces, firsts, seconds, lates))
+    held[0] = (*held[0][:2], after(held[0][2], firsts[-1]), held[0][3])
+    swapped_early = swap(lambda: square_codes()[1:2] * half, held[:half])
+    second_move(count - 1, after(firsts[-1], own), *())
+    held.append((pieces[-1], firsts[-1], seconds[-1], lates[-1]))
+    swapped_late = swap(lambda: square_codes()[1:2] * (count - half), held[half:])
+    buffers = [buffer for group in held for buffer in group] + [swapped_early, swapped_late]
     groups = []
     for n in range(count):
-        swapped = (3 * count, n) if n < half else (3 * count + 1, n - half)
-        groups.append([(3 * n, None), (3 * n + 1, None), (3 * n + 2, None), swapped])
-    groups[-1].append((3 * count + 2, None))
-    return own, buffers, groups, lambda: square_codes()[3]
+        swapped = (4 * count, n) if n < half else (4 * count + 1, n - half)
+        groups.append([*((4 * n + k, None) for k in range(4)), swapped])
+    return own, buffers, groups, lambda: square_codes()[2:] * 2
 
 
 def on_device(traces, valid, reach):
@@ -398,14 +402,11 @@
     n_win, n_chan = lax.axis_size("win"), lax.axis_size("chan")
     offsets = BAND // n_win
     hops = [z * offsets // width for z in range(n_win)]
-    pieces = [whitened_chunk(traces, valid)]
-    while len(pieces) < n_win:
-        ring = [(z, (z + 1) % n_win) for z in range(n_win)]
-        pieces.append(lax.ppermute(pieces[-1], "win", ring))
+    piece = whitened_chunk(traces, valid)
     if n_chan == 8 and hops == list(range(4)):
-        own, buffers, groups, codes_of = square_partners(pieces, n_win, n_chan)
+        own, buffers, groups, codes_of = square_partners(piece, n_win, n_chan)
     else:
-        own, buffers, groups, codes_of = direct_partners(pieces, hops, n_win, n_chan)
+        own, buffers, groups, codes_of = direct_partners(piece, hops, n_win, n_chan)
     return stacked(own, buffers, groups, codes_of, reach, offsets, traces.shape[0] * n_win)
 
 

time: 86.3 us -> 90.2 us (1.045)
  the two profiles are of different devices: /device:TPU:11 before, /device:TPU:3 now
where the time goes in v13:
time: 90.2 us; the launch traced here: 89.8 us
  waiting for transfers between devices  41.9 us (46%)
  starting transfers between devices  27.5 us (30%)
  Pallas kernels  18.1 us (20%)
  local copies, waits for them, and re-layouts  2.12 us (2%)
    ppermute x3, waiting for transfers between devices, square_partners(): pieces.append(lax.ppermute(pieces[-1], 'win', ring))  39.6 us
    ppermute x12, starting transfers between devices, send(): return lax.ppermute(array, AXES, pairs)  24.7 us
    pallas_call x1, Pallas kernels, stacked(): pl.pallas_call(functools.partial(stack_kernel, 1.0 / math.sqrt(windows),...  10.2 us
    pallas_call x1, Pallas kernels, whitened_chunk(): pl.pallas_call(whiten_kernel, out_shape=jax.ShapeDtypeStruct((F, windows,...  4 us
    pallas_call x1, Pallas kernels, own_rows(): pl.pallas_call(own_kernel, out_shape=jax.ShapeDtypeStruct((bins, lanes //...  3.43 us
    ppermute x3, starting transfers between devices, square_partners(): pieces.append(lax.ppermute(pieces[-1], 'win', ring))  2.82 us
    ppermute x12, waiting for transfers between devices, send(): return lax.ppermute(array, AXES, pairs)  2.31 us
    unnamed x8, local copies, waits for them, and re-layouts  2.12 us
  transfers between devices with their start and end apart: 15, of which 4 were waited for; matrix products, arithmetic and copies ran while one was open for 0% of the time, Pallas kernels for 4%

profile of v13, /device:TPU:3, one launch (start us, length us, event | category | flops | bytes accessed | tf_op | source)
XLA Modules:
  0.0 89.8 jit_solution(13751892472232098220)
XLA Ops:
  0.0 4.0 %whiten.1.refs_0_ = bf16[128,16,128]{2,1,0:T(8,128)(2,1)} custom-call(bf16[256,512]{1,0:T(8,128)(2,1)} %constant.3.table_hbm, bf16[16,64,512]{2,1,0:T(8,128)(2,1)} %traces_hbm.1, s32[16,64]{1,0:T(8,128)} %valid_hbm.1), custom_call_target="tpu_custom_call" | custom-call | flops 268435456 | bytes 1048576 | tf_op jit(solution)/shard_map/whiten/pallas_call | solution.py:79
  4.0 0.7 collective-permute-start.3
  4.7 2.8 %collective-permute-start = (bf16[128,16,128]{2,1,0:T(8,128)(2,1)}, bf16[128,16,128]{2,1,0:T(8,128)(2,1)S(1)}, u32[]{:S(2)}, u32[]{:S(2)}) collective-permute-start(bf16[128,16,128]{2,1,0:T(8,128)(2,1)} %whiten.1.refs_0_), channel_id=1, source_target_pairs={{0,1},{1,2},{2,3},{3,0},{4,5},{5,6},{6,7},{7,4},{8,9},{9,10},{10,1... | collective-permute-start | bytes 1572872 | tf_op jit(solution)/shard_map/ppermute | solution.py:362
  7.5 1.1 %copy-done = bf16[128,16,128]{2,1,0:T(8,128)(2,1)S(1)} copy-done((bf16[128,16,128]{2,1,0:T(8,128)(2,1)S(1)}, bf16[128,16,128]{2,1,0:T(8,128)(2,1)}, u32[]{:S(2)}) %copy-start) | copy-done | bytes 524312
  8.6 0.7 collective-permute-start.6
  9.3 0.7 collective-permute-start.4
  10.0 12.9 %collective-permute-done.refs_1_.refs_0_.refs_4_ = bf16[128,16,128]{2,1,0:T(8,128)(2,1)S(1)} collective-permute-done((bf16[128,16,128]{2,1,0:T(8,128)(2,1)}, bf16[128,16,128]{2,1,0:T(8,128)(2,1)S(1)}, u32[]{:S(2)}, u32[]{:S(2)}) %collective-permute-start) | collective-permute-done | bytes 524320 | tf_op jit(solution)/shard_map/ppermute | solution.py:362
  22.9 0.0 collective-permute-done.6.refs_3_
  22.9 0.0 collective-permute-done.4.refs_2_
  22.9 0.7 collective-permute-start.7
  23.6 14.2 %collective-permute-done.1.refs_2_.refs_0_.refs_8_ = bf16[128,16,128]{2,1,0:T(8,128)(2,1)S(1)} collective-permute-done((bf16[128,16,128]{2,1,0:T(8,128)(2,1)S(1)}, bf16[128,16,128]{2,1,0:T(8,128)(2,1)S(1)}, u32[]{:S(2)}, u32[]{:S(2)}) %collective-permute-start.1) | collective-permute-done | bytes 524320 | tf_op jit(solution)/shard_map/ppermute | solution.py:362
  37.8 0.7 collective-permute-start.9
  38.5 0.1 choose.7
  38.6 0.7 collective-permute-start.8
  39.3 12.5 %collective-permute-done.2.refs_3_.refs_0_.refs_4_.refs_12_ = bf16[128,16,128]{2,1,0:T(8,128)(2,1)S(1)} collective-permute-done((bf16[128,16,128]{2,1,0:T(8,128)(2,1)S(1)}, bf16[128,16,128]{2,1,0:T(8,128)(2,1)S(1)}, u32[]{:S(2)}, u32[]{:S(2)}) %collective-permute-start.2) | collective-permute-done | bytes 524320 | tf_op jit(solution)/shard_map/ppermute | solution.py:362
  51.8 0.7 collective-permute-start.5
  52.5 0.0 copy-start.1
  52.5 1.0 %copy-done.1 = bf16[128,16,128]{2,1,0:T(8,128)(2,1)S(1)} copy-done((bf16[128,16,128]{2,1,0:T(8,128)(2,1)S(1)}, bf16[128,16,128]{2,1,0:T(8,128)(2,1)}, u32[]{:S(2)}) %copy-start.1) | copy-done | bytes 524312
  53.5 3.4 %own_rows.1.own = bf16[128,64,128]{2,1,0:T(8,128)(2,1)S(1)} custom-call(bf16[128,16,128]{2,1,0:T(8,128)(2,1)S(1)} %copy-done.1, bf16[128,16,128]{2,1,0:T(8,128)(2,1)S(1)} %collective-permute-done.refs_1_.refs_0_.refs_4_, bf16[128,16,128]{2,1,0:T(8,128)(2,1)S(1)} %collective-permute-done.1.refs_2_.refs_0_.refs_8_, ...), custom_call_target="tpu_custom_call" | custom-call | flops 1 | bytes 1 | tf_op jit(solution)/shard_map/own_rows/pallas_call | solution.py:146
  57.0 0.1 choose.8
  57.1 0.7 collective-permute-start.10
  57.8 0.1 choose.9
  57.8 0.0 copy-start.2
  57.9 0.0 copy-start.3
  57.9 0.8 collective-permute-start.12
  58.7 0.7 collective-permute-start.11
  59.4 0.1 choose.10
  59.5 8.5 %collective-permute-start.13 = (bf16[2,128,16,128]{3,2,1,0:T(8,128)(2,1)S(1)}, bf16[2,128,16,128]{3,2,1,0:T(8,128)(2,1)S(1)}, u32[]{:S(2)}, u32[]{:S(2)}) collective-permute-start(bf16[2,128,16,128]{3,2,1,0:T(8,128)(2,1)S(1)} %choose.10), channel_id=1, source_target_pairs={{0,4},{4,0},{8,12},{12,8},{16,20},{20,16},{24,28},{28,24},{1,5},{5... | collective-permute-start | bytes 3145736 | tf_op jit(solution)/shard_map/ppermute | solution.py:278
  68.0 0.1 choose.11
  68.2 9.1 %collective-permute-start.14 = (bf16[2,128,16,128]{3,2,1,0:T(8,128)(2,1)S(1)}, bf16[2,128,16,128]{3,2,1,0:T(8,128)(2,1)S(1)}, u32[]{:S(2)}, u32[]{:S(2)}) collective-permute-start(bf16[2,128,16,128]{3,2,1,0:T(8,128)(2,1)S(1)} %choose.11), channel_id=1, source_target_pairs={{0,4},{4,0},{8,12},{12,8},{16,20},{20,16},{24,28},{28,24},{1,5},{5... | collective-permute-start | bytes 3145736 | tf_op jit(solution)/shard_map/ppermute | solution.py:278
  77.3 2.3 %collective-permute-done.14.refs_17_ = bf16[2,128,16,128]{3,2,1,0:T(8,128)(2,1)S(1)} collective-permute-done((bf16[2,128,16,128]{3,2,1,0:T(8,128)(2,1)S(1)}, bf16[2,128,16,128]{3,2,1,0:T(8,128)(2,1)S(1)}, u32[]{:S(2)}, u32[]{:S(2)}) %collective-permute-start.14) | collective-permute-done | bytes 1048608 | tf_op jit(solution)/shard_map/ppermute | solution.py:278
  79.6 10.2 %stack.1 = f32[64,64,256]{2,1,0:T(8,128)} custom-call(s32[64]{0:T(128)S(1)} %copy-done.3, bf16[128,64,128]{2,1,0:T(8,128)(2,1)S(1)} %own_rows.1.own, bf16[128,16,128]{2,1,0:T(8,128)(2,1)S(1)} %copy-done.2, bf16[128,16,128]{2,1,0:T(8,128)(2,1)S(1)} %collective-permute-done.3.refs_1_, bf16[128,16,128]{2,1,0:T(8,128)(2,1)S(1)} %collective-permute-done.4.refs_2_, ...), custom_call_target="tpu_custom_call" | custom-call | flops 1 | bytes 1 | tf_op jit(solution)/shard_map/stack/pallas_call | solution.py:260
  (15 shorter events, 0.1 us)
Async XLA Ops:
  4.0 3.5 %collective-permute-start.3 = (bf16[128,16,128]{2,1,0:T(8,128)(2,1)}, bf16[128,16,128]{2,1,0:T(8,128)(2,1)S(1)}, u32[]{:S(2)}, u32[]{:S(2)}) collective-permute-start(bf16[128,16,128]{2,1,0:T(8,128)(2,1)} %whiten.1.refs_0_), channel_id=1, source_target_pairs={{0,8},{8,0},{16,24},{24,16},{1,17},{5,13},{13,5},{17,1},{21,29},{2... | collective-permute-start | bytes 1572872 | tf_op jit(solution)/shard_map/ppermute | solution.py:278
  4.7 18.2 %collective-permute-start = (bf16[128,16,128]{2,1,0:T(8,128)(2,1)}, bf16[128,16,128]{2,1,0:T(8,128)(2,1)S(1)}, u32[]{:S(2)}, u32[]{:S(2)}) collective-permute-start(bf16[128,16,128]{2,1,0:T(8,128)(2,1)} %whiten.1.refs_0_), channel_id=1, source_target_pairs={{0,1},{1,2},{2,3},{3,0},{4,5},{5,6},{6,7},{7,4},{8,9},{9,10},{10,1... | collective-permute-start | bytes 1572872 | tf_op jit(solution)/shard_map/ppermute | solution.py:362
  7.5 1.1 %copy-start = (bf16[128,16,128]{2,1,0:T(8,128)(2,1)S(1)}, bf16[128,16,128]{2,1,0:T(8,128)(2,1)}, u32[]{:S(2)}) copy-start(bf16[128,16,128]{2,1,0:T(8,128)(2,1)} %whiten.1.refs_0_) | copy-start | bytes 1572868
  8.6 14.3 %collective-permute-start.6 = (bf16[128,16,128]{2,1,0:T(8,128)(2,1)S(1)}, bf16[128,16,128]{2,1,0:T(8,128)(2,1)S(1)}, u32[]{:S(2)}, u32[]{:S(2)}) collective-permute-start(bf16[128,16,128]{2,1,0:T(8,128)(2,1)S(1)} %copy-done), channel_id=1, source_target_pairs={{3,19},{11,27},{19,3},{27,11}} | collective-permute-start | bytes 1572872 | tf_op jit(solution)/shard_map/ppermute | solution.py:278
  9.3 13.6 %collective-permute-start.4 = (bf16[128,16,128]{2,1,0:T(8,128)(2,1)S(1)}, bf16[128,16,128]{2,1,0:T(8,128)(2,1)S(1)}, u32[]{:S(2)}, u32[]{:S(2)}) collective-permute-start(bf16[128,16,128]{2,1,0:T(8,128)(2,1)S(1)} %bitcast.6), channel_id=1, source_target_pairs={{8,24},{24,8},{1,9},{9,1},{13,29},{17,25},{25,17},{29,13},{2,10},{... | collective-permute-start | bytes 1572872 | tf_op jit(solution)/shard_map/ppermute | solution.py:278
  22.9 14.9 %collective-permute-start.1 = (bf16[128,16,128]{2,1,0:T(8,128)(2,1)S(1)}, bf16[128,16,128]{2,1,0:T(8,128)(2,1)S(1)}, u32[]{:S(2)}, u32[]{:S(2)}) collective-permute-start(bf16[128,16,128]{2,1,0:T(8,128)(2,1)S(1)} %collective-permute-done.refs_1_.refs_0_.refs_4_), channel_id=1, source_target_pairs={{0,1},{1,2},{2,3},{3,0},{4,5},{5,6},{6,7},{7,4},{8,9},{9,10},{10,1... | collective-permute-start | bytes 1572872 | tf_op jit(solution)/shard_map/ppermute | solution.py:362
  22.9 15.6 %collective-permute-start.7 = (bf16[128,16,128]{2,1,0:T(8,128)(2,1)S(1)}, bf16[128,16,128]{2,1,0:T(8,128)(2,1)S(1)}, u32[]{:S(2)}, u32[]{:S(2)}) collective-permute-start(bf16[128,16,128]{2,1,0:T(8,128)(2,1)S(1)} %collective-permute-done.refs_1_.refs_0_.refs_4_), channel_id=1, source_target_pairs={{0,8},{8,0},{16,24},{24,16},{1,17},{5,13},{13,5},{17,1},{21,29},{2... | collective-permute-start | bytes 1572872 | tf_op jit(solution)/shard_map/ppermute | solution.py:278
  37.8 14.0 %collective-permute-start.2 = (bf16[128,16,128]{2,1,0:T(8,128)(2,1)S(1)}, bf16[128,16,128]{2,1,0:T(8,128)(2,1)S(1)}, u32[]{:S(2)}, u32[]{:S(2)}) collective-permute-start(bf16[128,16,128]{2,1,0:T(8,128)(2,1)S(1)} %collective-permute-done.1.refs_2_.refs_0_.refs_8_), channel_id=1, source_target_pairs={{0,1},{1,2},{2,3},{3,0},{4,5},{5,6},{6,7},{7,4},{8,9},{9,10},{10,1... | collective-permute-start | bytes 1572872 | tf_op jit(solution)/shard_map/ppermute | solution.py:362
  37.8 19.2 %collective-permute-start.9 = (bf16[128,16,128]{2,1,0:T(8,128)(2,1)S(1)}, bf16[128,16,128]{2,1,0:T(8,128)(2,1)S(1)}, u32[]{:S(2)}, u32[]{:S(2)}) collective-permute-start(bf16[128,16,128]{2,1,0:T(8,128)(2,1)S(1)} %collective-permute-done.1.refs_2_.refs_0_.refs_8_), channel_id=1, source_target_pairs={{0,8},{8,0},{16,24},{24,16},{1,17},{5,13},{13,5},{17,1},{21,29},{2... | collective-permute-start | bytes 1572872 | tf_op jit(solution)/shard_map/ppermute | solution.py:278
  38.6 18.5 %collective-permute-start.8 = (bf16[128,16,128]{2,1,0:T(8,128)(2,1)S(1)}, bf16[128,16,128]{2,1,0:T(8,128)(2,1)S(1)}, u32[]{:S(2)}, u32[]{:S(2)}) collective-permute-start(bf16[128,16,128]{2,1,0:T(8,128)(2,1)S(1)} %bitcast.7), channel_id=1, source_target_pairs={{8,24},{24,8},{1,9},{9,1},{13,29},{17,25},{25,17},{29,13},{2,10},{... | collective-permute-start | bytes 1572872 | tf_op jit(solution)/shard_map/ppermute | solution.py:278
  51.8 6.0 %collective-permute-start.5 = (bf16[128,16,128]{2,1,0:T(8,128)(2,1)S(1)}, bf16[128,16,128]{2,1,0:T(8,128)(2,1)S(1)}, u32[]{:S(2)}, u32[]{:S(2)}) collective-permute-start(bf16[128,16,128]{2,1,0:T(8,128)(2,1)S(1)} %collective-permute-done.2.refs_3_.refs_0_.refs_4_.refs_12_), channel_id=1, source_target_pairs={{0,8},{8,0},{16,24},{24,16},{1,17},{5,13},{13,5},{17,1},{21,29},{2... | collective-permute-start | bytes 1572872 | tf_op jit(solution)/shard_map/ppermute | solution.py:278
  52.5 1.0 %copy-start.1 = (bf16[128,16,128]{2,1,0:T(8,128)(2,1)S(1)}, bf16[128,16,128]{2,1,0:T(8,128)(2,1)}, u32[]{:S(2)}) copy-start(bf16[128,16,128]{2,1,0:T(8,128)(2,1)} %whiten.1.refs_0_) | copy-start | bytes 1572868
  57.1 11.0 %collective-permute-start.10 = (bf16[128,16,128]{2,1,0:T(8,128)(2,1)S(1)}, bf16[128,16,128]{2,1,0:T(8,128)(2,1)S(1)}, u32[]{:S(2)}, u32[]{:S(2)}) collective-permute-start(bf16[128,16,128]{2,1,0:T(8,128)(2,1)S(1)} %bitcast.4), channel_id=1, source_target_pairs={{8,24},{24,8},{1,9},{9,1},{13,29},{17,25},{25,17},{29,13},{2,10},{... | collective-permute-start | bytes 1572872 | tf_op jit(solution)/shard_map/ppermute | solution.py:278
  57.8 21.7 %copy-start.2 = (bf16[128,16,128]{2,1,0:T(8,128)(2,1)S(1)}, bf16[128,16,128]{2,1,0:T(8,128)(2,1)}, u32[]{:S(2)}) copy-start(bf16[128,16,128]{2,1,0:T(8,128)(2,1)} %whiten.1.refs_0_) | copy-start | bytes 1572868
  57.9 21.7 %copy-start.3 = (s32[64]{0:T(128)S(1)}, s32[64]{0:T(128)}, u32[]{:S(2)}) copy-start(s32[64]{0:T(128)} %reach_ref.1) | copy-start | bytes 772
  57.9 10.2 %collective-permute-start.12 = (bf16[128,16,128]{2,1,0:T(8,128)(2,1)S(1)}, bf16[128,16,128]{2,1,0:T(8,128)(2,1)S(1)}, u32[]{:S(2)}, u32[]{:S(2)}) collective-permute-start(bf16[128,16,128]{2,1,0:T(8,128)(2,1)S(1)} %collective-permute-done.2.refs_3_.refs_0_.refs_4_.refs_12_), channel_id=1, source_target_pairs={{3,19},{11,27},{19,3},{27,11}} | collective-permute-start | bytes 1572872 | tf_op jit(solution)/shard_map/ppermute | solution.py:278
  58.7 9.3 %collective-permute-start.11 = (bf16[128,16,128]{2,1,0:T(8,128)(2,1)S(1)}, bf16[128,16,128]{2,1,0:T(8,128)(2,1)S(1)}, u32[]{:S(2)}, u32[]{:S(2)}) collective-permute-start(bf16[128,16,128]{2,1,0:T(8,128)(2,1)S(1)} %bitcast.5), channel_id=1, source_target_pairs={{8,24},{24,8},{1,9},{9,1},{13,29},{17,25},{25,17},{29,13},{2,10},{... | collective-permute-start | bytes 1572872 | tf_op jit(solution)/shard_map/ppermute | solution.py:278
  59.5 17.8 %collective-permute-start.13 = (bf16[2,128,16,128]{3,2,1,0:T(8,128)(2,1)S(1)}, bf16[2,128,16,128]{3,2,1,0:T(8,128)(2,1)S(1)}, u32[]{:S(2)}, u32[]{:S(2)}) collective-permute-start(bf16[2,128,16,128]{3,2,1,0:T(8,128)(2,1)S(1)} %choose.10), channel_id=1, source_target_pairs={{0,4},{4,0},{8,12},{12,8},{16,20},{20,16},{24,28},{28,24},{1,5},{5... | collective-permute-start | bytes 3145736 | tf_op jit(solution)/shard_map/ppermute | solution.py:278
  68.2 11.4 %collective-permute-start.14 = (bf16[2,128,16,128]{3,2,1,0:T(8,128)(2,1)S(1)}, bf16[2,128,16,128]{3,2,1,0:T(8,128)(2,1)S(1)}, u32[]{:S(2)}, u32[]{:S(2)}) collective-permute-start(bf16[2,128,16,128]{3,2,1,0:T(8,128)(2,1)S(1)} %choose.11), channel_id=1, source_target_pairs={{0,4},{4,0},{8,12},{12,8},{16,20},{20,16},{24,28},{28,24},{1,5},{5... | collective-permute-start | bytes 3145736 | tf_op jit(solution)/shard_map/ppermute | solution.py:278

commit v14 on v12

--- a/solution.py
+++ b/solution.py
@@ -131,11 +131,9 @@
 
 def own_kernel(*refs):
     out_ref = refs[-1]
-    width = out_ref.shape[1]
 
     def one_bin(f, carry):
-        turned = jnp.concatenate([ref[f] for ref in refs[:-1]], axis=0).T
-        out_ref[f] = jnp.concatenate([turned[:width], turned[width:]], axis=1)
+        out_ref[f] = jnp.concatenate([ref[f] for ref in refs[:-1]], axis=0).T
         return carry
 
     lax.fori_loop(0, out_ref.shape[0], one_bin, 0, unroll=8)
@@ -146,7 +144,7 @@
     return pl.pallas_call(
         own_kernel,
         out_shape=jax.ShapeDtypeStruct(
-            (bins, lanes // 2, 2 * windows * len(pieces)), jnp.bfloat16
+            (bins, lanes, windows * len(pieces)), jnp.bfloat16
         ),
         in_specs=[VMEM] * len(pieces),
         out_specs=VMEM,
@@ -158,8 +156,8 @@
 
 def stack_kernel(scale, groups, codes_of, reach_ref, own, *refs):
     buffers, (out_hbm, partners, products, out, sems) = refs[:-5], refs[-5:]
-    bins, width, _ = own.shape
-    lanes = 2 * width
+    bins, lanes, _ = own.shape
+    width = lanes // 2
     offsets = out_hbm.shape[0]
     pitch = products.shape[0] // bins
     slots = len(groups)
@@ -181,17 +179,20 @@
     lane = lax.broadcasted_iota(jnp.int32, (width, lanes), 1)
     in_first = lane % width >= lax.broadcasted_iota(jnp.int32, (width, lanes), 0) + first
 
+    sign = jnp.where(lane < width, 1.0, -1.0)
+
     def products_of(f):
-        tops = [
-            jnp.concatenate([partners[which, slot, f] for slot in range(slots)], axis=0)
-            for which in range(2)
-        ]
-        bottoms = [jnp.concatenate([b[:, width:], -b[:, :width]], axis=1) for b in tops]
         right = jnp.concatenate(
-            [jnp.concatenate(tops, axis=1), jnp.concatenate(bottoms, axis=1)], axis=0
+            [
+                jnp.concatenate([partners[which, slot, f] for slot in range(slots)], axis=0)
+                for which in range(2)
+            ],
+            axis=1,
         )
         both = jnp.dot(own[f], right, preferred_element_type=jnp.float32)
-        return jnp.where(in_first, both[:, :lanes], both[:, lanes:])
+        with_re = jnp.where(in_first, both[:width, :lanes], both[:width, lanes:])
+        with_im = jnp.where(in_first, both[width:, :lanes], both[width:, lanes:])
+        return with_re + sign * pltpu.roll(with_im, width, 1)
 
     def one_group(group, carry):
         results = [products_of(group * GROUP + n) for n in range(GROUP)]
@@ -254,8 +255,9 @@
 
 
 def stacked(own, buffers, groups, codes_of, reach, offsets, windows):
-    bins, width, _ = own.shape
-    chunk_windows, lanes = buffers[0].shape[-2:]
+    bins, lanes, _ = own.shape
+    width = lanes // 2
+    chunk_windows = buffers[0].shape[-2]
     pitch = width + PITCH_PAD
     return pl.pallas_call(
         functools.partial(stack_kernel, 1.0 / math.sqrt(windows), groups, codes_of),

time: 86.3 us -> 85.9 us (level)
  Pallas kernels: 18 us -> 16.2 us
  waiting for transfers between devices: 41.3 us -> 42.7 us
    pallas_call x1, Pallas kernels: 3.44 us -> 2.03 us  [own_rows(): pl.pallas_call(own_kernel, out_shape=jax.ShapeDtypeStruct((bins, lanes, w...]
    ppermute x11, waiting for transfers between devices: 26.3 us -> 27.7 us  [send(): return lax.ppermute(array, AXES, pairs)]
  transfers between devices with their start and end apart: 14 -> 14, of which waited for: 9 -> 9; matrix products, arithmetic and copies ran while one was open for 0% -> 0% of each run, Pallas kernels for 4% -> 3%
where the time goes in v14:
time: 85.9 us; the launch traced here: 85.5 us
  waiting for transfers between devices  42.7 us (50%)
  starting transfers between devices  25.3 us (29%)
  Pallas kernels  16.2 us (19%)
  local copies, waits for them, and re-layouts  1.05 us (1%)
    ppermute x11, waiting for transfers between devices, send(): return lax.ppermute(array, AXES, pairs)  27.7 us
    ppermute x11, starting transfers between devices, send(): return lax.ppermute(array, AXES, pairs)  22.4 us
    ppermute x3, waiting for transfers between devices, on_device(): pieces.append(lax.ppermute(pieces[-1], 'win', ring))  15 us
    pallas_call x1, Pallas kernels, stacked(): pl.pallas_call(functools.partial(stack_kernel, 1.0 / math.sqrt(windows),...  9.85 us
    pallas_call x1, Pallas kernels, whitened_chunk(): pl.pallas_call(whiten_kernel, out_shape=jax.ShapeDtypeStruct((F, windows,...  4 us
    ppermute x3, starting transfers between devices, on_device(): pieces.append(lax.ppermute(pieces[-1], 'win', ring))  2.93 us
    pallas_call x1, Pallas kernels, own_rows(): pl.pallas_call(own_kernel, out_shape=jax.ShapeDtypeStruct((bins, lanes, w...  2.03 us
  transfers between devices with their start and end apart: 14, of which 9 were waited for; matrix products, arithmetic and copies ran while one was open for 0% of the time, Pallas kernels for 3%

profile of v14, /device:TPU:11, one launch (start us, length us, event | category | flops | bytes accessed | tf_op | source)
XLA Modules:
  0.0 85.5 jit_solution(10618394424464254306)
XLA Ops:
  0.0 4.0 %whiten.1.refs_0_ = bf16[128,16,128]{2,1,0:T(8,128)(2,1)} custom-call(bf16[256,512]{1,0:T(8,128)(2,1)} %constant.3.table_hbm, bf16[16,64,512]{2,1,0:T(8,128)(2,1)} %traces_hbm.1, s32[16,64]{1,0:T(8,128)} %valid_hbm.1), custom_call_target="tpu_custom_call" | custom-call | flops 268435456 | bytes 1048576 | tf_op jit(solution)/shard_map/whiten/pallas_call | solution.py:79
  4.0 1.3 %collective-permute-start = (bf16[128,16,128]{2,1,0:T(8,128)(2,1)}, bf16[128,16,128]{2,1,0:T(8,128)(2,1)S(1)}, u32[]{:S(2)}, u32[]{:S(2)}) collective-permute-start(bf16[128,16,128]{2,1,0:T(8,128)(2,1)} %whiten.1.refs_0_), channel_id=1, source_target_pairs={{0,1},{1,2},{2,3},{3,0},{4,5},{5,6},{6,7},{7,4},{8,9},{9,10},{10,1... | collective-permute-start | bytes 1572872 | tf_op jit(solution)/shard_map/ppermute | solution.py:406
  5.4 2.2 %collective-permute-start.3 = (bf16[128,16,128]{2,1,0:T(8,128)(2,1)}, bf16[128,16,128]{2,1,0:T(8,128)(2,1)S(1)}, u32[]{:S(2)}, u32[]{:S(2)}) collective-permute-start(bf16[128,16,128]{2,1,0:T(8,128)(2,1)} %whiten.1.refs_0_), channel_id=1, source_target_pairs={{0,8},{8,0},{16,24},{24,16},{1,17},{5,13},{13,5},{17,1},{21,29},{2... | collective-permute-start | bytes 1572872 | tf_op jit(solution)/shard_map/ppermute | solution.py:280
  7.5 9.5 %collective-permute-done.refs_1_.refs_0_.refs_3_ = bf16[128,16,128]{2,1,0:T(8,128)(2,1)S(1)} collective-permute-done((bf16[128,16,128]{2,1,0:T(8,128)(2,1)}, bf16[128,16,128]{2,1,0:T(8,128)(2,1)S(1)}, u32[]{:S(2)}, u32[]{:S(2)}) %collective-permute-start) | collective-permute-done | bytes 524320 | tf_op jit(solution)/shard_map/ppermute | solution.py:406
  17.1 1.3 %collective-permute-start.1 = (bf16[128,16,128]{2,1,0:T(8,128)(2,1)S(1)}, bf16[128,16,128]{2,1,0:T(8,128)(2,1)S(1)}, u32[]{:S(2)}, u32[]{:S(2)}) collective-permute-start(bf16[128,16,128]{2,1,0:T(8,128)(2,1)S(1)} %collective-permute-done.refs_1_.refs_0_.refs_3_), channel_id=1, source_target_pairs={{0,1},{1,2},{2,3},{3,0},{4,5},{5,6},{6,7},{7,4},{8,9},{9,10},{10,1... | collective-permute-start | bytes 1572872 | tf_op jit(solution)/shard_map/ppermute | solution.py:406
  18.4 1.0 %copy-done = bf16[128,16,128]{2,1,0:T(8,128)(2,1)S(1)} copy-done((bf16[128,16,128]{2,1,0:T(8,128)(2,1)S(1)}, bf16[128,16,128]{2,1,0:T(8,128)(2,1)}, u32[]{:S(2)}) %copy-start) | copy-done | bytes 524312
  19.4 3.3 %collective-permute-start.4 = (bf16[128,16,128]{2,1,0:T(8,128)(2,1)S(1)}, bf16[128,16,128]{2,1,0:T(8,128)(2,1)S(1)}, u32[]{:S(2)}, u32[]{:S(2)}) collective-permute-start(bf16[128,16,128]{2,1,0:T(8,128)(2,1)S(1)} %bitcast.6), channel_id=1, source_target_pairs={{8,24},{24,8},{1,9},{9,1},{13,29},{17,25},{25,17},{29,13},{2,10},{... | collective-permute-start | bytes 1572872 | tf_op jit(solution)/shard_map/ppermute | solution.py:280
  22.7 1.9 %collective-permute-start.5 = (bf16[128,16,128]{2,1,0:T(8,128)(2,1)S(1)}, bf16[128,16,128]{2,1,0:T(8,128)(2,1)S(1)}, u32[]{:S(2)}, u32[]{:S(2)}) collective-permute-start(bf16[128,16,128]{2,1,0:T(8,128)(2,1)S(1)} %collective-permute-done.refs_1_.refs_0_.refs_3_), channel_id=1, source_target_pairs={{0,8},{8,0},{16,24},{24,16},{1,17},{5,13},{13,5},{17,1},{21,29},{2... | collective-permute-start | bytes 1572872 | tf_op jit(solution)/shard_map/ppermute | solution.py:280
  24.7 5.3 %collective-permute-done.1.refs_2_.refs_0_.refs_6_ = bf16[128,16,128]{2,1,0:T(8,128)(2,1)S(1)} collective-permute-done((bf16[128,16,128]{2,1,0:T(8,128)(2,1)S(1)}, bf16[128,16,128]{2,1,0:T(8,128)(2,1)S(1)}, u32[]{:S(2)}, u32[]{:S(2)}) %collective-permute-start.1) | collective-permute-done | bytes 524320 | tf_op jit(solution)/shard_map/ppermute | solution.py:406
  29.9 0.3 collective-permute-start.2
  30.2 0.0 collective-permute-done.4.refs_2_
  30.2 7.5 %collective-permute-done.5.refs_1_.refs_4_ = bf16[128,16,128]{2,1,0:T(8,128)(2,1)S(1)} collective-permute-done((bf16[128,16,128]{2,1,0:T(8,128)(2,1)S(1)}, bf16[128,16,128]{2,1,0:T(8,128)(2,1)S(1)}, u32[]{:S(2)}, u32[]{:S(2)}) %collective-permute-start.5) | collective-permute-done | bytes 524320 | tf_op jit(solution)/shard_map/ppermute | solution.py:280
  37.7 2.8 %collective-permute-start.7 = (bf16[128,16,128]{2,1,0:T(8,128)(2,1)S(1)}, bf16[128,16,128]{2,1,0:T(8,128)(2,1)S(1)}, u32[]{:S(2)}, u32[]{:S(2)}) collective-permute-start(bf16[128,16,128]{2,1,0:T(8,128)(2,1)S(1)} %bitcast.7), channel_id=1, source_target_pairs={{8,24},{24,8},{1,9},{9,1},{13,29},{17,25},{25,17},{29,13},{2,10},{... | collective-permute-start | bytes 1572872 | tf_op jit(solution)/shard_map/ppermute | solution.py:280
  40.6 1.9 %collective-permute-start.8 = (bf16[128,16,128]{2,1,0:T(8,128)(2,1)S(1)}, bf16[128,16,128]{2,1,0:T(8,128)(2,1)S(1)}, u32[]{:S(2)}, u32[]{:S(2)}) collective-permute-start(bf16[128,16,128]{2,1,0:T(8,128)(2,1)S(1)} %collective-permute-done.1.refs_2_.refs_0_.refs_6_), channel_id=1, source_target_pairs={{0,8},{8,0},{16,24},{24,16},{1,17},{5,13},{13,5},{17,1},{21,29},{2... | collective-permute-start | bytes 1572872 | tf_op jit(solution)/shard_map/ppermute | solution.py:280
  42.5 0.2 collective-permute-done.2.refs_3_.refs_0_.refs_4_.refs_9_
  42.7 3.1 %collective-permute-start.6 = (bf16[128,16,128]{2,1,0:T(8,128)(2,1)S(1)}, bf16[128,16,128]{2,1,0:T(8,128)(2,1)S(1)}, u32[]{:S(2)}, u32[]{:S(2)}) collective-permute-start(bf16[128,16,128]{2,1,0:T(8,128)(2,1)S(1)} %collective-permute-done.2.refs_3_.refs_0_.refs_4_.refs_9_), channel_id=1, source_target_pairs={{0,8},{8,0},{16,24},{24,16},{1,17},{5,13},{13,5},{17,1},{21,29},{2... | collective-permute-start | bytes 1572872 | tf_op jit(solution)/shard_map/ppermute | solution.py:280
  45.9 2.1 %collective-permute-done.7.refs_5_ = bf16[128,16,128]{2,1,0:T(8,128)(2,1)S(1)} collective-permute-done((bf16[128,16,128]{2,1,0:T(8,128)(2,1)S(1)}, bf16[128,16,128]{2,1,0:T(8,128)(2,1)S(1)}, u32[]{:S(2)}, u32[]{:S(2)}) %collective-permute-start.7) | collective-permute-done | bytes 524320 | tf_op jit(solution)/shard_map/ppermute | solution.py:280
  48.0 5.3 %collective-permute-done.8.refs_1_.refs_3_.refs_7_ = bf16[128,16,128]{2,1,0:T(8,128)(2,1)S(1)} collective-permute-done((bf16[128,16,128]{2,1,0:T(8,128)(2,1)S(1)}, bf16[128,16,128]{2,1,0:T(8,128)(2,1)S(1)}, u32[]{:S(2)}, u32[]{:S(2)}) %collective-permute-start.8) | collective-permute-done | bytes 524320 | tf_op jit(solution)/shard_map/ppermute | solution.py:280
  53.3 3.8 %collective-permute-start.9 = (bf16[128,16,128]{2,1,0:T(8,128)(2,1)S(1)}, bf16[128,16,128]{2,1,0:T(8,128)(2,1)S(1)}, u32[]{:S(2)}, u32[]{:S(2)}) collective-permute-start(bf16[128,16,128]{2,1,0:T(8,128)(2,1)S(1)} %bitcast.4), channel_id=1, source_target_pairs={{8,24},{24,8},{1,9},{9,1},{13,29},{17,25},{25,17},{29,13},{2,10},{... | collective-permute-start | bytes 1572872 | tf_op jit(solution)/shard_map/ppermute | solution.py:280
  57.2 2.0 %own_rows.1.own = bf16[128,128,64]{2,1,0:T(8,128)(2,1)S(1)} custom-call(bf16[128,16,128]{2,1,0:T(8,128)(2,1)S(1)} %copy-done.1, bf16[128,16,128]{2,1,0:T(8,128)(2,1)S(1)} %collective-permute-done.refs_1_.refs_0_.refs_3_, bf16[128,16,128]{2,1,0:T(8,128)(2,1)S(1)} %collective-permute-done.1.refs_2_.refs_0_.refs_6_, ...), custom_call_target="tpu_custom_call" | custom-call | flops 1 | bytes 1 | tf_op jit(solution)/shard_map/own_rows/pallas_call | solution.py:144
  59.2 2.9 %collective-permute-done.6.refs_1_.refs_5_.refs_10_ = bf16[128,16,128]{2,1,0:T(8,128)(2,1)S(1)} collective-permute-done((bf16[128,16,128]{2,1,0:T(8,128)(2,1)S(1)}, bf16[128,16,128]{2,1,0:T(8,128)(2,1)S(1)}, u32[]{:S(2)}, u32[]{:S(2)}) %collective-permute-start.6) | collective-permute-done | bytes 524320 | tf_op jit(solution)/shard_map/ppermute | solution.py:280
  62.2 0.0 copy-start.2
  62.2 0.7 collective-permute-start.12
  62.9 2.4 %collective-permute-start.10 = (bf16[128,16,128]{2,1,0:T(8,128)(2,1)S(1)}, bf16[128,16,128]{2,1,0:T(8,128)(2,1)S(1)}, u32[]{:S(2)}, u32[]{:S(2)}) collective-permute-start(bf16[128,16,128]{2,1,0:T(8,128)(2,1)S(1)} %bitcast.5), channel_id=1, source_target_pairs={{8,24},{24,8},{1,9},{9,1},{13,29},{17,25},{25,17},{29,13},{2,10},{... | collective-permute-start | bytes 1572872 | tf_op jit(solution)/shard_map/ppermute | solution.py:280
  65.4 0.1 choose.10
  65.5 0.1 collective-permute-start.11
  65.6 0.0 collective-permute-done.12.refs_7_.refs_14_
  65.6 7.3 %collective-permute-done.10.refs_6_.refs_11_ = bf16[128,16,128]{2,1,0:T(8,128)(2,1)S(1)} collective-permute-done((bf16[128,16,128]{2,1,0:T(8,128)(2,1)S(1)}, bf16[128,16,128]{2,1,0:T(8,128)(2,1)S(1)}, u32[]{:S(2)}, u32[]{:S(2)}) %collective-permute-start.10) | collective-permute-done | bytes 524320 | tf_op jit(solution)/shard_map/ppermute | solution.py:280
  72.8 0.1 choose.11
  72.9 0.1 collective-permute-start.13
  73.0 2.6 %collective-permute-done.13.refs_13_ = bf16[2,128,16,128]{3,2,1,0:T(8,128)(2,1)S(1)} collective-permute-done((bf16[2,128,16,128]{3,2,1,0:T(8,128)(2,1)S(1)}, bf16[2,128,16,128]{3,2,1,0:T(8,128)(2,1)S(1)}, u32[]{:S(2)}, u32[]{:S(2)}) %collective-permute-start.13) | collective-permute-done | bytes 1048608 | tf_op jit(solution)/shard_map/ppermute | solution.py:280
  75.7 9.9 %stack.1 = f32[64,64,256]{2,1,0:T(8,128)} custom-call(s32[64]{0:T(128)S(1)} %copy-done.2, bf16[128,128,64]{2,1,0:T(8,128)(2,1)S(1)} %own_rows.1.own, bf16[128,16,128]{2,1,0:T(8,128)(2,1)S(1)} %copy-done.1, bf16[128,16,128]{2,1,0:T(8,128)(2,1)S(1)} %collective-permute-done.3.refs_1_, bf16[128,16,128]{2,1,0:T(8,128)(2,1)S(1)} %collective-permute-done.4.refs_2_, ...), custom_call_target="tpu_custom_call" | custom-call | flops 1 | bytes 1 | tf_op jit(solution)/shard_map/stack/pallas_call | solution.py:262
  (11 shorter events, 0.2 us)
Async XLA Ops:
  4.0 13.1 %collective-permute-start = (bf16[128,16,128]{2,1,0:T(8,128)(2,1)}, bf16[128,16,128]{2,1,0:T(8,128)(2,1)S(1)}, u32[]{:S(2)}, u32[]{:S(2)}) collective-permute-start(bf16[128,16,128]{2,1,0:T(8,128)(2,1)} %whiten.1.refs_0_), channel_id=1, source_target_pairs={{0,1},{1,2},{2,3},{3,0},{4,5},{5,6},{6,7},{7,4},{8,9},{9,10},{10,1... | collective-permute-start | bytes 1572872 | tf_op jit(solution)/shard_map/ppermute | solution.py:406
  5.4 13.0 %collective-permute-start.3 = (bf16[128,16,128]{2,1,0:T(8,128)(2,1)}, bf16[128,16,128]{2,1,0:T(8,128)(2,1)S(1)}, u32[]{:S(2)}, u32[]{:S(2)}) collective-permute-start(bf16[128,16,128]{2,1,0:T(8,128)(2,1)} %whiten.1.refs_0_), channel_id=1, source_target_pairs={{0,8},{8,0},{16,24},{24,16},{1,17},{5,13},{13,5},{17,1},{21,29},{2... | collective-permute-start | bytes 1572872 | tf_op jit(solution)/shard_map/ppermute | solution.py:280
  17.1 12.9 %collective-permute-start.1 = (bf16[128,16,128]{2,1,0:T(8,128)(2,1)S(1)}, bf16[128,16,128]{2,1,0:T(8,128)(2,1)S(1)}, u32[]{:S(2)}, u32[]{:S(2)}) collective-permute-start(bf16[128,16,128]{2,1,0:T(8,128)(2,1)S(1)} %collective-permute-done.refs_1_.refs_0_.refs_3_), channel_id=1, source_target_pairs={{0,1},{1,2},{2,3},{3,0},{4,5},{5,6},{6,7},{7,4},{8,9},{9,10},{10,1... | collective-permute-start | bytes 1572872 | tf_op jit(solution)/shard_map/ppermute | solution.py:406
  18.4 1.0 %copy-start = (bf16[128,16,128]{2,1,0:T(8,128)(2,1)S(1)}, bf16[128,16,128]{2,1,0:T(8,128)(2,1)}, u32[]{:S(2)}) copy-start(bf16[128,16,128]{2,1,0:T(8,128)(2,1)} %whiten.1.refs_0_) | copy-start | bytes 1572868
  19.4 37.8 %copy-start.1 = (bf16[128,16,128]{2,1,0:T(8,128)(2,1)S(1)}, bf16[128,16,128]{2,1,0:T(8,128)(2,1)}, u32[]{:S(2)}) copy-start(bf16[128,16,128]{2,1,0:T(8,128)(2,1)} %whiten.1.refs_0_) | copy-start | bytes 1572868
  19.4 10.8 %collective-permute-start.4 = (bf16[128,16,128]{2,1,0:T(8,128)(2,1)S(1)}, bf16[128,16,128]{2,1,0:T(8,128)(2,1)S(1)}, u32[]{:S(2)}, u32[]{:S(2)}) collective-permute-start(bf16[128,16,128]{2,1,0:T(8,128)(2,1)S(1)} %bitcast.6), channel_id=1, source_target_pairs={{8,24},{24,8},{1,9},{9,1},{13,29},{17,25},{25,17},{29,13},{2,10},{... | collective-permute-start | bytes 1572872 | tf_op jit(solution)/shard_map/ppermute | solution.py:280
  22.7 15.0 %collective-permute-start.5 = (bf16[128,16,128]{2,1,0:T(8,128)(2,1)S(1)}, bf16[128,16,128]{2,1,0:T(8,128)(2,1)S(1)}, u32[]{:S(2)}, u32[]{:S(2)}) collective-permute-start(bf16[128,16,128]{2,1,0:T(8,128)(2,1)S(1)} %collective-permute-done.refs_1_.refs_0_.refs_3_), channel_id=1, source_target_pairs={{0,8},{8,0},{16,24},{24,16},{1,17},{5,13},{13,5},{17,1},{21,29},{2... | collective-permute-start | bytes 1572872 | tf_op jit(solution)/shard_map/ppermute | solution.py:280
  29.9 12.8 %collective-permute-start.2 = (bf16[128,16,128]{2,1,0:T(8,128)(2,1)S(1)}, bf16[128,16,128]{2,1,0:T(8,128)(2,1)S(1)}, u32[]{:S(2)}, u32[]{:S(2)}) collective-permute-start(bf16[128,16,128]{2,1,0:T(8,128)(2,1)S(1)} %collective-permute-done.1.refs_2_.refs_0_.refs_6_), channel_id=1, source_target_pairs={{0,1},{1,2},{2,3},{3,0},{4,5},{5,6},{6,7},{7,4},{8,9},{9,10},{10,1... | collective-permute-start | bytes 1572872 | tf_op jit(solution)/shard_map/ppermute | solution.py:406
  37.7 10.2 %collective-permute-start.7 = (bf16[128,16,128]{2,1,0:T(8,128)(2,1)S(1)}, bf16[128,16,128]{2,1,0:T(8,128)(2,1)S(1)}, u32[]{:S(2)}, u32[]{:S(2)}) collective-permute-start(bf16[128,16,128]{2,1,0:T(8,128)(2,1)S(1)} %bitcast.7), channel_id=1, source_target_pairs={{8,24},{24,8},{1,9},{9,1},{13,29},{17,25},{25,17},{29,13},{2,10},{... | collective-permute-start | bytes 1572872 | tf_op jit(solution)/shard_map/ppermute | solution.py:280
  40.6 12.7 %collective-permute-start.8 = (bf16[128,16,128]{2,1,0:T(8,128)(2,1)S(1)}, bf16[128,16,128]{2,1,0:T(8,128)(2,1)S(1)}, u32[]{:S(2)}, u32[]{:S(2)}) collective-permute-start(bf16[128,16,128]{2,1,0:T(8,128)(2,1)S(1)} %collective-permute-done.1.refs_2_.refs_0_.refs_6_), channel_id=1, source_target_pairs={{0,8},{8,0},{16,24},{24,16},{1,17},{5,13},{13,5},{17,1},{21,29},{2... | collective-permute-start | bytes 1572872 | tf_op jit(solution)/shard_map/ppermute | solution.py:280
  42.7 19.4 %collective-permute-start.6 = (bf16[128,16,128]{2,1,0:T(8,128)(2,1)S(1)}, bf16[128,16,128]{2,1,0:T(8,128)(2,1)S(1)}, u32[]{:S(2)}, u32[]{:S(2)}) collective-permute-start(bf16[128,16,128]{2,1,0:T(8,128)(2,1)S(1)} %collective-permute-done.2.refs_3_.refs_0_.refs_4_.refs_9_), channel_id=1, source_target_pairs={{0,8},{8,0},{16,24},{24,16},{1,17},{5,13},{13,5},{17,1},{21,29},{2... | collective-permute-start | bytes 1572872 | tf_op jit(solution)/shard_map/ppermute | solution.py:280
  53.3 12.2 %collective-permute-start.9 = (bf16[128,16,128]{2,1,0:T(8,128)(2,1)S(1)}, bf16[128,16,128]{2,1,0:T(8,128)(2,1)S(1)}, u32[]{:S(2)}, u32[]{:S(2)}) collective-permute-start(bf16[128,16,128]{2,1,0:T(8,128)(2,1)S(1)} %bitcast.4), channel_id=1, source_target_pairs={{8,24},{24,8},{1,9},{9,1},{13,29},{17,25},{25,17},{29,13},{2,10},{... | collective-permute-start | bytes 1572872 | tf_op jit(solution)/shard_map/ppermute | solution.py:280
  62.2 13.5 %copy-start.2 = (s32[64]{0:T(128)S(1)}, s32[64]{0:T(128)}, u32[]{:S(2)}) copy-start(s32[64]{0:T(128)} %reach_ref.1) | copy-start | bytes 772
  62.2 3.4 %collective-permute-start.12 = (bf16[128,16,128]{2,1,0:T(8,128)(2,1)S(1)}, bf16[128,16,128]{2,1,0:T(8,128)(2,1)S(1)}, u32[]{:S(2)}, u32[]{:S(2)}) collective-permute-start(bf16[128,16,128]{2,1,0:T(8,128)(2,1)S(1)} %collective-permute-done.2.refs_3_.refs_0_.refs_4_.refs_9_), channel_id=1, source_target_pairs={{3,19},{11,27},{19,3},{27,11}} | collective-permute-start | bytes 1572872 | tf_op jit(solution)/shard_map/ppermute | solution.py:280
  62.9 9.9 %collective-permute-start.10 = (bf16[128,16,128]{2,1,0:T(8,128)(2,1)S(1)}, bf16[128,16,128]{2,1,0:T(8,128)(2,1)S(1)}, u32[]{:S(2)}, u32[]{:S(2)}) collective-permute-start(bf16[128,16,128]{2,1,0:T(8,128)(2,1)S(1)} %bitcast.5), channel_id=1, source_target_pairs={{8,24},{24,8},{1,9},{9,1},{13,29},{17,25},{25,17},{29,13},{2,10},{... | collective-permute-start | bytes 1572872 | tf_op jit(solution)/shard_map/ppermute | solution.py:280
  65.5 7.5 %collective-permute-start.11 = (bf16[2,128,16,128]{3,2,1,0:T(8,128)(2,1)S(1)}, bf16[2,128,16,128]{3,2,1,0:T(8,128)(2,1)S(1)}, u32[]{:S(2)}, u32[]{:S(2)}) collective-permute-start(bf16[2,128,16,128]{3,2,1,0:T(8,128)(2,1)S(1)} %choose.10), channel_id=1, source_target_pairs={{0,4},{4,0},{8,12},{12,8},{16,20},{20,16},{24,28},{28,24},{1,5},{5... | collective-permute-start | bytes 3145736 | tf_op jit(solution)/shard_map/ppermute | solution.py:280
  72.9 2.7 %collective-permute-start.13 = (bf16[2,128,16,128]{3,2,1,0:T(8,128)(2,1)S(1)}, bf16[2,128,16,128]{3,2,1,0:T(8,128)(2,1)S(1)}, u32[]{:S(2)}, u32[]{:S(2)}) collective-permute-start(bf16[2,128,16,128]{3,2,1,0:T(8,128)(2,1)S(1)} %choose.11), channel_id=1, source_target_pairs={{0,4},{4,0},{8,12},{12,8},{16,20},{20,16},{24,28},{28,24},{1,5},{5... | collective-permute-start | bytes 3145736 | tf_op jit(solution)/shard_map/ppermute | solution.py:280

commit v15 on v14

--- a/solution.py
+++ b/solution.py
@@ -155,11 +155,12 @@
 
 
 def stack_kernel(scale, groups, codes_of, reach_ref, own, *refs):
-    buffers, (out_hbm, partners, products, out, sems) = refs[:-5], refs[-5:]
+    buffers, (out_hbm, partners, products, rows, out, sems) = refs[:-6], refs[-6:]
     bins, lanes, _ = own.shape
     width = lanes // 2
     offsets = out_hbm.shape[0]
     pitch = products.shape[0] // bins
+    channel_pitch = rows.shape[0] // width
     slots = len(groups)
     first_offset = lax.axis_index("win") * offsets
     codes = codes_of()
@@ -213,7 +214,7 @@
         columns = pl.ds(pl.multiple_of(block * CHANNEL_BLOCK, CHANNEL_BLOCK), CHANNEL_BLOCK)
         return [
             pltpu.make_async_copy(
-                out.at[part].reshape(offsets, pitch, F).at[:, columns, :],
+                out.at[part, :, columns, :],
                 out_hbm.at[:, columns, pl.ds(part * F, F)],
                 sems.at[block, part],
             )
@@ -238,7 +239,16 @@
             results = [picked(i) for i in channels]
             for i, result in zip(channels, results):
                 for part in range(2):
-                    out[part, pl.ds(i, offsets, stride=pitch), :] = result[part]
+                    row = pl.multiple_of(i * channel_pitch + part * offsets, 8)
+                    rows[pl.ds(row, offsets), :] = result[part]
+        begin = block * CHANNEL_BLOCK
+        columns = pl.ds(pl.multiple_of(begin, CHANNEL_BLOCK), CHANNEL_BLOCK)
+        for part in range(2):
+            for k in range(offsets):
+                row = begin * channel_pitch + part * offsets + k
+                out[part, k, columns, :] = rows[
+                    pl.ds(row, CHANNEL_BLOCK, stride=channel_pitch), :
+                ]
         for copy in copies(block):
             copy.start()
         return carry
@@ -267,10 +277,11 @@
         scratch_shapes=[
             pltpu.VMEM((2, len(groups), bins, chunk_windows, lanes), jnp.bfloat16),
             pltpu.VMEM((bins * pitch, lanes), jnp.float32),
-            pltpu.VMEM((2, offsets * pitch, F), jnp.float32),
+            pltpu.VMEM((width * (2 * offsets + PITCH_PAD), F), jnp.float32),
+            pltpu.VMEM((2, offsets, width, F), jnp.float32),
             pltpu.SemaphoreType.DMA((width // CHANNEL_BLOCK, 2)),
         ],
-        compiler_params=pltpu.CompilerParams(vmem_limit_bytes=28 * MIB),
+        compiler_params=pltpu.CompilerParams(vmem_limit_bytes=32 * MIB),
         cost_estimate=SMALL,
         name="stack",
     )(reach, own, *buffers)

time: 85.9 us -> 86.5 us (level)
  no operation moved by 1% of the time
where the time goes in v15:
time: 86.5 us; the launch traced here: 86.1 us
  waiting for transfers between devices  42.7 us (49%)
  starting transfers between devices  25.3 us (29%)
  Pallas kernels  16.8 us (19%)
  local copies, waits for them, and re-layouts  1.05 us (1%)
    ppermute x11, waiting for transfers between devices, send(): return lax.ppermute(array, AXES, pairs)  27.7 us
    ppermute x11, starting transfers between devices, send(): return lax.ppermute(array, AXES, pairs)  22.4 us
    ppermute x3, waiting for transfers between devices, on_device(): pieces.append(lax.ppermute(pieces[-1], 'win', ring))  15 us
    pallas_call x1, Pallas kernels, stacked(): pl.pallas_call(functools.partial(stack_kernel, 1.0 / math.sqrt(windows),...  10.5 us
    pallas_call x1, Pallas kernels, whitened_chunk(): pl.pallas_call(whiten_kernel, out_shape=jax.ShapeDtypeStruct((F, windows,...  4 us
    ppermute x3, starting transfers between devices, on_device(): pieces.append(lax.ppermute(pieces[-1], 'win', ring))  2.93 us
    pallas_call x1, Pallas kernels, own_rows(): pl.pallas_call(own_kernel, out_shape=jax.ShapeDtypeStruct((bins, lanes, w...  2.03 us
  transfers between devices with their start and end apart: 14, of which 9 were waited for; matrix products, arithmetic and copies ran while one was open for 0% of the time, Pallas kernels for 3%

profile of v15, /device:TPU:11, one launch (start us, length us, event | category | flops | bytes accessed | tf_op | source)
XLA Modules:
  0.0 86.1 jit_solution(7536303518608329501)
XLA Ops:
  0.0 4.0 %whiten.1.refs_0_ = bf16[128,16,128]{2,1,0:T(8,128)(2,1)} custom-call(bf16[256,512]{1,0:T(8,128)(2,1)} %constant.3.table_hbm, bf16[16,64,512]{2,1,0:T(8,128)(2,1)} %traces_hbm.1, s32[16,64]{1,0:T(8,128)} %valid_hbm.1), custom_call_target="tpu_custom_call" | custom-call | flops 268435456 | bytes 1048576 | tf_op jit(solution)/shard_map/whiten/pallas_call | solution.py:79
  4.0 1.3 %collective-permute-start = (bf16[128,16,128]{2,1,0:T(8,128)(2,1)}, bf16[128,16,128]{2,1,0:T(8,128)(2,1)S(1)}, u32[]{:S(2)}, u32[]{:S(2)}) collective-permute-start(bf16[128,16,128]{2,1,0:T(8,128)(2,1)} %whiten.1.refs_0_), channel_id=1, source_target_pairs={{0,1},{1,2},{2,3},{3,0},{4,5},{5,6},{6,7},{7,4},{8,9},{9,10},{10,1... | collective-permute-start | bytes 1572872 | tf_op jit(solution)/shard_map/ppermute | solution.py:417
  5.4 2.2 %collective-permute-start.3 = (bf16[128,16,128]{2,1,0:T(8,128)(2,1)}, bf16[128,16,128]{2,1,0:T(8,128)(2,1)S(1)}, u32[]{:S(2)}, u32[]{:S(2)}) collective-permute-start(bf16[128,16,128]{2,1,0:T(8,128)(2,1)} %whiten.1.refs_0_), channel_id=1, source_target_pairs={{0,8},{8,0},{16,24},{24,16},{1,17},{5,13},{13,5},{17,1},{21,29},{2... | collective-permute-start | bytes 1572872 | tf_op jit(solution)/shard_map/ppermute | solution.py:291
  7.5 9.5 %collective-permute-done.refs_1_.refs_0_.refs_3_ = bf16[128,16,128]{2,1,0:T(8,128)(2,1)S(1)} collective-permute-done((bf16[128,16,128]{2,1,0:T(8,128)(2,1)}, bf16[128,16,128]{2,1,0:T(8,128)(2,1)S(1)}, u32[]{:S(2)}, u32[]{:S(2)}) %collective-permute-start) | collective-permute-done | bytes 524320 | tf_op jit(solution)/shard_map/ppermute | solution.py:417
  17.1 1.3 %collective-permute-start.1 = (bf16[128,16,128]{2,1,0:T(8,128)(2,1)S(1)}, bf16[128,16,128]{2,1,0:T(8,128)(2,1)S(1)}, u32[]{:S(2)}, u32[]{:S(2)}) collective-permute-start(bf16[128,16,128]{2,1,0:T(8,128)(2,1)S(1)} %collective-permute-done.refs_1_.refs_0_.refs_3_), channel_id=1, source_target_pairs={{0,1},{1,2},{2,3},{3,0},{4,5},{5,6},{6,7},{7,4},{8,9},{9,10},{10,1... | collective-permute-start | bytes 1572872 | tf_op jit(solution)/shard_map/ppermute | solution.py:417
  18.4 1.0 %copy-done = bf16[128,16,128]{2,1,0:T(8,128)(2,1)S(1)} copy-done((bf16[128,16,128]{2,1,0:T(8,128)(2,1)S(1)}, bf16[128,16,128]{2,1,0:T(8,128)(2,1)}, u32[]{:S(2)}) %copy-start) | copy-done | bytes 524312
  19.4 3.3 %collective-permute-start.4 = (bf16[128,16,128]{2,1,0:T(8,128)(2,1)S(1)}, bf16[128,16,128]{2,1,0:T(8,128)(2,1)S(1)}, u32[]{:S(2)}, u32[]{:S(2)}) collective-permute-start(bf16[128,16,128]{2,1,0:T(8,128)(2,1)S(1)} %bitcast.6), channel_id=1, source_target_pairs={{8,24},{24,8},{1,9},{9,1},{13,29},{17,25},{25,17},{29,13},{2,10},{... | collective-permute-start | bytes 1572872 | tf_op jit(solution)/shard_map/ppermute | solution.py:291
  22.7 1.9 %collective-permute-start.5 = (bf16[128,16,128]{2,1,0:T(8,128)(2,1)S(1)}, bf16[128,16,128]{2,1,0:T(8,128)(2,1)S(1)}, u32[]{:S(2)}, u32[]{:S(2)}) collective-permute-start(bf16[128,16,128]{2,1,0:T(8,128)(2,1)S(1)} %collective-permute-done.refs_1_.refs_0_.refs_3_), channel_id=1, source_target_pairs={{0,8},{8,0},{16,24},{24,16},{1,17},{5,13},{13,5},{17,1},{21,29},{2... | collective-permute-start | bytes 1572872 | tf_op jit(solution)/shard_map/ppermute | solution.py:291
  24.7 5.3 %collective-permute-done.1.refs_2_.refs_0_.refs_6_ = bf16[128,16,128]{2,1,0:T(8,128)(2,1)S(1)} collective-permute-done((bf16[128,16,128]{2,1,0:T(8,128)(2,1)S(1)}, bf16[128,16,128]{2,1,0:T(8,128)(2,1)S(1)}, u32[]{:S(2)}, u32[]{:S(2)}) %collective-permute-start.1) | collective-permute-done | bytes 524320 | tf_op jit(solution)/shard_map/ppermute | solution.py:417
  29.9 0.3 collective-permute-start.2
  30.2 0.0 collective-permute-done.4.refs_2_
  30.2 7.5 %collective-permute-done.5.refs_1_.refs_4_ = bf16[128,16,128]{2,1,0:T(8,128)(2,1)S(1)} collective-permute-done((bf16[128,16,128]{2,1,0:T(8,128)(2,1)S(1)}, bf16[128,16,128]{2,1,0:T(8,128)(2,1)S(1)}, u32[]{:S(2)}, u32[]{:S(2)}) %collective-permute-start.5) | collective-permute-done | bytes 524320 | tf_op jit(solution)/shard_map/ppermute | solution.py:291
  37.7 2.8 %collective-permute-start.7 = (bf16[128,16,128]{2,1,0:T(8,128)(2,1)S(1)}, bf16[128,16,128]{2,1,0:T(8,128)(2,1)S(1)}, u32[]{:S(2)}, u32[]{:S(2)}) collective-permute-start(bf16[128,16,128]{2,1,0:T(8,128)(2,1)S(1)} %bitcast.7), channel_id=1, source_target_pairs={{8,24},{24,8},{1,9},{9,1},{13,29},{17,25},{25,17},{29,13},{2,10},{... | collective-permute-start | bytes 1572872 | tf_op jit(solution)/shard_map/ppermute | solution.py:291
  40.6 1.9 %collective-permute-start.8 = (bf16[128,16,128]{2,1,0:T(8,128)(2,1)S(1)}, bf16[128,16,128]{2,1,0:T(8,128)(2,1)S(1)}, u32[]{:S(2)}, u32[]{:S(2)}) collective-permute-start(bf16[128,16,128]{2,1,0:T(8,128)(2,1)S(1)} %collective-permute-done.1.refs_2_.refs_0_.refs_6_), channel_id=1, source_target_pairs={{0,8},{8,0},{16,24},{24,16},{1,17},{5,13},{13,5},{17,1},{21,29},{2... | collective-permute-start | bytes 1572872 | tf_op jit(solution)/shard_map/ppermute | solution.py:291
  42.5 0.2 collective-permute-done.2.refs_3_.refs_0_.refs_4_.refs_9_
  42.7 3.1 %collective-permute-start.6 = (bf16[128,16,128]{2,1,0:T(8,128)(2,1)S(1)}, bf16[128,16,128]{2,1,0:T(8,128)(2,1)S(1)}, u32[]{:S(2)}, u32[]{:S(2)}) collective-permute-start(bf16[128,16,128]{2,1,0:T(8,128)(2,1)S(1)} %collective-permute-done.2.refs_3_.refs_0_.refs_4_.refs_9_), channel_id=1, source_target_pairs={{0,8},{8,0},{16,24},{24,16},{1,17},{5,13},{13,5},{17,1},{21,29},{2... | collective-permute-start | bytes 1572872 | tf_op jit(solution)/shard_map/ppermute | solution.py:291
  45.9 2.1 %collective-permute-done.7.refs_5_ = bf16[128,16,128]{2,1,0:T(8,128)(2,1)S(1)} collective-permute-done((bf16[128,16,128]{2,1,0:T(8,128)(2,1)S(1)}, bf16[128,16,128]{2,1,0:T(8,128)(2,1)S(1)}, u32[]{:S(2)}, u32[]{:S(2)}) %collective-permute-start.7) | collective-permute-done | bytes 524320 | tf_op jit(solution)/shard_map/ppermute | solution.py:291
  48.0 5.3 %collective-permute-done.8.refs_1_.refs_3_.refs_7_ = bf16[128,16,128]{2,1,0:T(8,128)(2,1)S(1)} collective-permute-done((bf16[128,16,128]{2,1,0:T(8,128)(2,1)S(1)}, bf16[128,16,128]{2,1,0:T(8,128)(2,1)S(1)}, u32[]{:S(2)}, u32[]{:S(2)}) %collective-permute-start.8) | collective-permute-done | bytes 524320 | tf_op jit(solution)/shard_map/ppermute | solution.py:291
  53.3 3.8 %collective-permute-start.9 = (bf16[128,16,128]{2,1,0:T(8,128)(2,1)S(1)}, bf16[128,16,128]{2,1,0:T(8,128)(2,1)S(1)}, u32[]{:S(2)}, u32[]{:S(2)}) collective-permute-start(bf16[128,16,128]{2,1,0:T(8,128)(2,1)S(1)} %bitcast.4), channel_id=1, source_target_pairs={{8,24},{24,8},{1,9},{9,1},{13,29},{17,25},{25,17},{29,13},{2,10},{... | collective-permute-start | bytes 1572872 | tf_op jit(solution)/shard_map/ppermute | solution.py:291
  57.2 2.0 %own_rows.1.own = bf16[128,128,64]{2,1,0:T(8,128)(2,1)S(1)} custom-call(bf16[128,16,128]{2,1,0:T(8,128)(2,1)S(1)} %copy-done.1, bf16[128,16,128]{2,1,0:T(8,128)(2,1)S(1)} %collective-permute-done.refs_1_.refs_0_.refs_3_, bf16[128,16,128]{2,1,0:T(8,128)(2,1)S(1)} %collective-permute-done.1.refs_2_.refs_0_.refs_6_, ...), custom_call_target="tpu_custom_call" | custom-call | flops 1 | bytes 1 | tf_op jit(solution)/shard_map/own_rows/pallas_call | solution.py:144
  59.2 2.9 %collective-permute-done.6.refs_1_.refs_5_.refs_10_ = bf16[128,16,128]{2,1,0:T(8,128)(2,1)S(1)} collective-permute-done((bf16[128,16,128]{2,1,0:T(8,128)(2,1)S(1)}, bf16[128,16,128]{2,1,0:T(8,128)(2,1)S(1)}, u32[]{:S(2)}, u32[]{:S(2)}) %collective-permute-start.6) | collective-permute-done | bytes 524320 | tf_op jit(solution)/shard_map/ppermute | solution.py:291
  62.2 0.0 copy-start.2
  62.2 0.7 collective-permute-start.12
  62.9 2.4 %collective-permute-start.10 = (bf16[128,16,128]{2,1,0:T(8,128)(2,1)S(1)}, bf16[128,16,128]{2,1,0:T(8,128)(2,1)S(1)}, u32[]{:S(2)}, u32[]{:S(2)}) collective-permute-start(bf16[128,16,128]{2,1,0:T(8,128)(2,1)S(1)} %bitcast.5), channel_id=1, source_target_pairs={{8,24},{24,8},{1,9},{9,1},{13,29},{17,25},{25,17},{29,13},{2,10},{... | collective-permute-start | bytes 1572872 | tf_op jit(solution)/shard_map/ppermute | solution.py:291
  65.4 0.1 choose.10
  65.5 0.1 collective-permute-start.11
  65.6 0.0 collective-permute-done.12.refs_7_.refs_14_
  65.6 7.3 %collective-permute-done.10.refs_6_.refs_11_ = bf16[128,16,128]{2,1,0:T(8,128)(2,1)S(1)} collective-permute-done((bf16[128,16,128]{2,1,0:T(8,128)(2,1)S(1)}, bf16[128,16,128]{2,1,0:T(8,128)(2,1)S(1)}, u32[]{:S(2)}, u32[]{:S(2)}) %collective-permute-start.10) | collective-permute-done | bytes 524320 | tf_op jit(solution)/shard_map/ppermute | solution.py:291
  72.8 0.1 choose.11
  72.9 0.1 collective-permute-start.13
  73.0 2.6 %collective-permute-done.13.refs_13_ = bf16[2,128,16,128]{3,2,1,0:T(8,128)(2,1)S(1)} collective-permute-done((bf16[2,128,16,128]{3,2,1,0:T(8,128)(2,1)S(1)}, bf16[2,128,16,128]{3,2,1,0:T(8,128)(2,1)S(1)}, u32[]{:S(2)}, u32[]{:S(2)}) %collective-permute-start.13) | collective-permute-done | bytes 1048608 | tf_op jit(solution)/shard_map/ppermute | solution.py:291
  75.7 10.5 %stack.1 = f32[64,64,256]{2,1,0:T(8,128)} custom-call(s32[64]{0:T(128)S(1)} %copy-done.2, bf16[128,128,64]{2,1,0:T(8,128)(2,1)S(1)} %own_rows.1.own, bf16[128,16,128]{2,1,0:T(8,128)(2,1)S(1)} %copy-done.1, bf16[128,16,128]{2,1,0:T(8,128)(2,1)S(1)} %collective-permute-done.3.refs_1_, bf16[128,16,128]{2,1,0:T(8,128)(2,1)S(1)} %collective-permute-done.4.refs_2_, ...), custom_call_target="tpu_custom_call" | custom-call | flops 1 | bytes 1 | tf_op jit(solution)/shard_map/stack/pallas_call | solution.py:272
  (11 shorter events, 0.2 us)
Async XLA Ops:
  4.0 13.1 %collective-permute-start = (bf16[128,16,128]{2,1,0:T(8,128)(2,1)}, bf16[128,16,128]{2,1,0:T(8,128)(2,1)S(1)}, u32[]{:S(2)}, u32[]{:S(2)}) collective-permute-start(bf16[128,16,128]{2,1,0:T(8,128)(2,1)} %whiten.1.refs_0_), channel_id=1, source_target_pairs={{0,1},{1,2},{2,3},{3,0},{4,5},{5,6},{6,7},{7,4},{8,9},{9,10},{10,1... | collective-permute-start | bytes 1572872 | tf_op jit(solution)/shard_map/ppermute | solution.py:417
  5.4 13.0 %collective-permute-start.3 = (bf16[128,16,128]{2,1,0:T(8,128)(2,1)}, bf16[128,16,128]{2,1,0:T(8,128)(2,1)S(1)}, u32[]{:S(2)}, u32[]{:S(2)}) collective-permute-start(bf16[128,16,128]{2,1,0:T(8,128)(2,1)} %whiten.1.refs_0_), channel_id=1, source_target_pairs={{0,8},{8,0},{16,24},{24,16},{1,17},{5,13},{13,5},{17,1},{21,29},{2... | collective-permute-start | bytes 1572872 | tf_op jit(solution)/shard_map/ppermute | solution.py:291
  17.1 12.9 %collective-permute-start.1 = (bf16[128,16,128]{2,1,0:T(8,128)(2,1)S(1)}, bf16[128,16,128]{2,1,0:T(8,128)(2,1)S(1)}, u32[]{:S(2)}, u32[]{:S(2)}) collective-permute-start(bf16[128,16,128]{2,1,0:T(8,128)(2,1)S(1)} %collective-permute-done.refs_1_.refs_0_.refs_3_), channel_id=1, source_target_pairs={{0,1},{1,2},{2,3},{3,0},{4,5},{5,6},{6,7},{7,4},{8,9},{9,10},{10,1... | collective-permute-start | bytes 1572872 | tf_op jit(solution)/shard_map/ppermute | solution.py:417
  18.4 1.0 %copy-start = (bf16[128,16,128]{2,1,0:T(8,128)(2,1)S(1)}, bf16[128,16,128]{2,1,0:T(8,128)(2,1)}, u32[]{:S(2)}) copy-start(bf16[128,16,128]{2,1,0:T(8,128)(2,1)} %whiten.1.refs_0_) | copy-start | bytes 1572868
  19.4 37.8 %copy-start.1 = (bf16[128,16,128]{2,1,0:T(8,128)(2,1)S(1)}, bf16[128,16,128]{2,1,0:T(8,128)(2,1)}, u32[]{:S(2)}) copy-start(bf16[128,16,128]{2,1,0:T(8,128)(2,1)} %whiten.1.refs_0_) | copy-start | bytes 1572868
  19.4 10.8 %collective-permute-start.4 = (bf16[128,16,128]{2,1,0:T(8,128)(2,1)S(1)}, bf16[128,16,128]{2,1,0:T(8,128)(2,1)S(1)}, u32[]{:S(2)}, u32[]{:S(2)}) collective-permute-start(bf16[128,16,128]{2,1,0:T(8,128)(2,1)S(1)} %bitcast.6), channel_id=1, source_target_pairs={{8,24},{24,8},{1,9},{9,1},{13,29},{17,25},{25,17},{29,13},{2,10},{... | collective-permute-start | bytes 1572872 | tf_op jit(solution)/shard_map/ppermute | solution.py:291
  22.7 15.0 %collective-permute-start.5 = (bf16[128,16,128]{2,1,0:T(8,128)(2,1)S(1)}, bf16[128,16,128]{2,1,0:T(8,128)(2,1)S(1)}, u32[]{:S(2)}, u32[]{:S(2)}) collective-permute-start(bf16[128,16,128]{2,1,0:T(8,128)(2,1)S(1)} %collective-permute-done.refs_1_.refs_0_.refs_3_), channel_id=1, source_target_pairs={{0,8},{8,0},{16,24},{24,16},{1,17},{5,13},{13,5},{17,1},{21,29},{2... | collective-permute-start | bytes 1572872 | tf_op jit(solution)/shard_map/ppermute | solution.py:291
  29.9 12.8 %collective-permute-start.2 = (bf16[128,16,128]{2,1,0:T(8,128)(2,1)S(1)}, bf16[128,16,128]{2,1,0:T(8,128)(2,1)S(1)}, u32[]{:S(2)}, u32[]{:S(2)}) collective-permute-start(bf16[128,16,128]{2,1,0:T(8,128)(2,1)S(1)} %collective-permute-done.1.refs_2_.refs_0_.refs_6_), channel_id=1, source_target_pairs={{0,1},{1,2},{2,3},{3,0},{4,5},{5,6},{6,7},{7,4},{8,9},{9,10},{10,1... | collective-permute-start | bytes 1572872 | tf_op jit(solution)/shard_map/ppermute | solution.py:417
  37.7 10.2 %collective-permute-start.7 = (bf16[128,16,128]{2,1,0:T(8,128)(2,1)S(1)}, bf16[128,16,128]{2,1,0:T(8,128)(2,1)S(1)}, u32[]{:S(2)}, u32[]{:S(2)}) collective-permute-start(bf16[128,16,128]{2,1,0:T(8,128)(2,1)S(1)} %bitcast.7), channel_id=1, source_target_pairs={{8,24},{24,8},{1,9},{9,1},{13,29},{17,25},{25,17},{29,13},{2,10},{... | collective-permute-start | bytes 1572872 | tf_op jit(solution)/shard_map/ppermute | solution.py:291
  40.6 12.7 %collective-permute-start.8 = (bf16[128,16,128]{2,1,0:T(8,128)(2,1)S(1)}, bf16[128,16,128]{2,1,0:T(8,128)(2,1)S(1)}, u32[]{:S(2)}, u32[]{:S(2)}) collective-permute-start(bf16[128,16,128]{2,1,0:T(8,128)(2,1)S(1)} %collective-permute-done.1.refs_2_.refs_0_.refs_6_), channel_id=1, source_target_pairs={{0,8},{8,0},{16,24},{24,16},{1,17},{5,13},{13,5},{17,1},{21,29},{2... | collective-permute-start | bytes 1572872 | tf_op jit(solution)/shard_map/ppermute | solution.py:291
  42.7 19.4 %collective-permute-start.6 = (bf16[128,16,128]{2,1,0:T(8,128)(2,1)S(1)}, bf16[128,16,128]{2,1,0:T(8,128)(2,1)S(1)}, u32[]{:S(2)}, u32[]{:S(2)}) collective-permute-start(bf16[128,16,128]{2,1,0:T(8,128)(2,1)S(1)} %collective-permute-done.2.refs_3_.refs_0_.refs_4_.refs_9_), channel_id=1, source_target_pairs={{0,8},{8,0},{16,24},{24,16},{1,17},{5,13},{13,5},{17,1},{21,29},{2... | collective-permute-start | bytes 1572872 | tf_op jit(solution)/shard_map/ppermute | solution.py:291
  53.3 12.2 %collective-permute-start.9 = (bf16[128,16,128]{2,1,0:T(8,128)(2,1)S(1)}, bf16[128,16,128]{2,1,0:T(8,128)(2,1)S(1)}, u32[]{:S(2)}, u32[]{:S(2)}) collective-permute-start(bf16[128,16,128]{2,1,0:T(8,128)(2,1)S(1)} %bitcast.4), channel_id=1, source_target_pairs={{8,24},{24,8},{1,9},{9,1},{13,29},{17,25},{25,17},{29,13},{2,10},{... | collective-permute-start | bytes 1572872 | tf_op jit(solution)/shard_map/ppermute | solution.py:291
  62.2 13.5 %copy-start.2 = (s32[64]{0:T(128)S(1)}, s32[64]{0:T(128)}, u32[]{:S(2)}) copy-start(s32[64]{0:T(128)} %reach_ref.1) | copy-start | bytes 772
  62.2 3.4 %collective-permute-start.12 = (bf16[128,16,128]{2,1,0:T(8,128)(2,1)S(1)}, bf16[128,16,128]{2,1,0:T(8,128)(2,1)S(1)}, u32[]{:S(2)}, u32[]{:S(2)}) collective-permute-start(bf16[128,16,128]{2,1,0:T(8,128)(2,1)S(1)} %collective-permute-done.2.refs_3_.refs_0_.refs_4_.refs_9_), channel_id=1, source_target_pairs={{3,19},{11,27},{19,3},{27,11}} | collective-permute-start | bytes 1572872 | tf_op jit(solution)/shard_map/ppermute | solution.py:291
  62.9 9.9 %collective-permute-start.10 = (bf16[128,16,128]{2,1,0:T(8,128)(2,1)S(1)}, bf16[128,16,128]{2,1,0:T(8,128)(2,1)S(1)}, u32[]{:S(2)}, u32[]{:S(2)}) collective-permute-start(bf16[128,16,128]{2,1,0:T(8,128)(2,1)S(1)} %bitcast.5), channel_id=1, source_target_pairs={{8,24},{24,8},{1,9},{9,1},{13,29},{17,25},{25,17},{29,13},{2,10},{... | collective-permute-start | bytes 1572872 | tf_op jit(solution)/shard_map/ppermute | solution.py:291
  65.5 7.5 %collective-permute-start.11 = (bf16[2,128,16,128]{3,2,1,0:T(8,128)(2,1)S(1)}, bf16[2,128,16,128]{3,2,1,0:T(8,128)(2,1)S(1)}, u32[]{:S(2)}, u32[]{:S(2)}) collective-permute-start(bf16[2,128,16,128]{3,2,1,0:T(8,128)(2,1)S(1)} %choose.10), channel_id=1, source_target_pairs={{0,4},{4,0},{8,12},{12,8},{16,20},{20,16},{24,28},{28,24},{1,5},{5... | collective-permute-start | bytes 3145736 | tf_op jit(solution)/shard_map/ppermute | solution.py:291
  72.9 2.7 %collective-permute-start.13 = (bf16[2,128,16,128]{3,2,1,0:T(8,128)(2,1)S(1)}, bf16[2,128,16,128]{3,2,1,0:T(8,128)(2,1)S(1)}, u32[]{:S(2)}, u32[]{:S(2)}) collective-permute-start(bf16[2,128,16,128]{3,2,1,0:T(8,128)(2,1)S(1)} %choose.11), channel_id=1, source_target_pairs={{0,4},{4,0},{8,12},{12,8},{16,20},{20,16},{24,28},{28,24},{1,5},{5... | collective-permute-start | bytes 3145736 | tf_op jit(solution)/shard_map/ppermute | solution.py:291

commit v16 on v14

--- a/solution.py
+++ b/solution.py
@@ -14,7 +14,7 @@
 BAND = 256
 AXES = ("chan", "win")
 CHANNEL_BLOCK = 8
-GROUP = 4
+MATMUL_DEPTH = 256
 WHITEN_BLOCKS = 4
 PITCH_PAD = 8
 MIB = 1024 * 1024
@@ -131,20 +131,33 @@
 
 def own_kernel(*refs):
     out_ref = refs[-1]
-
-    def one_bin(f, carry):
-        out_ref[f] = jnp.concatenate([ref[f] for ref in refs[:-1]], axis=0).T
+    _, rows, depth = out_ref.shape
+    lanes = refs[0].shape[-1]
+    together = rows // lanes
+    windows = depth // together
+
+    def one_group(group, carry):
+        for n in range(together):
+            f = group * together + n
+            turned = jnp.concatenate([ref[f] for ref in refs[:-1]], axis=0).T
+            parts = [
+                turned if m == n else jnp.zeros((lanes, windows), turned.dtype)
+                for m in range(together)
+            ]
+            out_ref[group, n * lanes : (n + 1) * lanes, :] = jnp.concatenate(parts, axis=1)
         return carry
 
-    lax.fori_loop(0, out_ref.shape[0], one_bin, 0, unroll=8)
+    lax.fori_loop(0, out_ref.shape[0], one_group, 0, unroll=2)
 
 
 def own_rows(pieces):
     bins, windows, lanes = pieces[0].shape
+    depth = windows * len(pieces)
+    together = max(1, MATMUL_DEPTH // depth)
     return pl.pallas_call(
         own_kernel,
         out_shape=jax.ShapeDtypeStruct(
-            (bins, lanes, windows * len(pieces)), jnp.bfloat16
+            (bins // together, together * lanes, together * depth), jnp.bfloat16
         ),
         in_specs=[VMEM] * len(pieces),
         out_specs=VMEM,
@@ -156,8 +169,9 @@
 
 def stack_kernel(scale, groups, codes_of, reach_ref, own, *refs):
     buffers, (out_hbm, partners, products, out, sems) = refs[:-5], refs[-5:]
-    bins, lanes, _ = own.shape
+    _, _, bins, _, lanes = partners.shape
     width = lanes // 2
+    together = bins // own.shape[0]
     offsets = out_hbm.shape[0]
     pitch = products.shape[0] // bins
     slots = len(groups)
@@ -181,27 +195,28 @@
 
     sign = jnp.where(lane < width, 1.0, -1.0)
 
-    def products_of(f):
+    def one_group(group, carry):
+        bins_here = [group * together + n for n in range(together)]
         right = jnp.concatenate(
             [
-                jnp.concatenate([partners[which, slot, f] for slot in range(slots)], axis=0)
+                jnp.concatenate(
+                    [partners[which, slot, f] for f in bins_here for slot in range(slots)], axis=0
+                )
                 for which in range(2)
             ],
             axis=1,
         )
-        both = jnp.dot(own[f], right, preferred_element_type=jnp.float32)
-        with_re = jnp.where(in_first, both[:width, :lanes], both[:width, lanes:])
-        with_im = jnp.where(in_first, both[width:, :lanes], both[width:, lanes:])
-        return with_re + sign * pltpu.roll(with_im, width, 1)
-
-    def one_group(group, carry):
-        results = [products_of(group * GROUP + n) for n in range(GROUP)]
-        for n, result in enumerate(results):
-            row = pl.multiple_of((group * GROUP + n) * pitch, 8)
-            products[pl.ds(row, width), :] = result
+        both = jnp.dot(own[group], right, preferred_element_type=jnp.float32)
+        for n, f in enumerate(bins_here):
+            re = both[2 * n * width : (2 * n + 1) * width]
+            im = both[(2 * n + 1) * width : (2 * n + 2) * width]
+            with_re = jnp.where(in_first, re[:, :lanes], re[:, lanes:])
+            with_im = jnp.where(in_first, im[:, :lanes], im[:, lanes:])
+            row = pl.multiple_of(f * pitch, 8)
+            products[pl.ds(row, width), :] = with_re + sign * pltpu.roll(with_im, width, 1)
         return carry
 
-    lax.fori_loop(0, bins // GROUP, one_group, 0, unroll=2)
+    lax.fori_loop(0, own.shape[0], one_group, 0, unroll=2)
 
     lane = lax.broadcasted_iota(jnp.int32, (offsets, lanes), 1)
     shift = (lane + offsets * width - lax.broadcasted_iota(jnp.int32, (offsets, lanes), 0)) % width
@@ -225,20 +240,33 @@
         pick = jnp.concatenate(
             [jnp.where(shift_re == at, 1.0, 0.0), jnp.where(shift_im == at, -1.0, 0.0)], axis=0
         ).astype(jnp.bfloat16)
-        x = products[pl.ds(i, F, stride=pitch), :].astype(jnp.bfloat16)
-        y = lax.dot_general(
-            pick, x, (((1,), (1,)), ((), ())), preferred_element_type=jnp.float32
-        )
-        inside = jnp.where(row_k < reach_ref[i], scale, 0.0)
-        return [y[part * offsets : (part + 1) * offsets] * inside for part in range(2)]
+        return pick, products[pl.ds(i, F, stride=pitch), :].astype(jnp.bfloat16)
 
     def one_block(block, carry):
-        for begin in range(0, CHANNEL_BLOCK, GROUP):
-            channels = [block * CHANNEL_BLOCK + begin + n for n in range(GROUP)]
-            results = [picked(i) for i in channels]
-            for i, result in zip(channels, results):
+        for begin in range(0, CHANNEL_BLOCK, 2):
+            channels = [block * CHANNEL_BLOCK + begin + n for n in range(2)]
+            (pick0, x0), (pick1, x1) = [picked(i) for i in channels]
+            none = jnp.zeros_like(pick0)
+            pick = jnp.concatenate(
+                [
+                    jnp.concatenate([pick0, none], axis=1),
+                    jnp.concatenate([none, pick1], axis=1),
+                ],
+                axis=0,
+            )
+            y = lax.dot_general(
+                pick,
+                jnp.concatenate([x0, x1], axis=1),
+                (((1,), (1,)), ((), ())),
+                preferred_element_type=jnp.float32,
+            )
+            for n, i in enumerate(channels):
+                inside = jnp.where(row_k < reach_ref[i], scale, 0.0)
                 for part in range(2):
-                    out[part, pl.ds(i, offsets, stride=pitch), :] = result[part]
+                    begin_row = (2 * n + part) * offsets
+                    out[part, pl.ds(i, offsets, stride=pitch), :] = (
+                        y[begin_row : begin_row + offsets] * inside
+                    )
         for copy in copies(block):
             copy.start()
         return carry
@@ -255,9 +283,8 @@
 
 
 def stacked(own, buffers, groups, codes_of, reach, offsets, windows):
-    bins, lanes, _ = own.shape
+    bins, chunk_windows, lanes = buffers[0].shape
     width = lanes // 2
-    chunk_windows = buffers[0].shape[-2]
     pitch = width + PITCH_PAD
     return pl.pallas_call(
         functools.partial(stack_kernel, 1.0 / math.sqrt(windows), groups, codes_of),

time: 85.9 us -> 87.4 us (1.017); the launches traced: 85.5 us -> 86 us
  waiting for transfers between devices: 42.7 us -> 40.3 us
  Pallas kernels: 16.2 us -> 18.1 us
  local copies, waits for them, and re-layouts: 1.05 us -> 2.09 us
    ppermute x11, waiting for transfers between devices: 27.7 us -> 25.3 us  [send(): return lax.ppermute(array, AXES, pairs)]
    pallas_call x1, Pallas kernels: 2.03 us -> 3.39 us  [own_rows(): pl.pallas_call(own_kernel, out_shape=jax.ShapeDtypeStruct((bins // togeth...]
    unnamed x6 -> x8, local copies, waits for them, and re-layouts: 1.05 us -> 2.09 us
  transfers between devices with their start and end apart: 14 -> 14, of which waited for: 9 -> 9; matrix products, arithmetic and copies ran while one was open for 0% -> 0% of each run, Pallas kernels for 3% -> 4%
where the time goes in v16:
time: 87.4 us; the launch traced here: 86 us
  waiting for transfers between devices  40.3 us (46%)
  starting transfers between devices  25.3 us (29%)
  Pallas kernels  18.1 us (21%)
  local copies, waits for them, and re-layouts  2.09 us (2%)
    ppermute x11, waiting for transfers between devices, send(): return lax.ppermute(array, AXES, pairs)  25.3 us
    ppermute x11, starting transfers between devices, send(): return lax.ppermute(array, AXES, pairs)  22.4 us
    ppermute x3, waiting for transfers between devices, on_device(): pieces.append(lax.ppermute(pieces[-1], 'win', ring))  15 us
    pallas_call x1, Pallas kernels, stacked(): pl.pallas_call(functools.partial(stack_kernel, 1.0 / math.sqrt(windows),...  10.3 us
    pallas_call x1, Pallas kernels, whitened_chunk(): pl.pallas_call(whiten_kernel, out_shape=jax.ShapeDtypeStruct((F, windows,...  4 us
    pallas_call x1, Pallas kernels, own_rows(): pl.pallas_call(own_kernel, out_shape=jax.ShapeDtypeStruct((bins // togeth...  3.39 us
    ppermute x3, starting transfers between devices, on_device(): pieces.append(lax.ppermute(pieces[-1], 'win', ring))  2.93 us
    unnamed x8, local copies, waits for them, and re-layouts  2.09 us
  transfers between devices with their start and end apart: 14, of which 9 were waited for; matrix products, arithmetic and copies ran while one was open for 0% of the time, Pallas kernels for 4%

profile of v16, /device:TPU:11, one launch (start us, length us, event | category | flops | bytes accessed | tf_op | source)
XLA Modules:
  0.0 86.0 jit_solution(13663869919598593328)
XLA Ops:
  0.0 4.0 %whiten.1.refs_0_ = bf16[128,16,128]{2,1,0:T(8,128)(2,1)} custom-call(bf16[256,512]{1,0:T(8,128)(2,1)} %constant.3.table_hbm, bf16[16,64,512]{2,1,0:T(8,128)(2,1)} %traces_hbm.1, s32[16,64]{1,0:T(8,128)} %valid_hbm.1), custom_call_target="tpu_custom_call" | custom-call | flops 268435456 | bytes 1048576 | tf_op jit(solution)/shard_map/whiten/pallas_call | solution.py:79
  4.0 1.3 %collective-permute-start = (bf16[128,16,128]{2,1,0:T(8,128)(2,1)}, bf16[128,16,128]{2,1,0:T(8,128)(2,1)S(1)}, u32[]{:S(2)}, u32[]{:S(2)}) collective-permute-start(bf16[128,16,128]{2,1,0:T(8,128)(2,1)} %whiten.1.refs_0_), channel_id=1, source_target_pairs={{0,1},{1,2},{2,3},{3,0},{4,5},{5,6},{6,7},{7,4},{8,9},{9,10},{10,1... | collective-permute-start | bytes 1572872 | tf_op jit(solution)/shard_map/ppermute | solution.py:433
  5.4 2.2 %collective-permute-start.3 = (bf16[128,16,128]{2,1,0:T(8,128)(2,1)}, bf16[128,16,128]{2,1,0:T(8,128)(2,1)S(1)}, u32[]{:S(2)}, u32[]{:S(2)}) collective-permute-start(bf16[128,16,128]{2,1,0:T(8,128)(2,1)} %whiten.1.refs_0_), channel_id=1, source_target_pairs={{0,8},{8,0},{16,24},{24,16},{1,17},{5,13},{13,5},{17,1},{21,29},{2... | collective-permute-start | bytes 1572872 | tf_op jit(solution)/shard_map/ppermute | solution.py:307
  7.5 9.5 %collective-permute-done.refs_1_.refs_0_.refs_3_ = bf16[128,16,128]{2,1,0:T(8,128)(2,1)S(1)} collective-permute-done((bf16[128,16,128]{2,1,0:T(8,128)(2,1)}, bf16[128,16,128]{2,1,0:T(8,128)(2,1)S(1)}, u32[]{:S(2)}, u32[]{:S(2)}) %collective-permute-start) | collective-permute-done | bytes 524320 | tf_op jit(solution)/shard_map/ppermute | solution.py:433
  17.1 1.3 %collective-permute-start.1 = (bf16[128,16,128]{2,1,0:T(8,128)(2,1)S(1)}, bf16[128,16,128]{2,1,0:T(8,128)(2,1)S(1)}, u32[]{:S(2)}, u32[]{:S(2)}) collective-permute-start(bf16[128,16,128]{2,1,0:T(8,128)(2,1)S(1)} %collective-permute-done.refs_1_.refs_0_.refs_3_), channel_id=1, source_target_pairs={{0,1},{1,2},{2,3},{3,0},{4,5},{5,6},{6,7},{7,4},{8,9},{9,10},{10,1... | collective-permute-start | bytes 1572872 | tf_op jit(solution)/shard_map/ppermute | solution.py:433
  18.4 0.0 collective-permute-done.3.refs_1_
  18.4 1.0 %copy-done = bf16[128,16,128]{2,1,0:T(8,128)(2,1)S(1)} copy-done((bf16[128,16,128]{2,1,0:T(8,128)(2,1)S(1)}, bf16[128,16,128]{2,1,0:T(8,128)(2,1)}, u32[]{:S(2)}) %copy-start) | copy-done | bytes 524312
  19.4 3.3 %collective-permute-start.4 = (bf16[128,16,128]{2,1,0:T(8,128)(2,1)S(1)}, bf16[128,16,128]{2,1,0:T(8,128)(2,1)S(1)}, u32[]{:S(2)}, u32[]{:S(2)}) collective-permute-start(bf16[128,16,128]{2,1,0:T(8,128)(2,1)S(1)} %bitcast.6), channel_id=1, source_target_pairs={{8,24},{24,8},{1,9},{9,1},{13,29},{17,25},{25,17},{29,13},{2,10},{... | collective-permute-start | bytes 1572872 | tf_op jit(solution)/shard_map/ppermute | solution.py:307
  22.7 1.9 %collective-permute-start.5 = (bf16[128,16,128]{2,1,0:T(8,128)(2,1)S(1)}, bf16[128,16,128]{2,1,0:T(8,128)(2,1)S(1)}, u32[]{:S(2)}, u32[]{:S(2)}) collective-permute-start(bf16[128,16,128]{2,1,0:T(8,128)(2,1)S(1)} %collective-permute-done.refs_1_.refs_0_.refs_3_), channel_id=1, source_target_pairs={{0,8},{8,0},{16,24},{24,16},{1,17},{5,13},{13,5},{17,1},{21,29},{2... | collective-permute-start | bytes 1572872 | tf_op jit(solution)/shard_map/ppermute | solution.py:307
  24.7 5.3 %collective-permute-done.1.refs_2_.refs_0_.refs_6_ = bf16[128,16,128]{2,1,0:T(8,128)(2,1)S(1)} collective-permute-done((bf16[128,16,128]{2,1,0:T(8,128)(2,1)S(1)}, bf16[128,16,128]{2,1,0:T(8,128)(2,1)S(1)}, u32[]{:S(2)}, u32[]{:S(2)}) %collective-permute-start.1) | collective-permute-done | bytes 524320 | tf_op jit(solution)/shard_map/ppermute | solution.py:433
  29.9 0.3 collective-permute-start.2
  30.2 7.5 %collective-permute-done.5.refs_1_.refs_4_ = bf16[128,16,128]{2,1,0:T(8,128)(2,1)S(1)} collective-permute-done((bf16[128,16,128]{2,1,0:T(8,128)(2,1)S(1)}, bf16[128,16,128]{2,1,0:T(8,128)(2,1)S(1)}, u32[]{:S(2)}, u32[]{:S(2)}) %collective-permute-start.5) | collective-permute-done | bytes 524320 | tf_op jit(solution)/shard_map/ppermute | solution.py:307
  37.7 2.8 %collective-permute-start.7 = (bf16[128,16,128]{2,1,0:T(8,128)(2,1)S(1)}, bf16[128,16,128]{2,1,0:T(8,128)(2,1)S(1)}, u32[]{:S(2)}, u32[]{:S(2)}) collective-permute-start(bf16[128,16,128]{2,1,0:T(8,128)(2,1)S(1)} %bitcast.7), channel_id=1, source_target_pairs={{8,24},{24,8},{1,9},{9,1},{13,29},{17,25},{25,17},{29,13},{2,10},{... | collective-permute-start | bytes 1572872 | tf_op jit(solution)/shard_map/ppermute | solution.py:307
  40.6 1.9 %collective-permute-start.8 = (bf16[128,16,128]{2,1,0:T(8,128)(2,1)S(1)}, bf16[128,16,128]{2,1,0:T(8,128)(2,1)S(1)}, u32[]{:S(2)}, u32[]{:S(2)}) collective-permute-start(bf16[128,16,128]{2,1,0:T(8,128)(2,1)S(1)} %collective-permute-done.1.refs_2_.refs_0_.refs_6_), channel_id=1, source_target_pairs={{0,8},{8,0},{16,24},{24,16},{1,17},{5,13},{13,5},{17,1},{21,29},{2... | collective-permute-start | bytes 1572872 | tf_op jit(solution)/shard_map/ppermute | solution.py:307
  42.5 0.2 collective-permute-done.2.refs_3_.refs_0_.refs_4_.refs_9_
  42.7 3.1 %collective-permute-start.6 = (bf16[128,16,128]{2,1,0:T(8,128)(2,1)S(1)}, bf16[128,16,128]{2,1,0:T(8,128)(2,1)S(1)}, u32[]{:S(2)}, u32[]{:S(2)}) collective-permute-start(bf16[128,16,128]{2,1,0:T(8,128)(2,1)S(1)} %collective-permute-done.2.refs_3_.refs_0_.refs_4_.refs_9_), channel_id=1, source_target_pairs={{0,8},{8,0},{16,24},{24,16},{1,17},{5,13},{13,5},{17,1},{21,29},{2... | collective-permute-start | bytes 1572872 | tf_op jit(solution)/shard_map/ppermute | solution.py:307
  45.9 2.1 %collective-permute-done.7.refs_5_ = bf16[128,16,128]{2,1,0:T(8,128)(2,1)S(1)} collective-permute-done((bf16[128,16,128]{2,1,0:T(8,128)(2,1)S(1)}, bf16[128,16,128]{2,1,0:T(8,128)(2,1)S(1)}, u32[]{:S(2)}, u32[]{:S(2)}) %collective-permute-start.7) | collective-permute-done | bytes 524320 | tf_op jit(solution)/shard_map/ppermute | solution.py:307
  48.0 5.3 %collective-permute-done.8.refs_1_.refs_3_.refs_7_ = bf16[128,16,128]{2,1,0:T(8,128)(2,1)S(1)} collective-permute-done((bf16[128,16,128]{2,1,0:T(8,128)(2,1)S(1)}, bf16[128,16,128]{2,1,0:T(8,128)(2,1)S(1)}, u32[]{:S(2)}, u32[]{:S(2)}) %collective-permute-start.8) | collective-permute-done | bytes 524320 | tf_op jit(solution)/shard_map/ppermute | solution.py:307
  53.3 3.8 %collective-permute-start.9 = (bf16[128,16,128]{2,1,0:T(8,128)(2,1)S(1)}, bf16[128,16,128]{2,1,0:T(8,128)(2,1)S(1)}, u32[]{:S(2)}, u32[]{:S(2)}) collective-permute-start(bf16[128,16,128]{2,1,0:T(8,128)(2,1)S(1)} %bitcast.4), channel_id=1, source_target_pairs={{8,24},{24,8},{1,9},{9,1},{13,29},{17,25},{25,17},{29,13},{2,10},{... | collective-permute-start | bytes 1572872 | tf_op jit(solution)/shard_map/ppermute | solution.py:307
  57.2 0.0 copy-start.1
  57.2 1.0 %copy-done.1 = bf16[128,16,128]{2,1,0:T(8,128)(2,1)S(1)} copy-done((bf16[128,16,128]{2,1,0:T(8,128)(2,1)S(1)}, bf16[128,16,128]{2,1,0:T(8,128)(2,1)}, u32[]{:S(2)}) %copy-start.1) | copy-done | bytes 524312
  58.2 3.4 %own_rows.1.own = bf16[32,512,256]{2,1,0:T(8,128)(2,1)S(1)} custom-call(bf16[128,16,128]{2,1,0:T(8,128)(2,1)S(1)} %copy-done.1, bf16[128,16,128]{2,1,0:T(8,128)(2,1)S(1)} %collective-permute-done.refs_1_.refs_0_.refs_3_, bf16[128,16,128]{2,1,0:T(8,128)(2,1)S(1)} %collective-permute-done.1.refs_2_.refs_0_.refs_6_, ...), custom_call_target="tpu_custom_call" | custom-call | flops 1 | bytes 1 | tf_op jit(solution)/shard_map/own_rows/pallas_call | solution.py:157
  61.6 0.5 collective-permute-done.6.refs_1_.refs_5_.refs_10_
  62.2 0.7 collective-permute-start.12
  62.9 2.4 %collective-permute-start.10 = (bf16[128,16,128]{2,1,0:T(8,128)(2,1)S(1)}, bf16[128,16,128]{2,1,0:T(8,128)(2,1)S(1)}, u32[]{:S(2)}, u32[]{:S(2)}) collective-permute-start(bf16[128,16,128]{2,1,0:T(8,128)(2,1)S(1)} %bitcast.5), channel_id=1, source_target_pairs={{8,24},{24,8},{1,9},{9,1},{13,29},{17,25},{25,17},{29,13},{2,10},{... | collective-permute-start | bytes 1572872 | tf_op jit(solution)/shard_map/ppermute | solution.py:307
  65.4 0.1 choose.10
  65.5 0.1 collective-permute-start.11
  65.6 7.2 %collective-permute-done.10.refs_6_.refs_11_ = bf16[128,16,128]{2,1,0:T(8,128)(2,1)S(1)} collective-permute-done((bf16[128,16,128]{2,1,0:T(8,128)(2,1)S(1)}, bf16[128,16,128]{2,1,0:T(8,128)(2,1)S(1)}, u32[]{:S(2)}, u32[]{:S(2)}) %collective-permute-start.10) | collective-permute-done | bytes 524320 | tf_op jit(solution)/shard_map/ppermute | solution.py:307
  72.8 0.1 choose.11
  72.9 0.1 collective-permute-start.13
  73.0 2.6 %collective-permute-done.13.refs_13_ = bf16[2,128,16,128]{3,2,1,0:T(8,128)(2,1)S(1)} collective-permute-done((bf16[2,128,16,128]{3,2,1,0:T(8,128)(2,1)S(1)}, bf16[2,128,16,128]{3,2,1,0:T(8,128)(2,1)S(1)}, u32[]{:S(2)}, u32[]{:S(2)}) %collective-permute-start.13) | collective-permute-done | bytes 1048608 | tf_op jit(solution)/shard_map/ppermute | solution.py:307
  75.6 10.3 %stack.1 = f32[64,64,256]{2,1,0:T(8,128)} custom-call(s32[64]{0:T(128)S(1)} %copy-done.3, bf16[32,512,256]{2,1,0:T(8,128)(2,1)S(1)} %own_rows.1.own, bf16[128,16,128]{2,1,0:T(8,128)(2,1)S(1)} %copy-done.2, bf16[128,16,128]{2,1,0:T(8,128)(2,1)S(1)} %collective-permute-done.3.refs_1_, bf16[128,16,128]{2,1,0:T(8,128)(2,1)S(1)} %collective-permute-done.4.refs_2_, ...), custom_call_target="tpu_custom_call" | custom-call | flops 1 | bytes 1 | tf_op jit(solution)/shard_map/stack/pallas_call | solution.py:289
  (13 shorter events, 0.2 us)
Async XLA Ops:
  4.0 13.1 %collective-permute-start = (bf16[128,16,128]{2,1,0:T(8,128)(2,1)}, bf16[128,16,128]{2,1,0:T(8,128)(2,1)S(1)}, u32[]{:S(2)}, u32[]{:S(2)}) collective-permute-start(bf16[128,16,128]{2,1,0:T(8,128)(2,1)} %whiten.1.refs_0_), channel_id=1, source_target_pairs={{0,1},{1,2},{2,3},{3,0},{4,5},{5,6},{6,7},{7,4},{8,9},{9,10},{10,1... | collective-permute-start | bytes 1572872 | tf_op jit(solution)/shard_map/ppermute | solution.py:433
  5.4 13.0 %collective-permute-start.3 = (bf16[128,16,128]{2,1,0:T(8,128)(2,1)}, bf16[128,16,128]{2,1,0:T(8,128)(2,1)S(1)}, u32[]{:S(2)}, u32[]{:S(2)}) collective-permute-start(bf16[128,16,128]{2,1,0:T(8,128)(2,1)} %whiten.1.refs_0_), channel_id=1, source_target_pairs={{0,8},{8,0},{16,24},{24,16},{1,17},{5,13},{13,5},{17,1},{21,29},{2... | collective-permute-start | bytes 1572872 | tf_op jit(solution)/shard_map/ppermute | solution.py:307
  17.1 12.9 %collective-permute-start.1 = (bf16[128,16,128]{2,1,0:T(8,128)(2,1)S(1)}, bf16[128,16,128]{2,1,0:T(8,128)(2,1)S(1)}, u32[]{:S(2)}, u32[]{:S(2)}) collective-permute-start(bf16[128,16,128]{2,1,0:T(8,128)(2,1)S(1)} %collective-permute-done.refs_1_.refs_0_.refs_3_), channel_id=1, source_target_pairs={{0,1},{1,2},{2,3},{3,0},{4,5},{5,6},{6,7},{7,4},{8,9},{9,10},{10,1... | collective-permute-start | bytes 1572872 | tf_op jit(solution)/shard_map/ppermute | solution.py:433
  18.4 1.0 %copy-start = (bf16[128,16,128]{2,1,0:T(8,128)(2,1)S(1)}, bf16[128,16,128]{2,1,0:T(8,128)(2,1)}, u32[]{:S(2)}) copy-start(bf16[128,16,128]{2,1,0:T(8,128)(2,1)} %whiten.1.refs_0_) | copy-start | bytes 1572868
  19.4 46.0 %copy-start.2 = (bf16[128,16,128]{2,1,0:T(8,128)(2,1)S(1)}, bf16[128,16,128]{2,1,0:T(8,128)(2,1)}, u32[]{:S(2)}) copy-start(bf16[128,16,128]{2,1,0:T(8,128)(2,1)} %whiten.1.refs_0_) | copy-start | bytes 1572868
  19.4 10.8 %collective-permute-start.4 = (bf16[128,16,128]{2,1,0:T(8,128)(2,1)S(1)}, bf16[128,16,128]{2,1,0:T(8,128)(2,1)S(1)}, u32[]{:S(2)}, u32[]{:S(2)}) collective-permute-start(bf16[128,16,128]{2,1,0:T(8,128)(2,1)S(1)} %bitcast.6), channel_id=1, source_target_pairs={{8,24},{24,8},{1,9},{9,1},{13,29},{17,25},{25,17},{29,13},{2,10},{... | collective-permute-start | bytes 1572872 | tf_op jit(solution)/shard_map/ppermute | solution.py:307
  22.7 15.0 %collective-permute-start.5 = (bf16[128,16,128]{2,1,0:T(8,128)(2,1)S(1)}, bf16[128,16,128]{2,1,0:T(8,128)(2,1)S(1)}, u32[]{:S(2)}, u32[]{:S(2)}) collective-permute-start(bf16[128,16,128]{2,1,0:T(8,128)(2,1)S(1)} %collective-permute-done.refs_1_.refs_0_.refs_3_), channel_id=1, source_target_pairs={{0,8},{8,0},{16,24},{24,16},{1,17},{5,13},{13,5},{17,1},{21,29},{2... | collective-permute-start | bytes 1572872 | tf_op jit(solution)/shard_map/ppermute | solution.py:307
  29.9 12.8 %collective-permute-start.2 = (bf16[128,16,128]{2,1,0:T(8,128)(2,1)S(1)}, bf16[128,16,128]{2,1,0:T(8,128)(2,1)S(1)}, u32[]{:S(2)}, u32[]{:S(2)}) collective-permute-start(bf16[128,16,128]{2,1,0:T(8,128)(2,1)S(1)} %collective-permute-done.1.refs_2_.refs_0_.refs_6_), channel_id=1, source_target_pairs={{0,1},{1,2},{2,3},{3,0},{4,5},{5,6},{6,7},{7,4},{8,9},{9,10},{10,1... | collective-permute-start | bytes 1572872 | tf_op jit(solution)/shard_map/ppermute | solution.py:433
  37.7 10.2 %collective-permute-start.7 = (bf16[128,16,128]{2,1,0:T(8,128)(2,1)S(1)}, bf16[128,16,128]{2,1,0:T(8,128)(2,1)S(1)}, u32[]{:S(2)}, u32[]{:S(2)}) collective-permute-start(bf16[128,16,128]{2,1,0:T(8,128)(2,1)S(1)} %bitcast.7), channel_id=1, source_target_pairs={{8,24},{24,8},{1,9},{9,1},{13,29},{17,25},{25,17},{29,13},{2,10},{... | collective-permute-start | bytes 1572872 | tf_op jit(solution)/shard_map/ppermute | solution.py:307
  40.6 12.7 %collective-permute-start.8 = (bf16[128,16,128]{2,1,0:T(8,128)(2,1)S(1)}, bf16[128,16,128]{2,1,0:T(8,128)(2,1)S(1)}, u32[]{:S(2)}, u32[]{:S(2)}) collective-permute-start(bf16[128,16,128]{2,1,0:T(8,128)(2,1)S(1)} %collective-permute-done.1.refs_2_.refs_0_.refs_6_), channel_id=1, source_target_pairs={{0,8},{8,0},{16,24},{24,16},{1,17},{5,13},{13,5},{17,1},{21,29},{2... | collective-permute-start | bytes 1572872 | tf_op jit(solution)/shard_map/ppermute | solution.py:307
  42.7 19.4 %collective-permute-start.6 = (bf16[128,16,128]{2,1,0:T(8,128)(2,1)S(1)}, bf16[128,16,128]{2,1,0:T(8,128)(2,1)S(1)}, u32[]{:S(2)}, u32[]{:S(2)}) collective-permute-start(bf16[128,16,128]{2,1,0:T(8,128)(2,1)S(1)} %collective-permute-done.2.refs_3_.refs_0_.refs_4_.refs_9_), channel_id=1, source_target_pairs={{0,8},{8,0},{16,24},{24,16},{1,17},{5,13},{13,5},{17,1},{21,29},{2... | collective-permute-start | bytes 1572872 | tf_op jit(solution)/shard_map/ppermute | solution.py:307
  53.3 12.2 %collective-permute-start.9 = (bf16[128,16,128]{2,1,0:T(8,128)(2,1)S(1)}, bf16[128,16,128]{2,1,0:T(8,128)(2,1)S(1)}, u32[]{:S(2)}, u32[]{:S(2)}) collective-permute-start(bf16[128,16,128]{2,1,0:T(8,128)(2,1)S(1)} %bitcast.4), channel_id=1, source_target_pairs={{8,24},{24,8},{1,9},{9,1},{13,29},{17,25},{25,17},{29,13},{2,10},{... | collective-permute-start | bytes 1572872 | tf_op jit(solution)/shard_map/ppermute | solution.py:307
  57.2 1.0 %copy-start.1 = (bf16[128,16,128]{2,1,0:T(8,128)(2,1)S(1)}, bf16[128,16,128]{2,1,0:T(8,128)(2,1)}, u32[]{:S(2)}) copy-start(bf16[128,16,128]{2,1,0:T(8,128)(2,1)} %whiten.1.refs_0_) | copy-start | bytes 1572868
  58.2 17.4 %copy-start.3 = (s32[64]{0:T(128)S(1)}, s32[64]{0:T(128)}, u32[]{:S(2)}) copy-start(s32[64]{0:T(128)} %reach_ref.1) | copy-start | bytes 772
  62.2 3.4 %collective-permute-start.12 = (bf16[128,16,128]{2,1,0:T(8,128)(2,1)S(1)}, bf16[128,16,128]{2,1,0:T(8,128)(2,1)S(1)}, u32[]{:S(2)}, u32[]{:S(2)}) collective-permute-start(bf16[128,16,128]{2,1,0:T(8,128)(2,1)S(1)} %collective-permute-done.2.refs_3_.refs_0_.refs_4_.refs_9_), channel_id=1, source_target_pairs={{3,19},{11,27},{19,3},{27,11}} | collective-permute-start | bytes 1572872 | tf_op jit(solution)/shard_map/ppermute | solution.py:307
  62.9 9.9 %collective-permute-start.10 = (bf16[128,16,128]{2,1,0:T(8,128)(2,1)S(1)}, bf16[128,16,128]{2,1,0:T(8,128)(2,1)S(1)}, u32[]{:S(2)}, u32[]{:S(2)}) collective-permute-start(bf16[128,16,128]{2,1,0:T(8,128)(2,1)S(1)} %bitcast.5), channel_id=1, source_target_pairs={{8,24},{24,8},{1,9},{9,1},{13,29},{17,25},{25,17},{29,13},{2,10},{... | collective-permute-start | bytes 1572872 | tf_op jit(solution)/shard_map/ppermute | solution.py:307
  65.5 7.5 %collective-permute-start.11 = (bf16[2,128,16,128]{3,2,1,0:T(8,128)(2,1)S(1)}, bf16[2,128,16,128]{3,2,1,0:T(8,128)(2,1)S(1)}, u32[]{:S(2)}, u32[]{:S(2)}) collective-permute-start(bf16[2,128,16,128]{3,2,1,0:T(8,128)(2,1)S(1)} %choose.10), channel_id=1, source_target_pairs={{0,4},{4,0},{8,12},{12,8},{16,20},{20,16},{24,28},{28,24},{1,5},{5... | collective-permute-start | bytes 3145736 | tf_op jit(solution)/shard_map/ppermute | solution.py:307
  72.9 2.7 %collective-permute-start.13 = (bf16[2,128,16,128]{3,2,1,0:T(8,128)(2,1)S(1)}, bf16[2,128,16,128]{3,2,1,0:T(8,128)(2,1)S(1)}, u32[]{:S(2)}, u32[]{:S(2)}) collective-permute-start(bf16[2,128,16,128]{3,2,1,0:T(8,128)(2,1)S(1)} %choose.11), channel_id=1, source_target_pairs={{0,4},{4,0},{8,12},{12,8},{16,20},{20,16},{24,28},{28,24},{1,5},{5... | collective-permute-start | bytes 3145736 | tf_op jit(solution)/shard_map/ppermute | solution.py:307

commit v17 on v14

--- a/solution.py
+++ b/solution.py
@@ -15,12 +15,10 @@
 AXES = ("chan", "win")
 CHANNEL_BLOCK = 8
 GROUP = 4
-WHITEN_BLOCKS = 4
 PITCH_PAD = 8
 MIB = 1024 * 1024
 VMEM = pl.BlockSpec(memory_space=pltpu.VMEM)
 FEW_MIB = pltpu.CompilerParams(vmem_limit_bytes=4 * MIB)
-WHOLE_VMEM = pltpu.CompilerParams(vmem_limit_bytes=62 * MIB)
 SMEM = pl.BlockSpec(memory_space=pltpu.SMEM)
 SMALL = pl.CostEstimate(flops=1, bytes_accessed=1, transcendentals=0)
 ANY = pl.BlockSpec(memory_space=pl.ANY)
@@ -35,25 +33,9 @@
     return jnp.asarray(rows.astype(np.float32)).astype(jnp.bfloat16)
 
 
-def whiten_kernel(table_hbm, traces_hbm, valid_hbm, out_ref, table, traces, valid, rows, sems):
+def whiten_kernel(table, traces, valid, out_ref, rows):
     windows, width, samples = traces.shape
-    block = windows // WHITEN_BLOCKS if windows % (2 * WHITEN_BLOCKS) == 0 else windows
-    copies = [
-        pltpu.make_async_copy(table_hbm, table, sems.at[0]),
-        pltpu.make_async_copy(valid_hbm, valid, sems.at[1]),
-    ]
-    for n in range(windows // block):
-        part = pl.ds(n * block, block)
-        copies.append(
-            pltpu.make_async_copy(traces_hbm.at[part], traces.at[part], sems.at[2 + n])
-        )
-    for copy in copies:
-        copy.start()
-    copies[0].wait()
-    copies[1].wait()
     for w in range(0, windows, 2):
-        if w % block == 0:
-            copies[2 + w // block].wait()
         spectra = lax.dot_general(
             table[...],
             traces[w : w + 2].reshape(2 * width, samples),
@@ -79,19 +61,11 @@
     return pl.pallas_call(
         whiten_kernel,
         out_shape=jax.ShapeDtypeStruct((F, windows, 2 * width), jnp.bfloat16),
-        in_specs=[ANY] * 3,
+        in_specs=[VMEM] * 3,
         out_specs=VMEM,
-        scratch_shapes=[
-            pltpu.VMEM((2 * F, samples), jnp.bfloat16),
-            pltpu.VMEM(traces.shape, traces.dtype),
-            pltpu.VMEM(valid.shape, valid.dtype),
-            pltpu.VMEM((F * windows, 2 * width), jnp.float32),
-            pltpu.SemaphoreType.DMA((2 + WHITEN_BLOCKS,)),
-        ],
-        compiler_params=WHOLE_VMEM,
-        cost_estimate=pl.CostEstimate(
-            flops=4 * F * traces.size, bytes_accessed=2 * traces.size, transcendentals=0
-        ),
+        scratch_shapes=[pltpu.VMEM((F * windows, 2 * width), jnp.float32)],
+        compiler_params=FEW_MIB,
+        cost_estimate=SMALL,
         name="whiten",
     )(make_table(samples), traces, valid)
 

time: 85.9 us -> 84.7 us (0.986)
  Pallas kernels: 16.2 us -> 13.5 us
  local copies, waits for them, and re-layouts: 1.05 us -> 2.88 us
    pallas_call x1, Pallas kernels: 4 us -> 1.25 us  [whitened_chunk(): pl.pallas_call(whiten_kernel, out_shape=jax.ShapeDtypeStruct((F, windows,...]
    ppermute x3, waiting for transfers between devices: 15 us -> 17.2 us  [on_device(): pieces.append(lax.ppermute(pieces[-1], 'win', ring))]
    ppermute x11, waiting for transfers between devices: 27.7 us -> 25.7 us  [send(): return lax.ppermute(array, AXES, pairs)]
    unnamed x6 -> x8, local copies, waits for them, and re-layouts: 1.05 us -> 2.88 us
where the time goes in v17:
time: 84.7 us; the launch traced here: 84.3 us
  waiting for transfers between devices  42.9 us (51%)
  starting transfers between devices  24.8 us (29%)
  Pallas kernels  13.5 us (16%)
  local copies, waits for them, and re-layouts  2.88 us (3%)
    ppermute x11, waiting for transfers between devices, send(): return lax.ppermute(array, AXES, pairs)  25.7 us
    ppermute x11, starting transfers between devices, send(): return lax.ppermute(array, AXES, pairs)  21.9 us
    ppermute x3, waiting for transfers between devices, on_device(): pieces.append(lax.ppermute(pieces[-1], 'win', ring))  17.2 us
    pallas_call x1, Pallas kernels, stacked(): pl.pallas_call(functools.partial(stack_kernel, 1.0 / math.sqrt(windows),...  9.92 us
    ppermute x3, starting transfers between devices, on_device(): pieces.append(lax.ppermute(pieces[-1], 'win', ring))  2.94 us
    unnamed x8, local copies, waits for them, and re-layouts  2.88 us
    pallas_call x1, Pallas kernels, own_rows(): pl.pallas_call(own_kernel, out_shape=jax.ShapeDtypeStruct((bins, lanes, w...  2.03 us
  transfers between devices with their start and end apart: 14, of which 9 were waited for; matrix products, arithmetic and copies ran while one was open for 0% of the time, Pallas kernels for 3%

profile of v17, /device:TPU:11, one launch (start us, length us, event | category | flops | bytes accessed | tf_op | source)
XLA Modules:
  0.0 84.3 jit_solution(5542736651554595106)
XLA Ops:
  0.0 1.2 %copy-done = bf16[16,64,512]{2,1,0:T(8,128)(2,1)S(1)} copy-done((bf16[16,64,512]{2,1,0:T(8,128)(2,1)S(1)}, bf16[16,64,512]{2,1,0:T(8,128)(2,1)}, u32[]{:S(2)}) %copy-start) | copy-done | bytes 1048600
  1.2 0.9 %copy-done.1 = bf16[256,512]{1,0:T(8,128)(2,1)S(1)} copy-done((bf16[256,512]{1,0:T(8,128)(2,1)S(1)}, bf16[256,512]{1,0:T(8,128)(2,1)}, u32[]{:S(2)}) %copy-start.1) | copy-done | bytes 262168
  2.2 0.7 copy-done.2
  2.9 1.2 %whiten.1.refs_0_ = bf16[128,16,128]{2,1,0:T(8,128)(2,1)S(1)} custom-call(bf16[256,512]{1,0:T(8,128)(2,1)S(1)} %copy-done.1, bf16[16,64,512]{2,1,0:T(8,128)(2,1)S(1)} %copy-done, s32[16,64]{1,0:T(8,128)S(1)} %copy-done.2), custom_call_target="tpu_custom_call" | custom-call | flops 1 | bytes 1 | tf_op jit(solution)/shard_map/whiten/pallas_call | solution.py:61
  4.1 1.4 %collective-permute-start = (bf16[128,16,128]{2,1,0:T(8,128)(2,1)S(1)}, bf16[128,16,128]{2,1,0:T(8,128)(2,1)S(1)}, u32[]{:S(2)}, u32[]{:S(2)}) collective-permute-start(bf16[128,16,128]{2,1,0:T(8,128)(2,1)S(1)} %whiten.1.refs_0_), channel_id=1, source_target_pairs={{0,1},{1,2},{2,3},{3,0},{4,5},{5,6},{6,7},{7,4},{8,9},{9,10},{10,1... | collective-permute-start | bytes 1572872 | tf_op jit(solution)/shard_map/ppermute | solution.py:380
  5.5 2.1 %collective-permute-start.3 = (bf16[128,16,128]{2,1,0:T(8,128)(2,1)S(1)}, bf16[128,16,128]{2,1,0:T(8,128)(2,1)S(1)}, u32[]{:S(2)}, u32[]{:S(2)}) collective-permute-start(bf16[128,16,128]{2,1,0:T(8,128)(2,1)S(1)} %whiten.1.refs_0_), channel_id=1, source_target_pairs={{0,8},{8,0},{16,24},{24,16},{1,17},{5,13},{13,5},{17,1},{21,29},{2... | collective-permute-start | bytes 1572872 | tf_op jit(solution)/shard_map/ppermute | solution.py:254
  7.6 9.3 %collective-permute-done.refs_1_.refs_0_.refs_3_ = bf16[128,16,128]{2,1,0:T(8,128)(2,1)S(1)} collective-permute-done((bf16[128,16,128]{2,1,0:T(8,128)(2,1)S(1)}, bf16[128,16,128]{2,1,0:T(8,128)(2,1)S(1)}, u32[]{:S(2)}, u32[]{:S(2)}) %collective-permute-start) | collective-permute-done | bytes 524320 | tf_op jit(solution)/shard_map/ppermute | solution.py:380
  17.0 1.3 %collective-permute-start.1 = (bf16[128,16,128]{2,1,0:T(8,128)(2,1)S(1)}, bf16[128,16,128]{2,1,0:T(8,128)(2,1)S(1)}, u32[]{:S(2)}, u32[]{:S(2)}) collective-permute-start(bf16[128,16,128]{2,1,0:T(8,128)(2,1)S(1)} %collective-permute-done.refs_1_.refs_0_.refs_3_), channel_id=1, source_target_pairs={{0,1},{1,2},{2,3},{3,0},{4,5},{5,6},{6,7},{7,4},{8,9},{9,10},{10,1... | collective-permute-start | bytes 1572872 | tf_op jit(solution)/shard_map/ppermute | solution.py:380
  18.3 3.1 %collective-permute-start.4 = (bf16[128,16,128]{2,1,0:T(8,128)(2,1)S(1)}, bf16[128,16,128]{2,1,0:T(8,128)(2,1)S(1)}, u32[]{:S(2)}, u32[]{:S(2)}) collective-permute-start(bf16[128,16,128]{2,1,0:T(8,128)(2,1)S(1)} %bitcast.6), channel_id=1, source_target_pairs={{8,24},{24,8},{1,9},{9,1},{13,29},{17,25},{25,17},{29,13},{2,10},{... | collective-permute-start | bytes 1572872 | tf_op jit(solution)/shard_map/ppermute | solution.py:254
  21.5 1.9 %collective-permute-start.5 = (bf16[128,16,128]{2,1,0:T(8,128)(2,1)S(1)}, bf16[128,16,128]{2,1,0:T(8,128)(2,1)S(1)}, u32[]{:S(2)}, u32[]{:S(2)}) collective-permute-start(bf16[128,16,128]{2,1,0:T(8,128)(2,1)S(1)} %collective-permute-done.refs_1_.refs_0_.refs_3_), channel_id=1, source_target_pairs={{0,8},{8,0},{16,24},{24,16},{1,17},{5,13},{13,5},{17,1},{21,29},{2... | collective-permute-start | bytes 1572872 | tf_op jit(solution)/shard_map/ppermute | solution.py:254
  23.4 6.4 %collective-permute-done.1.refs_2_.refs_0_.refs_6_ = bf16[128,16,128]{2,1,0:T(8,128)(2,1)S(1)} collective-permute-done((bf16[128,16,128]{2,1,0:T(8,128)(2,1)S(1)}, bf16[128,16,128]{2,1,0:T(8,128)(2,1)S(1)}, u32[]{:S(2)}, u32[]{:S(2)}) %collective-permute-start.1) | collective-permute-done | bytes 524320 | tf_op jit(solution)/shard_map/ppermute | solution.py:380
  29.8 0.3 collective-permute-start.2
  30.1 6.0 %collective-permute-done.5.refs_1_.refs_4_ = bf16[128,16,128]{2,1,0:T(8,128)(2,1)S(1)} collective-permute-done((bf16[128,16,128]{2,1,0:T(8,128)(2,1)S(1)}, bf16[128,16,128]{2,1,0:T(8,128)(2,1)S(1)}, u32[]{:S(2)}, u32[]{:S(2)}) %collective-permute-start.5) | collective-permute-done | bytes 524320 | tf_op jit(solution)/shard_map/ppermute | solution.py:254
  36.2 3.1 %collective-permute-start.7 = (bf16[128,16,128]{2,1,0:T(8,128)(2,1)S(1)}, bf16[128,16,128]{2,1,0:T(8,128)(2,1)S(1)}, u32[]{:S(2)}, u32[]{:S(2)}) collective-permute-start(bf16[128,16,128]{2,1,0:T(8,128)(2,1)S(1)} %bitcast.7), channel_id=1, source_target_pairs={{8,24},{24,8},{1,9},{9,1},{13,29},{17,25},{25,17},{29,13},{2,10},{... | collective-permute-start | bytes 1572872 | tf_op jit(solution)/shard_map/ppermute | solution.py:254
  39.3 1.9 %collective-permute-start.8 = (bf16[128,16,128]{2,1,0:T(8,128)(2,1)S(1)}, bf16[128,16,128]{2,1,0:T(8,128)(2,1)S(1)}, u32[]{:S(2)}, u32[]{:S(2)}) collective-permute-start(bf16[128,16,128]{2,1,0:T(8,128)(2,1)S(1)} %collective-permute-done.1.refs_2_.refs_0_.refs_6_), channel_id=1, source_target_pairs={{0,8},{8,0},{16,24},{24,16},{1,17},{5,13},{13,5},{17,1},{21,29},{2... | collective-permute-start | bytes 1572872 | tf_op jit(solution)/shard_map/ppermute | solution.py:254
  41.3 1.4 %collective-permute-done.2.refs_3_.refs_0_.refs_4_.refs_9_ = bf16[128,16,128]{2,1,0:T(8,128)(2,1)S(1)} collective-permute-done((bf16[128,16,128]{2,1,0:T(8,128)(2,1)S(1)}, bf16[128,16,128]{2,1,0:T(8,128)(2,1)S(1)}, u32[]{:S(2)}, u32[]{:S(2)}) %collective-permute-start.2) | collective-permute-done | bytes 524320 | tf_op jit(solution)/shard_map/ppermute | solution.py:380
  42.7 2.9 %collective-permute-start.6 = (bf16[128,16,128]{2,1,0:T(8,128)(2,1)S(1)}, bf16[128,16,128]{2,1,0:T(8,128)(2,1)S(1)}, u32[]{:S(2)}, u32[]{:S(2)}) collective-permute-start(bf16[128,16,128]{2,1,0:T(8,128)(2,1)S(1)} %collective-permute-done.2.refs_3_.refs_0_.refs_4_.refs_9_), channel_id=1, source_target_pairs={{0,8},{8,0},{16,24},{24,16},{1,17},{5,13},{13,5},{17,1},{21,29},{2... | collective-permute-start | bytes 1572872 | tf_op jit(solution)/shard_map/ppermute | solution.py:254
  45.5 0.9 %collective-permute-done.7.refs_5_ = bf16[128,16,128]{2,1,0:T(8,128)(2,1)S(1)} collective-permute-done((bf16[128,16,128]{2,1,0:T(8,128)(2,1)S(1)}, bf16[128,16,128]{2,1,0:T(8,128)(2,1)S(1)}, u32[]{:S(2)}, u32[]{:S(2)}) %collective-permute-start.7) | collective-permute-done | bytes 524320 | tf_op jit(solution)/shard_map/ppermute | solution.py:254
  46.4 5.6 %collective-permute-done.8.refs_1_.refs_3_.refs_7_ = bf16[128,16,128]{2,1,0:T(8,128)(2,1)S(1)} collective-permute-done((bf16[128,16,128]{2,1,0:T(8,128)(2,1)S(1)}, bf16[128,16,128]{2,1,0:T(8,128)(2,1)S(1)}, u32[]{:S(2)}, u32[]{:S(2)}) %collective-permute-start.8) | collective-permute-done | bytes 524320 | tf_op jit(solution)/shard_map/ppermute | solution.py:254
  52.1 3.8 %collective-permute-start.9 = (bf16[128,16,128]{2,1,0:T(8,128)(2,1)S(1)}, bf16[128,16,128]{2,1,0:T(8,128)(2,1)S(1)}, u32[]{:S(2)}, u32[]{:S(2)}) collective-permute-start(bf16[128,16,128]{2,1,0:T(8,128)(2,1)S(1)} %bitcast.4), channel_id=1, source_target_pairs={{8,24},{24,8},{1,9},{9,1},{13,29},{17,25},{25,17},{29,13},{2,10},{... | collective-permute-start | bytes 1572872 | tf_op jit(solution)/shard_map/ppermute | solution.py:254
  55.9 2.0 %own_rows.1.own = bf16[128,128,64]{2,1,0:T(8,128)(2,1)S(1)} custom-call(bf16[128,16,128]{2,1,0:T(8,128)(2,1)S(1)} %whiten.1.refs_0_, bf16[128,16,128]{2,1,0:T(8,128)(2,1)S(1)} %collective-permute-done.refs_1_.refs_0_.refs_3_, bf16[128,16,128]{2,1,0:T(8,128)(2,1)S(1)} %collective-permute-done.1.refs_2_.refs_0_.refs_6_, ...), custom_call_target="tpu_custom_call" | custom-call | flops 1 | bytes 1 | tf_op jit(solution)/shard_map/own_rows/pallas_call | solution.py:118
  58.0 2.9 %collective-permute-done.6.refs_1_.refs_5_.refs_10_ = bf16[128,16,128]{2,1,0:T(8,128)(2,1)S(1)} collective-permute-done((bf16[128,16,128]{2,1,0:T(8,128)(2,1)S(1)}, bf16[128,16,128]{2,1,0:T(8,128)(2,1)S(1)}, u32[]{:S(2)}, u32[]{:S(2)}) %collective-permute-start.6) | collective-permute-done | bytes 524320 | tf_op jit(solution)/shard_map/ppermute | solution.py:254
  60.9 0.0 copy-start.3
  61.0 0.7 collective-permute-start.12
  61.7 2.1 %collective-permute-start.10 = (bf16[128,16,128]{2,1,0:T(8,128)(2,1)S(1)}, bf16[128,16,128]{2,1,0:T(8,128)(2,1)S(1)}, u32[]{:S(2)}, u32[]{:S(2)}) collective-permute-start(bf16[128,16,128]{2,1,0:T(8,128)(2,1)S(1)} %bitcast.5), channel_id=1, source_target_pairs={{8,24},{24,8},{1,9},{9,1},{13,29},{17,25},{25,17},{29,13},{2,10},{... | collective-permute-start | bytes 1572872 | tf_op jit(solution)/shard_map/ppermute | solution.py:254
  63.8 0.1 choose.10
  63.9 0.1 collective-permute-start.11
  64.0 7.6 %collective-permute-done.10.refs_6_.refs_11_ = bf16[128,16,128]{2,1,0:T(8,128)(2,1)S(1)} collective-permute-done((bf16[128,16,128]{2,1,0:T(8,128)(2,1)S(1)}, bf16[128,16,128]{2,1,0:T(8,128)(2,1)S(1)}, u32[]{:S(2)}, u32[]{:S(2)}) %collective-permute-start.10) | collective-permute-done | bytes 524320 | tf_op jit(solution)/shard_map/ppermute | solution.py:254
  71.6 0.1 choose.11
  71.7 0.1 collective-permute-start.13
  71.8 2.6 %collective-permute-done.13.refs_13_ = bf16[2,128,16,128]{3,2,1,0:T(8,128)(2,1)S(1)} collective-permute-done((bf16[2,128,16,128]{3,2,1,0:T(8,128)(2,1)S(1)}, bf16[2,128,16,128]{3,2,1,0:T(8,128)(2,1)S(1)}, u32[]{:S(2)}, u32[]{:S(2)}) %collective-permute-start.13) | collective-permute-done | bytes 1048608 | tf_op jit(solution)/shard_map/ppermute | solution.py:254
  74.4 9.9 %stack.1 = f32[64,64,256]{2,1,0:T(8,128)} custom-call(s32[64]{0:T(128)S(1)} %copy-done.3, bf16[128,128,64]{2,1,0:T(8,128)(2,1)S(1)} %own_rows.1.own, bf16[128,16,128]{2,1,0:T(8,128)(2,1)S(1)} %whiten.1.refs_0_, bf16[128,16,128]{2,1,0:T(8,128)(2,1)S(1)} %collective-permute-done.3.refs_1_, bf16[128,16,128]{2,1,0:T(8,128)(2,1)S(1)} %collective-permute-done.4.refs_2_, ...), custom_call_target="tpu_custom_call" | custom-call | flops 1 | bytes 1 | tf_op jit(solution)/shard_map/stack/pallas_call | solution.py:236
  (13 shorter events, 0.2 us)
Async XLA Ops:
  0.0 1.2 %copy-start = (bf16[16,64,512]{2,1,0:T(8,128)(2,1)S(1)}, bf16[16,64,512]{2,1,0:T(8,128)(2,1)}, u32[]{:S(2)}) copy-start(bf16[16,64,512]{2,1,0:T(8,128)(2,1)} %traces.1) | copy-start | bytes 3145732
  1.2 0.9 %copy-start.1 = (bf16[256,512]{1,0:T(8,128)(2,1)S(1)}, bf16[256,512]{1,0:T(8,128)(2,1)}, u32[]{:S(2)}) copy-start(bf16[256,512]{1,0:T(8,128)(2,1)} %constant.3.table) | copy-start | bytes 786436
  2.2 0.7 copy-start.2
  4.1 12.8 %collective-permute-start = (bf16[128,16,128]{2,1,0:T(8,128)(2,1)S(1)}, bf16[128,16,128]{2,1,0:T(8,128)(2,1)S(1)}, u32[]{:S(2)}, u32[]{:S(2)}) collective-permute-start(bf16[128,16,128]{2,1,0:T(8,128)(2,1)S(1)} %whiten.1.refs_0_), channel_id=1, source_target_pairs={{0,1},{1,2},{2,3},{3,0},{4,5},{5,6},{6,7},{7,4},{8,9},{9,10},{10,1... | collective-permute-start | bytes 1572872 | tf_op jit(solution)/shard_map/ppermute | solution.py:380
  5.5 12.8 %collective-permute-start.3 = (bf16[128,16,128]{2,1,0:T(8,128)(2,1)S(1)}, bf16[128,16,128]{2,1,0:T(8,128)(2,1)S(1)}, u32[]{:S(2)}, u32[]{:S(2)}) collective-permute-start(bf16[128,16,128]{2,1,0:T(8,128)(2,1)S(1)} %whiten.1.refs_0_), channel_id=1, source_target_pairs={{0,8},{8,0},{16,24},{24,16},{1,17},{5,13},{13,5},{17,1},{21,29},{2... | collective-permute-start | bytes 1572872 | tf_op jit(solution)/shard_map/ppermute | solution.py:254
  17.0 12.9 %collective-permute-start.1 = (bf16[128,16,128]{2,1,0:T(8,128)(2,1)S(1)}, bf16[128,16,128]{2,1,0:T(8,128)(2,1)S(1)}, u32[]{:S(2)}, u32[]{:S(2)}) collective-permute-start(bf16[128,16,128]{2,1,0:T(8,128)(2,1)S(1)} %collective-permute-done.refs_1_.refs_0_.refs_3_), channel_id=1, source_target_pairs={{0,1},{1,2},{2,3},{3,0},{4,5},{5,6},{6,7},{7,4},{8,9},{9,10},{10,1... | collective-permute-start | bytes 1572872 | tf_op jit(solution)/shard_map/ppermute | solution.py:380
  18.3 11.8 %collective-permute-start.4 = (bf16[128,16,128]{2,1,0:T(8,128)(2,1)S(1)}, bf16[128,16,128]{2,1,0:T(8,128)(2,1)S(1)}, u32[]{:S(2)}, u32[]{:S(2)}) collective-permute-start(bf16[128,16,128]{2,1,0:T(8,128)(2,1)S(1)} %bitcast.6), channel_id=1, source_target_pairs={{8,24},{24,8},{1,9},{9,1},{13,29},{17,25},{25,17},{29,13},{2,10},{... | collective-permute-start | bytes 1572872 | tf_op jit(solution)/shard_map/ppermute | solution.py:254
  21.5 14.7 %collective-permute-start.5 = (bf16[128,16,128]{2,1,0:T(8,128)(2,1)S(1)}, bf16[128,16,128]{2,1,0:T(8,128)(2,1)S(1)}, u32[]{:S(2)}, u32[]{:S(2)}) collective-permute-start(bf16[128,16,128]{2,1,0:T(8,128)(2,1)S(1)} %collective-permute-done.refs_1_.refs_0_.refs_3_), channel_id=1, source_target_pairs={{0,8},{8,0},{16,24},{24,16},{1,17},{5,13},{13,5},{17,1},{21,29},{2... | collective-permute-start | bytes 1572872 | tf_op jit(solution)/shard_map/ppermute | solution.py:254
  29.8 12.8 %collective-permute-start.2 = (bf16[128,16,128]{2,1,0:T(8,128)(2,1)S(1)}, bf16[128,16,128]{2,1,0:T(8,128)(2,1)S(1)}, u32[]{:S(2)}, u32[]{:S(2)}) collective-permute-start(bf16[128,16,128]{2,1,0:T(8,128)(2,1)S(1)} %collective-permute-done.1.refs_2_.refs_0_.refs_6_), channel_id=1, source_target_pairs={{0,1},{1,2},{2,3},{3,0},{4,5},{5,6},{6,7},{7,4},{8,9},{9,10},{10,1... | collective-permute-start | bytes 1572872 | tf_op jit(solution)/shard_map/ppermute | solution.py:380
  36.2 10.2 %collective-permute-start.7 = (bf16[128,16,128]{2,1,0:T(8,128)(2,1)S(1)}, bf16[128,16,128]{2,1,0:T(8,128)(2,1)S(1)}, u32[]{:S(2)}, u32[]{:S(2)}) collective-permute-start(bf16[128,16,128]{2,1,0:T(8,128)(2,1)S(1)} %bitcast.7), channel_id=1, source_target_pairs={{8,24},{24,8},{1,9},{9,1},{13,29},{17,25},{25,17},{29,13},{2,10},{... | collective-permute-start | bytes 1572872 | tf_op jit(solution)/shard_map/ppermute | solution.py:254
  39.3 12.7 %collective-permute-start.8 = (bf16[128,16,128]{2,1,0:T(8,128)(2,1)S(1)}, bf16[128,16,128]{2,1,0:T(8,128)(2,1)S(1)}, u32[]{:S(2)}, u32[]{:S(2)}) collective-permute-start(bf16[128,16,128]{2,1,0:T(8,128)(2,1)S(1)} %collective-permute-done.1.refs_2_.refs_0_.refs_6_), channel_id=1, source_target_pairs={{0,8},{8,0},{16,24},{24,16},{1,17},{5,13},{13,5},{17,1},{21,29},{2... | collective-permute-start | bytes 1572872 | tf_op jit(solution)/shard_map/ppermute | solution.py:254
  42.7 18.2 %collective-permute-start.6 = (bf16[128,16,128]{2,1,0:T(8,128)(2,1)S(1)}, bf16[128,16,128]{2,1,0:T(8,128)(2,1)S(1)}, u32[]{:S(2)}, u32[]{:S(2)}) collective-permute-start(bf16[128,16,128]{2,1,0:T(8,128)(2,1)S(1)} %collective-permute-done.2.refs_3_.refs_0_.refs_4_.refs_9_), channel_id=1, source_target_pairs={{0,8},{8,0},{16,24},{24,16},{1,17},{5,13},{13,5},{17,1},{21,29},{2... | collective-permute-start | bytes 1572872 | tf_op jit(solution)/shard_map/ppermute | solution.py:254
  52.1 11.9 %collective-permute-start.9 = (bf16[128,16,128]{2,1,0:T(8,128)(2,1)S(1)}, bf16[128,16,128]{2,1,0:T(8,128)(2,1)S(1)}, u32[]{:S(2)}, u32[]{:S(2)}) collective-permute-start(bf16[128,16,128]{2,1,0:T(8,128)(2,1)S(1)} %bitcast.4), channel_id=1, source_target_pairs={{8,24},{24,8},{1,9},{9,1},{13,29},{17,25},{25,17},{29,13},{2,10},{... | collective-permute-start | bytes 1572872 | tf_op jit(solution)/shard_map/ppermute | solution.py:254
  60.9 13.5 %copy-start.3 = (s32[64]{0:T(128)S(1)}, s32[64]{0:T(128)}, u32[]{:S(2)}) copy-start(s32[64]{0:T(128)} %reach_ref.1) | copy-start | bytes 772
  61.0 3.0 %collective-permute-start.12 = (bf16[128,16,128]{2,1,0:T(8,128)(2,1)S(1)}, bf16[128,16,128]{2,1,0:T(8,128)(2,1)S(1)}, u32[]{:S(2)}, u32[]{:S(2)}) collective-permute-start(bf16[128,16,128]{2,1,0:T(8,128)(2,1)S(1)} %collective-permute-done.2.refs_3_.refs_0_.refs_4_.refs_9_), channel_id=1, source_target_pairs={{3,19},{11,27},{19,3},{27,11}} | collective-permute-start | bytes 1572872 | tf_op jit(solution)/shard_map/ppermute | solution.py:254
  61.7 9.9 %collective-permute-start.10 = (bf16[128,16,128]{2,1,0:T(8,128)(2,1)S(1)}, bf16[128,16,128]{2,1,0:T(8,128)(2,1)S(1)}, u32[]{:S(2)}, u32[]{:S(2)}) collective-permute-start(bf16[128,16,128]{2,1,0:T(8,128)(2,1)S(1)} %bitcast.5), channel_id=1, source_target_pairs={{8,24},{24,8},{1,9},{9,1},{13,29},{17,25},{25,17},{29,13},{2,10},{... | collective-permute-start | bytes 1572872 | tf_op jit(solution)/shard_map/ppermute | solution.py:254
  63.9 7.9 %collective-permute-start.11 = (bf16[2,128,16,128]{3,2,1,0:T(8,128)(2,1)S(1)}, bf16[2,128,16,128]{3,2,1,0:T(8,128)(2,1)S(1)}, u32[]{:S(2)}, u32[]{:S(2)}) collective-permute-start(bf16[2,128,16,128]{3,2,1,0:T(8,128)(2,1)S(1)} %choose.10), channel_id=1, source_target_pairs={{0,4},{4,0},{8,12},{12,8},{16,20},{20,16},{24,28},{28,24},{1,5},{5... | collective-permute-start | bytes 3145736 | tf_op jit(solution)/shard_map/ppermute | solution.py:254
  71.7 2.7 %collective-permute-start.13 = (bf16[2,128,16,128]{3,2,1,0:T(8,128)(2,1)S(1)}, bf16[2,128,16,128]{3,2,1,0:T(8,128)(2,1)S(1)}, u32[]{:S(2)}, u32[]{:S(2)}) collective-permute-start(bf16[2,128,16,128]{3,2,1,0:T(8,128)(2,1)S(1)} %choose.11), channel_id=1, source_target_pairs={{0,4},{4,0},{8,12},{12,8},{16,20},{20,16},{24,28},{28,24},{1,5},{5... | collective-permute-start | bytes 3145736 | tf_op jit(solution)/shard_map/ppermute | solution.py:254

commit v18 on v17

--- a/solution.py
+++ b/solution.py
@@ -349,10 +349,9 @@
             second_move(slot - 1, arrived)
     held = list(zip(pieces, firsts, seconds))
     own = own_rows(pieces)
-    held[0] = (*held[0][:2], after(held[0][2], firsts[-1]))
+    held[0] = (*held[0][:2], after(held[0][2], firsts[-1], own))
     swapped_early = swap(lambda: square_codes()[1], held[:half])
-    arrived = after(firsts[-1], own)
-    relay = second_move(count - 1, arrived)
+    relay = second_move(count - 1, firsts[-1])
     held.append((pieces[-1], firsts[-1], seconds[-1]))
     late = send(
         after(pieces[-1], relay),

time: 84.7 us -> 84.7 us (level)
  no operation moved by 1% of the time
where the time goes in v18:
time: 84.7 us; the launch traced here: 84.3 us
  waiting for transfers between devices  42.9 us (51%)
  starting transfers between devices  24.8 us (29%)
  Pallas kernels  13.5 us (16%)
  local copies, waits for them, and re-layouts  2.88 us (3%)
    ppermute x11, waiting for transfers between devices, send(): return lax.ppermute(array, AXES, pairs)  25.7 us
    ppermute x11, starting transfers between devices, send(): return lax.ppermute(array, AXES, pairs)  21.9 us
    ppermute x3, waiting for transfers between devices, on_device(): pieces.append(lax.ppermute(pieces[-1], 'win', ring))  17.2 us
    pallas_call x1, Pallas kernels, stacked(): pl.pallas_call(functools.partial(stack_kernel, 1.0 / math.sqrt(windows),...  9.85 us
    ppermute x3, starting transfers between devices, on_device(): pieces.append(lax.ppermute(pieces[-1], 'win', ring))  2.94 us
    unnamed x8, local copies, waits for them, and re-layouts  2.88 us
    pallas_call x1, Pallas kernels, own_rows(): pl.pallas_call(own_kernel, out_shape=jax.ShapeDtypeStruct((bins, lanes, w...  2.03 us
  transfers between devices with their start and end apart: 14, of which 9 were waited for; matrix products, arithmetic and copies ran while one was open for 0% of the time, Pallas kernels for 3%

profile of v18, /device:TPU:11, one launch (start us, length us, event | category | flops | bytes accessed | tf_op | source)
XLA Modules:
  0.0 84.3 jit_solution(15383872949731466231)
XLA Ops:
  0.0 1.2 %copy-done = bf16[16,64,512]{2,1,0:T(8,128)(2,1)S(1)} copy-done((bf16[16,64,512]{2,1,0:T(8,128)(2,1)S(1)}, bf16[16,64,512]{2,1,0:T(8,128)(2,1)}, u32[]{:S(2)}) %copy-start) | copy-done | bytes 1048600
  1.2 0.9 %copy-done.1 = bf16[256,512]{1,0:T(8,128)(2,1)S(1)} copy-done((bf16[256,512]{1,0:T(8,128)(2,1)S(1)}, bf16[256,512]{1,0:T(8,128)(2,1)}, u32[]{:S(2)}) %copy-start.1) | copy-done | bytes 262168
  2.2 0.7 copy-done.2
  2.9 1.2 %whiten.1.refs_0_ = bf16[128,16,128]{2,1,0:T(8,128)(2,1)S(1)} custom-call(bf16[256,512]{1,0:T(8,128)(2,1)S(1)} %copy-done.1, bf16[16,64,512]{2,1,0:T(8,128)(2,1)S(1)} %copy-done, s32[16,64]{1,0:T(8,128)S(1)} %copy-done.2), custom_call_target="tpu_custom_call" | custom-call | flops 1 | bytes 1 | tf_op jit(solution)/shard_map/whiten/pallas_call | solution.py:61
  4.1 1.4 %collective-permute-start = (bf16[128,16,128]{2,1,0:T(8,128)(2,1)S(1)}, bf16[128,16,128]{2,1,0:T(8,128)(2,1)S(1)}, u32[]{:S(2)}, u32[]{:S(2)}) collective-permute-start(bf16[128,16,128]{2,1,0:T(8,128)(2,1)S(1)} %whiten.1.refs_0_), channel_id=1, source_target_pairs={{0,1},{1,2},{2,3},{3,0},{4,5},{5,6},{6,7},{7,4},{8,9},{9,10},{10,1... | collective-permute-start | bytes 1572872 | tf_op jit(solution)/shard_map/ppermute | solution.py:379
  5.5 2.1 %collective-permute-start.3 = (bf16[128,16,128]{2,1,0:T(8,128)(2,1)S(1)}, bf16[128,16,128]{2,1,0:T(8,128)(2,1)S(1)}, u32[]{:S(2)}, u32[]{:S(2)}) collective-permute-start(bf16[128,16,128]{2,1,0:T(8,128)(2,1)S(1)} %whiten.1.refs_0_), channel_id=1, source_target_pairs={{0,8},{8,0},{16,24},{24,16},{1,17},{5,13},{13,5},{17,1},{21,29},{2... | collective-permute-start | bytes 1572872 | tf_op jit(solution)/shard_map/ppermute | solution.py:254
  7.6 9.3 %collective-permute-done.refs_1_.refs_0_.refs_3_ = bf16[128,16,128]{2,1,0:T(8,128)(2,1)S(1)} collective-permute-done((bf16[128,16,128]{2,1,0:T(8,128)(2,1)S(1)}, bf16[128,16,128]{2,1,0:T(8,128)(2,1)S(1)}, u32[]{:S(2)}, u32[]{:S(2)}) %collective-permute-start) | collective-permute-done | bytes 524320 | tf_op jit(solution)/shard_map/ppermute | solution.py:379
  17.0 1.3 %collective-permute-start.1 = (bf16[128,16,128]{2,1,0:T(8,128)(2,1)S(1)}, bf16[128,16,128]{2,1,0:T(8,128)(2,1)S(1)}, u32[]{:S(2)}, u32[]{:S(2)}) collective-permute-start(bf16[128,16,128]{2,1,0:T(8,128)(2,1)S(1)} %collective-permute-done.refs_1_.refs_0_.refs_3_), channel_id=1, source_target_pairs={{0,1},{1,2},{2,3},{3,0},{4,5},{5,6},{6,7},{7,4},{8,9},{9,10},{10,1... | collective-permute-start | bytes 1572872 | tf_op jit(solution)/shard_map/ppermute | solution.py:379
  18.3 3.1 %collective-permute-start.4 = (bf16[128,16,128]{2,1,0:T(8,128)(2,1)S(1)}, bf16[128,16,128]{2,1,0:T(8,128)(2,1)S(1)}, u32[]{:S(2)}, u32[]{:S(2)}) collective-permute-start(bf16[128,16,128]{2,1,0:T(8,128)(2,1)S(1)} %bitcast.6), channel_id=1, source_target_pairs={{8,24},{24,8},{1,9},{9,1},{13,29},{17,25},{25,17},{29,13},{2,10},{... | collective-permute-start | bytes 1572872 | tf_op jit(solution)/shard_map/ppermute | solution.py:254
  21.5 1.9 %collective-permute-start.5 = (bf16[128,16,128]{2,1,0:T(8,128)(2,1)S(1)}, bf16[128,16,128]{2,1,0:T(8,128)(2,1)S(1)}, u32[]{:S(2)}, u32[]{:S(2)}) collective-permute-start(bf16[128,16,128]{2,1,0:T(8,128)(2,1)S(1)} %collective-permute-done.refs_1_.refs_0_.refs_3_), channel_id=1, source_target_pairs={{0,8},{8,0},{16,24},{24,16},{1,17},{5,13},{13,5},{17,1},{21,29},{2... | collective-permute-start | bytes 1572872 | tf_op jit(solution)/shard_map/ppermute | solution.py:254
  23.4 6.4 %collective-permute-done.1.refs_2_.refs_0_.refs_6_ = bf16[128,16,128]{2,1,0:T(8,128)(2,1)S(1)} collective-permute-done((bf16[128,16,128]{2,1,0:T(8,128)(2,1)S(1)}, bf16[128,16,128]{2,1,0:T(8,128)(2,1)S(1)}, u32[]{:S(2)}, u32[]{:S(2)}) %collective-permute-start.1) | collective-permute-done | bytes 524320 | tf_op jit(solution)/shard_map/ppermute | solution.py:379
  29.8 0.3 collective-permute-start.2
  30.1 6.0 %collective-permute-done.5.refs_1_.refs_4_ = bf16[128,16,128]{2,1,0:T(8,128)(2,1)S(1)} collective-permute-done((bf16[128,16,128]{2,1,0:T(8,128)(2,1)S(1)}, bf16[128,16,128]{2,1,0:T(8,128)(2,1)S(1)}, u32[]{:S(2)}, u32[]{:S(2)}) %collective-permute-start.5) | collective-permute-done | bytes 524320 | tf_op jit(solution)/shard_map/ppermute | solution.py:254
  36.2 3.1 %collective-permute-start.7 = (bf16[128,16,128]{2,1,0:T(8,128)(2,1)S(1)}, bf16[128,16,128]{2,1,0:T(8,128)(2,1)S(1)}, u32[]{:S(2)}, u32[]{:S(2)}) collective-permute-start(bf16[128,16,128]{2,1,0:T(8,128)(2,1)S(1)} %bitcast.7), channel_id=1, source_target_pairs={{8,24},{24,8},{1,9},{9,1},{13,29},{17,25},{25,17},{29,13},{2,10},{... | collective-permute-start | bytes 1572872 | tf_op jit(solution)/shard_map/ppermute | solution.py:254
  39.3 1.9 %collective-permute-start.8 = (bf16[128,16,128]{2,1,0:T(8,128)(2,1)S(1)}, bf16[128,16,128]{2,1,0:T(8,128)(2,1)S(1)}, u32[]{:S(2)}, u32[]{:S(2)}) collective-permute-start(bf16[128,16,128]{2,1,0:T(8,128)(2,1)S(1)} %collective-permute-done.1.refs_2_.refs_0_.refs_6_), channel_id=1, source_target_pairs={{0,8},{8,0},{16,24},{24,16},{1,17},{5,13},{13,5},{17,1},{21,29},{2... | collective-permute-start | bytes 1572872 | tf_op jit(solution)/shard_map/ppermute | solution.py:254
  41.3 1.4 %collective-permute-done.2.refs_3_.refs_0_.refs_4_.refs_9_ = bf16[128,16,128]{2,1,0:T(8,128)(2,1)S(1)} collective-permute-done((bf16[128,16,128]{2,1,0:T(8,128)(2,1)S(1)}, bf16[128,16,128]{2,1,0:T(8,128)(2,1)S(1)}, u32[]{:S(2)}, u32[]{:S(2)}) %collective-permute-start.2) | collective-permute-done | bytes 524320 | tf_op jit(solution)/shard_map/ppermute | solution.py:379
  42.7 2.9 %collective-permute-start.6 = (bf16[128,16,128]{2,1,0:T(8,128)(2,1)S(1)}, bf16[128,16,128]{2,1,0:T(8,128)(2,1)S(1)}, u32[]{:S(2)}, u32[]{:S(2)}) collective-permute-start(bf16[128,16,128]{2,1,0:T(8,128)(2,1)S(1)} %collective-permute-done.2.refs_3_.refs_0_.refs_4_.refs_9_), channel_id=1, source_target_pairs={{0,8},{8,0},{16,24},{24,16},{1,17},{5,13},{13,5},{17,1},{21,29},{2... | collective-permute-start | bytes 1572872 | tf_op jit(solution)/shard_map/ppermute | solution.py:254
  45.5 0.9 %collective-permute-done.7.refs_5_ = bf16[128,16,128]{2,1,0:T(8,128)(2,1)S(1)} collective-permute-done((bf16[128,16,128]{2,1,0:T(8,128)(2,1)S(1)}, bf16[128,16,128]{2,1,0:T(8,128)(2,1)S(1)}, u32[]{:S(2)}, u32[]{:S(2)}) %collective-permute-start.7) | collective-permute-done | bytes 524320 | tf_op jit(solution)/shard_map/ppermute | solution.py:254
  46.4 5.6 %collective-permute-done.8.refs_1_.refs_3_.refs_7_ = bf16[128,16,128]{2,1,0:T(8,128)(2,1)S(1)} collective-permute-done((bf16[128,16,128]{2,1,0:T(8,128)(2,1)S(1)}, bf16[128,16,128]{2,1,0:T(8,128)(2,1)S(1)}, u32[]{:S(2)}, u32[]{:S(2)}) %collective-permute-start.8) | collective-permute-done | bytes 524320 | tf_op jit(solution)/shard_map/ppermute | solution.py:254
  52.1 3.8 %collective-permute-start.9 = (bf16[128,16,128]{2,1,0:T(8,128)(2,1)S(1)}, bf16[128,16,128]{2,1,0:T(8,128)(2,1)S(1)}, u32[]{:S(2)}, u32[]{:S(2)}) collective-permute-start(bf16[128,16,128]{2,1,0:T(8,128)(2,1)S(1)} %bitcast.4), channel_id=1, source_target_pairs={{8,24},{24,8},{1,9},{9,1},{13,29},{17,25},{25,17},{29,13},{2,10},{... | collective-permute-start | bytes 1572872 | tf_op jit(solution)/shard_map/ppermute | solution.py:254
  55.9 5.0 %collective-permute-done.6.refs_1_.refs_5_.refs_10_ = bf16[128,16,128]{2,1,0:T(8,128)(2,1)S(1)} collective-permute-done((bf16[128,16,128]{2,1,0:T(8,128)(2,1)S(1)}, bf16[128,16,128]{2,1,0:T(8,128)(2,1)S(1)}, u32[]{:S(2)}, u32[]{:S(2)}) %collective-permute-start.6) | collective-permute-done | bytes 524320 | tf_op jit(solution)/shard_map/ppermute | solution.py:254
  60.9 0.7 collective-permute-start.12
  61.7 2.1 %collective-permute-start.10 = (bf16[128,16,128]{2,1,0:T(8,128)(2,1)S(1)}, bf16[128,16,128]{2,1,0:T(8,128)(2,1)S(1)}, u32[]{:S(2)}, u32[]{:S(2)}) collective-permute-start(bf16[128,16,128]{2,1,0:T(8,128)(2,1)S(1)} %bitcast.5), channel_id=1, source_target_pairs={{8,24},{24,8},{1,9},{9,1},{13,29},{17,25},{25,17},{29,13},{2,10},{... | collective-permute-start | bytes 1572872 | tf_op jit(solution)/shard_map/ppermute | solution.py:254
  63.7 2.0 %own_rows.1.own = bf16[128,128,64]{2,1,0:T(8,128)(2,1)S(1)} custom-call(bf16[128,16,128]{2,1,0:T(8,128)(2,1)S(1)} %whiten.1.refs_0_, bf16[128,16,128]{2,1,0:T(8,128)(2,1)S(1)} %collective-permute-done.refs_1_.refs_0_.refs_3_, bf16[128,16,128]{2,1,0:T(8,128)(2,1)S(1)} %collective-permute-done.1.refs_2_.refs_0_.refs_6_, ...), custom_call_target="tpu_custom_call" | custom-call | flops 1 | bytes 1 | tf_op jit(solution)/shard_map/own_rows/pallas_call | solution.py:118
  65.8 0.0 copy-start.3
  65.8 0.1 choose.10
  65.9 0.1 collective-permute-start.11
  66.0 5.6 %collective-permute-done.10.refs_6_.refs_11_ = bf16[128,16,128]{2,1,0:T(8,128)(2,1)S(1)} collective-permute-done((bf16[128,16,128]{2,1,0:T(8,128)(2,1)S(1)}, bf16[128,16,128]{2,1,0:T(8,128)(2,1)S(1)}, u32[]{:S(2)}, u32[]{:S(2)}) %collective-permute-start.10) | collective-permute-done | bytes 524320 | tf_op jit(solution)/shard_map/ppermute | solution.py:254
  71.6 0.1 choose.11
  71.7 0.1 collective-permute-start.13
  71.8 2.6 %collective-permute-done.13.refs_13_ = bf16[2,128,16,128]{3,2,1,0:T(8,128)(2,1)S(1)} collective-permute-done((bf16[2,128,16,128]{3,2,1,0:T(8,128)(2,1)S(1)}, bf16[2,128,16,128]{3,2,1,0:T(8,128)(2,1)S(1)}, u32[]{:S(2)}, u32[]{:S(2)}) %collective-permute-start.13) | collective-permute-done | bytes 1048608 | tf_op jit(solution)/shard_map/ppermute | solution.py:254
  74.4 9.9 %stack.1 = f32[64,64,256]{2,1,0:T(8,128)} custom-call(s32[64]{0:T(128)S(1)} %copy-done.3, bf16[128,128,64]{2,1,0:T(8,128)(2,1)S(1)} %own_rows.1.own, bf16[128,16,128]{2,1,0:T(8,128)(2,1)S(1)} %whiten.1.refs_0_, bf16[128,16,128]{2,1,0:T(8,128)(2,1)S(1)} %collective-permute-done.3.refs_1_, bf16[128,16,128]{2,1,0:T(8,128)(2,1)S(1)} %collective-permute-done.4.refs_2_, ...), custom_call_target="tpu_custom_call" | custom-call | flops 1 | bytes 1 | tf_op jit(solution)/shard_map/stack/pallas_call | solution.py:236
  (13 shorter events, 0.2 us)
Async XLA Ops:
  0.0 1.2 %copy-start = (bf16[16,64,512]{2,1,0:T(8,128)(2,1)S(1)}, bf16[16,64,512]{2,1,0:T(8,128)(2,1)}, u32[]{:S(2)}) copy-start(bf16[16,64,512]{2,1,0:T(8,128)(2,1)} %traces.1) | copy-start | bytes 3145732
  1.2 0.9 %copy-start.1 = (bf16[256,512]{1,0:T(8,128)(2,1)S(1)}, bf16[256,512]{1,0:T(8,128)(2,1)}, u32[]{:S(2)}) copy-start(bf16[256,512]{1,0:T(8,128)(2,1)} %constant.3.table) | copy-start | bytes 786436
  2.2 0.7 copy-start.2
  4.1 12.8 %collective-permute-start = (bf16[128,16,128]{2,1,0:T(8,128)(2,1)S(1)}, bf16[128,16,128]{2,1,0:T(8,128)(2,1)S(1)}, u32[]{:S(2)}, u32[]{:S(2)}) collective-permute-start(bf16[128,16,128]{2,1,0:T(8,128)(2,1)S(1)} %whiten.1.refs_0_), channel_id=1, source_target_pairs={{0,1},{1,2},{2,3},{3,0},{4,5},{5,6},{6,7},{7,4},{8,9},{9,10},{10,1... | collective-permute-start | bytes 1572872 | tf_op jit(solution)/shard_map/ppermute | solution.py:379
  5.5 12.8 %collective-permute-start.3 = (bf16[128,16,128]{2,1,0:T(8,128)(2,1)S(1)}, bf16[128,16,128]{2,1,0:T(8,128)(2,1)S(1)}, u32[]{:S(2)}, u32[]{:S(2)}) collective-permute-start(bf16[128,16,128]{2,1,0:T(8,128)(2,1)S(1)} %whiten.1.refs_0_), channel_id=1, source_target_pairs={{0,8},{8,0},{16,24},{24,16},{1,17},{5,13},{13,5},{17,1},{21,29},{2... | collective-permute-start | bytes 1572872 | tf_op jit(solution)/shard_map/ppermute | solution.py:254
  17.0 12.9 %collective-permute-start.1 = (bf16[128,16,128]{2,1,0:T(8,128)(2,1)S(1)}, bf16[128,16,128]{2,1,0:T(8,128)(2,1)S(1)}, u32[]{:S(2)}, u32[]{:S(2)}) collective-permute-start(bf16[128,16,128]{2,1,0:T(8,128)(2,1)S(1)} %collective-permute-done.refs_1_.refs_0_.refs_3_), channel_id=1, source_target_pairs={{0,1},{1,2},{2,3},{3,0},{4,5},{5,6},{6,7},{7,4},{8,9},{9,10},{10,1... | collective-permute-start | bytes 1572872 | tf_op jit(solution)/shard_map/ppermute | solution.py:379
  18.3 11.8 %collective-permute-start.4 = (bf16[128,16,128]{2,1,0:T(8,128)(2,1)S(1)}, bf16[128,16,128]{2,1,0:T(8,128)(2,1)S(1)}, u32[]{:S(2)}, u32[]{:S(2)}) collective-permute-start(bf16[128,16,128]{2,1,0:T(8,128)(2,1)S(1)} %bitcast.6), channel_id=1, source_target_pairs={{8,24},{24,8},{1,9},{9,1},{13,29},{17,25},{25,17},{29,13},{2,10},{... | collective-permute-start | bytes 1572872 | tf_op jit(solution)/shard_map/ppermute | solution.py:254
  21.5 14.7 %collective-permute-start.5 = (bf16[128,16,128]{2,1,0:T(8,128)(2,1)S(1)}, bf16[128,16,128]{2,1,0:T(8,128)(2,1)S(1)}, u32[]{:S(2)}, u32[]{:S(2)}) collective-permute-start(bf16[128,16,128]{2,1,0:T(8,128)(2,1)S(1)} %collective-permute-done.refs_1_.refs_0_.refs_3_), channel_id=1, source_target_pairs={{0,8},{8,0},{16,24},{24,16},{1,17},{5,13},{13,5},{17,1},{21,29},{2... | collective-permute-start | bytes 1572872 | tf_op jit(solution)/shard_map/ppermute | solution.py:254
  29.8 12.8 %collective-permute-start.2 = (bf16[128,16,128]{2,1,0:T(8,128)(2,1)S(1)}, bf16[128,16,128]{2,1,0:T(8,128)(2,1)S(1)}, u32[]{:S(2)}, u32[]{:S(2)}) collective-permute-start(bf16[128,16,128]{2,1,0:T(8,128)(2,1)S(1)} %collective-permute-done.1.refs_2_.refs_0_.refs_6_), channel_id=1, source_target_pairs={{0,1},{1,2},{2,3},{3,0},{4,5},{5,6},{6,7},{7,4},{8,9},{9,10},{10,1... | collective-permute-start | bytes 1572872 | tf_op jit(solution)/shard_map/ppermute | solution.py:379
  36.2 10.2 %collective-permute-start.7 = (bf16[128,16,128]{2,1,0:T(8,128)(2,1)S(1)}, bf16[128,16,128]{2,1,0:T(8,128)(2,1)S(1)}, u32[]{:S(2)}, u32[]{:S(2)}) collective-permute-start(bf16[128,16,128]{2,1,0:T(8,128)(2,1)S(1)} %bitcast.7), channel_id=1, source_target_pairs={{8,24},{24,8},{1,9},{9,1},{13,29},{17,25},{25,17},{29,13},{2,10},{... | collective-permute-start | bytes 1572872 | tf_op jit(solution)/shard_map/ppermute | solution.py:254
  39.3 12.7 %collective-permute-start.8 = (bf16[128,16,128]{2,1,0:T(8,128)(2,1)S(1)}, bf16[128,16,128]{2,1,0:T(8,128)(2,1)S(1)}, u32[]{:S(2)}, u32[]{:S(2)}) collective-permute-start(bf16[128,16,128]{2,1,0:T(8,128)(2,1)S(1)} %collective-permute-done.1.refs_2_.refs_0_.refs_6_), channel_id=1, source_target_pairs={{0,8},{8,0},{16,24},{24,16},{1,17},{5,13},{13,5},{17,1},{21,29},{2... | collective-permute-start | bytes 1572872 | tf_op jit(solution)/shard_map/ppermute | solution.py:254
  42.7 18.2 %collective-permute-start.6 = (bf16[128,16,128]{2,1,0:T(8,128)(2,1)S(1)}, bf16[128,16,128]{2,1,0:T(8,128)(2,1)S(1)}, u32[]{:S(2)}, u32[]{:S(2)}) collective-permute-start(bf16[128,16,128]{2,1,0:T(8,128)(2,1)S(1)} %collective-permute-done.2.refs_3_.refs_0_.refs_4_.refs_9_), channel_id=1, source_target_pairs={{0,8},{8,0},{16,24},{24,16},{1,17},{5,13},{13,5},{17,1},{21,29},{2... | collective-permute-start | bytes 1572872 | tf_op jit(solution)/shard_map/ppermute | solution.py:254
  52.1 13.9 %collective-permute-start.9 = (bf16[128,16,128]{2,1,0:T(8,128)(2,1)S(1)}, bf16[128,16,128]{2,1,0:T(8,128)(2,1)S(1)}, u32[]{:S(2)}, u32[]{:S(2)}) collective-permute-start(bf16[128,16,128]{2,1,0:T(8,128)(2,1)S(1)} %bitcast.4), channel_id=1, source_target_pairs={{8,24},{24,8},{1,9},{9,1},{13,29},{17,25},{25,17},{29,13},{2,10},{... | collective-permute-start | bytes 1572872 | tf_op jit(solution)/shard_map/ppermute | solution.py:254
  60.9 5.1 %collective-permute-start.12 = (bf16[128,16,128]{2,1,0:T(8,128)(2,1)S(1)}, bf16[128,16,128]{2,1,0:T(8,128)(2,1)S(1)}, u32[]{:S(2)}, u32[]{:S(2)}) collective-permute-start(bf16[128,16,128]{2,1,0:T(8,128)(2,1)S(1)} %collective-permute-done.2.refs_3_.refs_0_.refs_4_.refs_9_), channel_id=1, source_target_pairs={{3,19},{11,27},{19,3},{27,11}} | collective-permute-start | bytes 1572872 | tf_op jit(solution)/shard_map/ppermute | solution.py:254
  61.7 9.9 %collective-permute-start.10 = (bf16[128,16,128]{2,1,0:T(8,128)(2,1)S(1)}, bf16[128,16,128]{2,1,0:T(8,128)(2,1)S(1)}, u32[]{:S(2)}, u32[]{:S(2)}) collective-permute-start(bf16[128,16,128]{2,1,0:T(8,128)(2,1)S(1)} %bitcast.5), channel_id=1, source_target_pairs={{8,24},{24,8},{1,9},{9,1},{13,29},{17,25},{25,17},{29,13},{2,10},{... | collective-permute-start | bytes 1572872 | tf_op jit(solution)/shard_map/ppermute | solution.py:254
  65.8 8.6 %copy-start.3 = (s32[64]{0:T(128)S(1)}, s32[64]{0:T(128)}, u32[]{:S(2)}) copy-start(s32[64]{0:T(128)} %reach_ref.1) | copy-start | bytes 772
  65.9 5.8 %collective-permute-start.11 = (bf16[2,128,16,128]{3,2,1,0:T(8,128)(2,1)S(1)}, bf16[2,128,16,128]{3,2,1,0:T(8,128)(2,1)S(1)}, u32[]{:S(2)}, u32[]{:S(2)}) collective-permute-start(bf16[2,128,16,128]{3,2,1,0:T(8,128)(2,1)S(1)} %choose.10), channel_id=1, source_target_pairs={{0,4},{4,0},{8,12},{12,8},{16,20},{20,16},{24,28},{28,24},{1,5},{5... | collective-permute-start | bytes 3145736 | tf_op jit(solution)/shard_map/ppermute | solution.py:254
  71.7 2.7 %collective-permute-start.13 = (bf16[2,128,16,128]{3,2,1,0:T(8,128)(2,1)S(1)}, bf16[2,128,16,128]{3,2,1,0:T(8,128)(2,1)S(1)}, u32[]{:S(2)}, u32[]{:S(2)}) collective-permute-start(bf16[2,128,16,128]{3,2,1,0:T(8,128)(2,1)S(1)} %choose.11), channel_id=1, source_target_pairs={{0,4},{4,0},{8,12},{12,8},{16,20},{20,16},{24,28},{28,24},{1,5},{5... | collective-permute-start | bytes 3145736 | tf_op jit(solution)/shard_map/ppermute | solution.py:254

commit v19 on v18

--- a/solution.py
+++ b/solution.py
@@ -14,7 +14,7 @@
 BAND = 256
 AXES = ("chan", "win")
 CHANNEL_BLOCK = 8
-GROUP = 4
+GROUP = 8
 PITCH_PAD = 8
 MIB = 1024 * 1024
 VMEM = pl.BlockSpec(memory_space=pltpu.VMEM)

time: 84.7 us -> 83 us (0.980)
  Pallas kernels: 13.5 us -> 11.8 us
    pallas_call x1, Pallas kernels: 9.85 us -> 8.2 us  [stacked(): pl.pallas_call(functools.partial(stack_kernel, 1.0 / math.sqrt(windows),...]
where the time goes in v19:
time: 83 us; the launch traced here: 82.6 us
  waiting for transfers between devices  42.9 us (52%)
  starting transfers between devices  24.8 us (30%)
  Pallas kernels  11.8 us (14%)
  local copies, waits for them, and re-layouts  2.88 us (3%)
    ppermute x11, waiting for transfers between devices, send(): return lax.ppermute(array, AXES, pairs)  25.7 us
    ppermute x11, starting transfers between devices, send(): return lax.ppermute(array, AXES, pairs)  21.9 us
    ppermute x3, waiting for transfers between devices, on_device(): pieces.append(lax.ppermute(pieces[-1], 'win', ring))  17.2 us
    pallas_call x1, Pallas kernels, stacked(): pl.pallas_call(functools.partial(stack_kernel, 1.0 / math.sqrt(windows),...  8.2 us
    ppermute x3, starting transfers between devices, on_device(): pieces.append(lax.ppermute(pieces[-1], 'win', ring))  2.94 us
    unnamed x8, local copies, waits for them, and re-layouts  2.88 us
    pallas_call x1, Pallas kernels, own_rows(): pl.pallas_call(own_kernel, out_shape=jax.ShapeDtypeStruct((bins, lanes, w...  2.03 us
  transfers between devices with their start and end apart: 14, of which 9 were waited for; matrix products, arithmetic and copies ran while one was open for 0% of the time, Pallas kernels for 3%

profile of v19, /device:TPU:11, one launch (start us, length us, event | category | flops | bytes accessed | tf_op | source)
XLA Modules:
  0.0 82.6 jit_solution(12755673752772518261)
XLA Ops:
  0.0 1.2 %copy-done = bf16[16,64,512]{2,1,0:T(8,128)(2,1)S(1)} copy-done((bf16[16,64,512]{2,1,0:T(8,128)(2,1)S(1)}, bf16[16,64,512]{2,1,0:T(8,128)(2,1)}, u32[]{:S(2)}) %copy-start) | copy-done | bytes 1048600
  1.2 0.9 %copy-done.1 = bf16[256,512]{1,0:T(8,128)(2,1)S(1)} copy-done((bf16[256,512]{1,0:T(8,128)(2,1)S(1)}, bf16[256,512]{1,0:T(8,128)(2,1)}, u32[]{:S(2)}) %copy-start.1) | copy-done | bytes 262168
  2.2 0.7 copy-done.2
  2.9 1.2 %whiten.1.refs_0_ = bf16[128,16,128]{2,1,0:T(8,128)(2,1)S(1)} custom-call(bf16[256,512]{1,0:T(8,128)(2,1)S(1)} %copy-done.1, bf16[16,64,512]{2,1,0:T(8,128)(2,1)S(1)} %copy-done, s32[16,64]{1,0:T(8,128)S(1)} %copy-done.2), custom_call_target="tpu_custom_call" | custom-call | flops 1 | bytes 1 | tf_op jit(solution)/shard_map/whiten/pallas_call | solution.py:61
  4.1 1.4 %collective-permute-start = (bf16[128,16,128]{2,1,0:T(8,128)(2,1)S(1)}, bf16[128,16,128]{2,1,0:T(8,128)(2,1)S(1)}, u32[]{:S(2)}, u32[]{:S(2)}) collective-permute-start(bf16[128,16,128]{2,1,0:T(8,128)(2,1)S(1)} %whiten.1.refs_0_), channel_id=1, source_target_pairs={{0,1},{1,2},{2,3},{3,0},{4,5},{5,6},{6,7},{7,4},{8,9},{9,10},{10,1... | collective-permute-start | bytes 1572872 | tf_op jit(solution)/shard_map/ppermute | solution.py:379
  5.5 2.1 %collective-permute-start.3 = (bf16[128,16,128]{2,1,0:T(8,128)(2,1)S(1)}, bf16[128,16,128]{2,1,0:T(8,128)(2,1)S(1)}, u32[]{:S(2)}, u32[]{:S(2)}) collective-permute-start(bf16[128,16,128]{2,1,0:T(8,128)(2,1)S(1)} %whiten.1.refs_0_), channel_id=1, source_target_pairs={{0,8},{8,0},{16,24},{24,16},{1,17},{5,13},{13,5},{17,1},{21,29},{2... | collective-permute-start | bytes 1572872 | tf_op jit(solution)/shard_map/ppermute | solution.py:254
  7.6 9.3 %collective-permute-done.refs_1_.refs_0_.refs_3_ = bf16[128,16,128]{2,1,0:T(8,128)(2,1)S(1)} collective-permute-done((bf16[128,16,128]{2,1,0:T(8,128)(2,1)S(1)}, bf16[128,16,128]{2,1,0:T(8,128)(2,1)S(1)}, u32[]{:S(2)}, u32[]{:S(2)}) %collective-permute-start) | collective-permute-done | bytes 524320 | tf_op jit(solution)/shard_map/ppermute | solution.py:379
  17.0 1.3 %collective-permute-start.1 = (bf16[128,16,128]{2,1,0:T(8,128)(2,1)S(1)}, bf16[128,16,128]{2,1,0:T(8,128)(2,1)S(1)}, u32[]{:S(2)}, u32[]{:S(2)}) collective-permute-start(bf16[128,16,128]{2,1,0:T(8,128)(2,1)S(1)} %collective-permute-done.refs_1_.refs_0_.refs_3_), channel_id=1, source_target_pairs={{0,1},{1,2},{2,3},{3,0},{4,5},{5,6},{6,7},{7,4},{8,9},{9,10},{10,1... | collective-permute-start | bytes 1572872 | tf_op jit(solution)/shard_map/ppermute | solution.py:379
  18.3 3.1 %collective-permute-start.4 = (bf16[128,16,128]{2,1,0:T(8,128)(2,1)S(1)}, bf16[128,16,128]{2,1,0:T(8,128)(2,1)S(1)}, u32[]{:S(2)}, u32[]{:S(2)}) collective-permute-start(bf16[128,16,128]{2,1,0:T(8,128)(2,1)S(1)} %bitcast.6), channel_id=1, source_target_pairs={{8,24},{24,8},{1,9},{9,1},{13,29},{17,25},{25,17},{29,13},{2,10},{... | collective-permute-start | bytes 1572872 | tf_op jit(solution)/shard_map/ppermute | solution.py:254
  21.5 1.9 %collective-permute-start.5 = (bf16[128,16,128]{2,1,0:T(8,128)(2,1)S(1)}, bf16[128,16,128]{2,1,0:T(8,128)(2,1)S(1)}, u32[]{:S(2)}, u32[]{:S(2)}) collective-permute-start(bf16[128,16,128]{2,1,0:T(8,128)(2,1)S(1)} %collective-permute-done.refs_1_.refs_0_.refs_3_), channel_id=1, source_target_pairs={{0,8},{8,0},{16,24},{24,16},{1,17},{5,13},{13,5},{17,1},{21,29},{2... | collective-permute-start | bytes 1572872 | tf_op jit(solution)/shard_map/ppermute | solution.py:254
  23.4 6.4 %collective-permute-done.1.refs_2_.refs_0_.refs_6_ = bf16[128,16,128]{2,1,0:T(8,128)(2,1)S(1)} collective-permute-done((bf16[128,16,128]{2,1,0:T(8,128)(2,1)S(1)}, bf16[128,16,128]{2,1,0:T(8,128)(2,1)S(1)}, u32[]{:S(2)}, u32[]{:S(2)}) %collective-permute-start.1) | collective-permute-done | bytes 524320 | tf_op jit(solution)/shard_map/ppermute | solution.py:379
  29.8 0.3 collective-permute-start.2
  30.1 6.0 %collective-permute-done.5.refs_1_.refs_4_ = bf16[128,16,128]{2,1,0:T(8,128)(2,1)S(1)} collective-permute-done((bf16[128,16,128]{2,1,0:T(8,128)(2,1)S(1)}, bf16[128,16,128]{2,1,0:T(8,128)(2,1)S(1)}, u32[]{:S(2)}, u32[]{:S(2)}) %collective-permute-start.5) | collective-permute-done | bytes 524320 | tf_op jit(solution)/shard_map/ppermute | solution.py:254
  36.2 3.1 %collective-permute-start.7 = (bf16[128,16,128]{2,1,0:T(8,128)(2,1)S(1)}, bf16[128,16,128]{2,1,0:T(8,128)(2,1)S(1)}, u32[]{:S(2)}, u32[]{:S(2)}) collective-permute-start(bf16[128,16,128]{2,1,0:T(8,128)(2,1)S(1)} %bitcast.7), channel_id=1, source_target_pairs={{8,24},{24,8},{1,9},{9,1},{13,29},{17,25},{25,17},{29,13},{2,10},{... | collective-permute-start | bytes 1572872 | tf_op jit(solution)/shard_map/ppermute | solution.py:254
  39.3 1.9 %collective-permute-start.8 = (bf16[128,16,128]{2,1,0:T(8,128)(2,1)S(1)}, bf16[128,16,128]{2,1,0:T(8,128)(2,1)S(1)}, u32[]{:S(2)}, u32[]{:S(2)}) collective-permute-start(bf16[128,16,128]{2,1,0:T(8,128)(2,1)S(1)} %collective-permute-done.1.refs_2_.refs_0_.refs_6_), channel_id=1, source_target_pairs={{0,8},{8,0},{16,24},{24,16},{1,17},{5,13},{13,5},{17,1},{21,29},{2... | collective-permute-start | bytes 1572872 | tf_op jit(solution)/shard_map/ppermute | solution.py:254
  41.3 1.4 %collective-permute-done.2.refs_3_.refs_0_.refs_4_.refs_9_ = bf16[128,16,128]{2,1,0:T(8,128)(2,1)S(1)} collective-permute-done((bf16[128,16,128]{2,1,0:T(8,128)(2,1)S(1)}, bf16[128,16,128]{2,1,0:T(8,128)(2,1)S(1)}, u32[]{:S(2)}, u32[]{:S(2)}) %collective-permute-start.2) | collective-permute-done | bytes 524320 | tf_op jit(solution)/shard_map/ppermute | solution.py:379
  42.7 2.9 %collective-permute-start.6 = (bf16[128,16,128]{2,1,0:T(8,128)(2,1)S(1)}, bf16[128,16,128]{2,1,0:T(8,128)(2,1)S(1)}, u32[]{:S(2)}, u32[]{:S(2)}) collective-permute-start(bf16[128,16,128]{2,1,0:T(8,128)(2,1)S(1)} %collective-permute-done.2.refs_3_.refs_0_.refs_4_.refs_9_), channel_id=1, source_target_pairs={{0,8},{8,0},{16,24},{24,16},{1,17},{5,13},{13,5},{17,1},{21,29},{2... | collective-permute-start | bytes 1572872 | tf_op jit(solution)/shard_map/ppermute | solution.py:254
  45.5 0.9 %collective-permute-done.7.refs_5_ = bf16[128,16,128]{2,1,0:T(8,128)(2,1)S(1)} collective-permute-done((bf16[128,16,128]{2,1,0:T(8,128)(2,1)S(1)}, bf16[128,16,128]{2,1,0:T(8,128)(2,1)S(1)}, u32[]{:S(2)}, u32[]{:S(2)}) %collective-permute-start.7) | collective-permute-done | bytes 524320 | tf_op jit(solution)/shard_map/ppermute | solution.py:254
  46.4 5.6 %collective-permute-done.8.refs_1_.refs_3_.refs_7_ = bf16[128,16,128]{2,1,0:T(8,128)(2,1)S(1)} collective-permute-done((bf16[128,16,128]{2,1,0:T(8,128)(2,1)S(1)}, bf16[128,16,128]{2,1,0:T(8,128)(2,1)S(1)}, u32[]{:S(2)}, u32[]{:S(2)}) %collective-permute-start.8) | collective-permute-done | bytes 524320 | tf_op jit(solution)/shard_map/ppermute | solution.py:254
  52.1 3.8 %collective-permute-start.9 = (bf16[128,16,128]{2,1,0:T(8,128)(2,1)S(1)}, bf16[128,16,128]{2,1,0:T(8,128)(2,1)S(1)}, u32[]{:S(2)}, u32[]{:S(2)}) collective-permute-start(bf16[128,16,128]{2,1,0:T(8,128)(2,1)S(1)} %bitcast.4), channel_id=1, source_target_pairs={{8,24},{24,8},{1,9},{9,1},{13,29},{17,25},{25,17},{29,13},{2,10},{... | collective-permute-start | bytes 1572872 | tf_op jit(solution)/shard_map/ppermute | solution.py:254
  55.9 5.0 %collective-permute-done.6.refs_1_.refs_5_.refs_10_ = bf16[128,16,128]{2,1,0:T(8,128)(2,1)S(1)} collective-permute-done((bf16[128,16,128]{2,1,0:T(8,128)(2,1)S(1)}, bf16[128,16,128]{2,1,0:T(8,128)(2,1)S(1)}, u32[]{:S(2)}, u32[]{:S(2)}) %collective-permute-start.6) | collective-permute-done | bytes 524320 | tf_op jit(solution)/shard_map/ppermute | solution.py:254
  60.9 0.7 collective-permute-start.12
  61.7 2.1 %collective-permute-start.10 = (bf16[128,16,128]{2,1,0:T(8,128)(2,1)S(1)}, bf16[128,16,128]{2,1,0:T(8,128)(2,1)S(1)}, u32[]{:S(2)}, u32[]{:S(2)}) collective-permute-start(bf16[128,16,128]{2,1,0:T(8,128)(2,1)S(1)} %bitcast.5), channel_id=1, source_target_pairs={{8,24},{24,8},{1,9},{9,1},{13,29},{17,25},{25,17},{29,13},{2,10},{... | collective-permute-start | bytes 1572872 | tf_op jit(solution)/shard_map/ppermute | solution.py:254
  63.7 2.0 %own_rows.1.own = bf16[128,128,64]{2,1,0:T(8,128)(2,1)S(1)} custom-call(bf16[128,16,128]{2,1,0:T(8,128)(2,1)S(1)} %whiten.1.refs_0_, bf16[128,16,128]{2,1,0:T(8,128)(2,1)S(1)} %collective-permute-done.refs_1_.refs_0_.refs_3_, bf16[128,16,128]{2,1,0:T(8,128)(2,1)S(1)} %collective-permute-done.1.refs_2_.refs_0_.refs_6_, ...), custom_call_target="tpu_custom_call" | custom-call | flops 1 | bytes 1 | tf_op jit(solution)/shard_map/own_rows/pallas_call | solution.py:118
  65.8 0.0 copy-start.3
  65.8 0.1 choose.10
  65.9 0.1 collective-permute-start.11
  66.0 5.6 %collective-permute-done.10.refs_6_.refs_11_ = bf16[128,16,128]{2,1,0:T(8,128)(2,1)S(1)} collective-permute-done((bf16[128,16,128]{2,1,0:T(8,128)(2,1)S(1)}, bf16[128,16,128]{2,1,0:T(8,128)(2,1)S(1)}, u32[]{:S(2)}, u32[]{:S(2)}) %collective-permute-start.10) | collective-permute-done | bytes 524320 | tf_op jit(solution)/shard_map/ppermute | solution.py:254
  71.6 0.1 choose.11
  71.7 0.1 collective-permute-start.13
  71.8 2.6 %collective-permute-done.13.refs_13_ = bf16[2,128,16,128]{3,2,1,0:T(8,128)(2,1)S(1)} collective-permute-done((bf16[2,128,16,128]{3,2,1,0:T(8,128)(2,1)S(1)}, bf16[2,128,16,128]{3,2,1,0:T(8,128)(2,1)S(1)}, u32[]{:S(2)}, u32[]{:S(2)}) %collective-permute-start.13) | collective-permute-done | bytes 1048608 | tf_op jit(solution)/shard_map/ppermute | solution.py:254
  74.4 8.2 %stack.1 = f32[64,64,256]{2,1,0:T(8,128)} custom-call(s32[64]{0:T(128)S(1)} %copy-done.3, bf16[128,128,64]{2,1,0:T(8,128)(2,1)S(1)} %own_rows.1.own, bf16[128,16,128]{2,1,0:T(8,128)(2,1)S(1)} %whiten.1.refs_0_, bf16[128,16,128]{2,1,0:T(8,128)(2,1)S(1)} %collective-permute-done.3.refs_1_, bf16[128,16,128]{2,1,0:T(8,128)(2,1)S(1)} %collective-permute-done.4.refs_2_, ...), custom_call_target="tpu_custom_call" | custom-call | flops 1 | bytes 1 | tf_op jit(solution)/shard_map/stack/pallas_call | solution.py:236
  (13 shorter events, 0.2 us)
Async XLA Ops:
  0.0 1.2 %copy-start = (bf16[16,64,512]{2,1,0:T(8,128)(2,1)S(1)}, bf16[16,64,512]{2,1,0:T(8,128)(2,1)}, u32[]{:S(2)}) copy-start(bf16[16,64,512]{2,1,0:T(8,128)(2,1)} %traces.1) | copy-start | bytes 3145732
  1.2 0.9 %copy-start.1 = (bf16[256,512]{1,0:T(8,128)(2,1)S(1)}, bf16[256,512]{1,0:T(8,128)(2,1)}, u32[]{:S(2)}) copy-start(bf16[256,512]{1,0:T(8,128)(2,1)} %constant.3.table) | copy-start | bytes 786436
  2.2 0.7 copy-start.2
  4.1 12.8 %collective-permute-start = (bf16[128,16,128]{2,1,0:T(8,128)(2,1)S(1)}, bf16[128,16,128]{2,1,0:T(8,128)(2,1)S(1)}, u32[]{:S(2)}, u32[]{:S(2)}) collective-permute-start(bf16[128,16,128]{2,1,0:T(8,128)(2,1)S(1)} %whiten.1.refs_0_), channel_id=1, source_target_pairs={{0,1},{1,2},{2,3},{3,0},{4,5},{5,6},{6,7},{7,4},{8,9},{9,10},{10,1... | collective-permute-start | bytes 1572872 | tf_op jit(solution)/shard_map/ppermute | solution.py:379
  5.5 12.8 %collective-permute-start.3 = (bf16[128,16,128]{2,1,0:T(8,128)(2,1)S(1)}, bf16[128,16,128]{2,1,0:T(8,128)(2,1)S(1)}, u32[]{:S(2)}, u32[]{:S(2)}) collective-permute-start(bf16[128,16,128]{2,1,0:T(8,128)(2,1)S(1)} %whiten.1.refs_0_), channel_id=1, source_target_pairs={{0,8},{8,0},{16,24},{24,16},{1,17},{5,13},{13,5},{17,1},{21,29},{2... | collective-permute-start | bytes 1572872 | tf_op jit(solution)/shard_map/ppermute | solution.py:254
  17.0 12.9 %collective-permute-start.1 = (bf16[128,16,128]{2,1,0:T(8,128)(2,1)S(1)}, bf16[128,16,128]{2,1,0:T(8,128)(2,1)S(1)}, u32[]{:S(2)}, u32[]{:S(2)}) collective-permute-start(bf16[128,16,128]{2,1,0:T(8,128)(2,1)S(1)} %collective-permute-done.refs_1_.refs_0_.refs_3_), channel_id=1, source_target_pairs={{0,1},{1,2},{2,3},{3,0},{4,5},{5,6},{6,7},{7,4},{8,9},{9,10},{10,1... | collective-permute-start | bytes 1572872 | tf_op jit(solution)/shard_map/ppermute | solution.py:379
  18.3 11.8 %collective-permute-start.4 = (bf16[128,16,128]{2,1,0:T(8,128)(2,1)S(1)}, bf16[128,16,128]{2,1,0:T(8,128)(2,1)S(1)}, u32[]{:S(2)}, u32[]{:S(2)}) collective-permute-start(bf16[128,16,128]{2,1,0:T(8,128)(2,1)S(1)} %bitcast.6), channel_id=1, source_target_pairs={{8,24},{24,8},{1,9},{9,1},{13,29},{17,25},{25,17},{29,13},{2,10},{... | collective-permute-start | bytes 1572872 | tf_op jit(solution)/shard_map/ppermute | solution.py:254
  21.5 14.7 %collective-permute-start.5 = (bf16[128,16,128]{2,1,0:T(8,128)(2,1)S(1)}, bf16[128,16,128]{2,1,0:T(8,128)(2,1)S(1)}, u32[]{:S(2)}, u32[]{:S(2)}) collective-permute-start(bf16[128,16,128]{2,1,0:T(8,128)(2,1)S(1)} %collective-permute-done.refs_1_.refs_0_.refs_3_), channel_id=1, source_target_pairs={{0,8},{8,0},{16,24},{24,16},{1,17},{5,13},{13,5},{17,1},{21,29},{2... | collective-permute-start | bytes 1572872 | tf_op jit(solution)/shard_map/ppermute | solution.py:254
  29.8 12.8 %collective-permute-start.2 = (bf16[128,16,128]{2,1,0:T(8,128)(2,1)S(1)}, bf16[128,16,128]{2,1,0:T(8,128)(2,1)S(1)}, u32[]{:S(2)}, u32[]{:S(2)}) collective-permute-start(bf16[128,16,128]{2,1,0:T(8,128)(2,1)S(1)} %collective-permute-done.1.refs_2_.refs_0_.refs_6_), channel_id=1, source_target_pairs={{0,1},{1,2},{2,3},{3,0},{4,5},{5,6},{6,7},{7,4},{8,9},{9,10},{10,1... | collective-permute-start | bytes 1572872 | tf_op jit(solution)/shard_map/ppermute | solution.py:379
  36.2 10.2 %collective-permute-start.7 = (bf16[128,16,128]{2,1,0:T(8,128)(2,1)S(1)}, bf16[128,16,128]{2,1,0:T(8,128)(2,1)S(1)}, u32[]{:S(2)}, u32[]{:S(2)}) collective-permute-start(bf16[128,16,128]{2,1,0:T(8,128)(2,1)S(1)} %bitcast.7), channel_id=1, source_target_pairs={{8,24},{24,8},{1,9},{9,1},{13,29},{17,25},{25,17},{29,13},{2,10},{... | collective-permute-start | bytes 1572872 | tf_op jit(solution)/shard_map/ppermute | solution.py:254
  39.3 12.7 %collective-permute-start.8 = (bf16[128,16,128]{2,1,0:T(8,128)(2,1)S(1)}, bf16[128,16,128]{2,1,0:T(8,128)(2,1)S(1)}, u32[]{:S(2)}, u32[]{:S(2)}) collective-permute-start(bf16[128,16,128]{2,1,0:T(8,128)(2,1)S(1)} %collective-permute-done.1.refs_2_.refs_0_.refs_6_), channel_id=1, source_target_pairs={{0,8},{8,0},{16,24},{24,16},{1,17},{5,13},{13,5},{17,1},{21,29},{2... | collective-permute-start | bytes 1572872 | tf_op jit(solution)/shard_map/ppermute | solution.py:254
  42.7 18.2 %collective-permute-start.6 = (bf16[128,16,128]{2,1,0:T(8,128)(2,1)S(1)}, bf16[128,16,128]{2,1,0:T(8,128)(2,1)S(1)}, u32[]{:S(2)}, u32[]{:S(2)}) collective-permute-start(bf16[128,16,128]{2,1,0:T(8,128)(2,1)S(1)} %collective-permute-done.2.refs_3_.refs_0_.refs_4_.refs_9_), channel_id=1, source_target_pairs={{0,8},{8,0},{16,24},{24,16},{1,17},{5,13},{13,5},{17,1},{21,29},{2... | collective-permute-start | bytes 1572872 | tf_op jit(solution)/shard_map/ppermute | solution.py:254
  52.1 13.9 %collective-permute-start.9 = (bf16[128,16,128]{2,1,0:T(8,128)(2,1)S(1)}, bf16[128,16,128]{2,1,0:T(8,128)(2,1)S(1)}, u32[]{:S(2)}, u32[]{:S(2)}) collective-permute-start(bf16[128,16,128]{2,1,0:T(8,128)(2,1)S(1)} %bitcast.4), channel_id=1, source_target_pairs={{8,24},{24,8},{1,9},{9,1},{13,29},{17,25},{25,17},{29,13},{2,10},{... | collective-permute-start | bytes 1572872 | tf_op jit(solution)/shard_map/ppermute | solution.py:254
  60.9 5.1 %collective-permute-start.12 = (bf16[128,16,128]{2,1,0:T(8,128)(2,1)S(1)}, bf16[128,16,128]{2,1,0:T(8,128)(2,1)S(1)}, u32[]{:S(2)}, u32[]{:S(2)}) collective-permute-start(bf16[128,16,128]{2,1,0:T(8,128)(2,1)S(1)} %collective-permute-done.2.refs_3_.refs_0_.refs_4_.refs_9_), channel_id=1, source_target_pairs={{3,19},{11,27},{19,3},{27,11}} | collective-permute-start | bytes 1572872 | tf_op jit(solution)/shard_map/ppermute | solution.py:254
  61.7 9.9 %collective-permute-start.10 = (bf16[128,16,128]{2,1,0:T(8,128)(2,1)S(1)}, bf16[128,16,128]{2,1,0:T(8,128)(2,1)S(1)}, u32[]{:S(2)}, u32[]{:S(2)}) collective-permute-start(bf16[128,16,128]{2,1,0:T(8,128)(2,1)S(1)} %bitcast.5), channel_id=1, source_target_pairs={{8,24},{24,8},{1,9},{9,1},{13,29},{17,25},{25,17},{29,13},{2,10},{... | collective-permute-start | bytes 1572872 | tf_op jit(solution)/shard_map/ppermute | solution.py:254
  65.8 8.6 %copy-start.3 = (s32[64]{0:T(128)S(1)}, s32[64]{0:T(128)}, u32[]{:S(2)}) copy-start(s32[64]{0:T(128)} %reach_ref.1) | copy-start | bytes 772
  65.9 5.8 %collective-permute-start.11 = (bf16[2,128,16,128]{3,2,1,0:T(8,128)(2,1)S(1)}, bf16[2,128,16,128]{3,2,1,0:T(8,128)(2,1)S(1)}, u32[]{:S(2)}, u32[]{:S(2)}) collective-permute-start(bf16[2,128,16,128]{3,2,1,0:T(8,128)(2,1)S(1)} %choose.10), channel_id=1, source_target_pairs={{0,4},{4,0},{8,12},{12,8},{16,20},{20,16},{24,28},{28,24},{1,5},{5... | collective-permute-start | bytes 3145736 | tf_op jit(solution)/shard_map/ppermute | solution.py:254
  71.7 2.7 %collective-permute-start.13 = (bf16[2,128,16,128]{3,2,1,0:T(8,128)(2,1)S(1)}, bf16[2,128,16,128]{3,2,1,0:T(8,128)(2,1)S(1)}, u32[]{:S(2)}, u32[]{:S(2)}) collective-permute-start(bf16[2,128,16,128]{3,2,1,0:T(8,128)(2,1)S(1)} %choose.11), channel_id=1, source_target_pairs={{0,4},{4,0},{8,12},{12,8},{16,20},{20,16},{24,28},{28,24},{1,5},{5... | collective-permute-start | bytes 3145736 | tf_op jit(solution)/shard_map/ppermute | solution.py:254
